TPU v7x, 32 devices: a whole 2x2x4 slice. The times are simulated.
32 devices in a mesh: dp: 2 (over core), context: 16 (over z, y, x).
Axes of the slice: x: 2, y: 2, z: 4, core: 2. Of those that a mesh axis runs over, the one named last changes fastest.
Arguments:
- query_input: float32 [2, 2048, 2048], P('dp', None, 'context'), may hold values from -6 to 6
- key_input: float32 [2, 2048, 2048], P('dp', None, 'context'), may hold values from -6 to 6
- value_input: float32 [2, 2048, 2048], P('dp', None, 'context'), may hold values from -6 to 6
- filters: float32 [2048, 2048], P('context'), may hold values from -2 to 2, as said below
- cotangent: float32 [2, 2048, 2048], P('dp', None, 'context'), may hold values from -6 to 6
Outputs:
- gated_output: float32 [2, 2048, 2048], P('dp', None, 'context')
- grad_query: float32 [2, 2048, 2048], P('dp', None, 'context')
- grad_key: float32 [2, 2048, 2048], P('dp', None, 'context')
- grad_value: float32 [2, 2048, 2048], P('dp', None, 'context')
- grad_filter: float32 [2048, 2048], P('context')
Inputs may be any that keep to these rules, and one draw needn't show every extreme that they name: `filters`: real-valued filter taps, one for each channel and lag.
All inputs are finite; a program needn't handle non-finite values.
Results may differ from a plain program's by a relative error of at most 0.000098.
Values sent between devices are 32-bit elements; how exact they have to be, the bound alone decides.
No kernel may reach another device: no remote copies, remote signals or barrier semaphores. Data moves between devices by JAX's collectives and lax.ppermute only.
A program may use at most 128 MiB of HBM per device.

v0:
```python
import math

import jax
import jax.numpy as jnp
import ml_dtypes
import numpy as np
from jax import lax
from jax.experimental import pallas as pl
from jax.experimental.pallas import tpu as pltpu
from jax.sharding import PartitionSpec as P

ROWS = 8
VMEM_BYTES = 48 * 1024 * 1024


def twist(value, turn):
    re, im = value
    turn = turn % 1.0
    if turn == 0.0:
        return re, im
    if turn == 0.25:
        return im, -re
    if turn == 0.5:
        return -re, -im
    if turn == 0.75:
        return -im, re
    if turn in (0.125, 0.375, 0.625, 0.875):
        half = math.sqrt(0.5)
        a, b = (re + im) * half, (im - re) * half
        return twist((a, b), turn - 0.125)
    c, s = math.cos(2 * math.pi * turn), math.sin(2 * math.pi * turn)
    return re * c + im * s, im * c - re * s


def dft(values, sign):
    n = len(values)
    if n == 1:
        return values
    even, odd = dft(values[0::2], sign), dft(values[1::2], sign)
    out = [None] * n
    for k in range(n // 2):
        a, b = even[k], twist(odd[k], sign * k / n)
        out[k] = (a[0] + b[0], a[1] + b[1])
        out[k + n // 2] = (a[0] - b[0], a[1] - b[1])
    return out


def split(x):
    hi = x.astype(jnp.bfloat16)
    lo = (x - hi.astype(jnp.float32)).astype(jnp.bfloat16)
    return hi, lo


def times_table(x, table_ref):
    hi, lo = split(x)
    out = jnp.dot(hi, table_ref[0], preferred_element_type=jnp.float32)
    out += jnp.dot(lo, table_ref[0], preferred_element_type=jnp.float32)
    out += jnp.dot(hi, table_ref[1], preferred_element_type=jnp.float32)
    return out


def outer_forward(read, n, channels, tokens, tw_ref, y_ref):
    @pl.loop(0, channels // ROWS)
    def _(r):
        rows = pl.ds(pl.multiple_of(r * ROWS, ROWS), ROWS)
        values = []
        for n1 in range(n):
            x = read(n1, rows)
            turn = 2 * math.pi * n1 / (4 * n)
            if n1 == 0:
                values.append((x, jnp.zeros_like(x)))
            else:
                values.append((x * math.cos(turn), x * -math.sin(turn)))
        for m, (re, im) in enumerate(dft(values, 1)):
            c, s = tw_ref[0, m], tw_ref[1, m]
            y_ref[m, rows, :tokens] = re * c + im * s
            y_ref[m, rows, tokens:] = im * c - re * s


def outer_inverse(write, n, channels, tokens, tw_ref, y_ref):
    @pl.loop(0, channels // ROWS)
    def _(r):
        rows = pl.ds(pl.multiple_of(r * ROWS, ROWS), ROWS)
        values = []
        for m in range(n):
            re, im = y_ref[m, rows, :tokens], y_ref[m, rows, tokens:]
            c, s = tw_ref[0, m], tw_ref[1, m]
            values.append((re * c - im * s, im * c + re * s))
        for n1, (re, im) in enumerate(dft(values, -1)):
            turn = 2 * math.pi * n1 / (4 * n)
            if n1 == 0:
                write(n1, rows, re)
            else:
                write(n1, rows, re * math.cos(turn) - im * math.sin(turn))


def groups(n, channels, body):
    size = max(1, min(n, 512 // channels))

    @pl.loop(0, n // size)
    def _(i):
        body(pl.ds(i * size, size), size)


def flat(x):
    return x.reshape(x.shape[0] * x.shape[1], x.shape[2])


def filter_kernel(n, channels, tokens, f_ref, tw_ref, fwd_ref, out_ref, y_ref):
    outer_forward(
        lambda n1, rows: f_ref[rows, n1 * tokens : (n1 + 1) * tokens],
        n, channels, tokens, tw_ref, y_ref,
    )

    def body(ms, size):
        out_ref[ms] = times_table(flat(y_ref[ms]), fwd_ref).reshape(size, channels, 2 * tokens)

    groups(n, channels, body)


def conv_kernel(
    sign, n, channels, tokens, x_ref, spec_ref, tw_ref, fwd_ref, inv_ref, out_ref, own_ref, y_ref
):
    outer_forward(lambda n1, rows: x_ref[n1, rows], n, channels, tokens, tw_ref, y_ref)

    def body(ms, size):
        own = times_table(flat(y_ref[ms]), fwd_ref)
        own_ref[ms] = own.reshape(size, channels, 2 * tokens)
        spec = flat(spec_ref[ms])
        re, im = own[:, :tokens], own[:, tokens:]
        s_re, s_im = spec[:, :tokens], spec[:, tokens:] * sign
        both = jnp.concatenate([re * s_re - im * s_im, re * s_im + im * s_re], axis=1)
        y_ref[ms] = times_table(both, inv_ref).reshape(size, channels, 2 * tokens)

    groups(n, channels, body)

    def write(n1, rows, value):
        out_ref[n1, rows] = value

    outer_inverse(write, n, channels, tokens, tw_ref, y_ref)


def filter_grad_kernel(scale, n, channels, tokens, p_ref, g_ref, tw_ref, inv_ref, out_ref, y_ref):
    def body(ms, size):
        p, g = flat(p_ref[ms]), flat(g_ref[ms])
        p_re, p_im = p[:, :tokens], p[:, tokens:]
        re, im = g[:, :tokens], g[:, tokens:]
        both = jnp.concatenate([re * p_re + im * p_im, im * p_re - re * p_im], axis=1)
        y_ref[ms] = times_table(both, inv_ref).reshape(size, channels, 2 * tokens)

    groups(n, channels, body)

    def write(n1, rows, value):
        out_ref[rows, n1 * tokens : (n1 + 1) * tokens] = value * scale

    outer_inverse(write, n, channels, tokens, tw_ref, y_ref)


def call(body, outs, n, channels, tokens, passes):
    size = n * channels * tokens
    return pl.pallas_call(
        body,
        out_shape=outs,
        scratch_shapes=[pltpu.VMEM((n, channels, 2 * tokens), jnp.float32)],
        compiler_params=pltpu.CompilerParams(vmem_limit_bytes=VMEM_BYTES),
        cost_estimate=pl.CostEstimate(
            flops=passes * size * 2 * 2 * tokens * 4, bytes_accessed=6 * size * 4, transcendentals=0
        ),
    )


def product_kernel(a_ref, b_ref, out_ref):
    out_ref[...] = a_ref[...] * b_ref[...]


def gate_kernel(x_ref, a_ref, b_ref, oa_ref, ob_ref):
    x = x_ref[...]
    oa_ref[...] = x * a_ref[...]
    ob_ref[...] = x * b_ref[...]


def tiled(body, n_in, n_out, shape):
    rows = math.gcd(shape[0], 512)
    spec = pl.BlockSpec((rows, shape[1]), lambda i: (i, 0))
    return pl.pallas_call(
        body,
        grid=(shape[0] // rows,),
        in_specs=[spec] * n_in,
        out_specs=[spec] * n_out,
        out_shape=[jax.ShapeDtypeStruct(shape, jnp.float32)] * n_out,
        compiler_params=pltpu.CompilerParams(vmem_limit_bytes=VMEM_BYTES),
        cost_estimate=pl.CostEstimate(
            flops=n_out * shape[0] * shape[1],
            bytes_accessed=(n_in + n_out) * 4 * shape[0] * shape[1],
            transcendentals=0,
        ),
    )


def tables(n, tokens):
    length = n * tokens
    m = np.arange(n)[:, None] + 0.25
    angle = 2 * np.pi * m * np.arange(tokens)[None, :] / length
    tw = np.stack([np.cos(angle), np.sin(angle)])[:, :, None, :]
    tw = np.broadcast_to(tw, (2, n, ROWS, tokens)).astype(np.float32)
    k = np.arange(tokens)
    inner = 2 * np.pi * ((k[:, None] * k[None, :]) % tokens) / tokens
    c, s = np.cos(inner), np.sin(inner)

    def pair(table):
        hi = table.astype(ml_dtypes.bfloat16)
        lo = (table - hi.astype(np.float64)).astype(ml_dtypes.bfloat16)
        return jnp.asarray(np.stack([hi, lo]))

    fwd = pair(np.block([[c, -s], [s, c]]))
    inv = pair(np.block([[c, s], [-s, c]]) / length)
    return jnp.asarray(tw), fwd, inv


def on_device(query_input, key_input, value_input, filters, cotangent):
    n = lax.axis_size("context")
    pair_size = lax.axis_size("dp")
    _, width, tokens = query_input.shape
    channels, length = filters.shape
    scale = 1.0 / math.sqrt(pair_size * length)
    sizes = (n, channels, tokens)
    tw, fwd, inv = tables(n, tokens)
    spectrum = jax.ShapeDtypeStruct((n, channels, 2 * tokens), jnp.float32)
    rows = jax.ShapeDtypeStruct((n, channels, tokens), jnp.float32)
    lags = jax.ShapeDtypeStruct((channels, length), jnp.float32)

    def exchange(x):
        return lax.all_to_all(x.reshape(rows.shape), "context", 0, 0, tiled=True)

    def part(body, *args):
        return lambda *refs: body(*args, *sizes, *refs)

    query, key, value, cot = (
        x.reshape(width, tokens) for x in (query_input, key_input, value_input, cotangent)
    )
    multiply = tiled(product_kernel, 2, 1, (width, tokens))
    (product,) = multiply(key, value)
    (conv_grad,) = multiply(cot, query)
    product_ch = exchange(product)
    grad_ch = exchange(conv_grad)
    filt = call(part(filter_kernel), spectrum, *sizes, 1)(filters, tw, fwd)
    conv_ch, prod_spec = call(part(conv_kernel, 1.0), [rows, spectrum], *sizes, 2)(
        product_ch, filt, tw, fwd, inv
    )
    conv_tok = exchange(conv_ch).reshape(width, tokens)
    back_ch, grad_spec = call(part(conv_kernel, -1.0), [rows, spectrum], *sizes, 2)(
        grad_ch, filt, tw, fwd, inv
    )
    back_tok = exchange(back_ch).reshape(width, tokens)
    own = call(part(filter_grad_kernel, scale), lags, *sizes, 1)(prod_spec, grad_spec, tw, inv)
    if pair_size == 2:
        grad_filter = own + lax.ppermute(own, "dp", [(0, 1), (1, 0)])
    else:
        grad_filter = lax.psum(own, "dp")
    gate = tiled(gate_kernel, 3, 2, (width, tokens))
    gated, grad_query = gate(conv_tok, query, cot)
    grad_key, grad_value = gate(back_tok, value, key)
    shape = query_input.shape
    return (
        gated.reshape(shape),
        grad_query.reshape(shape),
        grad_key.reshape(shape),
        grad_value.reshape(shape),
        grad_filter,
    )


def solution(mesh):
    in_specs = (
        P("dp", None, "context"),
        P("dp", None, "context"),
        P("dp", None, "context"),
        P("context", None),
        P("dp", None, "context"),
    )
    out_specs = (
        P("dp", None, "context"),
        P("dp", None, "context"),
        P("dp", None, "context"),
        P("dp", None, "context"),
        P("context", None),
    )
    return jax.shard_map(
        on_device, mesh=mesh, in_specs=in_specs, out_specs=out_specs, check_vma=False
    )
```

profile of v0, /device:TPU:0, one launch (start us, length us, event | category | flops | bytes accessed | tf_op | source)
XLA Modules:
  0.0 129.1 jit_solution(17270929882498875154)
XLA Ops:
  1.9 1.2 copy-done.4
  3.1 1.5 %shard_map.123 = f32[2048,128]{1,0:T(8,128)} custom-call(f32[2048,128]{1,0:T(8,128)S(1)} %bitcast.18, f32[2048,128]{1,0:T(8,128)S(1)} %bitcast.16), custom_call_target="tpu_custom_call" | custom-call | flops 262144 | bytes 3145728 | tf_op jit(solution)/shard_map/pallas_call | solution.py:243
  4.6 8.4 %all-to-all-start.2 = ((f32[16,128,128]{2,1,0:T(8,128)}), f32[16,128,128]{2,1,0:T(8,128)}, u32[]{:S(2)}, u32[]{:S(2)}) async-start(f32[16,128,128]{2,1,0:T(8,128)} %bitcast.8), calls=%async_computation.2 | async-start | bytes 2097152 | tf_op jit(solution)/shard_map/all_to_all | solution.py:233
  13.1 1.6 %shard_map.119 = f32[2048,128]{1,0:T(8,128)} custom-call(f32[2048,128]{1,0:T(8,128)S(1)} %bitcast.12, f32[2048,128]{1,0:T(8,128)S(1)} %bitcast.14), custom_call_target="tpu_custom_call" | custom-call | flops 262144 | bytes 3145728 | tf_op jit(solution)/shard_map/pallas_call | solution.py:242
  14.6 22.9 %all-to-all-done.2.refs_0_ = f32[16,128,128]{2,1,0:T(8,128)} async-done(((f32[16,128,128]{2,1,0:T(8,128)}), f32[16,128,128]{2,1,0:T(8,128)}, u32[]{:S(2)}, u32[]{:S(2)}) %all-to-all-start.2) | async-done | bytes 1048608 | tf_op jit(solution)/shard_map/all_to_all | solution.py:233
  37.5 5.9 %all-to-all-start = ((f32[16,128,128]{2,1,0:T(8,128)}), f32[16,128,128]{2,1,0:T(8,128)}, u32[]{:S(2)}, u32[]{:S(2)}) async-start(f32[16,128,128]{2,1,0:T(8,128)} %bitcast.2), calls=%async_computation | async-start | bytes 2097152 | tf_op jit(solution)/shard_map/all_to_all | solution.py:233
  44.4 2.3 %shard_map.120.refs_1_ = f32[16,128,256]{2,1,0:T(8,128)S(1)} custom-call(f32[128,2048]{1,0:T(8,128)S(1)} %copy-done.13, f32[2,16,8,128]{3,2,1,0:T(8,128)S(1)} %copy-done.16, bf16[2,256,256]{2,1,0:T(8,128)(2,1)S(1)} %copy-done.18), custom_call_target="tpu_custom_call" | custom-call | flops 536870912 | bytes 6291456 | tf_op jit(solution)/shard_map/pallas_call | solution.py:246
  46.7 1.3 %copy-done.8 = f32[16,128,256]{2,1,0:T(8,128)} copy-done((f32[16,128,256]{2,1,0:T(8,128)}, f32[16,128,256]{2,1,0:T(8,128)S(1)}, u32[]{:S(2)}) %copy-start.8) | copy-done | bytes 2097176
  48.0 7.3 %shard_map.124 = (f32[16,128,128]{2,1,0:T(8,128)S(1)}, f32[16,128,256]{2,1,0:T(8,128)S(1)}) custom-call(f32[16,128,128]{2,1,0:T(8,128)} %all-to-all-done.2.refs_0_, f32[16,128,256]{2,1,0:T(8,128)} %copy-done.8, f32[2,16,8,128]{3,2,1,0:T(8,128)S(1)} %copy-done.16, bf16[2,256,256]{2,1,0:T(8,128)(2,1)S(1)} %copy-done.19, bf16[2,256,256]{2,1,0:T(8,128)(2,1)S(1)} %copy-done.17), custom_call_target="tpu_custom_call" | custom-call | flops 1073741824 | bytes 6291456 | tf_op jit(solution)/shard_map/pallas_call | solution.py:251
  55.3 1.3 %copy-done.9 = f32[16,128,256]{2,1,0:T(8,128)} copy-done((f32[16,128,256]{2,1,0:T(8,128)}, f32[16,128,256]{2,1,0:T(8,128)S(1)}, u32[]{:S(2)}) %copy-start.9) | copy-done | bytes 2097176
  57.6 8.8 %all-to-all-done.refs_0_ = f32[16,128,128]{2,1,0:T(8,128)} async-done(((f32[16,128,128]{2,1,0:T(8,128)}), f32[16,128,128]{2,1,0:T(8,128)}, u32[]{:S(2)}, u32[]{:S(2)}) %all-to-all-start) | async-done | bytes 1048608 | tf_op jit(solution)/shard_map/all_to_all | solution.py:233
  66.4 6.0 %all-to-all-start.3 = ((f32[16,128,128]{2,1,0:T(8,128)}), f32[16,128,128]{2,1,0:T(8,128)S(1)}, u32[]{:S(2)}, u32[]{:S(2)}) async-start(f32[16,128,128]{2,1,0:T(8,128)} %copy-done.15), calls=%async_computation.3 | async-start | bytes 2097152 | tf_op jit(solution)/shard_map/all_to_all | solution.py:233
  73.4 7.3 %shard_map.121 = (f32[16,128,128]{2,1,0:T(8,128)S(1)}, f32[16,128,256]{2,1,0:T(8,128)S(1)}) custom-call(f32[16,128,128]{2,1,0:T(8,128)} %all-to-all-done.refs_0_, f32[16,128,256]{2,1,0:T(8,128)} %copy-done.8, f32[2,16,8,128]{3,2,1,0:T(8,128)S(1)} %copy-done.16, bf16[2,256,256]{2,1,0:T(8,128)(2,1)S(1)} %copy-done.20, bf16[2,256,256]{2,1,0:T(8,128)(2,1)S(1)} %copy-done.17), custom_call_target="tpu_custom_call" | custom-call | flops 1073741824 | bytes 6291456 | tf_op jit(solution)/shard_map/pallas_call | solution.py:247
  80.7 1.3 %copy-done.11 = f32[16,128,256]{2,1,0:T(8,128)} copy-done((f32[16,128,256]{2,1,0:T(8,128)}, f32[16,128,256]{2,1,0:T(8,128)S(1)}, u32[]{:S(2)}) %copy-start.11) | copy-done | bytes 2097176
  83.0 12.3 %all-to-all-done.3 = f32[16,128,128]{2,1,0:T(8,128)S(1)} async-done(((f32[16,128,128]{2,1,0:T(8,128)}), f32[16,128,128]{2,1,0:T(8,128)S(1)}, u32[]{:S(2)}, u32[]{:S(2)}) %all-to-all-start.3) | async-done | bytes 1048608 | tf_op jit(solution)/shard_map/all_to_all | solution.py:233
  95.2 6.1 %all-to-all-start.1 = ((f32[16,128,128]{2,1,0:T(8,128)}), f32[16,128,128]{2,1,0:T(8,128)}, u32[]{:S(2)}, u32[]{:S(2)}) async-start(f32[16,128,128]{2,1,0:T(8,128)} %copy-done.14), calls=%async_computation.1 | async-start | bytes 2097152 | tf_op jit(solution)/shard_map/all_to_all | solution.py:233
  101.3 1.6 %copy-done.10 = f32[16,128,256]{2,1,0:T(8,128)S(1)} copy-done((f32[16,128,256]{2,1,0:T(8,128)S(1)}, f32[16,128,256]{2,1,0:T(8,128)}, u32[]{:S(2)}) %copy-start.10) | copy-done | bytes 2097176
  102.9 1.6 %copy-done.12 = f32[16,128,256]{2,1,0:T(8,128)S(1)} copy-done((f32[16,128,256]{2,1,0:T(8,128)S(1)}, f32[16,128,256]{2,1,0:T(8,128)}, u32[]{:S(2)}) %copy-start.12) | copy-done | bytes 2097176
  104.5 2.4 %shard_map.126 = f32[128,2048]{1,0:T(8,128)S(1)} custom-call(f32[16,128,256]{2,1,0:T(8,128)S(1)} %copy-done.12, f32[16,128,256]{2,1,0:T(8,128)S(1)} %copy-done.10, f32[2,16,8,128]{3,2,1,0:T(8,128)S(1)} %copy-done.16, bf16[2,256,256]{2,1,0:T(8,128)(2,1)S(1)} %copy-done.17), custom_call_target="tpu_custom_call" | custom-call | flops 536870912 | bytes 6291456 | tf_op jit(solution)/shard_map/pallas_call | solution.py:255
  107.0 2.6 %collective-permute-done = f32[128,2048]{1,0:T(8,128)S(1)} collective-permute-done((f32[128,2048]{1,0:T(8,128)S(1)}, f32[128,2048]{1,0:T(8,128)S(1)}, u32[]{:S(2)}, u32[]{:S(2)}) %collective-permute-start) | collective-permute-done | bytes 1048608 | tf_op jit(solution)/shard_map/ppermute | solution.py:257
  110.8 1.8 %shard_map.125 = (f32[2048,128]{1,0:T(8,128)}, f32[2048,128]{1,0:T(8,128)}) custom-call(f32[2048,128]{1,0:T(8,128)S(1)} %bitcast.20, f32[2048,128]{1,0:T(8,128)S(1)} %bitcast.15, f32[2048,128]{1,0:T(8,128)S(1)} %bitcast.13), custom_call_target="tpu_custom_call" | custom-call | flops 524288 | bytes 5242880 | tf_op jit(solution)/shard_map/pallas_call | solution.py:262
  112.6 11.7 %all-to-all-done.1 = f32[16,128,128]{2,1,0:T(8,128)} async-done(((f32[16,128,128]{2,1,0:T(8,128)}), f32[16,128,128]{2,1,0:T(8,128)}, u32[]{:S(2)}, u32[]{:S(2)}) %all-to-all-start.1) | async-done | bytes 1048608 | tf_op jit(solution)/shard_map/all_to_all | solution.py:233
  124.3 1.2 copy-done.5
  125.5 3.6 %shard_map.122 = (f32[2048,128]{1,0:T(8,128)}, f32[2048,128]{1,0:T(8,128)}) custom-call(f32[2048,128]{1,0:T(8,128)} %bitcast.3.x_ref, f32[2048,128]{1,0:T(8,128)S(1)} %bitcast.17, f32[2048,128]{1,0:T(8,128)S(1)} %bitcast.19), custom_call_target="tpu_custom_call" | custom-call | flops 524288 | bytes 5242880 | tf_op jit(solution)/shard_map/pallas_call | solution.py:261
  (37 shorter events, 6.3 us)
Async XLA Ops:
  0.6 1.2 copy-start.2
  1.9 1.2 copy-start.4
  3.1 9.9 %copy-start = (f32[1,2048,128]{2,1,0:T(8,128)S(1)}, f32[1,2048,128]{2,1,0:T(8,128)}, u32[]{:S(2)}) copy-start(f32[1,2048,128]{2,1,0:T(8,128)} %param.9) | copy-start | bytes 3145732
  3.1 9.9 %copy-start.1 = (f32[1,2048,128]{2,1,0:T(8,128)S(1)}, f32[1,2048,128]{2,1,0:T(8,128)}, u32[]{:S(2)}) copy-start(f32[1,2048,128]{2,1,0:T(8,128)} %param.10) | copy-start | bytes 3145732
  4.6 32.9 %all-to-all-start.2 = ((f32[16,128,128]{2,1,0:T(8,128)}), f32[16,128,128]{2,1,0:T(8,128)}, u32[]{:S(2)}, u32[]{:S(2)}) async-start(f32[16,128,128]{2,1,0:T(8,128)} %bitcast.8), calls=%async_computation.2 | async-start | bytes 2097152 | tf_op jit(solution)/shard_map/all_to_all | solution.py:233
  13.0 30.4 %copy-start.13 = (f32[128,2048]{1,0:T(8,128)S(1)}, f32[128,2048]{1,0:T(8,128)}, u32[]{:S(2)}) copy-start(f32[128,2048]{1,0:T(8,128)} %refs_0_.1) | copy-start | bytes 3145732
  13.0 30.4 %copy-start.16 = (f32[2,16,8,128]{3,2,1,0:T(8,128)S(1)}, f32[2,16,8,128]{3,2,1,0:T(8,128)}, u32[]{:S(2)}) copy-start(f32[2,16,8,128]{3,2,1,0:T(8,128)} %constant.8.clone.refs_1_.refs_2_) | copy-start | bytes 393220
  37.5 28.9 %all-to-all-start = ((f32[16,128,128]{2,1,0:T(8,128)}), f32[16,128,128]{2,1,0:T(8,128)}, u32[]{:S(2)}, u32[]{:S(2)}) async-start(f32[16,128,128]{2,1,0:T(8,128)} %bitcast.2), calls=%async_computation | async-start | bytes 2097152 | tf_op jit(solution)/shard_map/all_to_all | solution.py:233
  44.4 3.6 %copy-start.17 = (bf16[2,256,256]{2,1,0:T(8,128)(2,1)S(1)}, bf16[2,256,256]{2,1,0:T(8,128)(2,1)}, u32[]{:S(2)}) copy-start(bf16[2,256,256]{2,1,0:T(8,128)(2,1)} %constant.7.clone.refs_4_.refs_3_) | copy-start | bytes 786436
  44.4 3.6 %copy-start.19 = (bf16[2,256,256]{2,1,0:T(8,128)(2,1)S(1)}, bf16[2,256,256]{2,1,0:T(8,128)(2,1)}, u32[]{:S(2)}) copy-start(bf16[2,256,256]{2,1,0:T(8,128)(2,1)} %constant.6.clone.refs_2_.refs_3_) | copy-start | bytes 786436
  46.7 1.3 %copy-start.8 = (f32[16,128,256]{2,1,0:T(8,128)}, f32[16,128,256]{2,1,0:T(8,128)S(1)}, u32[]{:S(2)}) copy-start(f32[16,128,256]{2,1,0:T(8,128)S(1)} %shard_map.120.refs_1_) | copy-start | bytes 6291460
  55.3 1.4 %copy-start.9 = (f32[16,128,256]{2,1,0:T(8,128)}, f32[16,128,256]{2,1,0:T(8,128)S(1)}, u32[]{:S(2)}) copy-start(f32[16,128,256]{2,1,0:T(8,128)S(1)} %get-tuple-element.20.refs_1_) | copy-start | bytes 6291460
  56.6 1.0 copy-start.15
  66.4 28.8 %all-to-all-start.3 = ((f32[16,128,128]{2,1,0:T(8,128)}), f32[16,128,128]{2,1,0:T(8,128)S(1)}, u32[]{:S(2)}, u32[]{:S(2)}) async-start(f32[16,128,128]{2,1,0:T(8,128)} %copy-done.15), calls=%async_computation.3 | async-start | bytes 2097152 | tf_op jit(solution)/shard_map/all_to_all | solution.py:233
  80.7 1.3 %copy-start.11 = (f32[16,128,256]{2,1,0:T(8,128)}, f32[16,128,256]{2,1,0:T(8,128)S(1)}, u32[]{:S(2)}) copy-start(f32[16,128,256]{2,1,0:T(8,128)S(1)} %get-tuple-element.19.refs_0_) | copy-start | bytes 6291460
  82.0 1.0 copy-start.14
  95.2 11.7 %copy-start.6 = (f32[16,128,128]{2,1,0:T(8,128)}, f32[16,128,128]{2,1,0:T(8,128)S(1)}, u32[]{:S(2)}) copy-start(f32[16,128,128]{2,1,0:T(8,128)S(1)} %all-to-all-done.3) | copy-start | bytes 3145732
  95.2 29.0 %all-to-all-start.1 = ((f32[16,128,128]{2,1,0:T(8,128)}), f32[16,128,128]{2,1,0:T(8,128)}, u32[]{:S(2)}, u32[]{:S(2)}) async-start(f32[16,128,128]{2,1,0:T(8,128)} %copy-done.14), calls=%async_computation.1 | async-start | bytes 2097152 | tf_op jit(solution)/shard_map/all_to_all | solution.py:233
  101.3 1.6 %copy-start.10 = (f32[16,128,256]{2,1,0:T(8,128)S(1)}, f32[16,128,256]{2,1,0:T(8,128)}, u32[]{:S(2)}) copy-start(f32[16,128,256]{2,1,0:T(8,128)} %copy-done.9) | copy-start | bytes 6291460
  102.9 1.6 %copy-start.12 = (f32[16,128,256]{2,1,0:T(8,128)S(1)}, f32[16,128,256]{2,1,0:T(8,128)}, u32[]{:S(2)}) copy-start(f32[16,128,256]{2,1,0:T(8,128)} %copy-done.11) | copy-start | bytes 6291460
  106.9 2.7 %collective-permute-start = (f32[128,2048]{1,0:T(8,128)S(1)}, f32[128,2048]{1,0:T(8,128)S(1)}, u32[]{:S(2)}, u32[]{:S(2)}) collective-permute-start(f32[128,2048]{1,0:T(8,128)S(1)} %shard_map.126), channel_id=1, source_target_pairs={{0,16},{16,0},{1,17},{17,1},{2,18},{18,2},{3,19},{19,3},{4,20},{20... | collective-permute-start | bytes 3145736 | tf_op jit(solution)/shard_map/ppermute | solution.py:257
  107.0 3.8 %copy-start.7 = (f32[16,128,128]{2,1,0:T(8,128)S(1)}, f32[16,128,128]{2,1,0:T(8,128)}, u32[]{:S(2)}) copy-start(f32[16,128,128]{2,1,0:T(8,128)} %copy-done.6) | copy-start | bytes 3145732
  110.8 13.5 %copy-start.3 = (f32[1,2048,128]{2,1,0:T(8,128)S(1)}, f32[1,2048,128]{2,1,0:T(8,128)}, u32[]{:S(2)}) copy-start(f32[1,2048,128]{2,1,0:T(8,128)} %param.8) | copy-start | bytes 3145732
  124.3 1.2 copy-start.5
  (2 other events, 1.9 us)
where the time goes:
time: 130 us; the launch traced here: 129 us
  waiting for transfers between devices  58.2 us (45%)
  Pallas kernels  27.9 us (21%)
  starting transfers between devices  26.4 us (20%)
  local copies, waits for them, and re-layouts  14.7 us (11%)
    all_to_all x4, waiting for transfers between devices, exchange(): return lax.all_to_all(x.reshape(rows.shape), 'context', 0, 0, tiled=True)  55.6 us
    all_to_all x4, starting transfers between devices, exchange(): return lax.all_to_all(x.reshape(rows.shape), 'context', 0, 0, tiled=True)  26.3 us
    unnamed x42, local copies, waits for them, and re-layouts  14.7 us
    pallas_call x1, Pallas kernels, on_device(): call(part(conv_kernel, -1.0), [rows, spectrum], *sizes, 2)  7.3 us
    pallas_call x1, Pallas kernels, on_device(): call(part(conv_kernel, 1.0), [rows, spectrum], *sizes, 2)  7.3 us
    pallas_call x1, Pallas kernels, on_device(): gated, grad_query = gate(conv_tok, query, cot)  3.59 us
    ppermute x1, waiting for transfers between devices, on_device(): grad_filter = own + lax.ppermute(own, 'dp', [(0, 1), (1, 0)])  2.63 us
  transfers between devices with their start and end apart: 5, of which 5 were waited for; matrix products, arithmetic and copies ran while one was open for 1% of the time, Pallas kernels for 18%

commit v1 on v0

--- a/solution.py
+++ b/solution.py
@@ -10,7 +10,8 @@
 from jax.sharding import PartitionSpec as P
 
 ROWS = 8
-VMEM_BYTES = 48 * 1024 * 1024
+MOST_SWAPS = 32
+VMEM_BYTES = 24 * 1024 * 1024
 
 
 def twist(value, turn):
@@ -118,9 +119,19 @@
     groups(n, channels, body)
 
 
-def conv_kernel(
-    sign, n, channels, tokens, x_ref, spec_ref, tw_ref, fwd_ref, inv_ref, out_ref, own_ref, y_ref
-):
+def partners(n):
+    far = list(range(n - 1, n // 2 - 1, -1))
+    near = list(range(n // 2 - 1, -1, -1))
+    return [d for pair in zip(far, near) for d in pair]
+
+
+def conv_kernel(sign, n, channels, tokens, *refs):
+    x_refs, refs = refs[:n], refs[n:]
+    spec_ref, tw_ref, fwd_ref, inv_ref = refs[:4]
+    out_refs, (own_ref, x_ref, y_ref) = refs[4 : n + 4], refs[n + 4 :]
+    me = lax.axis_index("context")
+    for d in partners(n):
+        x_ref[me ^ d] = x_refs[d][...]
     outer_forward(lambda n1, rows: x_ref[n1, rows], n, channels, tokens, tw_ref, y_ref)
 
     def body(ms, size):
@@ -135,9 +146,11 @@
     groups(n, channels, body)
 
     def write(n1, rows, value):
-        out_ref[n1, rows] = value
+        x_ref[n1, rows] = value
 
     outer_inverse(write, n, channels, tokens, tw_ref, y_ref)
+    for d in partners(n):
+        out_refs[d][...] = x_ref[me ^ d]
 
 
 def filter_grad_kernel(scale, n, channels, tokens, p_ref, g_ref, tw_ref, inv_ref, out_ref, y_ref):
@@ -156,12 +169,12 @@
     outer_inverse(write, n, channels, tokens, tw_ref, y_ref)
 
 
-def call(body, outs, n, channels, tokens, passes):
+def call(body, outs, n, channels, tokens, passes, extra=()):
     size = n * channels * tokens
     return pl.pallas_call(
         body,
         out_shape=outs,
-        scratch_shapes=[pltpu.VMEM((n, channels, 2 * tokens), jnp.float32)],
+        scratch_shapes=[*extra, pltpu.VMEM((n, channels, 2 * tokens), jnp.float32)],
         compiler_params=pltpu.CompilerParams(vmem_limit_bytes=VMEM_BYTES),
         cost_estimate=pl.CostEstimate(
             flops=passes * size * 2 * 2 * tokens * 4, bytes_accessed=6 * size * 4, transcendentals=0
@@ -169,30 +182,63 @@
     )
 
 
-def product_kernel(a_ref, b_ref, out_ref):
-    out_ref[...] = a_ref[...] * b_ref[...]
-
-
-def gate_kernel(x_ref, a_ref, b_ref, oa_ref, ob_ref):
-    x = x_ref[...]
-    oa_ref[...] = x * a_ref[...]
-    ob_ref[...] = x * b_ref[...]
-
-
-def tiled(body, n_in, n_out, shape):
-    rows = math.gcd(shape[0], 512)
-    spec = pl.BlockSpec((rows, shape[1]), lambda i: (i, 0))
+def product_kernel(n, a_ref, b_ref, *refs):
+    out_refs, (a_buf, b_buf, sems) = refs[:n], refs[n:]
+    me = lax.axis_index("context")
+    copies = {}
+    for d in partners(n):
+        copies[d] = [
+            pltpu.make_async_copy(ref.at[me ^ d], buf.at[d], sems.at[i, d])
+            for i, (ref, buf) in enumerate(((a_ref, a_buf), (b_ref, b_buf)))
+        ]
+        for copy in copies[d]:
+            copy.start()
+    for d in partners(n):
+        for copy in copies[d]:
+            copy.wait()
+        out_refs[d][...] = a_buf[d] * b_buf[d]
+
+
+def gate_kernel(n, *refs):
+    x_refs, refs = refs[:n], refs[n:]
+    a_ref, b_ref, oa_ref, ob_ref, a_buf, b_buf, sems = refs
+    me = lax.axis_index("context")
+    loads, stores = {}, {}
+    for d in partners(n):
+        pairs = ((a_ref, a_buf, oa_ref), (b_ref, b_buf, ob_ref))
+        loads[d] = [
+            pltpu.make_async_copy(ref.at[me ^ d], buf.at[d], sems.at[i, d])
+            for i, (ref, buf, _) in enumerate(pairs)
+        ]
+        stores[d] = [
+            pltpu.make_async_copy(buf.at[d], out.at[me ^ d], sems.at[i + 2, d])
+            for i, (_, buf, out) in enumerate(pairs)
+        ]
+        for copy in loads[d]:
+            copy.start()
+    for d in partners(n):
+        x = x_refs[d][...]
+        for load, store, buf in zip(loads[d], stores[d], (a_buf, b_buf)):
+            load.wait()
+            buf[d] = buf[d] * x
+            store.start()
+    for d in partners(n):
+        for store in stores[d]:
+            store.wait()
+
+
+def local_call(body, n, n_in, n_out, shape, blocks):
+    whole, block = jax.ShapeDtypeStruct(shape, jnp.float32), jax.ShapeDtypeStruct(shape[1:], jnp.float32)
+    hbm, vmem = pl.BlockSpec(memory_space=pltpu.HBM), pl.BlockSpec(memory_space=pltpu.VMEM)
     return pl.pallas_call(
         body,
-        grid=(shape[0] // rows,),
-        in_specs=[spec] * n_in,
-        out_specs=[spec] * n_out,
-        out_shape=[jax.ShapeDtypeStruct(shape, jnp.float32)] * n_out,
+        in_specs=[vmem] * blocks + [hbm] * n_in,
+        out_specs=[hbm] * n_out if n_out else [vmem] * n,
+        out_shape=[whole] * n_out if n_out else [block] * n,
+        scratch_shapes=[pltpu.VMEM(shape, jnp.float32)] * 2 + [pltpu.SemaphoreType.DMA((4, n))],
         compiler_params=pltpu.CompilerParams(vmem_limit_bytes=VMEM_BYTES),
         cost_estimate=pl.CostEstimate(
-            flops=n_out * shape[0] * shape[1],
-            bytes_accessed=(n_in + n_out) * 4 * shape[0] * shape[1],
-            transcendentals=0,
+            flops=2 * math.prod(shape), bytes_accessed=4 * 4 * math.prod(shape), transcendentals=0
         ),
     )
 
@@ -229,37 +275,48 @@
     rows = jax.ShapeDtypeStruct((n, channels, tokens), jnp.float32)
     lags = jax.ShapeDtypeStruct((channels, length), jnp.float32)
 
-    def exchange(x):
-        return lax.all_to_all(x.reshape(rows.shape), "context", 0, 0, tiled=True)
+    block = jax.ShapeDtypeStruct(rows.shape[1:], jnp.float32)
+    swaps = [[(i, i ^ d) for i in range(n)] for d in range(n)]
+
+    def exchange(blocks):
+        if n > MOST_SWAPS:
+            order = lax.axis_index("context") ^ jnp.arange(n)
+            got = jnp.take(jnp.stack(blocks), order, axis=0)
+            got = lax.all_to_all(got, "context", 0, 0, tiled=True)
+            return list(jnp.take(got, order, axis=0))
+        got = {0: blocks[0]}
+        for d in partners(n):
+            if d:
+                got[d] = lax.ppermute(blocks[d], "context", swaps[d])
+        return [got[d] for d in range(n)]
 
     def part(body, *args):
         return lambda *refs: body(*args, *sizes, *refs)
 
     query, key, value, cot = (
-        x.reshape(width, tokens) for x in (query_input, key_input, value_input, cotangent)
-    )
-    multiply = tiled(product_kernel, 2, 1, (width, tokens))
-    (product,) = multiply(key, value)
-    (conv_grad,) = multiply(cot, query)
-    product_ch = exchange(product)
-    grad_ch = exchange(conv_grad)
+        x.reshape(rows.shape) for x in (query_input, key_input, value_input, cotangent)
+    )
+    multiply = local_call(lambda *refs: product_kernel(n, *refs), n, 2, 0, rows.shape, 0)
+    product_ch = exchange(multiply(key, value))
+    grad_ch = exchange(multiply(cot, query))
     filt = call(part(filter_kernel), spectrum, *sizes, 1)(filters, tw, fwd)
-    conv_ch, prod_spec = call(part(conv_kernel, 1.0), [rows, spectrum], *sizes, 2)(
-        product_ch, filt, tw, fwd, inv
-    )
-    conv_tok = exchange(conv_ch).reshape(width, tokens)
-    back_ch, grad_spec = call(part(conv_kernel, -1.0), [rows, spectrum], *sizes, 2)(
-        grad_ch, filt, tw, fwd, inv
-    )
-    back_tok = exchange(back_ch).reshape(width, tokens)
+    buffer = [pltpu.VMEM(rows.shape, jnp.float32)]
+    *conv_ch, prod_spec = call(part(conv_kernel, 1.0), [block] * n + [spectrum], *sizes, 2, buffer)(
+        *product_ch, filt, tw, fwd, inv
+    )
+    conv_tok = exchange(conv_ch)
+    *back_ch, grad_spec = call(part(conv_kernel, -1.0), [block] * n + [spectrum], *sizes, 2, buffer)(
+        *grad_ch, filt, tw, fwd, inv
+    )
+    back_tok = exchange(back_ch)
     own = call(part(filter_grad_kernel, scale), lags, *sizes, 1)(prod_spec, grad_spec, tw, inv)
     if pair_size == 2:
         grad_filter = own + lax.ppermute(own, "dp", [(0, 1), (1, 0)])
     else:
         grad_filter = lax.psum(own, "dp")
-    gate = tiled(gate_kernel, 3, 2, (width, tokens))
-    gated, grad_query = gate(conv_tok, query, cot)
-    grad_key, grad_value = gate(back_tok, value, key)
+    gate = local_call(lambda *refs: gate_kernel(n, *refs), n, 2, 2, rows.shape, n)
+    gated, grad_query = gate(*conv_tok, query, cot)
+    grad_key, grad_value = gate(*back_tok, value, key)
     shape = query_input.shape
     return (
         gated.reshape(shape),

time: 130 us -> 157 us (1.21)
  starting transfers between devices: 26.4 us -> 106 us
  waiting for transfers between devices: 58.2 us -> 14.4 us
  local copies, waits for them, and re-layouts: 14.7 us -> 2.63 us
  Pallas kernels: 27.9 us -> 32 us
    ppermute x0 -> x60, starting transfers between devices: none -> 106 us  [exchange(): got[d] = lax.ppermute(blocks[d], 'context', swaps[d])]
    all_to_all x4 -> x0, waiting for transfers between devices: 55.6 us -> none  [exchange(): return lax.all_to_all(x.reshape(rows.shape), 'context', 0, 0, tiled=True)]
    all_to_all x4 -> x0, starting transfers between devices: 26.3 us -> none  [exchange(): return lax.all_to_all(x.reshape(rows.shape), 'context', 0, 0, tiled=True)]
    ppermute x0 -> x60, waiting for transfers between devices: none -> 14.4 us  [exchange(): got[d] = lax.ppermute(blocks[d], 'context', swaps[d])]
    unnamed x42 -> x20, local copies, waits for them, and re-layouts: 14.7 us -> 2.63 us
    pallas_call x6, Pallas kernels: 23.2 us -> 27.3 us  [the longest x1 5.62 us: on_device(): call(part(conv_kernel, 1.0), [block] * n + [spectrum], *sizes, 2, buffer)]
    ppermute x1, waiting for transfers between devices: 2.63 us -> 0.01 us  [on_device(): grad_filter = own + lax.ppermute(own, 'dp', [(0, 1), (1, 0)])]
  transfers between devices with their start and end apart: 5 -> 61, of which waited for: 5 -> 13; matrix products, arithmetic and copies ran while one was open for 1% -> 0% of each run, Pallas kernels for 18% -> 13%
where the time goes in v1:
time: 157 us
  starting transfers between devices  106 us (68%)
  Pallas kernels  32 us (20%)
  waiting for transfers between devices  14.4 us (9%)
  local copies, waits for them, and re-layouts  2.63 us (2%)
    ppermute x60, starting transfers between devices, exchange(): got[d] = lax.ppermute(blocks[d], 'context', swaps[d])  106 us
    ppermute x60, waiting for transfers between devices, exchange(): got[d] = lax.ppermute(blocks[d], 'context', swaps[d])  14.4 us
    pallas_call x1, Pallas kernels, on_device(): call(part(conv_kernel, 1.0), [block] * n + [spectrum], *sizes, 2, buffer)  5.62 us
    pallas_call x1, Pallas kernels, on_device(): call(part(conv_kernel, -1.0), [block] * n + [spectrum], *sizes, 2, buffer)  5.57 us
    pallas_call x1, Pallas kernels, on_device(): gated, grad_query = gate(*conv_tok, query, cot)  4.57 us
    pallas_call x1, Pallas kernels, on_device(): grad_key, grad_value = gate(*back_tok, value, key)  4.55 us
    pallas_call x1, Pallas kernels, on_device(): grad_ch = exchange(multiply(cot, query))  3.5 us
    pallas_call x1, Pallas kernels, on_device(): product_ch = exchange(multiply(key, value))  3.5 us
  transfers between devices with their start and end apart: 61, of which 13 were waited for; matrix products, arithmetic and copies ran while one was open for 0% of the time, Pallas kernels for 13%

profile of v1, /device:TPU:0, one launch (start us, length us, event | category | flops | bytes accessed | tf_op | source)
XLA Modules:
  0.0 156.6 jit_solution(10317567848558625071)
XLA Ops:
  3.3 3.5 %shard_map.123 = (f32[128,128]{1,0:T(8,128)S(1)}, f32[128,128]{1,0:T(8,128)S(1)}, f32[128,128]{1,0:T(8,128)S(1)}, f32[128,128]{1,0:T(8,128)S(1)}, f32[128,128]{1...) custom-call(f32[16,128,128]{2,1,0:T(8,128)S(1)} %bitcast.14, ...), custom_call_target="tpu_custom_call" | custom-call | flops 524288 | bytes 4194304 | tf_op jit(solution)/shard_map/pallas_call | solution.py:301
  6.8 3.0 %collective-permute-start.30 = (f32[128,128]{1,0:T(8,128)S(1)}, f32[128,128]{1,0:T(8,128)S(1)}, u32[]{:S(2)}, u32[]{:S(2)}) collective-permute-start(f32[128,128]{1,0:T(8,128)S(1)} %get-tuple-element.110), channel_id=1, source_target_pairs={{0,1},{1,0},{2,3},{3,2},{4,5},{5,4},{6,7},{7,6},{8,9},{9,8},{10,11... | collective-permute-start | bytes 196616 | tf_op jit(solution)/shard_map/ppermute | solution.py:290
  17.3 2.9 %collective-permute-start.37 = (f32[128,128]{1,0:T(8,128)S(1)}, f32[128,128]{1,0:T(8,128)S(1)}, u32[]{:S(2)}, u32[]{:S(2)}) collective-permute-start(f32[128,128]{1,0:T(8,128)S(1)} %get-tuple-element.117), channel_id=1, source_target_pairs={{0,8},{1,9},{2,10},{3,11},{4,12},{5,13},{6,14},{7,15},{8,0},{9,1},... | collective-permute-start | bytes 196616 | tf_op jit(solution)/shard_map/ppermute | solution.py:290
  21.5 3.5 %collective-permute-start.39 = (f32[128,128]{1,0:T(8,128)S(1)}, f32[128,128]{1,0:T(8,128)S(1)}, u32[]{:S(2)}, u32[]{:S(2)}) collective-permute-start(f32[128,128]{1,0:T(8,128)S(1)} %get-tuple-element.119), channel_id=1, source_target_pairs={{0,10},{1,11},{2,8},{3,9},{4,14},{5,15},{6,12},{7,13},{8,2},{9,3},... | collective-permute-start | bytes 196616 | tf_op jit(solution)/shard_map/ppermute | solution.py:290
  25.1 3.8 %collective-permute-start.41 = (f32[128,128]{1,0:T(8,128)S(1)}, f32[128,128]{1,0:T(8,128)S(1)}, u32[]{:S(2)}, u32[]{:S(2)}) collective-permute-start(f32[128,128]{1,0:T(8,128)S(1)} %get-tuple-element.121), channel_id=1, source_target_pairs={{0,12},{1,13},{2,14},{3,15},{4,8},{5,9},{6,10},{7,11},{8,4},{9,5},... | collective-permute-start | bytes 196616 | tf_op jit(solution)/shard_map/ppermute | solution.py:290
  28.9 4.6 %collective-permute-start.42 = (f32[128,128]{1,0:T(8,128)S(1)}, f32[128,128]{1,0:T(8,128)S(1)}, u32[]{:S(2)}, u32[]{:S(2)}) collective-permute-start(f32[128,128]{1,0:T(8,128)S(1)} %get-tuple-element.122), channel_id=1, source_target_pairs={{0,13},{1,12},{2,15},{3,14},{4,9},{5,8},{6,11},{7,10},{8,5},{9,4},... | collective-permute-start | bytes 196616 | tf_op jit(solution)/shard_map/ppermute | solution.py:290
  36.0 3.4 %collective-permute-start.44 = (f32[128,128]{1,0:T(8,128)S(1)}, f32[128,128]{1,0:T(8,128)S(1)}, u32[]{:S(2)}, u32[]{:S(2)}) collective-permute-start(f32[128,128]{1,0:T(8,128)S(1)} %get-tuple-element.124), channel_id=1, source_target_pairs={{0,15},{1,14},{2,13},{3,12},{4,11},{5,10},{6,9},{7,8},{8,7},{9,6},... | collective-permute-start | bytes 196616 | tf_op jit(solution)/shard_map/ppermute | solution.py:290
  39.3 3.5 %shard_map.119 = (f32[128,128]{1,0:T(8,128)S(1)}, f32[128,128]{1,0:T(8,128)S(1)}, f32[128,128]{1,0:T(8,128)S(1)}, f32[128,128]{1,0:T(8,128)S(1)}, f32[128,128]{1...) custom-call(f32[16,128,128]{2,1,0:T(8,128)S(1)} %bitcast.8, ...), custom_call_target="tpu_custom_call" | custom-call | flops 524288 | bytes 4194304 | tf_op jit(solution)/shard_map/pallas_call | solution.py:300
  49.5 2.8 %collective-permute-start.6 = (f32[128,128]{1,0:T(8,128)S(1)}, f32[128,128]{1,0:T(8,128)S(1)}, u32[]{:S(2)}, u32[]{:S(2)}) collective-permute-start(f32[128,128]{1,0:T(8,128)S(1)} %get-tuple-element.82), channel_id=1, source_target_pairs={{0,7},{1,6},{2,5},{3,4},{4,3},{5,2},{6,1},{7,0},{8,15},{9,14},{10,... | collective-permute-start | bytes 196616 | tf_op jit(solution)/shard_map/ppermute | solution.py:290
  52.3 2.8 %collective-permute-start.8 = (f32[128,128]{1,0:T(8,128)S(1)}, f32[128,128]{1,0:T(8,128)S(1)}, u32[]{:S(2)}, u32[]{:S(2)}) collective-permute-start(f32[128,128]{1,0:T(8,128)S(1)} %get-tuple-element.84), channel_id=1, source_target_pairs={{0,9},{1,8},{2,11},{3,10},{4,13},{5,12},{6,15},{7,14},{8,1},{9,0},... | collective-permute-start | bytes 196616 | tf_op jit(solution)/shard_map/ppermute | solution.py:290
  58.5 3.8 %collective-permute-start.10 = (f32[128,128]{1,0:T(8,128)S(1)}, f32[128,128]{1,0:T(8,128)S(1)}, u32[]{:S(2)}, u32[]{:S(2)}) collective-permute-start(f32[128,128]{1,0:T(8,128)S(1)} %get-tuple-element.86), channel_id=1, source_target_pairs={{0,11},{1,10},{2,9},{3,8},{4,15},{5,14},{6,13},{7,12},{8,3},{9,2},... | collective-permute-start | bytes 196616 | tf_op jit(solution)/shard_map/ppermute | solution.py:290
  62.8 3.3 %collective-permute-start.12 = (f32[128,128]{1,0:T(8,128)S(1)}, f32[128,128]{1,0:T(8,128)S(1)}, u32[]{:S(2)}, u32[]{:S(2)}) collective-permute-start(f32[128,128]{1,0:T(8,128)S(1)} %get-tuple-element.88), channel_id=1, source_target_pairs={{0,13},{1,12},{2,15},{3,14},{4,9},{5,8},{6,11},{7,10},{8,5},{9,4},... | collective-permute-start | bytes 196616 | tf_op jit(solution)/shard_map/ppermute | solution.py:290
  68.4 3.4 %collective-permute-start.14 = (f32[128,128]{1,0:T(8,128)S(1)}, f32[128,128]{1,0:T(8,128)S(1)}, u32[]{:S(2)}, u32[]{:S(2)}) collective-permute-start(f32[128,128]{1,0:T(8,128)S(1)} %get-tuple-element.90), channel_id=1, source_target_pairs={{0,15},{1,14},{2,13},{3,12},{4,11},{5,10},{6,9},{7,8},{8,7},{9,6},... | collective-permute-start | bytes 196616 | tf_op jit(solution)/shard_map/ppermute | solution.py:290
  71.8 5.6 %shard_map.124 = (f32[128,128]{1,0:T(8,128)S(1)}, f32[128,128]{1,0:T(8,128)S(1)}, f32[128,128]{1,0:T(8,128)S(1)}, f32[128,128]{1,0:T(8,128)S(1)}, f32[128,128]{1...) custom-call(f32[128,128]{1,0:T(8,128)S(1)} %get-tuple-element.109.re, ...), custom_call_target="tpu_custom_call" | custom-call | flops 1073741824 | bytes 6291456 | tf_op jit(solution)/shard_map/pallas_call | solution.py:308
  77.4 5.6 %shard_map.121 = (f32[128,128]{1,0:T(8,128)S(1)}, f32[128,128]{1,0:T(8,128)S(1)}, f32[128,128]{1,0:T(8,128)S(1)}, f32[128,128]{1,0:T(8,128)S(1)}, f32[128,128]{1...) custom-call(f32[128,128]{1,0:T(8,128)S(1)} %get-tuple-element.75.ref, ...), custom_call_target="tpu_custom_call" | custom-call | flops 1073741824 | bytes 6291456 | tf_op jit(solution)/shard_map/pallas_call | solution.py:304
  99.7 3.7 %collective-permute-start.25 = (f32[128,128]{1,0:T(8,128)S(1)}, f32[128,128]{1,0:T(8,128)S(1)}, u32[]{:S(2)}, u32[]{:S(2)}) collective-permute-start(f32[128,128]{1,0:T(8,128)S(1)} %get-tuple-element.102), channel_id=1, source_target_pairs={{0,11},{1,10},{2,9},{3,8},{4,15},{5,14},{6,13},{7,12},{8,3},{9,2},... | collective-permute-start | bytes 196616 | tf_op jit(solution)/shard_map/ppermute | solution.py:290
  116.5 2.6 %collective-permute-start.53 = (f32[128,128]{1,0:T(8,128)S(1)}, f32[128,128]{1,0:T(8,128)S(1)}, u32[]{:S(2)}, u32[]{:S(2)}) collective-permute-start(f32[128,128]{1,0:T(8,128)S(1)} %get-tuple-element.134), channel_id=1, source_target_pairs={{0,9},{1,8},{2,11},{3,10},{4,13},{5,12},{6,15},{7,14},{8,1},{9,0},... | collective-permute-start | bytes 196616 | tf_op jit(solution)/shard_map/ppermute | solution.py:290
  122.9 2.7 %collective-permute-done.52.refs_8_ = f32[128,128]{1,0:T(8,128)S(1)} collective-permute-done((f32[128,128]{1,0:T(8,128)S(1)}, f32[128,128]{1,0:T(8,128)S(1)}, u32[]{:S(2)}, u32[]{:S(2)}) %collective-permute-start.52) | collective-permute-done | bytes 65568 | tf_op jit(solution)/shard_map/ppermute | solution.py:290
  125.6 3.2 %collective-permute-done.53.refs_9_ = f32[128,128]{1,0:T(8,128)S(1)} collective-permute-done((f32[128,128]{1,0:T(8,128)S(1)}, f32[128,128]{1,0:T(8,128)S(1)}, u32[]{:S(2)}, u32[]{:S(2)}) %collective-permute-start.53) | collective-permute-done | bytes 65568 | tf_op jit(solution)/shard_map/ppermute | solution.py:290
  131.0 2.6 %collective-permute-start.58 = (f32[128,128]{1,0:T(8,128)S(1)}, f32[128,128]{1,0:T(8,128)S(1)}, u32[]{:S(2)}, u32[]{:S(2)}) collective-permute-start(f32[128,128]{1,0:T(8,128)S(1)} %get-tuple-element.139), channel_id=1, source_target_pairs={{0,14},{1,15},{2,12},{3,13},{4,10},{5,11},{6,8},{7,9},{8,6},{9,7},... | collective-permute-start | bytes 196616 | tf_op jit(solution)/shard_map/ppermute | solution.py:290
  135.7 2.6 %collective-permute-start.26 = (f32[128,128]{1,0:T(8,128)S(1)}, f32[128,128]{1,0:T(8,128)S(1)}, u32[]{:S(2)}, u32[]{:S(2)}) collective-permute-start(f32[128,128]{1,0:T(8,128)S(1)} %get-tuple-element.103), channel_id=1, source_target_pairs={{0,12},{1,13},{2,14},{3,15},{4,8},{5,9},{6,10},{7,11},{8,4},{9,5},... | collective-permute-start | bytes 196616 | tf_op jit(solution)/shard_map/ppermute | solution.py:290
  140.4 2.6 %collective-permute-start.28 = (f32[128,128]{1,0:T(8,128)S(1)}, f32[128,128]{1,0:T(8,128)S(1)}, u32[]{:S(2)}, u32[]{:S(2)}) collective-permute-start(f32[128,128]{1,0:T(8,128)S(1)} %get-tuple-element.105), channel_id=1, source_target_pairs={{0,14},{1,15},{2,12},{3,13},{4,10},{5,11},{6,8},{7,9},{8,6},{9,7},... | collective-permute-start | bytes 196616 | tf_op jit(solution)/shard_map/ppermute | solution.py:290
  145.1 4.5 %shard_map.125 = (f32[16,128,128]{2,1,0:T(8,128)}, f32[16,128,128]{2,1,0:T(8,128)}) custom-call(f32[128,128]{1,0:T(8,128)S(1)} %get-tuple-element.125.refs_0_, f32[128,128]{1,0:T(8,128)S(1)} %collective-permute-done.45.refs_1_, f32[128,128]{1,0:T(8,128)S(1)} %collective-permute-done.46.refs_2_, f32[128,128]{1,0:T(8,128)S(1)} %collective-permute-done.47.refs_3_, ...), custom_call_target="tpu_custom_call" | custom-call | flops 524288 | bytes 4194304 | tf_op jit(solution)/shard_map/pallas_call | solution.py:319
  150.9 4.6 %shard_map.122 = (f32[16,128,128]{2,1,0:T(8,128)}, f32[16,128,128]{2,1,0:T(8,128)}) custom-call(f32[128,128]{1,0:T(8,128)S(1)} %get-tuple-element.91.refs_0_, f32[128,128]{1,0:T(8,128)S(1)} %collective-permute-done.15.refs_1_, f32[128,128]{1,0:T(8,128)S(1)} %collective-permute-done.16.refs_2_, f32[128,128]{1,0:T(8,128)S(1)} %collective-permute-done.17.refs_3_, ...), custom_call_target="tpu_custom_call" | custom-call | flops 524288 | bytes 4194304 | tf_op jit(solution)/shard_map/pallas_call | solution.py:318
  (127 shorter events, 70.9 us)
Async XLA Ops:
  17.3 11.6 %collective-permute-start.37 = (f32[128,128]{1,0:T(8,128)S(1)}, f32[128,128]{1,0:T(8,128)S(1)}, u32[]{:S(2)}, u32[]{:S(2)}) collective-permute-start(f32[128,128]{1,0:T(8,128)S(1)} %get-tuple-element.117), channel_id=1, source_target_pairs={{0,8},{1,9},{2,10},{3,11},{4,12},{5,13},{6,14},{7,15},{8,0},{9,1},... | collective-permute-start | bytes 196616 | tf_op jit(solution)/shard_map/ppermute | solution.py:290
  20.2 13.4 %collective-permute-start.38 = (f32[128,128]{1,0:T(8,128)S(1)}, f32[128,128]{1,0:T(8,128)S(1)}, u32[]{:S(2)}, u32[]{:S(2)}) collective-permute-start(f32[128,128]{1,0:T(8,128)S(1)} %get-tuple-element.118), channel_id=1, source_target_pairs={{0,9},{1,8},{2,11},{3,10},{4,13},{5,12},{6,15},{7,14},{8,1},{9,0},... | collective-permute-start | bytes 196616 | tf_op jit(solution)/shard_map/ppermute | solution.py:290
  21.5 14.5 %collective-permute-start.39 = (f32[128,128]{1,0:T(8,128)S(1)}, f32[128,128]{1,0:T(8,128)S(1)}, u32[]{:S(2)}, u32[]{:S(2)}) collective-permute-start(f32[128,128]{1,0:T(8,128)S(1)} %get-tuple-element.119), channel_id=1, source_target_pairs={{0,10},{1,11},{2,8},{3,9},{4,14},{5,15},{6,12},{7,13},{8,2},{9,3},... | collective-permute-start | bytes 196616 | tf_op jit(solution)/shard_map/ppermute | solution.py:290
  25.0 17.8 %collective-permute-start.40 = (f32[128,128]{1,0:T(8,128)S(1)}, f32[128,128]{1,0:T(8,128)S(1)}, u32[]{:S(2)}, u32[]{:S(2)}) collective-permute-start(f32[128,128]{1,0:T(8,128)S(1)} %get-tuple-element.120), channel_id=1, source_target_pairs={{0,11},{1,10},{2,9},{3,8},{4,15},{5,14},{6,13},{7,12},{8,3},{9,2},... | collective-permute-start | bytes 196616 | tf_op jit(solution)/shard_map/ppermute | solution.py:290
  25.1 18.3 %collective-permute-start.41 = (f32[128,128]{1,0:T(8,128)S(1)}, f32[128,128]{1,0:T(8,128)S(1)}, u32[]{:S(2)}, u32[]{:S(2)}) collective-permute-start(f32[128,128]{1,0:T(8,128)S(1)} %get-tuple-element.121), channel_id=1, source_target_pairs={{0,12},{1,13},{2,14},{3,15},{4,8},{5,9},{6,10},{7,11},{8,4},{9,5},... | collective-permute-start | bytes 196616 | tf_op jit(solution)/shard_map/ppermute | solution.py:290
  28.9 16.1 %collective-permute-start.42 = (f32[128,128]{1,0:T(8,128)S(1)}, f32[128,128]{1,0:T(8,128)S(1)}, u32[]{:S(2)}, u32[]{:S(2)}) collective-permute-start(f32[128,128]{1,0:T(8,128)S(1)} %get-tuple-element.122), channel_id=1, source_target_pairs={{0,13},{1,12},{2,15},{3,14},{4,9},{5,8},{6,11},{7,10},{8,5},{9,4},... | collective-permute-start | bytes 196616 | tf_op jit(solution)/shard_map/ppermute | solution.py:290
  33.6 12.8 %collective-permute-start.43 = (f32[128,128]{1,0:T(8,128)S(1)}, f32[128,128]{1,0:T(8,128)S(1)}, u32[]{:S(2)}, u32[]{:S(2)}) collective-permute-start(f32[128,128]{1,0:T(8,128)S(1)} %get-tuple-element.123), channel_id=1, source_target_pairs={{0,14},{1,15},{2,12},{3,13},{4,10},{5,11},{6,8},{7,9},{8,6},{9,7},... | collective-permute-start | bytes 196616 | tf_op jit(solution)/shard_map/ppermute | solution.py:290
  36.0 10.5 %collective-permute-start.44 = (f32[128,128]{1,0:T(8,128)S(1)}, f32[128,128]{1,0:T(8,128)S(1)}, u32[]{:S(2)}, u32[]{:S(2)}) collective-permute-start(f32[128,128]{1,0:T(8,128)S(1)} %get-tuple-element.124), channel_id=1, source_target_pairs={{0,15},{1,14},{2,13},{3,12},{4,11},{5,10},{6,9},{7,8},{8,7},{9,6},... | collective-permute-start | bytes 196616 | tf_op jit(solution)/shard_map/ppermute | solution.py:290
  49.5 12.9 %collective-permute-start.6 = (f32[128,128]{1,0:T(8,128)S(1)}, f32[128,128]{1,0:T(8,128)S(1)}, u32[]{:S(2)}, u32[]{:S(2)}) collective-permute-start(f32[128,128]{1,0:T(8,128)S(1)} %get-tuple-element.82), channel_id=1, source_target_pairs={{0,7},{1,6},{2,5},{3,4},{4,3},{5,2},{6,1},{7,0},{8,15},{9,14},{10,... | collective-permute-start | bytes 196616 | tf_op jit(solution)/shard_map/ppermute | solution.py:290
  52.3 10.5 %collective-permute-start.7 = (f32[128,128]{1,0:T(8,128)S(1)}, f32[128,128]{1,0:T(8,128)S(1)}, u32[]{:S(2)}, u32[]{:S(2)}) collective-permute-start(f32[128,128]{1,0:T(8,128)S(1)} %get-tuple-element.83), channel_id=1, source_target_pairs={{0,8},{1,9},{2,10},{3,11},{4,12},{5,13},{6,14},{7,15},{8,0},{9,1},... | collective-permute-start | bytes 196616 | tf_op jit(solution)/shard_map/ppermute | solution.py:290
  52.3 13.8 %collective-permute-start.8 = (f32[128,128]{1,0:T(8,128)S(1)}, f32[128,128]{1,0:T(8,128)S(1)}, u32[]{:S(2)}, u32[]{:S(2)}) collective-permute-start(f32[128,128]{1,0:T(8,128)S(1)} %get-tuple-element.84), channel_id=1, source_target_pairs={{0,9},{1,8},{2,11},{3,10},{4,13},{5,12},{6,15},{7,14},{8,1},{9,0},... | collective-permute-start | bytes 196616 | tf_op jit(solution)/shard_map/ppermute | solution.py:290
  55.1 13.3 %collective-permute-start.9 = (f32[128,128]{1,0:T(8,128)S(1)}, f32[128,128]{1,0:T(8,128)S(1)}, u32[]{:S(2)}, u32[]{:S(2)}) collective-permute-start(f32[128,128]{1,0:T(8,128)S(1)} %get-tuple-element.85), channel_id=1, source_target_pairs={{0,10},{1,11},{2,8},{3,9},{4,14},{5,15},{6,12},{7,13},{8,2},{9,3},... | collective-permute-start | bytes 196616 | tf_op jit(solution)/shard_map/ppermute | solution.py:290
  58.5 18.8 %collective-permute-start.10 = (f32[128,128]{1,0:T(8,128)S(1)}, f32[128,128]{1,0:T(8,128)S(1)}, u32[]{:S(2)}, u32[]{:S(2)}) collective-permute-start(f32[128,128]{1,0:T(8,128)S(1)} %get-tuple-element.86), channel_id=1, source_target_pairs={{0,11},{1,10},{2,9},{3,8},{4,15},{5,14},{6,13},{7,12},{8,3},{9,2},... | collective-permute-start | bytes 196616 | tf_op jit(solution)/shard_map/ppermute | solution.py:290
  62.3 15.1 %collective-permute-start.11 = (f32[128,128]{1,0:T(8,128)S(1)}, f32[128,128]{1,0:T(8,128)S(1)}, u32[]{:S(2)}, u32[]{:S(2)}) collective-permute-start(f32[128,128]{1,0:T(8,128)S(1)} %get-tuple-element.87), channel_id=1, source_target_pairs={{0,12},{1,13},{2,14},{3,15},{4,8},{5,9},{6,10},{7,11},{8,4},{9,5},... | collective-permute-start | bytes 196616 | tf_op jit(solution)/shard_map/ppermute | solution.py:290
  62.8 14.6 %collective-permute-start.12 = (f32[128,128]{1,0:T(8,128)S(1)}, f32[128,128]{1,0:T(8,128)S(1)}, u32[]{:S(2)}, u32[]{:S(2)}) collective-permute-start(f32[128,128]{1,0:T(8,128)S(1)} %get-tuple-element.88), channel_id=1, source_target_pairs={{0,13},{1,12},{2,15},{3,14},{4,9},{5,8},{6,11},{7,10},{8,5},{9,4},... | collective-permute-start | bytes 196616 | tf_op jit(solution)/shard_map/ppermute | solution.py:290
  66.1 11.3 %collective-permute-start.13 = (f32[128,128]{1,0:T(8,128)S(1)}, f32[128,128]{1,0:T(8,128)S(1)}, u32[]{:S(2)}, u32[]{:S(2)}) collective-permute-start(f32[128,128]{1,0:T(8,128)S(1)} %get-tuple-element.89), channel_id=1, source_target_pairs={{0,14},{1,15},{2,12},{3,13},{4,10},{5,11},{6,8},{7,9},{8,6},{9,7},... | collective-permute-start | bytes 196616 | tf_op jit(solution)/shard_map/ppermute | solution.py:290
  85.5 70.0 %collective-permute-start.60 = (f32[128,2048]{1,0:T(8,128)S(1)}, f32[128,2048]{1,0:T(8,128)S(1)}, u32[]{:S(2)}, u32[]{:S(2)}) collective-permute-start(f32[128,2048]{1,0:T(8,128)S(1)} %shard_map.126), channel_id=1, source_target_pairs={{0,16},{16,0},{1,17},{17,1},{2,18},{18,2},{3,19},{19,3},{4,20},{20... | collective-permute-start | bytes 3145736 | tf_op jit(solution)/shard_map/ppermute | solution.py:314
  95.9 11.0 %collective-permute-start.23 = (f32[128,128]{1,0:T(8,128)S(1)}, f32[128,128]{1,0:T(8,128)S(1)}, u32[]{:S(2)}, u32[]{:S(2)}) collective-permute-start(f32[128,128]{1,0:T(8,128)S(1)} %get-tuple-element.100), channel_id=1, source_target_pairs={{0,9},{1,8},{2,11},{3,10},{4,13},{5,12},{6,15},{7,14},{8,1},{9,0},... | collective-permute-start | bytes 196616 | tf_op jit(solution)/shard_map/ppermute | solution.py:290
  115.3 10.4 %collective-permute-start.52 = (f32[128,128]{1,0:T(8,128)S(1)}, f32[128,128]{1,0:T(8,128)S(1)}, u32[]{:S(2)}, u32[]{:S(2)}) collective-permute-start(f32[128,128]{1,0:T(8,128)S(1)} %get-tuple-element.133), channel_id=1, source_target_pairs={{0,8},{1,9},{2,10},{3,11},{4,12},{5,13},{6,14},{7,15},{8,0},{9,1},... | collective-permute-start | bytes 196616 | tf_op jit(solution)/shard_map/ppermute | solution.py:290
  116.5 12.3 %collective-permute-start.53 = (f32[128,128]{1,0:T(8,128)S(1)}, f32[128,128]{1,0:T(8,128)S(1)}, u32[]{:S(2)}, u32[]{:S(2)}) collective-permute-start(f32[128,128]{1,0:T(8,128)S(1)} %get-tuple-element.134), channel_id=1, source_target_pairs={{0,9},{1,8},{2,11},{3,10},{4,13},{5,12},{6,15},{7,14},{8,1},{9,0},... | collective-permute-start | bytes 196616 | tf_op jit(solution)/shard_map/ppermute | solution.py:290
  119.1 11.9 %collective-permute-start.54 = (f32[128,128]{1,0:T(8,128)S(1)}, f32[128,128]{1,0:T(8,128)S(1)}, u32[]{:S(2)}, u32[]{:S(2)}) collective-permute-start(f32[128,128]{1,0:T(8,128)S(1)} %get-tuple-element.135), channel_id=1, source_target_pairs={{0,10},{1,11},{2,8},{3,9},{4,14},{5,15},{6,12},{7,13},{8,2},{9,3},... | collective-permute-start | bytes 196616 | tf_op jit(solution)/shard_map/ppermute | solution.py:290
  120.8 12.8 %collective-permute-start.55 = (f32[128,128]{1,0:T(8,128)S(1)}, f32[128,128]{1,0:T(8,128)S(1)}, u32[]{:S(2)}, u32[]{:S(2)}) collective-permute-start(f32[128,128]{1,0:T(8,128)S(1)} %get-tuple-element.136), channel_id=1, source_target_pairs={{0,11},{1,10},{2,9},{3,8},{4,15},{5,14},{6,13},{7,12},{8,3},{9,2},... | collective-permute-start | bytes 196616 | tf_op jit(solution)/shard_map/ppermute | solution.py:290
  135.7 14.0 %collective-permute-start.26 = (f32[128,128]{1,0:T(8,128)S(1)}, f32[128,128]{1,0:T(8,128)S(1)}, u32[]{:S(2)}, u32[]{:S(2)}) collective-permute-start(f32[128,128]{1,0:T(8,128)S(1)} %get-tuple-element.103), channel_id=1, source_target_pairs={{0,12},{1,13},{2,14},{3,15},{4,8},{5,9},{6,10},{7,11},{8,4},{9,5},... | collective-permute-start | bytes 196616 | tf_op jit(solution)/shard_map/ppermute | solution.py:290
  138.3 11.4 %collective-permute-start.27 = (f32[128,128]{1,0:T(8,128)S(1)}, f32[128,128]{1,0:T(8,128)S(1)}, u32[]{:S(2)}, u32[]{:S(2)}) collective-permute-start(f32[128,128]{1,0:T(8,128)S(1)} %get-tuple-element.104), channel_id=1, source_target_pairs={{0,13},{1,12},{2,15},{3,14},{4,9},{5,8},{6,11},{7,10},{8,5},{9,4},... | collective-permute-start | bytes 196616 | tf_op jit(solution)/shard_map/ppermute | solution.py:290
  (47 other events, 675.8 us)

commit v2 on v0

--- a/solution.py
+++ b/solution.py
@@ -10,7 +10,9 @@
 from jax.sharding import PartitionSpec as P
 
 ROWS = 8
-VMEM_BYTES = 48 * 1024 * 1024
+PARTS = 4
+VMEM_BYTES = 24 * 1024 * 1024
+MOST_VMEM = 56 * 1024 * 1024
 
 
 def twist(value, turn):
@@ -94,74 +96,115 @@
                 write(n1, rows, re * math.cos(turn) - im * math.sin(turn))
 
 
-def groups(n, channels, body):
-    size = max(1, min(n, 512 // channels))
-
-    @pl.loop(0, n // size)
-    def _(i):
-        body(pl.ds(i * size, size), size)
-
-
 def flat(x):
     return x.reshape(x.shape[0] * x.shape[1], x.shape[2])
 
 
-def filter_kernel(n, channels, tokens, f_ref, tw_ref, fwd_ref, out_ref, y_ref):
+def spectrum_copies(n, pairs, sem):
+    size = max(1, n // PARTS)
+    return [
+        [
+            pltpu.make_async_copy(src.at[part], dst.at[part], sem.at[j, i])
+            for j, (src, dst) in enumerate(pairs)
+        ]
+        for i, part in enumerate(pl.ds(k, size) for k in range(0, n, size))
+    ]
+
+
+def start_all(copies):
+    for copy in copies:
+        copy.start()
+
+
+def wait_all(copies):
+    for copy in copies:
+        copy.wait()
+
+
+def filter_kernel(n, channels, tokens, f_ref, tw_ref, fwd_ref, out_ref, own_ref, y_ref, sem):
     outer_forward(
         lambda n1, rows: f_ref[rows, n1 * tokens : (n1 + 1) * tokens],
         n, channels, tokens, tw_ref, y_ref,
     )
-
-    def body(ms, size):
-        out_ref[ms] = times_table(flat(y_ref[ms]), fwd_ref).reshape(size, channels, 2 * tokens)
-
-    groups(n, channels, body)
+    stores = spectrum_copies(n, [(own_ref, out_ref)], sem)
+    size = n // len(stores)
+    for i, store in enumerate(stores):
+        ms = pl.ds(i * size, size)
+        own_ref[ms] = times_table(flat(y_ref[ms]), fwd_ref).reshape(size, channels, 2 * tokens)
+        start_all(store)
+    for store in stores:
+        wait_all(store)
 
 
 def conv_kernel(
-    sign, n, channels, tokens, x_ref, spec_ref, tw_ref, fwd_ref, inv_ref, out_ref, own_ref, y_ref
+    n, channels, tokens, x_ref, tw_ref, fwd_ref, inv_ref, spec_ref, out_ref, p_ref, g_ref,
+    spec_buf, p_buf, g_buf, p_y, g_y, sem,
 ):
-    outer_forward(lambda n1, rows: x_ref[n1, rows], n, channels, tokens, tw_ref, y_ref)
-
-    def body(ms, size):
-        own = times_table(flat(y_ref[ms]), fwd_ref)
-        own_ref[ms] = own.reshape(size, channels, 2 * tokens)
-        spec = flat(spec_ref[ms])
-        re, im = own[:, :tokens], own[:, tokens:]
-        s_re, s_im = spec[:, :tokens], spec[:, tokens:] * sign
-        both = jnp.concatenate([re * s_re - im * s_im, re * s_im + im * s_re], axis=1)
-        y_ref[ms] = times_table(both, inv_ref).reshape(size, channels, 2 * tokens)
-
-    groups(n, channels, body)
-
-    def write(n1, rows, value):
-        out_ref[n1, rows] = value
-
-    outer_inverse(write, n, channels, tokens, tw_ref, y_ref)
-
-
-def filter_grad_kernel(scale, n, channels, tokens, p_ref, g_ref, tw_ref, inv_ref, out_ref, y_ref):
-    def body(ms, size):
-        p, g = flat(p_ref[ms]), flat(g_ref[ms])
+    loads = spectrum_copies(n, [(spec_ref, spec_buf)], sem)
+    for load in loads:
+        start_all(load)
+    for j, y_ref in enumerate((p_y, g_y)):
+        outer_forward(
+            lambda n1, rows: x_ref[n1, j, rows], n, channels, tokens, tw_ref, y_ref
+        )
+    for load in loads:
+        wait_all(load)
+    stores = spectrum_copies(n, [(p_buf, p_ref), (g_buf, g_ref)], sem)
+    size = n // len(stores)
+    for i, store in enumerate(stores):
+        ms = pl.ds(i * size, size)
+        spec = flat(spec_buf[ms])
+        for sign, own_buf, y_ref in ((1.0, p_buf, p_y), (-1.0, g_buf, g_y)):
+            own = times_table(flat(y_ref[ms]), fwd_ref)
+            own_buf[ms] = own.reshape(size, channels, 2 * tokens)
+            re, im = own[:, :tokens], own[:, tokens:]
+            s_re, s_im = spec[:, :tokens], spec[:, tokens:] * sign
+            both = jnp.concatenate([re * s_re - im * s_im, re * s_im + im * s_re], axis=1)
+            y_ref[ms] = times_table(both, inv_ref).reshape(size, channels, 2 * tokens)
+        start_all(store)
+    for j, y_ref in enumerate((p_y, g_y)):
+
+        def write(n1, rows, value):
+            out_ref[n1, j, rows] = value
+
+        outer_inverse(write, n, channels, tokens, tw_ref, y_ref)
+    for store in stores:
+        wait_all(store)
+
+
+def filter_grad_kernel(
+    scale, n, channels, tokens, tw_ref, inv_ref, p_ref, g_ref, out_ref, p_buf, g_buf, y_ref, sem
+):
+    loads = spectrum_copies(n, [(p_ref, p_buf), (g_ref, g_buf)], sem)
+    for load in loads:
+        start_all(load)
+    size = n // len(loads)
+    for i, load in enumerate(loads):
+        ms = pl.ds(i * size, size)
+        wait_all(load)
+        p, g = flat(p_buf[ms]), flat(g_buf[ms])
         p_re, p_im = p[:, :tokens], p[:, tokens:]
         re, im = g[:, :tokens], g[:, tokens:]
         both = jnp.concatenate([re * p_re + im * p_im, im * p_re - re * p_im], axis=1)
         y_ref[ms] = times_table(both, inv_ref).reshape(size, channels, 2 * tokens)
 
-    groups(n, channels, body)
-
     def write(n1, rows, value):
         out_ref[rows, n1 * tokens : (n1 + 1) * tokens] = value * scale
 
     outer_inverse(write, n, channels, tokens, tw_ref, y_ref)
 
 
-def call(body, outs, n, channels, tokens, passes):
+def call(body, n_vmem, n_hbm, outs, spectra, n, channels, tokens, passes):
     size = n * channels * tokens
+    hbm, vmem = pl.BlockSpec(memory_space=pltpu.HBM), pl.BlockSpec(memory_space=pltpu.VMEM)
+    spectrum = (n, channels, 2 * tokens)
     return pl.pallas_call(
         body,
+        in_specs=[vmem] * n_vmem + [hbm] * n_hbm,
+        out_specs=[hbm if out.shape == spectrum else vmem for out in outs],
         out_shape=outs,
-        scratch_shapes=[pltpu.VMEM((n, channels, 2 * tokens), jnp.float32)],
+        scratch_shapes=[pltpu.VMEM(spectrum, jnp.float32)] * spectra
+        + [pltpu.SemaphoreType.DMA((2, PARTS))],
         compiler_params=pltpu.CompilerParams(vmem_limit_bytes=VMEM_BYTES),
         cost_estimate=pl.CostEstimate(
             flops=passes * size * 2 * 2 * tokens * 4, bytes_accessed=6 * size * 4, transcendentals=0
@@ -169,30 +212,53 @@
     )
 
 
-def product_kernel(a_ref, b_ref, out_ref):
-    out_ref[...] = a_ref[...] * b_ref[...]
-
-
-def gate_kernel(x_ref, a_ref, b_ref, oa_ref, ob_ref):
-    x = x_ref[...]
-    oa_ref[...] = x * a_ref[...]
-    ob_ref[...] = x * b_ref[...]
-
-
-def tiled(body, n_in, n_out, shape):
-    rows = math.gcd(shape[0], 512)
-    spec = pl.BlockSpec((rows, shape[1]), lambda i: (i, 0))
+def product_kernel(*refs):
+    in_refs, (out_ref, *bufs, sem) = refs[:4], refs[4:]
+    n = out_ref.shape[0]
+    size = max(1, n // PARTS)
+    parts = [pl.ds(k, size) for k in range(0, n, size)]
+    loads = [
+        [
+            pltpu.make_async_copy(ref.at[part], buf.at[part], sem.at[j, i])
+            for j, (ref, buf) in enumerate(zip(in_refs, bufs))
+        ]
+        for i, part in enumerate(parts)
+    ]
+    for load in loads:
+        start_all(load)
+    for load, part in zip(loads, parts):
+        wait_all(load)
+        out_ref[part, 0] = bufs[0][part] * bufs[1][part]
+        out_ref[part, 1] = bufs[2][part] * bufs[3][part]
+
+
+def gate_kernel(x_ref, *refs):
+    in_refs, out_refs, bufs, sem = refs[:4], refs[4:8], refs[8:12], refs[12]
+    n = x_ref.shape[0]
+    size = max(1, n // PARTS)
+    stores = []
+    for i, k in enumerate(range(0, n, size)):
+        part = pl.ds(k, size)
+        for j, (ref, buf, out) in enumerate(zip(in_refs, bufs, out_refs)):
+            buf[part] = x_ref[part, j // 2] * ref[part]
+            stores.append(pltpu.make_async_copy(buf.at[part], out.at[part], sem.at[j, i]))
+            stores[-1].start()
+    wait_all(stores)
+
+
+def rows_call(body, in_vmem, out, shape, grant):
+    hbm, vmem = pl.BlockSpec(memory_space=pltpu.HBM), pl.BlockSpec(memory_space=pltpu.VMEM)
     return pl.pallas_call(
         body,
-        grid=(shape[0] // rows,),
-        in_specs=[spec] * n_in,
-        out_specs=[spec] * n_out,
-        out_shape=[jax.ShapeDtypeStruct(shape, jnp.float32)] * n_out,
-        compiler_params=pltpu.CompilerParams(vmem_limit_bytes=VMEM_BYTES),
+        in_specs=[vmem if near else hbm for near in in_vmem],
+        out_specs=[hbm] * 4 if out == shape else vmem,
+        out_shape=[jax.ShapeDtypeStruct(out, jnp.float32)] * 4
+        if out == shape
+        else jax.ShapeDtypeStruct(out, jnp.float32),
+        scratch_shapes=[pltpu.VMEM(shape, jnp.float32)] * 4 + [pltpu.SemaphoreType.DMA((4, PARTS))],
+        compiler_params=pltpu.CompilerParams(vmem_limit_bytes=grant),
         cost_estimate=pl.CostEstimate(
-            flops=n_out * shape[0] * shape[1],
-            bytes_accessed=(n_in + n_out) * 4 * shape[0] * shape[1],
-            transcendentals=0,
+            flops=4 * math.prod(shape), bytes_accessed=10 * 4 * math.prod(shape), transcendentals=0
         ),
     )
 
@@ -229,37 +295,37 @@
     rows = jax.ShapeDtypeStruct((n, channels, tokens), jnp.float32)
     lags = jax.ShapeDtypeStruct((channels, length), jnp.float32)
 
+    pair = (n, 2, channels, tokens)
+
     def exchange(x):
-        return lax.all_to_all(x.reshape(rows.shape), "context", 0, 0, tiled=True)
+        return lax.all_to_all(x, "context", 0, 0, tiled=True)
 
     def part(body, *args):
         return lambda *refs: body(*args, *sizes, *refs)
 
     query, key, value, cot = (
-        x.reshape(width, tokens) for x in (query_input, key_input, value_input, cotangent)
-    )
-    multiply = tiled(product_kernel, 2, 1, (width, tokens))
-    (product,) = multiply(key, value)
-    (conv_grad,) = multiply(cot, query)
-    product_ch = exchange(product)
-    grad_ch = exchange(conv_grad)
-    filt = call(part(filter_kernel), spectrum, *sizes, 1)(filters, tw, fwd)
-    conv_ch, prod_spec = call(part(conv_kernel, 1.0), [rows, spectrum], *sizes, 2)(
-        product_ch, filt, tw, fwd, inv
-    )
-    conv_tok = exchange(conv_ch).reshape(width, tokens)
-    back_ch, grad_spec = call(part(conv_kernel, -1.0), [rows, spectrum], *sizes, 2)(
-        grad_ch, filt, tw, fwd, inv
-    )
-    back_tok = exchange(back_ch).reshape(width, tokens)
-    own = call(part(filter_grad_kernel, scale), lags, *sizes, 1)(prod_spec, grad_spec, tw, inv)
+        x.reshape(rows.shape) for x in (query_input, key_input, value_input, cotangent)
+    )
+    products = rows_call(product_kernel, [False] * 4, pair, rows.shape, MOST_VMEM)(
+        key, value, cot, query
+    )
+    products_ch = exchange(products)
+    (filt,) = call(part(filter_kernel), 3, 0, [spectrum], 2, *sizes, 1)(filters, tw, fwd)
+    outs = [jax.ShapeDtypeStruct(pair, jnp.float32), spectrum, spectrum]
+    results_ch, prod_spec, grad_spec = call(part(conv_kernel), 4, 1, outs, 5, *sizes, 4)(
+        products_ch, tw, fwd, inv, filt
+    )
+    results = exchange(results_ch)
+    (own,) = call(part(filter_grad_kernel, scale), 2, 2, [lags], 3, *sizes, 1)(
+        tw, inv, prod_spec, grad_spec
+    )
     if pair_size == 2:
         grad_filter = own + lax.ppermute(own, "dp", [(0, 1), (1, 0)])
     else:
         grad_filter = lax.psum(own, "dp")
-    gate = tiled(gate_kernel, 3, 2, (width, tokens))
-    gated, grad_query = gate(conv_tok, query, cot)
-    grad_key, grad_value = gate(back_tok, value, key)
+    gated, grad_query, grad_key, grad_value = rows_call(
+        gate_kernel, [True] * 5, rows.shape, rows.shape, VMEM_BYTES
+    )(results, query, cot, value, key)
     shape = query_input.shape
     return (
         gated.reshape(shape),

time: 130 us -> 134 us (1.031)
  the two profiles are of different devices: /device:TPU:0 before, /device:TPU:12 now
where the time goes in v2:
time: 134 us
  waiting for transfers between devices  83.8 us (63%)
  Pallas kernels  23.2 us (17%)
  local copies, waits for them, and re-layouts  12.8 us (10%)
  starting transfers between devices  12.3 us (9%)
    all_to_all x2, waiting for transfers between devices, exchange(): return lax.all_to_all(x, 'context', 0, 0, tiled=True)  81.1 us
    unnamed x28, local copies, waits for them, and re-layouts  12.8 us
    all_to_all x2, starting transfers between devices, exchange(): return lax.all_to_all(x, 'context', 0, 0, tiled=True)  12.2 us
    pallas_call x1, Pallas kernels, on_device(): call(part(conv_kernel), 4, 1, outs, 5, *sizes, 4)  10.8 us
    pallas_call x1, Pallas kernels, on_device(): rows_call(product_kernel, [False] * 4, pair, rows.shape, MOST_VMEM)  3.64 us
    pallas_call x1, Pallas kernels, on_device(): call(part(filter_grad_kernel, scale), 2, 2, [lags], 3, *sizes, 1)  3.45 us
    pallas_call x1, Pallas kernels, on_device(): call(part(filter_kernel), 3, 0, [spectrum], 2, *sizes, 1)(filters, tw, fwd)  3.2 us
  transfers between devices with their start and end apart: 3, of which 3 were waited for; matrix products, arithmetic and copies ran while one was open for 1% of the time, Pallas kernels for 5%

profile of v2, /device:TPU:12, one launch (start us, length us, event | category | flops | bytes accessed | tf_op | source)
XLA Modules:
  0.0 133.9 jit_solution(11602971407533052923)
XLA Ops:
  0.6 3.6 %shard_map.119 = f32[16,2,128,128]{3,2,1,0:T(8,128)} custom-call(f32[16,128,128]{2,1,0:T(8,128)} %bitcast.8, f32[16,128,128]{2,1,0:T(8,128)} %bitcast.10, f32[16,128,128]{2,1,0:T(8,128)} %bitcast.12, f32[16,128,128]{2,1,0:T(8,128)} %bitcast.14), custom_call_target="tpu_custom_call" | custom-call | flops 1048576 | bytes 10485760 | tf_op jit(solution)/shard_map/pallas_call | solution.py:309
  4.3 0.0 copy-start.10
  4.3 7.3 %all-to-all-start = ((f32[16,2,128,128]{3,2,1,0:T(8,128)}), f32[16,2,128,128]{3,2,1,0:T(8,128)}, u32[]{:S(2)}, u32[]{:S(2)}) async-start(f32[16,2,128,128]{3,2,1,0:T(8,128)} %shard_map.119), calls=%async_computation | async-start | bytes 4194304 | tf_op jit(solution)/shard_map/all_to_all | solution.py:301
  11.6 0.0 copy-start.12
  11.6 0.9 copy-done.12
  12.6 3.2 %shard_map.120.refs_4_ = f32[16,128,256]{2,1,0:T(8,128)S(1)} custom-call(f32[128,2048]{1,0:T(8,128)S(1)} %copy-done.9, f32[2,16,8,128]{3,2,1,0:T(8,128)S(1)} %copy-done.10, bf16[2,256,256]{2,1,0:T(8,128)(2,1)S(1)} %copy-done.12), custom_call_target="tpu_custom_call" | custom-call | flops 536870912 | bytes 6291456 | tf_op jit(solution)/shard_map/pallas_call | solution.py:313
  15.8 44.0 %all-to-all-done.refs_0_ = f32[16,2,128,128]{3,2,1,0:T(8,128)} async-done(((f32[16,2,128,128]{3,2,1,0:T(8,128)}), f32[16,2,128,128]{3,2,1,0:T(8,128)}, u32[]{:S(2)}, u32[]{:S(2)}) %all-to-all-start) | async-done | bytes 2097184 | tf_op jit(solution)/shard_map/all_to_all | solution.py:301
  59.8 0.9 copy-done.13
  60.8 10.8 %shard_map.121 = (f32[16,2,128,128]{3,2,1,0:T(8,128)S(1)}, f32[16,128,256]{2,1,0:T(8,128)S(1)}, f32[16,128,256]{2,1,0:T(8,128)S(1)}) custom-call(f32[16,2,128,128]{3,2,1,0:T(8,128)} %all-to-all-done.refs_0_, f32[2,16,8,128]{3,2,1,0:T(8,128)S(1)} %copy-done.10, bf16[2,256,256]{2,1,0:T(8,128)(2,1)S(1)} %copy-done.13, bf16[2,256,256]{2,1,0:T(8,128)(2,1)S(1)} %copy-done.11, ...), custom_call_target="tpu_custom_call" | custom-call | flops 2147483648 | bytes 6291456 | tf_op jit(solution)/shard_map/pallas_call | solution.py:315
  71.6 1.3 copy-done.4
  72.9 1.3 copy-done.5
  74.2 1.4 %copy-done.7 = f32[16,128,256]{2,1,0:T(8,128)} copy-done((f32[16,128,256]{2,1,0:T(8,128)}, f32[16,128,256]{2,1,0:T(8,128)S(1)}, u32[]{:S(2)}) %copy-start.7) | copy-done | bytes 2097176
  75.6 4.9 %all-to-all-start.1 = ((f32[16,2,128,128]{3,2,1,0:T(8,128)}), f32[16,2,128,128]{3,2,1,0:T(8,128)S(1)}, u32[]{:S(2)}, u32[]{:S(2)}) async-start(f32[16,2,128,128]{3,2,1,0:T(8,128)} %copy-done.4), calls=%async_computation.1 | async-start | bytes 4194304 | tf_op jit(solution)/shard_map/all_to_all | solution.py:301
  80.5 1.6 %copy-done.6 = f32[16,128,256]{2,1,0:T(8,128)S(1)} copy-done((f32[16,128,256]{2,1,0:T(8,128)S(1)}, f32[16,128,256]{2,1,0:T(8,128)}, u32[]{:S(2)}) %copy-start.6) | copy-done | bytes 2097176
  82.1 1.6 %copy-done.8 = f32[16,128,256]{2,1,0:T(8,128)S(1)} copy-done((f32[16,128,256]{2,1,0:T(8,128)S(1)}, f32[16,128,256]{2,1,0:T(8,128)}, u32[]{:S(2)}) %copy-start.8) | copy-done | bytes 2097176
  83.7 3.4 %shard_map.123 = f32[128,2048]{1,0:T(8,128)S(1)} custom-call(f32[2,16,8,128]{3,2,1,0:T(8,128)S(1)} %copy-done.10, bf16[2,256,256]{2,1,0:T(8,128)(2,1)S(1)} %copy-done.11, f32[16,128,256]{2,1,0:T(8,128)S(1)} %copy-done.6, f32[16,128,256]{2,1,0:T(8,128)S(1)} %copy-done.8), custom_call_target="tpu_custom_call" | custom-call | flops 536870912 | bytes 6291456 | tf_op jit(solution)/shard_map/pallas_call | solution.py:319
  87.1 0.1 collective-permute-start
  87.2 2.6 %collective-permute-done = f32[128,2048]{1,0:T(8,128)S(1)} collective-permute-done((f32[128,2048]{1,0:T(8,128)S(1)}, f32[128,2048]{1,0:T(8,128)S(1)}, u32[]{:S(2)}, u32[]{:S(2)}) %collective-permute-start) | collective-permute-done | bytes 1048608 | tf_op jit(solution)/shard_map/ppermute | solution.py:323
  89.9 1.1 add.3
  90.9 37.1 %all-to-all-done.1.x_ref = f32[16,2,128,128]{3,2,1,0:T(8,128)S(1)} async-done(((f32[16,2,128,128]{3,2,1,0:T(8,128)}), f32[16,2,128,128]{3,2,1,0:T(8,128)S(1)}, u32[]{:S(2)}, u32[]{:S(2)}) %all-to-all-start.1) | async-done | bytes 2097184 | tf_op jit(solution)/shard_map/all_to_all | solution.py:301
  128.0 1.2 copy-done.1
  129.2 1.2 copy-done.2
  130.5 1.2 copy-done.3
  131.7 2.2 %shard_map.122 = (f32[16,128,128]{2,1,0:T(8,128)}, f32[16,128,128]{2,1,0:T(8,128)}, f32[16,128,128]{2,1,0:T(8,128)}, f32[16,128,128]{2,1,0:T(8,128)}) custom-call(f32[16,2,128,128]{3,2,1,0:T(8,128)S(1)} %all-to-all-done.1.x_ref, f32[16,128,128]{2,1,0:T(8,128)S(1)} %bitcast.15, f32[16,128,128]{2,1,0:T(8,128)S(1)} %bitcast.13, f32[16,128,128]{2,1,0:T(8,128)S(1)} %bitcast.11, ...), custom_call_target="tpu_custom_call" | custom-call | flops 1048576 | bytes 10485760 | tf_op jit(solution)/shard_map/pallas_call | solution.py:326
  (16 shorter events, 0.0 us)
Async XLA Ops:
  4.3 7.3 %copy-start.9 = (f32[128,2048]{1,0:T(8,128)S(1)}, f32[128,2048]{1,0:T(8,128)}, u32[]{:S(2)}) copy-start(f32[128,2048]{1,0:T(8,128)} %refs_0_.2) | copy-start | bytes 3145732
  4.3 7.3 %copy-start.10 = (f32[2,16,8,128]{3,2,1,0:T(8,128)S(1)}, f32[2,16,8,128]{3,2,1,0:T(8,128)}, u32[]{:S(2)}) copy-start(f32[2,16,8,128]{3,2,1,0:T(8,128)} %constant.8.clone.refs_1_.refs_0_) | copy-start | bytes 393220
  4.3 55.5 %all-to-all-start = ((f32[16,2,128,128]{3,2,1,0:T(8,128)}), f32[16,2,128,128]{3,2,1,0:T(8,128)}, u32[]{:S(2)}, u32[]{:S(2)}) async-start(f32[16,2,128,128]{3,2,1,0:T(8,128)} %shard_map.119), calls=%async_computation | async-start | bytes 4194304 | tf_op jit(solution)/shard_map/all_to_all | solution.py:301
  11.6 1.0 copy-start.12
  12.6 47.3 %copy-start.11 = (bf16[2,256,256]{2,1,0:T(8,128)(2,1)S(1)}, bf16[2,256,256]{2,1,0:T(8,128)(2,1)}, u32[]{:S(2)}) copy-start(bf16[2,256,256]{2,1,0:T(8,128)(2,1)} %constant.7.clone.refs_3_.refs_1_) | copy-start | bytes 786436
  59.8 1.0 copy-start.13
  71.6 1.3 copy-start.4
  72.9 1.3 copy-start.5
  74.2 1.4 %copy-start.7 = (f32[16,128,256]{2,1,0:T(8,128)}, f32[16,128,256]{2,1,0:T(8,128)S(1)}, u32[]{:S(2)}) copy-start(f32[16,128,256]{2,1,0:T(8,128)S(1)} %get-tuple-element.18.refs_3_) | copy-start | bytes 6291460
  75.6 52.5 %all-to-all-start.1 = ((f32[16,2,128,128]{3,2,1,0:T(8,128)}), f32[16,2,128,128]{3,2,1,0:T(8,128)S(1)}, u32[]{:S(2)}, u32[]{:S(2)}) async-start(f32[16,2,128,128]{3,2,1,0:T(8,128)} %copy-done.4), calls=%async_computation.1 | async-start | bytes 4194304 | tf_op jit(solution)/shard_map/all_to_all | solution.py:301
  80.5 1.6 %copy-start.6 = (f32[16,128,256]{2,1,0:T(8,128)S(1)}, f32[16,128,256]{2,1,0:T(8,128)}, u32[]{:S(2)}) copy-start(f32[16,128,256]{2,1,0:T(8,128)} %copy-done.5) | copy-start | bytes 6291460
  82.1 1.6 %copy-start.8 = (f32[16,128,256]{2,1,0:T(8,128)S(1)}, f32[16,128,256]{2,1,0:T(8,128)}, u32[]{:S(2)}) copy-start(f32[16,128,256]{2,1,0:T(8,128)} %copy-done.7) | copy-start | bytes 6291460
  87.1 40.9 %copy-start = (f32[1,2048,128]{2,1,0:T(8,128)S(1)}, f32[1,2048,128]{2,1,0:T(8,128)}, u32[]{:S(2)}) copy-start(f32[1,2048,128]{2,1,0:T(8,128)} %param.9) | copy-start | bytes 3145732
  87.1 2.7 %collective-permute-start = (f32[128,2048]{1,0:T(8,128)S(1)}, f32[128,2048]{1,0:T(8,128)S(1)}, u32[]{:S(2)}, u32[]{:S(2)}) collective-permute-start(f32[128,2048]{1,0:T(8,128)S(1)} %shard_map.123), channel_id=1, source_target_pairs={{0,16},{16,0},{1,17},{17,1},{2,18},{18,2},{3,19},{19,3},{4,20},{20... | collective-permute-start | bytes 3145736 | tf_op jit(solution)/shard_map/ppermute | solution.py:323
  128.0 1.2 copy-start.1
  129.2 1.2 copy-start.2
  130.5 1.2 copy-start.3

commit v3 on v0

--- a/solution.py
+++ b/solution.py
@@ -10,7 +10,8 @@
 from jax.sharding import PartitionSpec as P
 
 ROWS = 8
-VMEM_BYTES = 48 * 1024 * 1024
+PARTS = 4
+VMEM_BYTES = 24 * 1024 * 1024
 
 
 def twist(value, turn):
@@ -94,16 +95,27 @@
                 write(n1, rows, re * math.cos(turn) - im * math.sin(turn))
 
 
-def groups(n, channels, body):
-    size = max(1, min(n, 512 // channels))
-
-    @pl.loop(0, n // size)
-    def _(i):
-        body(pl.ds(i * size, size), size)
-
-
 def flat(x):
     return x.reshape(x.shape[0] * x.shape[1], x.shape[2])
+
+
+def start_all(copies):
+    for copy in copies:
+        copy.start()
+
+
+def wait_all(copies):
+    for copy in copies:
+        copy.wait()
+
+
+def parts_of(size):
+    step = max(1, size // PARTS)
+    return [pl.ds(k, step) for k in range(0, size, step)]
+
+
+def side(half):
+    return lax.axis_index("context") // half
 
 
 def filter_kernel(n, channels, tokens, f_ref, tw_ref, fwd_ref, out_ref, y_ref):
@@ -111,44 +123,75 @@
         lambda n1, rows: f_ref[rows, n1 * tokens : (n1 + 1) * tokens],
         n, channels, tokens, tw_ref, y_ref,
     )
-
-    def body(ms, size):
-        out_ref[ms] = times_table(flat(y_ref[ms]), fwd_ref).reshape(size, channels, 2 * tokens)
-
-    groups(n, channels, body)
-
-
-def conv_kernel(
-    sign, n, channels, tokens, x_ref, spec_ref, tw_ref, fwd_ref, inv_ref, out_ref, own_ref, y_ref
-):
-    outer_forward(lambda n1, rows: x_ref[n1, rows], n, channels, tokens, tw_ref, y_ref)
-
-    def body(ms, size):
+    for ms in parts_of(n):
+        out_ref[ms] = times_table(flat(y_ref[ms]), fwd_ref).reshape(ms.size, channels, 2 * tokens)
+
+
+def conv_middle(sign, n, channels, tokens, fwd_ref, inv_ref, spec_ref, own_ref, y_ref):
+    for ms in parts_of(n):
         own = times_table(flat(y_ref[ms]), fwd_ref)
-        own_ref[ms] = own.reshape(size, channels, 2 * tokens)
+        own_ref[ms] = own.reshape(ms.size, channels, 2 * tokens)
         spec = flat(spec_ref[ms])
         re, im = own[:, :tokens], own[:, tokens:]
         s_re, s_im = spec[:, :tokens], spec[:, tokens:] * sign
         both = jnp.concatenate([re * s_re - im * s_im, re * s_im + im * s_re], axis=1)
-        y_ref[ms] = times_table(both, inv_ref).reshape(size, channels, 2 * tokens)
-
-    groups(n, channels, body)
+        y_ref[ms] = times_table(both, inv_ref).reshape(ms.size, channels, 2 * tokens)
+
+
+def conv_kernel(
+    n, channels, tokens, x_ref, tw_ref, fwd_ref, inv_ref, spec_ref, after_ref,
+    keep_ref, send_ref, own_ref, buf_ref, y_ref, sem,
+):
+    half = n // 2
+    mine = side(half)
+    outer_forward(
+        lambda n1, rows: x_ref[n1 % half, mine ^ (n1 // half), rows],
+        n, channels, tokens, tw_ref, y_ref,
+    )
+    conv_middle(1.0, n, channels, tokens, fwd_ref, inv_ref, spec_ref, own_ref, y_ref)
 
     def write(n1, rows, value):
-        out_ref[n1, rows] = value
+        buf_ref[n1, rows] = value
 
     outer_inverse(write, n, channels, tokens, tw_ref, y_ref)
-
-
-def filter_grad_kernel(scale, n, channels, tokens, p_ref, g_ref, tw_ref, inv_ref, out_ref, y_ref):
-    def body(ms, size):
+    keep_ref[...] = buf_ref[pl.ds(mine * half, half)]
+    send_ref[...] = buf_ref[pl.ds((1 - mine) * half, half)]
+
+
+def back_kernel(
+    n, channels, tokens, near_ref, far_ref, tw_ref, fwd_ref, inv_ref, spec_ref, after_ref,
+    out_ref, own_ref, buf_ref, y_ref, sem,
+):
+    half = n // 2
+    mine = side(half)
+    for r in range(half):
+        buf_ref[r, mine] = near_ref[r, mine]
+        buf_ref[r, 1 - mine] = far_ref[r]
+    outer_forward(
+        lambda n1, rows: buf_ref[n1 % half, n1 // half, rows],
+        n, channels, tokens, tw_ref, y_ref,
+    )
+    conv_middle(-1.0, n, channels, tokens, fwd_ref, inv_ref, spec_ref, own_ref, y_ref)
+
+    def write(n1, rows, value):
+        buf_ref[n1 % half, n1 // half, rows] = value
+
+    outer_inverse(write, n, channels, tokens, tw_ref, y_ref)
+    stores = [
+        pltpu.make_async_copy(buf_ref.at[part], out_ref.at[part], sem.at[i])
+        for i, part in enumerate(parts_of(half))
+    ]
+    start_all(stores)
+    wait_all(stores)
+
+
+def filter_grad_kernel(scale, n, channels, tokens, tw_ref, inv_ref, p_ref, g_ref, out_ref, y_ref):
+    for ms in parts_of(n):
         p, g = flat(p_ref[ms]), flat(g_ref[ms])
         p_re, p_im = p[:, :tokens], p[:, tokens:]
         re, im = g[:, :tokens], g[:, tokens:]
         both = jnp.concatenate([re * p_re + im * p_im, im * p_re - re * p_im], axis=1)
-        y_ref[ms] = times_table(both, inv_ref).reshape(size, channels, 2 * tokens)
-
-    groups(n, channels, body)
+        y_ref[ms] = times_table(both, inv_ref).reshape(ms.size, channels, 2 * tokens)
 
     def write(n1, rows, value):
         out_ref[rows, n1 * tokens : (n1 + 1) * tokens] = value * scale
@@ -156,45 +199,116 @@
     outer_inverse(write, n, channels, tokens, tw_ref, y_ref)
 
 
-def call(body, outs, n, channels, tokens, passes):
-    size = n * channels * tokens
-    return pl.pallas_call(
-        body,
-        out_shape=outs,
-        scratch_shapes=[pltpu.VMEM((n, channels, 2 * tokens), jnp.float32)],
-        compiler_params=pltpu.CompilerParams(vmem_limit_bytes=VMEM_BYTES),
-        cost_estimate=pl.CostEstimate(
-            flops=passes * size * 2 * 2 * tokens * 4, bytes_accessed=6 * size * 4, transcendentals=0
-        ),
-    )
-
-
-def product_kernel(a_ref, b_ref, out_ref):
-    out_ref[...] = a_ref[...] * b_ref[...]
-
-
-def gate_kernel(x_ref, a_ref, b_ref, oa_ref, ob_ref):
-    x = x_ref[...]
-    oa_ref[...] = x * a_ref[...]
-    ob_ref[...] = x * b_ref[...]
-
-
-def tiled(body, n_in, n_out, shape):
-    rows = math.gcd(shape[0], 512)
-    spec = pl.BlockSpec((rows, shape[1]), lambda i: (i, 0))
-    return pl.pallas_call(
-        body,
-        grid=(shape[0] // rows,),
-        in_specs=[spec] * n_in,
-        out_specs=[spec] * n_out,
-        out_shape=[jax.ShapeDtypeStruct(shape, jnp.float32)] * n_out,
-        compiler_params=pltpu.CompilerParams(vmem_limit_bytes=VMEM_BYTES),
-        cost_estimate=pl.CostEstimate(
-            flops=n_out * shape[0] * shape[1],
-            bytes_accessed=(n_in + n_out) * 4 * shape[0] * shape[1],
-            transcendentals=0,
-        ),
-    )
+def load_pairs(n, a_ref, b_ref, a_buf, b_buf, sem):
+    loads = []
+    for i, part in enumerate(parts_of(n)):
+        loads.append(
+            [
+                pltpu.make_async_copy(a_ref.at[part], a_buf.at[part], sem.at[0, i]),
+                pltpu.make_async_copy(b_ref.at[part], b_buf.at[part], sem.at[1, i]),
+            ]
+        )
+        start_all(loads[-1])
+    return loads
+
+
+def product_split_kernel(n, a_ref, b_ref, keep_ref, send_ref, a_buf, b_buf, sem):
+    half = n // 2
+    mine = side(half)
+    loads = load_pairs(n, a_ref, b_ref, a_buf, b_buf, sem)
+    for load in loads:
+        wait_all(load)
+    for ref, first in ((send_ref, (1 - mine) * half), (keep_ref, mine * half)):
+        for k in range(half):
+            ref[k] = a_buf[first + k] * b_buf[first + k]
+
+
+def product_kernel(n, a_ref, b_ref, after_ref, out_ref, a_buf, b_buf, buf_ref, sem):
+    half = n // 2
+    loads = load_pairs(n, a_ref, b_ref, a_buf, b_buf, sem)
+    for load in loads:
+        wait_all(load)
+    stores = [
+        pltpu.make_async_copy(buf_ref.at[part], out_ref.at[part], sem.at[2, i])
+        for i, part in enumerate(parts_of(half))
+    ]
+    for part, store in zip(parts_of(half), stores):
+        for s in range(2):
+            rows = pl.ds(part.start + s * half, part.size)
+            buf_ref[part, s] = a_buf[rows] * b_buf[rows]
+        store.start()
+    wait_all(stores)
+
+
+def send_kernel(half, x_ref, send_ref):
+    send_ref[...] = x_ref[:, 1 - side(half)]
+
+
+def merge_kernel(half, keep_ref, got_ref, after_ref, out_ref, sem):
+    stores = [
+        pltpu.make_async_copy(ref.at[part], out_ref.at[part, s], sem.at[s, i])
+        for i, part in enumerate(parts_of(half))
+        for s, ref in enumerate((keep_ref, got_ref))
+    ]
+    start_all(stores)
+    wait_all(stores)
+
+
+def gate_parts(n, blocks, a_ref, b_ref, outs, bufs, sem):
+    stores = []
+    size = max(1, n // 2 // PARTS)
+    for h, (read, first) in enumerate(blocks):
+        for i, k in enumerate(range(0, n // 2, size)):
+            part = pl.ds(first + k, size)
+            x = read(pl.ds(k, size))
+            for j, (ref, buf, out) in enumerate(zip((a_ref, b_ref), bufs, outs)):
+                buf[part] = x * ref[part]
+                stores.append(pltpu.make_async_copy(buf.at[part], out.at[part], sem.at[j, h, i]))
+                stores[-1].start()
+    wait_all(stores)
+
+
+def gate_kernel(n, x_ref, a_ref, b_ref, oa_ref, ob_ref, a_buf, b_buf, sem):
+    half = n // 2
+    blocks = [
+        (lambda part, s=s: x_ref[part, s], (side(half) ^ s) * half) for s in range(2)
+    ]
+    gate_parts(n, blocks, a_ref, b_ref, (oa_ref, ob_ref), (a_buf, b_buf), sem)
+
+
+def gate_split_kernel(n, near_ref, far_ref, a_ref, b_ref, oa_ref, ob_ref, a_buf, b_buf, sem):
+    half = n // 2
+    mine = side(half)
+    blocks = [
+        (lambda part: near_ref[part, mine], mine * half),
+        (lambda part: far_ref[part], (1 - mine) * half),
+    ]
+    gate_parts(n, blocks, a_ref, b_ref, (oa_ref, ob_ref), (a_buf, b_buf), sem)
+
+
+SPACES = {"v": pltpu.VMEM, "h": pltpu.HBM, "a": pl.ANY}
+
+
+def kernel_call(body, ins, outs, scratch, flops=0):
+    shapes = [SPACES[space](shape, jnp.float32) for space, shape in outs]
+
+    def run(*args):
+        args = [
+            pltpu.with_memory_space_constraint(x, pltpu.HBM) if space == "h" else x
+            for space, x in zip(ins, args, strict=True)
+        ]
+        size = sum(math.prod(x.shape) for x in (*args, *shapes))
+        return pl.pallas_call(
+            body,
+            in_specs=[pl.BlockSpec(memory_space=SPACES[space]) for space in ins],
+            out_specs=[pl.BlockSpec(memory_space=SPACES[space]) for space, _ in outs],
+            out_shape=shapes,
+            scratch_shapes=scratch,
+            compiler_params=pltpu.CompilerParams(vmem_limit_bytes=VMEM_BYTES),
+            cost_estimate=pl.CostEstimate(flops=flops, bytes_accessed=4 * size, transcendentals=0),
+        )(*args)
+
+    return run
 
 
 def tables(n, tokens):
@@ -225,41 +339,77 @@
     scale = 1.0 / math.sqrt(pair_size * length)
     sizes = (n, channels, tokens)
     tw, fwd, inv = tables(n, tokens)
-    spectrum = jax.ShapeDtypeStruct((n, channels, 2 * tokens), jnp.float32)
-    rows = jax.ShapeDtypeStruct((n, channels, tokens), jnp.float32)
-    lags = jax.ShapeDtypeStruct((channels, length), jnp.float32)
-
-    def exchange(x):
-        return lax.all_to_all(x.reshape(rows.shape), "context", 0, 0, tiled=True)
+    half = n // 2
+    blocks, spectrum = (n, channels, tokens), (n, channels, 2 * tokens)
+    halves, paired, lags = (half, channels, tokens), (half, 2, channels, tokens), (channels, length)
+    flops = 4 * 2 * 2 * tokens * n * channels * tokens
+    f32 = jnp.float32
+    y = pltpu.VMEM(spectrum, f32)
+
+    def semaphores(*shape):
+        return pltpu.SemaphoreType.DMA(shape)
 
     def part(body, *args):
-        return lambda *refs: body(*args, *sizes, *refs)
+        return lambda *refs: body(*args, *refs)
+
+    def mirror(x):
+        return lax.ppermute(x, "context", [(i, i ^ half) for i in range(n)])
+
+    def within_half(x):
+        members = [[h * half + r for r in range(half)] for h in range(2)]
+        return lax.all_to_all(x, "context", 0, 0, axis_index_groups=members, tiled=True)
 
     query, key, value, cot = (
-        x.reshape(width, tokens) for x in (query_input, key_input, value_input, cotangent)
-    )
-    multiply = tiled(product_kernel, 2, 1, (width, tokens))
-    (product,) = multiply(key, value)
-    (conv_grad,) = multiply(cot, query)
-    product_ch = exchange(product)
-    grad_ch = exchange(conv_grad)
-    filt = call(part(filter_kernel), spectrum, *sizes, 1)(filters, tw, fwd)
-    conv_ch, prod_spec = call(part(conv_kernel, 1.0), [rows, spectrum], *sizes, 2)(
-        product_ch, filt, tw, fwd, inv
-    )
-    conv_tok = exchange(conv_ch).reshape(width, tokens)
-    back_ch, grad_spec = call(part(conv_kernel, -1.0), [rows, spectrum], *sizes, 2)(
-        grad_ch, filt, tw, fwd, inv
-    )
-    back_tok = exchange(back_ch).reshape(width, tokens)
-    own = call(part(filter_grad_kernel, scale), lags, *sizes, 1)(prod_spec, grad_spec, tw, inv)
+        x.reshape(blocks) for x in (query_input, key_input, value_input, cotangent)
+    )
+    bufs = [pltpu.VMEM(blocks, f32)] * 2
+    send = kernel_call(part(send_kernel, half), "v", [("v", halves)], [])
+    merge = kernel_call(
+        part(merge_kernel, half), "aaa", [("h", paired)], [semaphores(2, PARTS)]
+    )
+
+    keep_p, send_p = kernel_call(
+        part(product_split_kernel, n), "hh", [("v", halves)] * 2, [*bufs, semaphores(2, PARTS)]
+    )(key, value)
+    got_p = mirror(send_p)
+    (conv_grad,) = kernel_call(
+        part(product_kernel, n), "hha", [("h", paired)],
+        [*bufs, pltpu.VMEM(paired, f32), semaphores(3, PARTS)],
+    )(cot, query, keep_p)
+    near_g = within_half(conv_grad)
+    (send_g,) = send(near_g)
+    far_g = mirror(send_g)
+    (filt,) = kernel_call(
+        part(filter_kernel, *sizes), "vvv", [("v", spectrum)], [y], flops
+    )(filters, tw, fwd)
+    product_ch = within_half(*merge(keep_p, got_p, send_g))
+    keep_c, send_c, prod_spec = kernel_call(
+        part(conv_kernel, *sizes), "vvvvva", [("v", halves)] * 2 + [("v", spectrum)],
+        [pltpu.VMEM(blocks, f32), y, semaphores(PARTS)], 2 * flops,
+    )(product_ch, tw, fwd, inv, filt, send_g)
+    got_c = mirror(send_c)
+    back_ch, grad_spec = kernel_call(
+        part(back_kernel, *sizes), "vvvvvva", [("h", paired), ("v", spectrum)],
+        [pltpu.VMEM(paired, f32), y, semaphores(PARTS)], 2 * flops,
+    )(near_g, far_g, tw, fwd, inv, filt, keep_c)
+    near_b = within_half(back_ch)
+    (send_b,) = send(near_b)
+    far_b = mirror(send_b)
+    conv_tok = within_half(*merge(keep_c, got_c, send_b))
+    (own,) = kernel_call(
+        part(filter_grad_kernel, scale, *sizes), "vvvv", [("v", lags)], [y], flops
+    )(tw, inv, prod_spec, grad_spec)
     if pair_size == 2:
         grad_filter = own + lax.ppermute(own, "dp", [(0, 1), (1, 0)])
     else:
         grad_filter = lax.psum(own, "dp")
-    gate = tiled(gate_kernel, 3, 2, (width, tokens))
-    gated, grad_query = gate(conv_tok, query, cot)
-    grad_key, grad_value = gate(back_tok, value, key)
+    gate_scratch = [*bufs, semaphores(2, 2, PARTS)]
+    gated, grad_query = kernel_call(
+        part(gate_kernel, n), "vvv", [("h", blocks)] * 2, gate_scratch
+    )(conv_tok, query, cot)
+    grad_key, grad_value = kernel_call(
+        part(gate_split_kernel, n), "vvvv", [("h", blocks)] * 2, gate_scratch
+    )(near_b, far_b, value, key)
     shape = query_input.shape
     return (
         gated.reshape(shape),

time: 130 us -> 153 us (1.18)
  waiting for transfers between devices: 58.2 us -> 88.9 us
  local copies, waits for them, and re-layouts: 14.7 us -> 9.79 us
    ppermute x0 -> x4, waiting for transfers between devices: none -> 24.6 us  [mirror(): return lax.ppermute(x, 'context', [(i, i ^ half) for i in range(n)])]
    all_to_all x4, starting transfers between devices: 26.3 us -> 18.9 us  [within_half(): lax.all_to_all(x, 'context', 0, 0, axis_index_groups=members, tiled=True)]
    all_to_all x4, waiting for transfers between devices: 55.6 us -> 62.1 us  [within_half(): lax.all_to_all(x, 'context', 0, 0, axis_index_groups=members, tiled=True)]
    ppermute x0 -> x4, starting transfers between devices: none -> 5.87 us  [mirror(): return lax.ppermute(x, 'context', [(i, i ^ half) for i in range(n)])]
    unnamed x42 -> x36, local copies, waits for them, and re-layouts: 14.7 us -> 9.79 us
    pallas_call x8 -> x12, Pallas kernels: 27.9 us -> 27.1 us  [run(): pl.pallas_call(body, in_specs=[pl.BlockSpec(memory_space=SPACES[space]) f...]
  transfers between devices with their start and end apart: 5 -> 9, of which waited for: 5 -> 6; matrix products, arithmetic and copies ran while one was open for 1% -> 1% of each run, Pallas kernels for 18% -> 8%
where the time goes in v3:
time: 153 us
  waiting for transfers between devices  88.9 us (58%)
  Pallas kernels  27.1 us (18%)
  starting transfers between devices  24.9 us (16%)
  local copies, waits for them, and re-layouts  9.79 us (6%)
    all_to_all x4, waiting for transfers between devices, within_half(): lax.all_to_all(x, 'context', 0, 0, axis_index_groups=members, tiled=True)  62.1 us
    pallas_call x12, Pallas kernels, run(): pl.pallas_call(body, in_specs=[pl.BlockSpec(memory_space=SPACES[space]) f...  27.1 us
    ppermute x4, waiting for transfers between devices, mirror(): return lax.ppermute(x, 'context', [(i, i ^ half) for i in range(n)])  24.6 us
    all_to_all x4, starting transfers between devices, within_half(): lax.all_to_all(x, 'context', 0, 0, axis_index_groups=members, tiled=True)  18.9 us
    unnamed x36, local copies, waits for them, and re-layouts  9.79 us
    ppermute x4, starting transfers between devices, mirror(): return lax.ppermute(x, 'context', [(i, i ^ half) for i in range(n)])  5.87 us
  transfers between devices with their start and end apart: 9, of which 6 were waited for; matrix products, arithmetic and copies ran while one was open for 1% of the time, Pallas kernels for 8%

profile of v3, /device:TPU:0, one launch (start us, length us, event | category | flops | bytes accessed | tf_op | source)
XLA Modules:
  0.0 152.5 jit_solution(8254971937727852652)
XLA Ops:
  0.6 1.7 %shard_map.119 = (f32[8,128,128]{2,1,0:T(8,128)S(1)}, f32[8,128,128]{2,1,0:T(8,128)S(1)}) custom-call(f32[16,128,128]{2,1,0:T(8,128)} %bitcast.12, f32[16,128,128]{2,1,0:T(8,128)} %bitcast.14), custom_call_target="tpu_custom_call" | custom-call | bytes 3145728 | tf_op jit(solution)/shard_map/pallas_call | solution.py:301
  2.3 2.6 %shard_map.120 = f32[8,2,128,128]{3,2,1,0:T(8,128)} custom-call(f32[16,128,128]{2,1,0:T(8,128)} %bitcast.8, f32[16,128,128]{2,1,0:T(8,128)} %bitcast.10, f32[8,128,128]{2,1,0:T(8,128)S(1)} %get-tuple-element.16.refs_2_.refs_0_), custom_call_target="tpu_custom_call" | custom-call | bytes 3670016 | tf_op jit(solution)/shard_map/pallas_call | solution.py:301
  4.9 6.2 %all-to-all-start = ((f32[8,2,128,128]{3,2,1,0:T(8,128)}), f32[8,2,128,128]{3,2,1,0:T(8,128)S(1)}, u32[]{:S(2)}, u32[]{:S(2)}) async-start(f32[8,2,128,128]{3,2,1,0:T(8,128)} %shard_map.120), calls=%async_computation | async-start | bytes 2097152 | tf_op jit(solution)/shard_map/all_to_all | solution.py:360
  11.1 2.6 %collective-permute-start = (f32[8,128,128]{2,1,0:T(8,128)S(1)}, f32[8,128,128]{2,1,0:T(8,128)S(1)}, u32[]{:S(2)}, u32[]{:S(2)}) collective-permute-start(f32[8,128,128]{2,1,0:T(8,128)S(1)} %get-tuple-element.17), channel_id=1, source_target_pairs={{0,8},{1,9},{2,10},{3,11},{4,12},{5,13},{6,14},{7,15},{8,0},{9,1},... | collective-permute-start | bytes 1572872 | tf_op jit(solution)/shard_map/ppermute | solution.py:356
  13.7 22.3 %all-to-all-done.refs_0_ = f32[8,2,128,128]{3,2,1,0:T(8,128)S(1)} async-done(((f32[8,2,128,128]{3,2,1,0:T(8,128)}), f32[8,2,128,128]{3,2,1,0:T(8,128)S(1)}, u32[]{:S(2)}, u32[]{:S(2)}) %all-to-all-start) | async-done | bytes 1048608 | tf_op jit(solution)/shard_map/all_to_all | solution.py:360
  37.9 4.8 %all-to-all-start.1 = ((f32[8,2,128,128]{3,2,1,0:T(8,128)}), f32[8,2,128,128]{3,2,1,0:T(8,128)}, u32[]{:S(2)}, u32[]{:S(2)}) async-start(f32[8,2,128,128]{3,2,1,0:T(8,128)} %shard_map.122), calls=%async_computation.1 | async-start | bytes 2097152 | tf_op jit(solution)/shard_map/all_to_all | solution.py:360
  42.7 2.5 %collective-permute-start.2 = (f32[8,128,128]{2,1,0:T(8,128)}, f32[8,128,128]{2,1,0:T(8,128)}, u32[]{:S(2)}, u32[]{:S(2)}) collective-permute-start(f32[8,128,128]{2,1,0:T(8,128)} %shard_map.121.refs_2_.refs_5_), channel_id=1, source_target_pairs={{0,8},{1,9},{2,10},{3,11},{4,12},{5,13},{6,14},{7,15},{8,0},{9,1},... | collective-permute-start | bytes 1572872 | tf_op jit(solution)/shard_map/ppermute | solution.py:356
  47.4 1.7 %shard_map.123.refs_4_.refs_5_ = f32[16,128,256]{2,1,0:T(8,128)S(1)} custom-call(f32[128,2048]{1,0:T(8,128)S(1)} %copy-done.15, f32[2,16,8,128]{3,2,1,0:T(8,128)S(1)} %copy-done.8, bf16[2,256,256]{2,1,0:T(8,128)(2,1)S(1)} %copy-done.5), custom_call_target="tpu_custom_call" | custom-call | flops 536870912 | bytes 3801088 | tf_op jit(solution)/shard_map/pallas_call | solution.py:301
  49.1 17.8 %all-to-all-done.1.refs_0_ = f32[8,2,128,128]{3,2,1,0:T(8,128)} async-done(((f32[8,2,128,128]{3,2,1,0:T(8,128)}), f32[8,2,128,128]{3,2,1,0:T(8,128)}, u32[]{:S(2)}, u32[]{:S(2)}) %all-to-all-start.1) | async-done | bytes 1048608 | tf_op jit(solution)/shard_map/all_to_all | solution.py:360
  67.9 5.2 %shard_map.124 = (f32[8,128,128]{2,1,0:T(8,128)S(1)}, f32[8,128,128]{2,1,0:T(8,128)S(1)}, f32[16,128,256]{2,1,0:T(8,128)S(1)}) custom-call(f32[8,2,128,128]{3,2,1,0:T(8,128)} %all-to-all-done.1.refs_0_, f32[2,16,8,128]{3,2,1,0:T(8,128)S(1)} %copy-done.8, bf16[2,256,256]{2,1,0:T(8,128)(2,1)S(1)} %copy-done.6, bf16[2,256,256]{2,1,0:T(8,128)(2,1)S(1)} %copy-done.4, ...), custom_call_target="tpu_custom_call" | custom-call | flops 1073741824 | bytes 7995392 | tf_op jit(solution)/shard_map/pallas_call | solution.py:301
  73.1 1.3 copy-done.11
  75.2 6.1 %shard_map.125 = (f32[8,2,128,128]{3,2,1,0:T(8,128)}, f32[16,128,256]{2,1,0:T(8,128)S(1)}) custom-call(f32[8,2,128,128]{3,2,1,0:T(8,128)S(1)} %all-to-all-done.refs_0_, f32[8,128,128]{2,1,0:T(8,128)} %collective-permute-done.2.refs_1_, f32[2,16,8,128]{3,2,1,0:T(8,128)S(1)} %copy-done.8, bf16[2,256,256]{2,1,0:T(8,128)(2,1)S(1)} %copy-done.7, ...), custom_call_target="tpu_custom_call" | custom-call | flops 1073741824 | bytes 8519680 | tf_op jit(solution)/shard_map/pallas_call | solution.py:301
  81.4 1.3 copy-done.13
  82.7 3.7 %all-to-all-start.2 = ((f32[8,2,128,128]{3,2,1,0:T(8,128)}), f32[8,2,128,128]{3,2,1,0:T(8,128)S(1)}, u32[]{:S(2)}, u32[]{:S(2)}) async-start(f32[8,2,128,128]{3,2,1,0:T(8,128)} %get-tuple-element.20), calls=%async_computation.2 | async-start | bytes 2097152 | tf_op jit(solution)/shard_map/all_to_all | solution.py:360
  86.7 22.0 %all-to-all-done.2.refs_0_ = f32[8,2,128,128]{3,2,1,0:T(8,128)S(1)} async-done(((f32[8,2,128,128]{3,2,1,0:T(8,128)}), f32[8,2,128,128]{3,2,1,0:T(8,128)S(1)}, u32[]{:S(2)}, u32[]{:S(2)}) %all-to-all-start.2) | async-done | bytes 1048608 | tf_op jit(solution)/shard_map/all_to_all | solution.py:360
  109.5 1.6 %collective-permute-done.1.refs_1_ = f32[8,128,128]{2,1,0:T(8,128)S(1)} collective-permute-done((f32[8,128,128]{2,1,0:T(8,128)S(1)}, f32[8,128,128]{2,1,0:T(8,128)S(1)}, u32[]{:S(2)}, u32[]{:S(2)}) %collective-permute-start.1) | collective-permute-done | bytes 524320 | tf_op jit(solution)/shard_map/ppermute | solution.py:356
  112.1 4.2 %all-to-all-start.3 = ((f32[8,2,128,128]{3,2,1,0:T(8,128)}), f32[8,2,128,128]{3,2,1,0:T(8,128)}, u32[]{:S(2)}, u32[]{:S(2)}) async-start(f32[8,2,128,128]{3,2,1,0:T(8,128)} %shard_map.127), calls=%async_computation.3 | async-start | bytes 2097152 | tf_op jit(solution)/shard_map/all_to_all | solution.py:360
  116.4 1.6 %copy-done.12 = f32[16,128,256]{2,1,0:T(8,128)S(1)} copy-done((f32[16,128,256]{2,1,0:T(8,128)S(1)}, f32[16,128,256]{2,1,0:T(8,128)}, u32[]{:S(2)}) %copy-start.12) | copy-done | bytes 2097176
  118.0 1.6 %copy-done.14 = f32[16,128,256]{2,1,0:T(8,128)S(1)} copy-done((f32[16,128,256]{2,1,0:T(8,128)S(1)}, f32[16,128,256]{2,1,0:T(8,128)}, u32[]{:S(2)}) %copy-start.14) | copy-done | bytes 2097176
  119.6 1.9 %shard_map.130 = f32[128,2048]{1,0:T(8,128)S(1)} custom-call(f32[2,16,8,128]{3,2,1,0:T(8,128)S(1)} %copy-done.8, bf16[2,256,256]{2,1,0:T(8,128)(2,1)S(1)} %copy-done.4, f32[16,128,256]{2,1,0:T(8,128)S(1)} %copy-done.12, f32[16,128,256]{2,1,0:T(8,128)S(1)} %copy-done.14), custom_call_target="tpu_custom_call" | custom-call | flops 536870912 | bytes 5898240 | tf_op jit(solution)/shard_map/pallas_call | solution.py:301
  122.1 2.2 %collective-permute-done.4 = f32[128,2048]{1,0:T(8,128)S(1)} collective-permute-done((f32[128,2048]{1,0:T(8,128)S(1)}, f32[128,2048]{1,0:T(8,128)S(1)}, u32[]{:S(2)}, u32[]{:S(2)}) %collective-permute-start.4) | collective-permute-done | bytes 1048608 | tf_op jit(solution)/shard_map/ppermute | solution.py:403
  125.3 23.0 %collective-permute-done.3.refs_1_ = f32[8,128,128]{2,1,0:T(8,128)S(1)} collective-permute-done((f32[8,128,128]{2,1,0:T(8,128)}, f32[8,128,128]{2,1,0:T(8,128)S(1)}, u32[]{:S(2)}, u32[]{:S(2)}) %collective-permute-start.3) | collective-permute-done | bytes 524320 | tf_op jit(solution)/shard_map/ppermute | solution.py:356
  148.3 1.5 shard_map.129
  149.8 2.7 %shard_map.128 = (f32[16,128,128]{2,1,0:T(8,128)}, f32[16,128,128]{2,1,0:T(8,128)}) custom-call(f32[8,2,128,128]{3,2,1,0:T(8,128)} %all-to-all-done.3.refs_0_, f32[16,128,128]{2,1,0:T(8,128)S(1)} %bitcast.11, f32[16,128,128]{2,1,0:T(8,128)S(1)} %bitcast.9), custom_call_target="tpu_custom_call" | custom-call | bytes 5242880 | tf_op jit(solution)/shard_map/pallas_call | solution.py:301
  (43 shorter events, 9.6 us)
Async XLA Ops:
  4.9 31.1 %all-to-all-start = ((f32[8,2,128,128]{3,2,1,0:T(8,128)}), f32[8,2,128,128]{3,2,1,0:T(8,128)S(1)}, u32[]{:S(2)}, u32[]{:S(2)}) async-start(f32[8,2,128,128]{3,2,1,0:T(8,128)} %shard_map.120), calls=%async_computation | async-start | bytes 2097152 | tf_op jit(solution)/shard_map/all_to_all | solution.py:360
  11.1 25.8 %collective-permute-start = (f32[8,128,128]{2,1,0:T(8,128)S(1)}, f32[8,128,128]{2,1,0:T(8,128)S(1)}, u32[]{:S(2)}, u32[]{:S(2)}) collective-permute-start(f32[8,128,128]{2,1,0:T(8,128)S(1)} %get-tuple-element.17), channel_id=1, source_target_pairs={{0,8},{1,9},{2,10},{3,11},{4,12},{5,13},{6,14},{7,15},{8,0},{9,1},... | collective-permute-start | bytes 1572872 | tf_op jit(solution)/shard_map/ppermute | solution.py:356
  36.9 8.3 %copy-start.8 = (f32[2,16,8,128]{3,2,1,0:T(8,128)S(1)}, f32[2,16,8,128]{3,2,1,0:T(8,128)}, u32[]{:S(2)}) copy-start(f32[2,16,8,128]{3,2,1,0:T(8,128)} %constant.8.clone.refs_1_.refs_2_.refs_0_) | copy-start | bytes 393220
  37.9 29.0 %all-to-all-start.1 = ((f32[8,2,128,128]{3,2,1,0:T(8,128)}), f32[8,2,128,128]{3,2,1,0:T(8,128)}, u32[]{:S(2)}, u32[]{:S(2)}) async-start(f32[8,2,128,128]{3,2,1,0:T(8,128)} %shard_map.122), calls=%async_computation.1 | async-start | bytes 2097152 | tf_op jit(solution)/shard_map/all_to_all | solution.py:360
  42.7 24.2 %copy-start.4 = (bf16[2,256,256]{2,1,0:T(8,128)(2,1)S(1)}, bf16[2,256,256]{2,1,0:T(8,128)(2,1)}, u32[]{:S(2)}) copy-start(bf16[2,256,256]{2,1,0:T(8,128)(2,1)} %constant.7.clone.refs_3_.refs_4_.refs_1_) | copy-start | bytes 786436
  42.7 32.5 %collective-permute-start.2 = (f32[8,128,128]{2,1,0:T(8,128)}, f32[8,128,128]{2,1,0:T(8,128)}, u32[]{:S(2)}, u32[]{:S(2)}) collective-permute-start(f32[8,128,128]{2,1,0:T(8,128)} %shard_map.121.refs_2_.refs_5_), channel_id=1, source_target_pairs={{0,8},{1,9},{2,10},{3,11},{4,12},{5,13},{6,14},{7,15},{8,0},{9,1},... | collective-permute-start | bytes 1572872 | tf_op jit(solution)/shard_map/ppermute | solution.py:356
  46.2 1.2 copy-start.15
  67.9 7.3 %copy-start.7 = (bf16[2,256,256]{2,1,0:T(8,128)(2,1)S(1)}, bf16[2,256,256]{2,1,0:T(8,128)(2,1)}, u32[]{:S(2)}) copy-start(bf16[2,256,256]{2,1,0:T(8,128)(2,1)} %constant.6.clone.refs_2_.refs_3_) | copy-start | bytes 786436
  73.1 1.3 copy-start.11
  75.2 6.2 %copy-start.9 = (f32[8,128,128]{2,1,0:T(8,128)}, f32[8,128,128]{2,1,0:T(8,128)S(1)}, u32[]{:S(2)}) copy-start(f32[8,128,128]{2,1,0:T(8,128)S(1)} %get-tuple-element.18.refs_6_.refs_0_) | copy-start | bytes 1572868
  81.4 1.3 copy-start.13
  82.7 3.7 %copy-start.17 = (f32[8,128,128]{2,1,0:T(8,128)S(1)}, f32[8,128,128]{2,1,0:T(8,128)}, u32[]{:S(2)}) copy-start(f32[8,128,128]{2,1,0:T(8,128)} %copy-done.16) | copy-start | bytes 1572868
  82.7 28.4 %copy-start.10 = (f32[8,128,128]{2,1,0:T(8,128)S(1)}, f32[8,128,128]{2,1,0:T(8,128)}, u32[]{:S(2)}) copy-start(f32[8,128,128]{2,1,0:T(8,128)} %copy-done.9) | copy-start | bytes 1572868
  82.7 26.0 %all-to-all-start.2 = ((f32[8,2,128,128]{3,2,1,0:T(8,128)}), f32[8,2,128,128]{3,2,1,0:T(8,128)S(1)}, u32[]{:S(2)}, u32[]{:S(2)}) async-start(f32[8,2,128,128]{3,2,1,0:T(8,128)} %get-tuple-element.20), calls=%async_computation.2 | async-start | bytes 2097152 | tf_op jit(solution)/shard_map/all_to_all | solution.py:360
  86.4 24.7 %collective-permute-start.1 = (f32[8,128,128]{2,1,0:T(8,128)S(1)}, f32[8,128,128]{2,1,0:T(8,128)S(1)}, u32[]{:S(2)}, u32[]{:S(2)}) collective-permute-start(f32[8,128,128]{2,1,0:T(8,128)S(1)} %copy-done.17), channel_id=1, source_target_pairs={{0,8},{1,9},{2,10},{3,11},{4,12},{5,13},{6,14},{7,15},{8,0},{9,1},... | collective-permute-start | bytes 1572872 | tf_op jit(solution)/shard_map/ppermute | solution.py:356
  112.1 37.7 %all-to-all-start.3 = ((f32[8,2,128,128]{3,2,1,0:T(8,128)}), f32[8,2,128,128]{3,2,1,0:T(8,128)}, u32[]{:S(2)}, u32[]{:S(2)}) async-start(f32[8,2,128,128]{3,2,1,0:T(8,128)} %shard_map.127), calls=%async_computation.3 | async-start | bytes 2097152 | tf_op jit(solution)/shard_map/all_to_all | solution.py:360
  116.4 1.6 %copy-start.12 = (f32[16,128,256]{2,1,0:T(8,128)S(1)}, f32[16,128,256]{2,1,0:T(8,128)}, u32[]{:S(2)}) copy-start(f32[16,128,256]{2,1,0:T(8,128)} %copy-done.11) | copy-start | bytes 6291460
  118.0 1.6 %copy-start.14 = (f32[16,128,256]{2,1,0:T(8,128)S(1)}, f32[16,128,256]{2,1,0:T(8,128)}, u32[]{:S(2)}) copy-start(f32[16,128,256]{2,1,0:T(8,128)} %copy-done.13) | copy-start | bytes 6291460
  121.5 26.8 %copy-start.2 = (f32[1,2048,128]{2,1,0:T(8,128)S(1)}, f32[1,2048,128]{2,1,0:T(8,128)}, u32[]{:S(2)}) copy-start(f32[1,2048,128]{2,1,0:T(8,128)} %param.9) | copy-start | bytes 3145732
  121.5 26.8 %copy-start.3 = (f32[1,2048,128]{2,1,0:T(8,128)S(1)}, f32[1,2048,128]{2,1,0:T(8,128)}, u32[]{:S(2)}) copy-start(f32[1,2048,128]{2,1,0:T(8,128)} %param.10) | copy-start | bytes 3145732
  121.5 2.7 %collective-permute-start.4 = (f32[128,2048]{1,0:T(8,128)S(1)}, f32[128,2048]{1,0:T(8,128)S(1)}, u32[]{:S(2)}, u32[]{:S(2)}) collective-permute-start(f32[128,2048]{1,0:T(8,128)S(1)} %shard_map.130), channel_id=1, source_target_pairs={{0,16},{16,0},{1,17},{17,1},{2,18},{18,2},{3,19},{19,3},{4,20},{20... | collective-permute-start | bytes 3145736 | tf_op jit(solution)/shard_map/ppermute | solution.py:403
  121.6 26.7 %collective-permute-start.3 = (f32[8,128,128]{2,1,0:T(8,128)}, f32[8,128,128]{2,1,0:T(8,128)S(1)}, u32[]{:S(2)}, u32[]{:S(2)}) collective-permute-start(f32[8,128,128]{2,1,0:T(8,128)} %shard_map.126.refs_2_), channel_id=1, source_target_pairs={{0,8},{1,9},{2,10},{3,11},{4,12},{5,13},{6,14},{7,15},{8,0},{9,1},... | collective-permute-start | bytes 1572872 | tf_op jit(solution)/shard_map/ppermute | solution.py:356
  125.3 24.5 %copy-start = (f32[1,2048,128]{2,1,0:T(8,128)S(1)}, f32[1,2048,128]{2,1,0:T(8,128)}, u32[]{:S(2)}) copy-start(f32[1,2048,128]{2,1,0:T(8,128)} %param.12) | copy-start | bytes 3145732
  125.3 24.5 %copy-start.1 = (f32[1,2048,128]{2,1,0:T(8,128)S(1)}, f32[1,2048,128]{2,1,0:T(8,128)}, u32[]{:S(2)}) copy-start(f32[1,2048,128]{2,1,0:T(8,128)} %param.8) | copy-start | bytes 3145732
  (3 other events, 2.7 us)

commit v4 on v3

--- a/solution.py
+++ b/solution.py
@@ -10,6 +10,7 @@
 from jax.sharding import PartitionSpec as P
 
 ROWS = 8
+PLANES = 4
 PARTS = 4
 VMEM_BYTES = 24 * 1024 * 1024
 
@@ -114,8 +115,8 @@
     return [pl.ds(k, step) for k in range(0, size, step)]
 
 
-def side(half):
-    return lax.axis_index("context") // half
+def plane(width):
+    return lax.axis_index("context") // width
 
 
 def filter_kernel(n, channels, tokens, f_ref, tw_ref, fwd_ref, out_ref, y_ref):
@@ -138,14 +139,13 @@
         y_ref[ms] = times_table(both, inv_ref).reshape(ms.size, channels, 2 * tokens)
 
 
-def conv_kernel(
-    n, channels, tokens, x_ref, tw_ref, fwd_ref, inv_ref, spec_ref, after_ref,
-    keep_ref, send_ref, own_ref, buf_ref, y_ref, sem,
-):
-    half = n // 2
-    mine = side(half)
+def conv_kernel(planes, n, channels, tokens, x_ref, *refs):
+    tw_ref, fwd_ref, inv_ref, spec_ref, after_ref = refs[:5]
+    out_refs, (own_ref, buf_ref, y_ref) = refs[5 : planes + 5], refs[planes + 5 :]
+    width = n // planes
+    z = plane(width)
     outer_forward(
-        lambda n1, rows: x_ref[n1 % half, mine ^ (n1 // half), rows],
+        lambda n1, rows: x_ref[n1 % width, z ^ (n1 // width), rows],
         n, channels, tokens, tw_ref, y_ref,
     )
     conv_middle(1.0, n, channels, tokens, fwd_ref, inv_ref, spec_ref, own_ref, y_ref)
@@ -154,32 +154,34 @@
         buf_ref[n1, rows] = value
 
     outer_inverse(write, n, channels, tokens, tw_ref, y_ref)
-    keep_ref[...] = buf_ref[pl.ds(mine * half, half)]
-    send_ref[...] = buf_ref[pl.ds((1 - mine) * half, half)]
-
-
-def back_kernel(
-    n, channels, tokens, near_ref, far_ref, tw_ref, fwd_ref, inv_ref, spec_ref, after_ref,
-    out_ref, own_ref, buf_ref, y_ref, sem,
-):
-    half = n // 2
-    mine = side(half)
-    for r in range(half):
-        buf_ref[r, mine] = near_ref[r, mine]
-        buf_ref[r, 1 - mine] = far_ref[r]
+    for d in range(planes):
+        out_refs[d][...] = buf_ref[pl.ds((z ^ d) * width, width)]
+
+
+def back_kernel(planes, n, channels, tokens, near_ref, *refs):
+    far_refs, refs = refs[: planes - 1], refs[planes - 1 :]
+    (
+        tw_ref, fwd_ref, inv_ref, spec_ref, after_ref, out_ref, own_ref, buf_ref, y_ref, sem
+    ) = refs
+    width = n // planes
+    z = plane(width)
+    for q in range(width):
+        buf_ref[q, z] = near_ref[q, z]
+        for d in range(1, planes):
+            buf_ref[q, z ^ d] = far_refs[d - 1][q]
     outer_forward(
-        lambda n1, rows: buf_ref[n1 % half, n1 // half, rows],
+        lambda n1, rows: buf_ref[n1 % width, n1 // width, rows],
         n, channels, tokens, tw_ref, y_ref,
     )
     conv_middle(-1.0, n, channels, tokens, fwd_ref, inv_ref, spec_ref, own_ref, y_ref)
 
     def write(n1, rows, value):
-        buf_ref[n1 % half, n1 // half, rows] = value
+        buf_ref[n1 % width, n1 // width, rows] = value
 
     outer_inverse(write, n, channels, tokens, tw_ref, y_ref)
     stores = [
         pltpu.make_async_copy(buf_ref.at[part], out_ref.at[part], sem.at[i])
-        for i, part in enumerate(parts_of(half))
+        for i, part in enumerate(parts_of(width))
     ]
     start_all(stores)
     wait_all(stores)
@@ -212,78 +214,75 @@
     return loads
 
 
-def product_split_kernel(n, a_ref, b_ref, keep_ref, send_ref, a_buf, b_buf, sem):
-    half = n // 2
-    mine = side(half)
-    loads = load_pairs(n, a_ref, b_ref, a_buf, b_buf, sem)
-    for load in loads:
+def product_split_kernel(planes, n, a_ref, b_ref, *refs):
+    out_refs, (a_buf, b_buf, sem) = refs[:planes], refs[planes:]
+    width = n // planes
+    z = plane(width)
+    for load in load_pairs(n, a_ref, b_ref, a_buf, b_buf, sem):
         wait_all(load)
-    for ref, first in ((send_ref, (1 - mine) * half), (keep_ref, mine * half)):
-        for k in range(half):
-            ref[k] = a_buf[first + k] * b_buf[first + k]
-
-
-def product_kernel(n, a_ref, b_ref, after_ref, out_ref, a_buf, b_buf, buf_ref, sem):
-    half = n // 2
-    loads = load_pairs(n, a_ref, b_ref, a_buf, b_buf, sem)
-    for load in loads:
+    for d in range(planes):
+        for q in range(width):
+            out_refs[d][q] = a_buf[(z ^ d) * width + q] * b_buf[(z ^ d) * width + q]
+
+
+def product_kernel(planes, n, a_ref, b_ref, after_ref, out_ref, a_buf, b_buf, buf_ref, sem):
+    width = n // planes
+    for load in load_pairs(n, a_ref, b_ref, a_buf, b_buf, sem):
         wait_all(load)
     stores = [
         pltpu.make_async_copy(buf_ref.at[part], out_ref.at[part], sem.at[2, i])
-        for i, part in enumerate(parts_of(half))
+        for i, part in enumerate(parts_of(width))
     ]
-    for part, store in zip(parts_of(half), stores):
-        for s in range(2):
-            rows = pl.ds(part.start + s * half, part.size)
-            buf_ref[part, s] = a_buf[rows] * b_buf[rows]
+    for part, store in zip(parts_of(width), stores):
+        for z in range(planes):
+            rows = pl.ds(part.start + z * width, part.size)
+            buf_ref[part, z] = a_buf[rows] * b_buf[rows]
         store.start()
     wait_all(stores)
 
 
-def send_kernel(half, x_ref, send_ref):
-    send_ref[...] = x_ref[:, 1 - side(half)]
-
-
-def merge_kernel(half, keep_ref, got_ref, after_ref, out_ref, sem):
+def send_kernel(planes, width, x_ref, *out_refs):
+    for d in range(1, planes):
+        out_refs[d - 1][...] = x_ref[:, plane(width) ^ d]
+
+
+def merge_kernel(planes, width, *refs):
+    in_refs, (after_ref, out_ref, sem) = refs[:planes], refs[planes:]
     stores = [
-        pltpu.make_async_copy(ref.at[part], out_ref.at[part, s], sem.at[s, i])
-        for i, part in enumerate(parts_of(half))
-        for s, ref in enumerate((keep_ref, got_ref))
+        pltpu.make_async_copy(ref.at[part], out_ref.at[part, d], sem.at[d, i])
+        for d, ref in enumerate(in_refs)
+        for i, part in enumerate(parts_of(width))
     ]
     start_all(stores)
     wait_all(stores)
 
 
-def gate_parts(n, blocks, a_ref, b_ref, outs, bufs, sem):
+def gate_parts(width, blocks, a_ref, b_ref, outs, bufs, sem):
     stores = []
-    size = max(1, n // 2 // PARTS)
-    for h, (read, first) in enumerate(blocks):
-        for i, k in enumerate(range(0, n // 2, size)):
-            part = pl.ds(first + k, size)
-            x = read(pl.ds(k, size))
-            for j, (ref, buf, out) in enumerate(zip((a_ref, b_ref), bufs, outs)):
-                buf[part] = x * ref[part]
-                stores.append(pltpu.make_async_copy(buf.at[part], out.at[part], sem.at[j, h, i]))
-                stores[-1].start()
+    for d, (read, first) in enumerate(blocks):
+        part = pl.ds(first, width)
+        x = read()
+        for j, (ref, buf, out) in enumerate(zip((a_ref, b_ref), bufs, outs)):
+            buf[part] = x * ref[part]
+            stores.append(pltpu.make_async_copy(buf.at[part], out.at[part], sem.at[j, d]))
+            stores[-1].start()
     wait_all(stores)
 
 
-def gate_kernel(n, x_ref, a_ref, b_ref, oa_ref, ob_ref, a_buf, b_buf, sem):
-    half = n // 2
-    blocks = [
-        (lambda part, s=s: x_ref[part, s], (side(half) ^ s) * half) for s in range(2)
-    ]
-    gate_parts(n, blocks, a_ref, b_ref, (oa_ref, ob_ref), (a_buf, b_buf), sem)
-
-
-def gate_split_kernel(n, near_ref, far_ref, a_ref, b_ref, oa_ref, ob_ref, a_buf, b_buf, sem):
-    half = n // 2
-    mine = side(half)
-    blocks = [
-        (lambda part: near_ref[part, mine], mine * half),
-        (lambda part: far_ref[part], (1 - mine) * half),
-    ]
-    gate_parts(n, blocks, a_ref, b_ref, (oa_ref, ob_ref), (a_buf, b_buf), sem)
+def gate_kernel(planes, width, x_ref, a_ref, b_ref, oa_ref, ob_ref, a_buf, b_buf, sem):
+    z = plane(width)
+    blocks = [(lambda d=d: x_ref[:, d], (z ^ d) * width) for d in range(planes)]
+    gate_parts(width, blocks, a_ref, b_ref, (oa_ref, ob_ref), (a_buf, b_buf), sem)
+
+
+def gate_split_kernel(planes, width, near_ref, *refs):
+    far_refs, refs = refs[: planes - 1], refs[planes - 1 :]
+    a_ref, b_ref, oa_ref, ob_ref, a_buf, b_buf, sem = refs
+    z = plane(width)
+    blocks = [(lambda: near_ref[:, z], z * width)]
+    for d in range(1, planes):
+        blocks.append((lambda d=d: far_refs[d - 1][...], (z ^ d) * width))
+    gate_parts(width, blocks, a_ref, b_ref, (oa_ref, ob_ref), (a_buf, b_buf), sem)
 
 
 SPACES = {"v": pltpu.VMEM, "h": pltpu.HBM, "a": pl.ANY}
@@ -339,9 +338,10 @@
     scale = 1.0 / math.sqrt(pair_size * length)
     sizes = (n, channels, tokens)
     tw, fwd, inv = tables(n, tokens)
-    half = n // 2
+    planes = math.gcd(n, PLANES)
+    width = n // planes
     blocks, spectrum = (n, channels, tokens), (n, channels, 2 * tokens)
-    halves, paired, lags = (half, channels, tokens), (half, 2, channels, tokens), (channels, length)
+    one, paired, lags = (width, channels, tokens), (width, planes, channels, tokens), (channels, length)
     flops = 4 * 2 * 2 * tokens * n * channels * tokens
     f32 = jnp.float32
     y = pltpu.VMEM(spectrum, f32)
@@ -352,50 +352,56 @@
     def part(body, *args):
         return lambda *refs: body(*args, *refs)
 
-    def mirror(x):
-        return lax.ppermute(x, "context", [(i, i ^ half) for i in range(n)])
-
-    def within_half(x):
-        members = [[h * half + r for r in range(half)] for h in range(2)]
+    def along_z(xs):
+        return [
+            lax.ppermute(x, "context", [(i, i ^ (d * width)) for i in range(n)])
+            for d, x in enumerate(xs, 1)
+        ]
+
+    def within_plane(x):
+        members = [[z * width + q for q in range(width)] for z in range(planes)]
         return lax.all_to_all(x, "context", 0, 0, axis_index_groups=members, tiled=True)
 
     query, key, value, cot = (
         x.reshape(blocks) for x in (query_input, key_input, value_input, cotangent)
     )
     bufs = [pltpu.VMEM(blocks, f32)] * 2
-    send = kernel_call(part(send_kernel, half), "v", [("v", halves)], [])
+    send = kernel_call(part(send_kernel, planes, width), "v", [("v", one)] * (planes - 1), [])
     merge = kernel_call(
-        part(merge_kernel, half), "aaa", [("h", paired)], [semaphores(2, PARTS)]
-    )
-
-    keep_p, send_p = kernel_call(
-        part(product_split_kernel, n), "hh", [("v", halves)] * 2, [*bufs, semaphores(2, PARTS)]
+        part(merge_kernel, planes, width), "a" * (planes + 1), [("h", paired)],
+        [semaphores(planes, PARTS)],
+    )
+
+    keep_p, *send_p = kernel_call(
+        part(product_split_kernel, planes, n), "hh", [("v", one)] * planes,
+        [*bufs, semaphores(2, PARTS)],
     )(key, value)
-    got_p = mirror(send_p)
+    got_p = along_z(send_p)
     (conv_grad,) = kernel_call(
-        part(product_kernel, n), "hha", [("h", paired)],
+        part(product_kernel, planes, n), "hha", [("h", paired)],
         [*bufs, pltpu.VMEM(paired, f32), semaphores(3, PARTS)],
     )(cot, query, keep_p)
-    near_g = within_half(conv_grad)
-    (send_g,) = send(near_g)
-    far_g = mirror(send_g)
+    near_g = within_plane(conv_grad)
+    send_g = send(near_g)
+    far_g = along_z(send_g)
     (filt,) = kernel_call(
         part(filter_kernel, *sizes), "vvv", [("v", spectrum)], [y], flops
     )(filters, tw, fwd)
-    product_ch = within_half(*merge(keep_p, got_p, send_g))
-    keep_c, send_c, prod_spec = kernel_call(
-        part(conv_kernel, *sizes), "vvvvva", [("v", halves)] * 2 + [("v", spectrum)],
-        [pltpu.VMEM(blocks, f32), y, semaphores(PARTS)], 2 * flops,
-    )(product_ch, tw, fwd, inv, filt, send_g)
-    got_c = mirror(send_c)
+    product_ch = within_plane(*merge(keep_p, *got_p, send_g[0]))
+    keep_c, *send_c, prod_spec = kernel_call(
+        part(conv_kernel, planes, *sizes), "vvvvva", [("v", one)] * planes + [("v", spectrum)],
+        [pltpu.VMEM(blocks, f32), y], 2 * flops,
+    )(product_ch, tw, fwd, inv, filt, send_g[0])
+    got_c = along_z(send_c)
     back_ch, grad_spec = kernel_call(
-        part(back_kernel, *sizes), "vvvvvva", [("h", paired), ("v", spectrum)],
+        part(back_kernel, planes, *sizes), "v" * (planes + 4) + "a",
+        [("h", paired), ("v", spectrum)],
         [pltpu.VMEM(paired, f32), y, semaphores(PARTS)], 2 * flops,
-    )(near_g, far_g, tw, fwd, inv, filt, keep_c)
-    near_b = within_half(back_ch)
-    (send_b,) = send(near_b)
-    far_b = mirror(send_b)
-    conv_tok = within_half(*merge(keep_c, got_c, send_b))
+    )(near_g, *far_g, tw, fwd, inv, filt, keep_c)
+    near_b = within_plane(back_ch)
+    send_b = send(near_b)
+    far_b = along_z(send_b)
+    conv_tok = within_plane(*merge(keep_c, *got_c, send_b[0]))
     (own,) = kernel_call(
         part(filter_grad_kernel, scale, *sizes), "vvvv", [("v", lags)], [y], flops
     )(tw, inv, prod_spec, grad_spec)
@@ -403,13 +409,13 @@
         grad_filter = own + lax.ppermute(own, "dp", [(0, 1), (1, 0)])
     else:
         grad_filter = lax.psum(own, "dp")
-    gate_scratch = [*bufs, semaphores(2, 2, PARTS)]
+    gate_scratch = [*bufs, semaphores(2, planes)]
     gated, grad_query = kernel_call(
-        part(gate_kernel, n), "vvv", [("h", blocks)] * 2, gate_scratch
+        part(gate_kernel, planes, width), "vvv", [("h", blocks)] * 2, gate_scratch
     )(conv_tok, query, cot)
     grad_key, grad_value = kernel_call(
-        part(gate_split_kernel, n), "vvvv", [("h", blocks)] * 2, gate_scratch
-    )(near_b, far_b, value, key)
+        part(gate_split_kernel, planes, width), "v" * (planes + 2), [("h", blocks)] * 2, gate_scratch
+    )(near_b, *far_b, value, key)
     shape = query_input.shape
     return (
         gated.reshape(shape),

time: 153 us -> 142 us (0.928)
  the two profiles are of different devices: /device:TPU:0 before, /device:TPU:10 now
where the time goes in v4:
time: 142 us
  waiting for transfers between devices  69.5 us (49%)
  starting transfers between devices  33.3 us (23%)
  Pallas kernels  27.9 us (20%)
  local copies, waits for them, and re-layouts  7.67 us (5%)
  other arithmetic  2.31 us (2%)
    ppermute x12, waiting for transfers between devices, along_z(): lax.ppermute(x, 'context', [(i, i ^ d * width) for i in range(n)])  52.8 us
    pallas_call x12, Pallas kernels, run(): pl.pallas_call(body, in_specs=[pl.BlockSpec(memory_space=SPACES[space]) f...  27.9 us
    all_to_all x4, starting transfers between devices, within_plane(): lax.all_to_all(x, 'context', 0, 0, axis_index_groups=members, tiled=True)  17.3 us
    all_to_all x4, waiting for transfers between devices, within_plane(): lax.all_to_all(x, 'context', 0, 0, axis_index_groups=members, tiled=True)  16.8 us
    ppermute x12, starting transfers between devices, along_z(): lax.ppermute(x, 'context', [(i, i ^ d * width) for i in range(n)])  15.9 us
    unnamed x32, local copies, waits for them, and re-layouts  7.67 us
  transfers between devices with their start and end apart: 17, of which 10 were waited for; matrix products, arithmetic and copies ran while one was open for 2% of the time, Pallas kernels for 10%

profile of v4, /device:TPU:10, one launch (start us, length us, event | category | flops | bytes accessed | tf_op | source)
XLA Modules:
  0.0 141.5 jit_solution(8165889875026454126)
XLA Ops:
  2.3 2.6 %shard_map.120 = f32[4,4,128,128]{3,2,1,0:T(8,128)} custom-call(f32[16,128,128]{2,1,0:T(8,128)} %bitcast.8, f32[16,128,128]{2,1,0:T(8,128)} %bitcast.10, f32[4,128,128]{2,1,0:T(8,128)S(1)} %get-tuple-element.26.refs_2_.refs_0_), custom_call_target="tpu_custom_call" | custom-call | bytes 3407872 | tf_op jit(solution)/shard_map/pallas_call | solution.py:300
  4.9 4.3 %all-to-all-start = ((f32[4,4,128,128]{3,2,1,0:T(8,128)}), f32[4,4,128,128]{3,2,1,0:T(8,128)S(1)}, u32[]{:S(2)}, u32[]{:S(2)}) async-start(f32[4,4,128,128]{3,2,1,0:T(8,128)} %shard_map.120), calls=%async_computation | async-start | bytes 2097152 | tf_op jit(solution)/shard_map/all_to_all | solution.py:363
  9.6 2.6 %collective-permute-start.1 = (f32[4,128,128]{2,1,0:T(8,128)S(1)}, f32[4,128,128]{2,1,0:T(8,128)S(1)}, u32[]{:S(2)}, u32[]{:S(2)}) collective-permute-start(f32[4,128,128]{2,1,0:T(8,128)S(1)} %get-tuple-element.28), channel_id=1, source_target_pairs={{0,8},{1,9},{2,10},{3,11},{4,12},{5,13},{6,14},{7,15},{8,0},{9,1},... | collective-permute-start | bytes 786440 | tf_op jit(solution)/shard_map/ppermute | solution.py:357
  12.7 9.6 %all-to-all-done.refs_0_ = f32[4,4,128,128]{3,2,1,0:T(8,128)S(1)} async-done(((f32[4,4,128,128]{3,2,1,0:T(8,128)}), f32[4,4,128,128]{3,2,1,0:T(8,128)S(1)}, u32[]{:S(2)}, u32[]{:S(2)}) %all-to-all-start) | async-done | bytes 1048608 | tf_op jit(solution)/shard_map/all_to_all | solution.py:363
  23.2 7.0 %collective-permute-done.1.refs_2_ = f32[4,128,128]{2,1,0:T(8,128)S(1)} collective-permute-done((f32[4,128,128]{2,1,0:T(8,128)S(1)}, f32[4,128,128]{2,1,0:T(8,128)S(1)}, u32[]{:S(2)}, u32[]{:S(2)}) %collective-permute-start.1) | collective-permute-done | bytes 262176 | tf_op jit(solution)/shard_map/ppermute | solution.py:357
  30.2 4.6 %collective-permute-done.2.refs_3_ = f32[4,128,128]{2,1,0:T(8,128)S(1)} collective-permute-done((f32[4,128,128]{2,1,0:T(8,128)S(1)}, f32[4,128,128]{2,1,0:T(8,128)S(1)}, u32[]{:S(2)}, u32[]{:S(2)}) %collective-permute-start.2) | collective-permute-done | bytes 262176 | tf_op jit(solution)/shard_map/ppermute | solution.py:357
  35.9 4.6 %all-to-all-start.1 = ((f32[4,4,128,128]{3,2,1,0:T(8,128)}), f32[4,4,128,128]{3,2,1,0:T(8,128)}, u32[]{:S(2)}, u32[]{:S(2)}) async-start(f32[4,4,128,128]{3,2,1,0:T(8,128)} %shard_map.122), calls=%async_computation.1 | async-start | bytes 2097152 | tf_op jit(solution)/shard_map/all_to_all | solution.py:363
  42.1 2.8 %collective-permute-start.6 = (f32[4,128,128]{2,1,0:T(8,128)}, f32[4,128,128]{2,1,0:T(8,128)}, u32[]{:S(2)}, u32[]{:S(2)}) collective-permute-start(f32[4,128,128]{2,1,0:T(8,128)} %get-tuple-element.30.refs_4_.refs_5_), channel_id=1, source_target_pairs={{0,4},{1,5},{2,6},{3,7},{4,0},{5,1},{6,2},{7,3},{8,12},{9,13},{10,... | collective-permute-start | bytes 786440 | tf_op jit(solution)/shard_map/ppermute | solution.py:357
  48.8 3.8 %all-to-all-done.1.refs_0_ = f32[4,4,128,128]{3,2,1,0:T(8,128)} async-done(((f32[4,4,128,128]{3,2,1,0:T(8,128)}), f32[4,4,128,128]{3,2,1,0:T(8,128)}, u32[]{:S(2)}, u32[]{:S(2)}) %all-to-all-start.1) | async-done | bytes 1048608 | tf_op jit(solution)/shard_map/all_to_all | solution.py:363
  53.6 6.0 %shard_map.124 = (f32[4,128,128]{2,1,0:T(8,128)S(1)}, f32[4,128,128]{2,1,0:T(8,128)}, f32[4,128,128]{2,1,0:T(8,128)}, f32[4,128,128]{2,1,0:T(8,128)}, f32[16,128,256]{2,1,0:T(8,128)S(1)}) custom-call(f32[4,4,128,128]{3,2,1,0:T(8,128)} %all-to-all-done.1.refs_0_, f32[2,16,8,128]{3,2,1,0:T(8,128)S(1)} %copy-done.8, bf16[2,256,256]{2,1,0:T(8,128)(2,1)S(1)} %copy-done.6, ...), custom_call_target="tpu_custom_call" | custom-call | flops 1073741824 | bytes 7733248 | tf_op jit(solution)/shard_map/pallas_call | solution.py:300
  59.6 4.4 %collective-permute-done.8.refs_3_ = f32[4,128,128]{2,1,0:T(8,128)} collective-permute-done((f32[4,128,128]{2,1,0:T(8,128)}, f32[4,128,128]{2,1,0:T(8,128)}, u32[]{:S(2)}, u32[]{:S(2)}) %collective-permute-start.8) | collective-permute-done | bytes 262176 | tf_op jit(solution)/shard_map/ppermute | solution.py:357
  64.0 6.0 %shard_map.125 = (f32[4,4,128,128]{3,2,1,0:T(8,128)}, f32[16,128,256]{2,1,0:T(8,128)S(1)}) custom-call(f32[4,4,128,128]{3,2,1,0:T(8,128)S(1)} %all-to-all-done.refs_0_, f32[4,128,128]{2,1,0:T(8,128)} %collective-permute-done.6.refs_1_, f32[4,128,128]{2,1,0:T(8,128)} %collective-permute-done.7.refs_2_, f32[4,128,128]{2,1,0:T(8,128)} %collective-permute-done.8.refs_3_, ...), custom_call_target="tpu_custom_call" | custom-call | flops 1073741824 | bytes 8519680 | tf_op jit(solution)/shard_map/pallas_call | solution.py:300
  71.4 4.2 %all-to-all-start.2 = ((f32[4,4,128,128]{3,2,1,0:T(8,128)}), f32[4,4,128,128]{3,2,1,0:T(8,128)S(1)}, u32[]{:S(2)}, u32[]{:S(2)}) async-start(f32[4,4,128,128]{3,2,1,0:T(8,128)} %get-tuple-element.37), calls=%async_computation.2 | async-start | bytes 2097152 | tf_op jit(solution)/shard_map/all_to_all | solution.py:363
  78.8 1.9 %shard_map.130 = f32[128,2048]{1,0:T(8,128)S(1)} custom-call(f32[2,16,8,128]{3,2,1,0:T(8,128)S(1)} %copy-done.8, bf16[2,256,256]{2,1,0:T(8,128)(2,1)S(1)} %copy-done.4, f32[16,128,256]{2,1,0:T(8,128)S(1)} %copy-done.10, f32[16,128,256]{2,1,0:T(8,128)S(1)} %copy-done.12), custom_call_target="tpu_custom_call" | custom-call | flops 536870912 | bytes 5898240 | tf_op jit(solution)/shard_map/pallas_call | solution.py:300
  80.8 2.0 %collective-permute-start.4 = (f32[4,128,128]{2,1,0:T(8,128)}, f32[4,128,128]{2,1,0:T(8,128)S(1)}, u32[]{:S(2)}, u32[]{:S(2)}) collective-permute-start(f32[4,128,128]{2,1,0:T(8,128)} %get-tuple-element.33), channel_id=1, source_target_pairs={{0,8},{1,9},{2,10},{3,11},{4,12},{5,13},{6,14},{7,15},{8,0},{9,1},... | collective-permute-start | bytes 786440 | tf_op jit(solution)/shard_map/ppermute | solution.py:357
  84.4 3.3 %all-to-all-done.2.refs_0_ = f32[4,4,128,128]{3,2,1,0:T(8,128)S(1)} async-done(((f32[4,4,128,128]{3,2,1,0:T(8,128)}), f32[4,4,128,128]{3,2,1,0:T(8,128)S(1)}, u32[]{:S(2)}, u32[]{:S(2)}) %all-to-all-start.2) | async-done | bytes 1048608 | tf_op jit(solution)/shard_map/all_to_all | solution.py:363
  88.5 11.8 %collective-permute-done.4.refs_2_ = f32[4,128,128]{2,1,0:T(8,128)S(1)} collective-permute-done((f32[4,128,128]{2,1,0:T(8,128)}, f32[4,128,128]{2,1,0:T(8,128)S(1)}, u32[]{:S(2)}, u32[]{:S(2)}) %collective-permute-start.4) | collective-permute-done | bytes 262176 | tf_op jit(solution)/shard_map/ppermute | solution.py:357
  100.4 7.1 %collective-permute-done.5.refs_3_ = f32[4,128,128]{2,1,0:T(8,128)S(1)} collective-permute-done((f32[4,128,128]{2,1,0:T(8,128)}, f32[4,128,128]{2,1,0:T(8,128)S(1)}, u32[]{:S(2)}, u32[]{:S(2)}) %collective-permute-start.5) | collective-permute-done | bytes 262176 | tf_op jit(solution)/shard_map/ppermute | solution.py:357
  108.6 4.3 %all-to-all-start.3 = ((f32[4,4,128,128]{3,2,1,0:T(8,128)}), f32[4,4,128,128]{3,2,1,0:T(8,128)}, u32[]{:S(2)}, u32[]{:S(2)}) async-start(f32[4,4,128,128]{3,2,1,0:T(8,128)} %shard_map.127), calls=%async_computation.3 | async-start | bytes 2097152 | tf_op jit(solution)/shard_map/all_to_all | solution.py:363
  113.9 3.5 %collective-permute-start.9 = (f32[4,128,128]{2,1,0:T(8,128)S(1)}, f32[4,128,128]{2,1,0:T(8,128)S(1)}, u32[]{:S(2)}, u32[]{:S(2)}) collective-permute-start(f32[4,128,128]{2,1,0:T(8,128)S(1)} %get-tuple-element.38.refs_4_), channel_id=1, source_target_pairs={{0,4},{1,5},{2,6},{3,7},{4,0},{5,1},{6,2},{7,3},{8,12},{9,13},{10,... | collective-permute-start | bytes 786440 | tf_op jit(solution)/shard_map/ppermute | solution.py:357
  117.3 2.3 %add.3 = f32[128,2048]{1,0:T(8,128)} add(f32[128,2048]{1,0:T(8,128)S(1)} %shard_map.130, f32[128,2048]{1,0:T(8,128)} %collective-permute-done.12) | non-fusion elementwise | flops 262144 | bytes 3145728 | tf_op jit(solution)/shard_map/add | solution.py:409
  119.7 11.5 %collective-permute-done.10.refs_2_ = f32[4,128,128]{2,1,0:T(8,128)S(1)} collective-permute-done((f32[4,128,128]{2,1,0:T(8,128)}, f32[4,128,128]{2,1,0:T(8,128)S(1)}, u32[]{:S(2)}, u32[]{:S(2)}) %collective-permute-start.10) | collective-permute-done | bytes 262176 | tf_op jit(solution)/shard_map/ppermute | solution.py:357
  131.2 6.2 %collective-permute-done.11.refs_3_ = f32[4,128,128]{2,1,0:T(8,128)S(1)} collective-permute-done((f32[4,128,128]{2,1,0:T(8,128)}, f32[4,128,128]{2,1,0:T(8,128)S(1)}, u32[]{:S(2)}, u32[]{:S(2)}) %collective-permute-start.11) | collective-permute-done | bytes 262176 | tf_op jit(solution)/shard_map/ppermute | solution.py:357
  138.9 2.6 %shard_map.128 = (f32[16,128,128]{2,1,0:T(8,128)}, f32[16,128,128]{2,1,0:T(8,128)}) custom-call(f32[4,4,128,128]{3,2,1,0:T(8,128)} %all-to-all-done.3.refs_0_, f32[16,128,128]{2,1,0:T(8,128)S(1)} %bitcast.11, f32[16,128,128]{2,1,0:T(8,128)S(1)} %bitcast.9), custom_call_target="tpu_custom_call" | custom-call | bytes 5242880 | tf_op jit(solution)/shard_map/pallas_call | solution.py:300
  (55 shorter events, 21.6 us)
Async XLA Ops:
  4.9 17.3 %all-to-all-start = ((f32[4,4,128,128]{3,2,1,0:T(8,128)}), f32[4,4,128,128]{3,2,1,0:T(8,128)S(1)}, u32[]{:S(2)}, u32[]{:S(2)}) async-start(f32[4,4,128,128]{3,2,1,0:T(8,128)} %shard_map.120), calls=%async_computation | async-start | bytes 2097152 | tf_op jit(solution)/shard_map/all_to_all | solution.py:363
  9.2 14.0 %collective-permute-start = (f32[4,128,128]{2,1,0:T(8,128)S(1)}, f32[4,128,128]{2,1,0:T(8,128)S(1)}, u32[]{:S(2)}, u32[]{:S(2)}) collective-permute-start(f32[4,128,128]{2,1,0:T(8,128)S(1)} %get-tuple-element.27), channel_id=1, source_target_pairs={{0,4},{1,5},{2,6},{3,7},{4,0},{5,1},{6,2},{7,3},{8,12},{9,13},{10,... | collective-permute-start | bytes 786440 | tf_op jit(solution)/shard_map/ppermute | solution.py:357
  9.6 20.6 %collective-permute-start.1 = (f32[4,128,128]{2,1,0:T(8,128)S(1)}, f32[4,128,128]{2,1,0:T(8,128)S(1)}, u32[]{:S(2)}, u32[]{:S(2)}) collective-permute-start(f32[4,128,128]{2,1,0:T(8,128)S(1)} %get-tuple-element.28), channel_id=1, source_target_pairs={{0,8},{1,9},{2,10},{3,11},{4,12},{5,13},{6,14},{7,15},{8,0},{9,1},... | collective-permute-start | bytes 786440 | tf_op jit(solution)/shard_map/ppermute | solution.py:357
  12.2 22.6 %collective-permute-start.2 = (f32[4,128,128]{2,1,0:T(8,128)S(1)}, f32[4,128,128]{2,1,0:T(8,128)S(1)}, u32[]{:S(2)}, u32[]{:S(2)}) collective-permute-start(f32[4,128,128]{2,1,0:T(8,128)S(1)} %get-tuple-element.29), channel_id=1, source_target_pairs={{0,12},{1,13},{2,14},{3,15},{4,8},{5,9},{6,10},{7,11},{8,4},{9,5},... | collective-permute-start | bytes 786440 | tf_op jit(solution)/shard_map/ppermute | solution.py:357
  35.9 16.7 %all-to-all-start.1 = ((f32[4,4,128,128]{3,2,1,0:T(8,128)}), f32[4,4,128,128]{3,2,1,0:T(8,128)}, u32[]{:S(2)}, u32[]{:S(2)}) async-start(f32[4,4,128,128]{3,2,1,0:T(8,128)} %shard_map.122), calls=%async_computation.1 | async-start | bytes 2097152 | tf_op jit(solution)/shard_map/all_to_all | solution.py:363
  40.5 12.1 %copy-start.4 = (bf16[2,256,256]{2,1,0:T(8,128)(2,1)S(1)}, bf16[2,256,256]{2,1,0:T(8,128)(2,1)}, u32[]{:S(2)}) copy-start(bf16[2,256,256]{2,1,0:T(8,128)(2,1)} %constant.7.clone.refs_3_.refs_6_.refs_1_) | copy-start | bytes 786436
  40.5 19.1 %collective-permute-start.7 = (f32[4,128,128]{2,1,0:T(8,128)}, f32[4,128,128]{2,1,0:T(8,128)}, u32[]{:S(2)}, u32[]{:S(2)}) collective-permute-start(f32[4,128,128]{2,1,0:T(8,128)} %get-tuple-element.35), channel_id=1, source_target_pairs={{0,8},{1,9},{2,10},{3,11},{4,12},{5,13},{6,14},{7,15},{8,0},{9,1},... | collective-permute-start | bytes 786440 | tf_op jit(solution)/shard_map/ppermute | solution.py:357
  40.5 23.5 %collective-permute-start.8 = (f32[4,128,128]{2,1,0:T(8,128)}, f32[4,128,128]{2,1,0:T(8,128)}, u32[]{:S(2)}, u32[]{:S(2)}) collective-permute-start(f32[4,128,128]{2,1,0:T(8,128)} %get-tuple-element.36), channel_id=1, source_target_pairs={{0,12},{1,13},{2,14},{3,15},{4,8},{5,9},{6,10},{7,11},{8,4},{9,5},... | collective-permute-start | bytes 786440 | tf_op jit(solution)/shard_map/ppermute | solution.py:357
  42.1 22.0 %collective-permute-start.6 = (f32[4,128,128]{2,1,0:T(8,128)}, f32[4,128,128]{2,1,0:T(8,128)}, u32[]{:S(2)}, u32[]{:S(2)}) collective-permute-start(f32[4,128,128]{2,1,0:T(8,128)} %get-tuple-element.30.refs_4_.refs_5_), channel_id=1, source_target_pairs={{0,4},{1,5},{2,6},{3,7},{4,0},{5,1},{6,2},{7,3},{8,12},{9,13},{10,... | collective-permute-start | bytes 786440 | tf_op jit(solution)/shard_map/ppermute | solution.py:357
  59.6 10.5 %copy-start.14 = (f32[4,128,128]{2,1,0:T(8,128)}, f32[4,128,128]{2,1,0:T(8,128)S(1)}, u32[]{:S(2)}) copy-start(f32[4,128,128]{2,1,0:T(8,128)S(1)} %get-tuple-element.31.refs_8_.refs_0_) | copy-start | bytes 786436
  71.4 16.3 %all-to-all-start.2 = ((f32[4,4,128,128]{3,2,1,0:T(8,128)}), f32[4,4,128,128]{3,2,1,0:T(8,128)S(1)}, u32[]{:S(2)}, u32[]{:S(2)}) async-start(f32[4,4,128,128]{3,2,1,0:T(8,128)} %get-tuple-element.37), calls=%async_computation.2 | async-start | bytes 2097152 | tf_op jit(solution)/shard_map/all_to_all | solution.py:363
  75.6 12.9 %collective-permute-start.3 = (f32[4,128,128]{2,1,0:T(8,128)}, f32[4,128,128]{2,1,0:T(8,128)S(1)}, u32[]{:S(2)}, u32[]{:S(2)}) collective-permute-start(f32[4,128,128]{2,1,0:T(8,128)} %get-tuple-element.32), channel_id=1, source_target_pairs={{0,4},{1,5},{2,6},{3,7},{4,0},{5,1},{6,2},{7,3},{8,12},{9,13},{10,... | collective-permute-start | bytes 786440 | tf_op jit(solution)/shard_map/ppermute | solution.py:357
  78.8 28.7 %copy-start.15 = (f32[4,128,128]{2,1,0:T(8,128)S(1)}, f32[4,128,128]{2,1,0:T(8,128)}, u32[]{:S(2)}) copy-start(f32[4,128,128]{2,1,0:T(8,128)} %copy-done.14) | copy-start | bytes 786436
  80.7 36.6 %collective-permute-start.12 = (f32[128,2048]{1,0:T(8,128)S(1)}, f32[128,2048]{1,0:T(8,128)}, u32[]{:S(2)}, u32[]{:S(2)}) collective-permute-start(f32[128,2048]{1,0:T(8,128)S(1)} %shard_map.130), channel_id=1, source_target_pairs={{0,16},{16,0},{1,17},{17,1},{2,18},{18,2},{3,19},{19,3},{4,20},{20... | collective-permute-start | bytes 3145736 | tf_op jit(solution)/shard_map/ppermute | solution.py:409
  80.8 19.6 %collective-permute-start.4 = (f32[4,128,128]{2,1,0:T(8,128)}, f32[4,128,128]{2,1,0:T(8,128)S(1)}, u32[]{:S(2)}, u32[]{:S(2)}) collective-permute-start(f32[4,128,128]{2,1,0:T(8,128)} %get-tuple-element.33), channel_id=1, source_target_pairs={{0,8},{1,9},{2,10},{3,11},{4,12},{5,13},{6,14},{7,15},{8,0},{9,1},... | collective-permute-start | bytes 786440 | tf_op jit(solution)/shard_map/ppermute | solution.py:357
  82.8 24.7 %collective-permute-start.5 = (f32[4,128,128]{2,1,0:T(8,128)}, f32[4,128,128]{2,1,0:T(8,128)S(1)}, u32[]{:S(2)}, u32[]{:S(2)}) collective-permute-start(f32[4,128,128]{2,1,0:T(8,128)} %get-tuple-element.34), channel_id=1, source_target_pairs={{0,12},{1,13},{2,14},{3,15},{4,8},{5,9},{6,10},{7,11},{8,4},{9,5},... | collective-permute-start | bytes 786440 | tf_op jit(solution)/shard_map/ppermute | solution.py:357
  108.6 30.3 %all-to-all-start.3 = ((f32[4,4,128,128]{3,2,1,0:T(8,128)}), f32[4,4,128,128]{3,2,1,0:T(8,128)}, u32[]{:S(2)}, u32[]{:S(2)}) async-start(f32[4,4,128,128]{3,2,1,0:T(8,128)} %shard_map.127), calls=%async_computation.3 | async-start | bytes 2097152 | tf_op jit(solution)/shard_map/all_to_all | solution.py:363
  112.9 24.6 %copy-start.2 = (f32[1,2048,128]{2,1,0:T(8,128)S(1)}, f32[1,2048,128]{2,1,0:T(8,128)}, u32[]{:S(2)}) copy-start(f32[1,2048,128]{2,1,0:T(8,128)} %param.9) | copy-start | bytes 3145732
  112.9 24.6 %copy-start.3 = (f32[1,2048,128]{2,1,0:T(8,128)S(1)}, f32[1,2048,128]{2,1,0:T(8,128)}, u32[]{:S(2)}) copy-start(f32[1,2048,128]{2,1,0:T(8,128)} %param.10) | copy-start | bytes 3145732
  112.9 18.3 %collective-permute-start.10 = (f32[4,128,128]{2,1,0:T(8,128)}, f32[4,128,128]{2,1,0:T(8,128)S(1)}, u32[]{:S(2)}, u32[]{:S(2)}) collective-permute-start(f32[4,128,128]{2,1,0:T(8,128)} %get-tuple-element.41), channel_id=1, source_target_pairs={{0,8},{1,9},{2,10},{3,11},{4,12},{5,13},{6,14},{7,15},{8,0},{9,1},... | collective-permute-start | bytes 786440 | tf_op jit(solution)/shard_map/ppermute | solution.py:357
  113.0 24.5 %collective-permute-start.11 = (f32[4,128,128]{2,1,0:T(8,128)}, f32[4,128,128]{2,1,0:T(8,128)S(1)}, u32[]{:S(2)}, u32[]{:S(2)}) collective-permute-start(f32[4,128,128]{2,1,0:T(8,128)} %get-tuple-element.42), channel_id=1, source_target_pairs={{0,12},{1,13},{2,14},{3,15},{4,8},{5,9},{6,10},{7,11},{8,4},{9,5},... | collective-permute-start | bytes 786440 | tf_op jit(solution)/shard_map/ppermute | solution.py:357
  113.9 23.6 %collective-permute-start.9 = (f32[4,128,128]{2,1,0:T(8,128)S(1)}, f32[4,128,128]{2,1,0:T(8,128)S(1)}, u32[]{:S(2)}, u32[]{:S(2)}) collective-permute-start(f32[4,128,128]{2,1,0:T(8,128)S(1)} %get-tuple-element.38.refs_4_), channel_id=1, source_target_pairs={{0,4},{1,5},{2,6},{3,7},{4,0},{5,1},{6,2},{7,3},{8,12},{9,13},{10,... | collective-permute-start | bytes 786440 | tf_op jit(solution)/shard_map/ppermute | solution.py:357
  119.6 19.2 %copy-start = (f32[1,2048,128]{2,1,0:T(8,128)S(1)}, f32[1,2048,128]{2,1,0:T(8,128)}, u32[]{:S(2)}) copy-start(f32[1,2048,128]{2,1,0:T(8,128)} %param.12) | copy-start | bytes 3145732
  119.6 19.2 %copy-start.1 = (f32[1,2048,128]{2,1,0:T(8,128)S(1)}, f32[1,2048,128]{2,1,0:T(8,128)}, u32[]{:S(2)}) copy-start(f32[1,2048,128]{2,1,0:T(8,128)} %param.8) | copy-start | bytes 3145732
  (9 other events, 38.6 us)

commit v5 on v4

v5 whole, which is shorter than its diff:
```python
import math

import jax
import jax.numpy as jnp
import ml_dtypes
import numpy as np
from jax import lax
from jax.experimental import pallas as pl
from jax.experimental.pallas import tpu as pltpu
from jax.sharding import PartitionSpec as P

ROWS = 8
PLANES = 4
PARTS = 4
VMEM_BYTES = 24 * 1024 * 1024


def twist(value, turn):
    re, im = value
    turn = turn % 1.0
    if turn == 0.0:
        return re, im
    if turn == 0.25:
        return im, -re
    if turn == 0.5:
        return -re, -im
    if turn == 0.75:
        return -im, re
    if turn in (0.125, 0.375, 0.625, 0.875):
        half = math.sqrt(0.5)
        a, b = (re + im) * half, (im - re) * half
        return twist((a, b), turn - 0.125)
    c, s = math.cos(2 * math.pi * turn), math.sin(2 * math.pi * turn)
    return re * c + im * s, im * c - re * s


def dft(values, sign):
    n = len(values)
    if n == 1:
        return values
    even, odd = dft(values[0::2], sign), dft(values[1::2], sign)
    out = [None] * n
    for k in range(n // 2):
        a, b = even[k], twist(odd[k], sign * k / n)
        out[k] = (a[0] + b[0], a[1] + b[1])
        out[k + n // 2] = (a[0] - b[0], a[1] - b[1])
    return out


def split(x):
    hi = x.astype(jnp.bfloat16)
    lo = (x - hi.astype(jnp.float32)).astype(jnp.bfloat16)
    return hi, lo


def times_table(x, table_ref):
    hi, lo = split(x)
    out = jnp.dot(hi, table_ref[0], preferred_element_type=jnp.float32)
    out += jnp.dot(lo, table_ref[0], preferred_element_type=jnp.float32)
    out += jnp.dot(hi, table_ref[1], preferred_element_type=jnp.float32)
    return out


def outer_forward(read, n, part, tokens, tw_ref, y_ref):
    @pl.loop(part.start // ROWS, (part.start + part.size) // ROWS)
    def _(r):
        rows = pl.ds(pl.multiple_of(r * ROWS, ROWS), ROWS)
        values = []
        for n1 in range(n):
            x = read(n1, rows)
            turn = 2 * math.pi * n1 / (4 * n)
            if n1 == 0:
                values.append((x, jnp.zeros_like(x)))
            else:
                values.append((x * math.cos(turn), x * -math.sin(turn)))
        for m, (re, im) in enumerate(dft(values, 1)):
            c, s = tw_ref[0, m], tw_ref[1, m]
            y_ref[m, rows, :tokens] = re * c + im * s
            y_ref[m, rows, tokens:] = im * c - re * s


def outer_inverse(write, n, part, tokens, tw_ref, y_ref):
    @pl.loop(part.start // ROWS, (part.start + part.size) // ROWS)
    def _(r):
        rows = pl.ds(pl.multiple_of(r * ROWS, ROWS), ROWS)
        values = []
        for m in range(n):
            re, im = y_ref[m, rows, :tokens], y_ref[m, rows, tokens:]
            c, s = tw_ref[0, m], tw_ref[1, m]
            values.append((re * c - im * s, im * c + re * s))
        for n1, (re, im) in enumerate(dft(values, -1)):
            turn = 2 * math.pi * n1 / (4 * n)
            if n1 == 0:
                write(n1, rows, re)
            else:
                write(n1, rows, re * math.cos(turn) - im * math.sin(turn))


def flat(x):
    return x.reshape(x.shape[0] * x.shape[1], x.shape[2])


def start_all(copies):
    for copy in copies:
        copy.start()


def wait_all(copies):
    for copy in copies:
        copy.wait()


def parts_of(size, least=1):
    step = max(least, size // PARTS)
    return [pl.ds(k, step) for k in range(0, size, step)]


def plane(width):
    return lax.axis_index("context") // width


def copies_of(pairs, sem):
    return [pltpu.make_async_copy(src, dst, sem.at[i]) for i, (src, dst) in enumerate(pairs)]


def filter_kernel(
    first, n, channels, tokens, f_ref, tw_ref, fwd_ref, out_ref, f_buf, y_ref, own_ref, sem
):
    rows = parts_of(channels, ROWS)
    loads = copies_of(
        [(f_ref.at[pl.ds(first + part.start, part.size)], f_buf.at[part]) for part in rows],
        sem.at[0],
    )
    start_all(loads)
    for part, load in zip(rows, loads):
        load.wait()
        outer_forward(
            lambda n1, r: f_buf[r, n1 * tokens : (n1 + 1) * tokens], n, part, tokens, tw_ref, y_ref
        )
    stores = copies_of([(own_ref.at[ms], out_ref.at[ms]) for ms in parts_of(n)], sem.at[1])
    for ms, store in zip(parts_of(n), stores):
        own_ref[ms] = times_table(flat(y_ref[ms]), fwd_ref).reshape(ms.size, channels, 2 * tokens)
        store.start()
    wait_all(stores)


def transform(
    sign, n, channels, tokens, sources, targets, tw_ref, fwd_ref, inv_ref, spec_refs, own_ref,
    buf_ref, spec_buf, own_buf, y_ref, sem,
):
    rows = parts_of(channels, ROWS)
    loads = [copies_of(sources(part), sem.at[0, i]) for i, part in enumerate(rows)]
    for load in loads:
        start_all(load)
    half = channels // 2
    spec_loads = [
        copies_of(
            [
                (ref.at[ms], spec_buf.at[ms, pl.ds(j * half, half)])
                for j, ref in enumerate(spec_refs)
            ],
            sem.at[1, i],
        )
        for i, ms in enumerate(parts_of(n))
    ]
    for load in spec_loads:
        start_all(load)
    for part, load in zip(rows, loads):
        wait_all(load)
        outer_forward(lambda n1, r: buf_ref[n1, r], n, part, tokens, tw_ref, y_ref)
    own_stores = copies_of([(own_buf.at[ms], own_ref.at[ms]) for ms in parts_of(n)], sem.at[2, 0])
    for ms, load, store in zip(parts_of(n), spec_loads, own_stores):
        own = times_table(flat(y_ref[ms]), fwd_ref)
        own_buf[ms] = own.reshape(ms.size, channels, 2 * tokens)
        store.start()
        wait_all(load)
        spec = flat(spec_buf[ms])
        re, im = own[:, :tokens], own[:, tokens:]
        s_re, s_im = spec[:, :tokens], spec[:, tokens:] * sign
        both = jnp.concatenate([re * s_re - im * s_im, re * s_im + im * s_re], axis=1)
        y_ref[ms] = times_table(both, inv_ref).reshape(ms.size, channels, 2 * tokens)

    def write(n1, r, value):
        buf_ref[n1, r] = value

    stores = [copies_of(targets(part), sem.at[3, i]) for i, part in enumerate(rows)]
    for part, store in zip(rows, stores):
        outer_inverse(write, n, part, tokens, tw_ref, y_ref)
        start_all(store)
    for store in (*stores, own_stores):
        wait_all(store)


def conv_kernel(planes, n, channels, tokens, x_ref, *refs):
    tables, spec_refs, refs = refs[:3], refs[3:5], refs[5:]
    out_refs, (own_ref, buf_ref, *scratch) = refs[:planes], refs[planes:]
    width = n // planes
    z = plane(width)

    def block(d, part):
        return buf_ref.at[pl.ds((z ^ d) * width, width), part]

    def sources(part):
        return [(x_ref.at[:, d, part], block(d, part)) for d in range(planes)]

    def targets(part):
        return [(block(d, part), out_refs[d].at[:, part]) for d in range(planes)]

    transform(
        1.0, n, channels, tokens, sources, targets, *tables, spec_refs, own_ref, buf_ref, *scratch
    )


def back_kernel(planes, n, channels, tokens, near_ref, *refs):
    far_refs, refs = refs[: planes - 1], refs[planes - 1 :]
    tables, spec_refs, refs = refs[:3], refs[3:5], refs[5:]
    after_ref, out_ref, own_ref, buf_ref, *scratch = refs
    width = n // planes
    z = plane(width)

    def block(z, part):
        return buf_ref.at[pl.ds(z * width, width), part]

    def sources(part):
        near = [(near_ref.at[:, z, part], block(z, part))]
        return near + [
            (ref.at[:, part], block(z ^ d, part)) for d, ref in enumerate(far_refs, 1)
        ]

    def targets(part):
        return [(block(z, part), out_ref.at[:, z, part]) for z in range(planes)]

    transform(
        -1.0, n, channels, tokens, sources, targets, *tables, spec_refs, own_ref, buf_ref, *scratch
    )


def filter_grad_kernel(
    scale, n, channels, tokens, tw_ref, inv_ref, p_ref, g_ref, out_ref, p_buf, g_buf, y_ref, sem
):
    loads = [
        copies_of([(p_ref.at[ms], p_buf.at[ms]), (g_ref.at[ms], g_buf.at[ms])], sem.at[i])
        for i, ms in enumerate(parts_of(n))
    ]
    for load in loads:
        start_all(load)
    for ms, load in zip(parts_of(n), loads):
        wait_all(load)
        p, g = flat(p_buf[ms]), flat(g_buf[ms])
        p_re, p_im = p[:, :tokens], p[:, tokens:]
        re, im = g[:, :tokens], g[:, tokens:]
        both = jnp.concatenate([re * p_re + im * p_im, im * p_re - re * p_im], axis=1)
        y_ref[ms] = times_table(both, inv_ref).reshape(ms.size, channels, 2 * tokens)

    def write(n1, r, value):
        out_ref[r, n1 * tokens : (n1 + 1) * tokens] = value * scale

    outer_inverse(write, n, pl.ds(0, channels), tokens, tw_ref, y_ref)


def load_pairs(n, a_ref, b_ref, a_buf, b_buf, sem):
    loads = [
        copies_of([(a_ref.at[part], a_buf.at[part]), (b_ref.at[part], b_buf.at[part])], sem.at[i])
        for i, part in enumerate(parts_of(n))
    ]
    for load in loads:
        start_all(load)
    return loads


def product_split_kernel(planes, n, a_ref, b_ref, *refs):
    out_refs, (a_buf, b_buf, sem) = refs[:planes], refs[planes:]
    width = n // planes
    z = plane(width)
    for load in load_pairs(n, a_ref, b_ref, a_buf, b_buf, sem):
        wait_all(load)
    for d in range(planes):
        for q in range(width):
            out_refs[d][q] = a_buf[(z ^ d) * width + q] * b_buf[(z ^ d) * width + q]


def product_kernel(planes, n, a_ref, b_ref, after_ref, out_ref, a_buf, b_buf, buf_ref, sem):
    width = n // planes
    parts = [pl.ds(z * width, width) for z in range(planes)]
    loads = [
        copies_of([(a_ref.at[part], a_buf.at[part]), (b_ref.at[part], b_buf.at[part])], sem.at[z])
        for z, part in enumerate(parts)
    ]
    for load in loads:
        start_all(load)
    stores = copies_of([(buf_ref.at[z], out_ref.at[:, z]) for z in range(planes)], sem.at[planes])
    for z, part in enumerate(parts):
        wait_all(loads[z])
        buf_ref[z] = a_buf[part] * b_buf[part]
        stores[z].start()
    wait_all(stores)


def send_kernel(planes, width, x_ref, *refs):
    out_refs, (buf_ref, sem) = refs[: planes - 1], refs[planes - 1 :]
    z = plane(width)
    parts = parts_of(width)
    loads = [
        copies_of([(x_ref.at[part, z ^ d], buf_ref.at[d, part]) for part in parts], sem.at[d])
        for d in range(1, planes)
    ]
    for load in loads:
        start_all(load)
    stores = copies_of([(buf_ref.at[d + 1], ref) for d, ref in enumerate(out_refs)], sem.at[0])
    for load, store in zip(loads, stores):
        wait_all(load)
        store.start()
    wait_all(stores)


def merge_kernel(planes, width, *refs):
    in_refs, (after_ref, out_ref, buf_ref, sem) = refs[:planes], refs[planes:]
    parts = parts_of(width)
    loads = [
        copies_of([(ref.at[part], buf_ref.at[part, d]) for d, ref in enumerate(in_refs)], sem.at[i])
        for i, part in enumerate(parts)
    ]
    for load in loads:
        start_all(load)
    stores = copies_of([(buf_ref.at[part], out_ref.at[part]) for part in parts], sem.at[len(parts)])
    for load, store in zip(loads, stores):
        wait_all(load)
        store.start()
    wait_all(stores)


def gate_parts(width, blocks, a_ref, b_ref, outs, a_buf, b_buf, sem):
    stores = []
    for d, (read, first) in enumerate(blocks):
        part = pl.ds(first, width)
        x = read()
        a_buf[part] = x * a_ref[part]
        b_buf[part] = x * b_ref[part]
        pairs = [(buf.at[part], out.at[part]) for buf, out in zip((a_buf, b_buf), outs)]
        stores.extend(copies_of(pairs, sem.at[d]))
        start_all(stores[-2:])
    wait_all(stores)


def gate_kernel(
    planes, width, x_ref, a_ref, b_ref, oa_ref, ob_ref, x_buf, a_in, b_in, a_buf, b_buf, sem
):
    z = plane(width)
    loads = []
    for d in range(planes):
        part = pl.ds((z ^ d) * width, width)
        pairs = [
            (x_ref.at[:, d], x_buf.at[d]),
            (a_ref.at[part], a_in.at[part]),
            (b_ref.at[part], b_in.at[part]),
        ]
        loads.append(copies_of(pairs, sem.at[planes + d]))
        start_all(loads[-1])

    def read(d):
        wait_all(loads[d])
        return x_buf[d]

    blocks = [(lambda d=d: read(d), (z ^ d) * width) for d in range(planes)]
    gate_parts(width, blocks, a_in, b_in, (oa_ref, ob_ref), a_buf, b_buf, sem)


def gate_split_kernel(planes, width, *refs):
    far_refs, refs = refs[: planes - 1], refs[planes - 1 :]
    a_ref, b_ref, near_ref, oa_ref, ob_ref, x_buf, a_buf, b_buf, sem = refs
    z = plane(width)
    load = pltpu.make_async_copy(near_ref.at[:, z], x_buf, sem.at[planes, 0])
    load.start()

    def read():
        load.wait()
        return x_buf[...]

    blocks = [(lambda d=d: far_refs[d - 1][...], (z ^ d) * width) for d in range(1, planes)]
    blocks.append((read, z * width))
    gate_parts(width, blocks, a_ref, b_ref, (oa_ref, ob_ref), a_buf, b_buf, sem)


SPACES = {"v": pltpu.VMEM, "u": pltpu.VMEM, "h": pltpu.HBM, "a": pl.ANY}


def kernel_call(body, ins, outs, scratch, flops=0):
    shapes = [
        jax.ShapeDtypeStruct(shape, jnp.float32) if space == "u" else SPACES[space](shape, jnp.float32)
        for space, shape in outs
    ]

    def run(*args):
        args = [
            pltpu.with_memory_space_constraint(x, pltpu.HBM) if space == "h" else x
            for space, x in zip(ins, args, strict=True)
        ]
        size = sum(math.prod(x.shape) for x in (*args, *shapes))
        return pl.pallas_call(
            body,
            in_specs=[pl.BlockSpec(memory_space=SPACES[space]) for space in ins],
            out_specs=[pl.BlockSpec(memory_space=SPACES[space]) for space, _ in outs],
            out_shape=shapes,
            scratch_shapes=scratch,
            compiler_params=pltpu.CompilerParams(vmem_limit_bytes=VMEM_BYTES),
            cost_estimate=pl.CostEstimate(flops=flops, bytes_accessed=4 * size, transcendentals=0),
        )(*args)

    return run


def tables(n, tokens):
    length = n * tokens
    m = np.arange(n)[:, None] + 0.25
    angle = 2 * np.pi * m * np.arange(tokens)[None, :] / length
    tw = np.stack([np.cos(angle), np.sin(angle)])[:, :, None, :]
    tw = np.broadcast_to(tw, (2, n, ROWS, tokens)).astype(np.float32)
    k = np.arange(tokens)
    inner = 2 * np.pi * ((k[:, None] * k[None, :]) % tokens) / tokens
    c, s = np.cos(inner), np.sin(inner)

    def pair(table):
        hi = table.astype(ml_dtypes.bfloat16)
        lo = (table - hi.astype(np.float64)).astype(ml_dtypes.bfloat16)
        return jnp.asarray(np.stack([hi, lo]))

    fwd = pair(np.block([[c, -s], [s, c]]))
    inv = pair(np.block([[c, s], [-s, c]]) / length)
    return jnp.asarray(tw), fwd, inv


def on_device(query_input, key_input, value_input, filters, cotangent):
    n = lax.axis_size("context")
    pair_size = lax.axis_size("dp")
    _, width, tokens = query_input.shape
    channels, length = filters.shape
    scale = 1.0 / math.sqrt(pair_size * length)
    sizes = (n, channels, tokens)
    tw, fwd, inv = tables(n, tokens)
    planes = math.gcd(n, PLANES)
    width = n // planes
    blocks, spectrum = (n, channels, tokens), (n, channels, 2 * tokens)
    one, paired, lags = (width, channels, tokens), (width, planes, channels, tokens), (channels, length)
    flops = 4 * 2 * 2 * tokens * n * channels * tokens
    f32 = jnp.float32
    y = pltpu.VMEM(spectrum, f32)

    def semaphores(*shape):
        return pltpu.SemaphoreType.DMA(shape)

    def part(body, *args):
        return lambda *refs: body(*args, *refs)

    def along_z(xs):
        return [
            lax.ppermute(x, "context", [(i, i ^ (d * width)) for i in range(n)])
            for d, x in enumerate(xs, 1)
        ]

    def within_plane(x):
        members = [[z * width + q for q in range(width)] for z in range(planes)]
        return lax.all_to_all(x, "context", 0, 0, axis_index_groups=members, tiled=True)

    query, key, value, cot = (
        x.reshape(blocks) for x in (query_input, key_input, value_input, cotangent)
    )
    rows, paired_buf = pltpu.VMEM(blocks, f32), pltpu.VMEM(paired, f32)
    by_plane = pltpu.VMEM((planes, *one), f32)
    outs = [("h", one)] * (planes - 1)
    send = kernel_call(
        part(send_kernel, planes, width), "h", outs, [by_plane, semaphores(planes, planes + PARTS)]
    )
    merge = kernel_call(
        part(merge_kernel, planes, width), "h" * planes + "a", [("h", paired)],
        [paired_buf, semaphores(PARTS + 1, planes + PARTS)],
    )
    half_sizes = (n, channels // 2, tokens)
    half_spectrum = (n, channels // 2, 2 * tokens)

    def transform_filters(first):
        return kernel_call(
            part(filter_kernel, first, *half_sizes), "hvv", [("h", half_spectrum)],
            [
                pltpu.VMEM((channels // 2, length), f32),
                *[pltpu.VMEM(half_spectrum, f32)] * 2,
                semaphores(2, PARTS),
            ],
            flops // 2,
        )(filters, tw, fwd)[0]

    transform_scratch = [rows, y, y, y, semaphores(4, PARTS, max(PARTS, planes))]
    always = lax.axis_index("context") < n

    def grouped(body, *args):
        shapes = jax.eval_shape(body, *args)

        def never(*args):
            return jax.tree.map(lambda x: jnp.zeros(x.shape, x.dtype), shapes)

        return lax.cond(always, body, never, *args)

    keep_p, *send_p = kernel_call(
        part(product_split_kernel, planes, n), "hh", [("u", one)] * planes,
        [rows, rows, semaphores(PARTS, 2)],
    )(key, value)
    got_p = along_z(send_p)

    def first(cot, query, keep_p):
        (conv_grad,) = kernel_call(
            part(product_kernel, planes, n), "hha", [("h", paired)],
            [rows, rows, by_plane, semaphores(planes + 1, planes)],
        )(cot, query, keep_p)
        near_g = within_plane(conv_grad)
        return near_g, send(near_g), transform_filters(0)

    near_g, send_g, filt_a = grouped(first, cot, query, keep_p)
    far_g = along_z(send_g)

    def second(keep_p, got_p, send_g, filt_a):
        product_ch = within_plane(*merge(keep_p, *got_p, send_g))
        filt = (filt_a, transform_filters(channels // 2))
        *outs, prod_spec = kernel_call(
            part(conv_kernel, planes, *sizes), "hvvvhh",
            [("h", one)] * planes + [("h", spectrum)], transform_scratch, 2 * flops,
        )(product_ch, tw, fwd, inv, *filt)
        return outs, prod_spec, filt

    (keep_c, *send_c), prod_spec, filt = grouped(second, keep_p, got_p, send_g[0], filt_a)
    got_c = along_z(send_c)

    def third(near_g, far_g, filt, keep_c, prod_spec):
        back_ch, grad_spec = kernel_call(
            part(back_kernel, planes, *sizes), "h" * planes + "vvvhha",
            [("h", paired), ("h", spectrum)], transform_scratch, 2 * flops,
        )(near_g, *far_g, tw, fwd, inv, *filt, keep_c)
        near_b = within_plane(back_ch)
        (own,) = kernel_call(
            part(filter_grad_kernel, scale, *sizes), "vvhh", [("u", lags)],
            [y, y, y, semaphores(PARTS, 2)], flops,
        )(tw, inv, prod_spec, grad_spec)
        return near_b, send(near_b), own

    near_b, send_b, own = grouped(third, near_g, far_g, filt, keep_c, prod_spec)
    far_b = along_z(send_b)

    def fourth(keep_c, got_c, send_b, query, cot, own):
        conv_tok = within_plane(*merge(keep_c, *got_c, send_b))
        if pair_size == 2:
            grad_filter = own + lax.ppermute(own, "dp", [(0, 1), (1, 0)])
        else:
            grad_filter = lax.psum(own, "dp")
        gated, grad_query = kernel_call(
            part(gate_kernel, planes, width), "hhh", [("h", blocks)] * 2,
            [by_plane, *[rows] * 4, semaphores(2 * planes, 3)],
        )(conv_tok, query, cot)
        return gated, grad_query, grad_filter

    gated, grad_query, grad_filter = grouped(
        fourth, keep_c, got_c, send_b[0], query, cot, own
    )
    grad_key, grad_value = kernel_call(
        part(gate_split_kernel, planes, width), "v" * (planes + 1) + "h", [("h", blocks)] * 2,
        [pltpu.VMEM(one, f32), rows, rows, semaphores(planes + 1, 2)],
    )(*far_b, value, key, near_b)
    shape = query_input.shape
    return (
        gated.reshape(shape),
        grad_query.reshape(shape),
        grad_key.reshape(shape),
        grad_value.reshape(shape),
        grad_filter,
    )


def solution(mesh):
    in_specs = (
        P("dp", None, "context"),
        P("dp", None, "context"),
        P("dp", None, "context"),
        P("context", None),
        P("dp", None, "context"),
    )
    out_specs = (
        P("dp", None, "context"),
        P("dp", None, "context"),
        P("dp", None, "context"),
        P("dp", None, "context"),
        P("context", None),
    )
    return jax.shard_map(
        on_device, mesh=mesh, in_specs=in_specs, out_specs=out_specs, check_vma=False
    )
```

time: 142 us -> 126 us (0.89)
  the two profiles are of different devices: /device:TPU:10 before, /device:TPU:0 now
where the time goes in v5:
time: 126 us
  Pallas kernels  41.2 us (33%)
  starting transfers between devices  31.1 us (25%)
  waiting for transfers between devices  28.4 us (23%)
  blocking collectives  18.7 us (15%)
  local copies, waits for them, and re-layouts  5.01 us (4%)
    pallas_call x13, Pallas kernels, run(): pl.pallas_call(body, in_specs=[pl.BlockSpec(memory_space=SPACES[space]) f...  41.2 us
    all_to_all x3, waiting for transfers between devices, within_plane(): lax.all_to_all(x, 'context', 0, 0, axis_index_groups=members, tiled=True)  28.4 us
    ppermute x12, starting transfers between devices, along_z(): lax.ppermute(x, 'context', [(i, i ^ d * width) for i in range(n)])  19 us
    all_to_all x1, blocking collectives, within_plane(): lax.all_to_all(x, 'context', 0, 0, axis_index_groups=members, tiled=True)  18.7 us
    all_to_all x3, starting transfers between devices, within_plane(): lax.all_to_all(x, 'context', 0, 0, axis_index_groups=members, tiled=True)  12.1 us
    cond x20, local copies, waits for them, and re-layouts  3.3 us
  transfers between devices with their start and end apart: 16, of which 3 were waited for; matrix products, arithmetic and copies ran while one was open for 0% of the time, Pallas kernels for 30%

profile of v5, /device:TPU:0, one launch (start us, length us, event | category | flops | bytes accessed | tf_op | source)
XLA Modules:
  0.0 125.5 jit_solution(1845650604452585648)
XLA Ops:
  2.5 3.1 %collective-permute-start.4 = (f32[4,128,128]{2,1,0:T(8,128)S(1)}, f32[4,128,128]{2,1,0:T(8,128)S(1)}, u32[]{:S(2)}, u32[]{:S(2)}) collective-permute-start(f32[4,128,128]{2,1,0:T(8,128)S(1)} %get-tuple-element.158), channel_id=1, source_target_pairs={{0,4},{1,5},{2,6},{3,7},{4,0},{5,1},{6,2},{7,3},{8,12},{9,13},{10,... | collective-permute-start | bytes 786440 | tf_op jit(solution)/shard_map/ppermute | solution.py:456
  5.6 2.6 %collective-permute-start.5 = (f32[4,128,128]{2,1,0:T(8,128)S(1)}, f32[4,128,128]{2,1,0:T(8,128)S(1)}, u32[]{:S(2)}, u32[]{:S(2)}) collective-permute-start(f32[4,128,128]{2,1,0:T(8,128)S(1)} %get-tuple-element.159), channel_id=1, source_target_pairs={{0,8},{1,9},{2,10},{3,11},{4,12},{5,13},{6,14},{7,15},{8,0},{9,1},... | collective-permute-start | bytes 786440 | tf_op jit(solution)/shard_map/ppermute | solution.py:456
  8.2 22.3 %conditional.4 = (f32[4,4,128,128]{3,2,1,0:T(8,128)}, f32[4,128,128]{2,1,0:T(8,128)}, f32[4,128,128]{2,1,0:T(8,128)}, f32[4,128,128]{2,1,0:T(8,128)}, f32[16,64,256]{2,1,0:T(8,128)}) conditional(s32[]{:T(128)} %convert_element_type.2, () %tuple.46, (f32[16,128,128]{2,1,0:T(8,128)}, f32[16,128,128]{2,1,0:T(8,128)}, f32[4,128,128]{2,1,0:T(8,128)S(1)}, ...), branch_computations={%region_0.0_spmd, %region_1.0_spmd} | conditional | flops 268435456 | bytes 11141192 | solution.py:500
  8.2 2.4 %branch_1_fun.11 = f32[4,4,128,128]{3,2,1,0:T(8,128)} custom-call(f32[16,128,128]{2,1,0:T(8,128)} %get-tuple-element.72.refs_0_, f32[16,128,128]{2,1,0:T(8,128)} %get-tuple-element.73.refs_1_, f32[4,128,128]{2,1,0:T(8,128)S(1)} %get-tuple-element.74.refs_2_), custom_call_target="tpu_custom_call" | custom-call | bytes 3407872 | tf_op jit(solution)/shard_map/cond/branch_1_fun/pallas_call | solution.py:399
  10.6 4.3 %all-to-all-start = ((f32[4,4,128,128]{3,2,1,0:T(8,128)}), f32[4,4,128,128]{3,2,1,0:T(8,128)}, u32[]{:S(2)}, u32[]{:S(2)}) async-start(f32[4,4,128,128]{3,2,1,0:T(8,128)} %branch_1_fun.11), calls=%async_computation | async-start | bytes 2097152 | tf_op jit(solution)/shard_map/cond/branch_1_fun/all_to_all | solution.py:462
  14.9 2.5 %branch_1_fun.13 = f32[16,64,256]{2,1,0:T(8,128)} custom-call(f32[128,2048]{1,0:T(8,128)S(1)} %get-tuple-element.78.refs_0_, f32[2,16,8,128]{3,2,1,0:T(8,128)S(1)} %get-tuple-element.79.refs_1_, bf16[2,256,256]{2,1,0:T(8,128)(2,1)S(1)} %get-tuple-element.80.refs_2_), custom_call_target="tpu_custom_call" | custom-call | flops 268435456 | bytes 2752512 | tf_op jit(solution)/shard_map/cond/branch_1_fun/pallas_call | solution.py:399
  17.5 10.9 %all-to-all-done.refs_0_ = f32[4,4,128,128]{3,2,1,0:T(8,128)} async-done(((f32[4,4,128,128]{3,2,1,0:T(8,128)}), f32[4,4,128,128]{3,2,1,0:T(8,128)}, u32[]{:S(2)}, u32[]{:S(2)}) %all-to-all-start) | async-done | bytes 1048608 | tf_op jit(solution)/shard_map/cond/branch_1_fun/all_to_all | solution.py:462
  31.2 3.5 %collective-permute-start.2 = (f32[4,128,128]{2,1,0:T(8,128)}, f32[4,128,128]{2,1,0:T(8,128)}, u32[]{:S(2)}, u32[]{:S(2)}) collective-permute-start(f32[4,128,128]{2,1,0:T(8,128)} %get-tuple-element.156), channel_id=1, source_target_pairs={{0,8},{1,9},{2,10},{3,11},{4,12},{5,13},{6,14},{7,15},{8,0},{9,1},... | collective-permute-start | bytes 786440 | tf_op jit(solution)/shard_map/ppermute | solution.py:456
  35.0 26.7 %conditional.5 = (f32[4,128,128]{2,1,0:T(8,128)}, f32[4,128,128]{2,1,0:T(8,128)}, f32[4,128,128]{2,1,0:T(8,128)}, f32[4,128,128]{2,1,0:T(8,128)}, f32[16,128,256...) conditional(s32[]{:T(128)} %convert_element_type.2, () %tuple.48, (f32[4,128,128]{2,1,0:T(8,128)S(1)}, ...), branch_computations={%region_2.0_spmd, %region_3.0_spmd} | conditional | flops 1342177280 | bytes 28311808 | solution.py:500
  38.2 3.5 %all-to-all-start.1 = ((f32[4,4,128,128]{3,2,1,0:T(8,128)}), f32[4,4,128,128]{3,2,1,0:T(8,128)S(1)}, u32[]{:S(2)}, u32[]{:S(2)}) async-start(f32[4,4,128,128]{3,2,1,0:T(8,128)} %branch_1_fun.14), calls=%async_computation.1 | async-start | bytes 2097152 | tf_op jit(solution)/shard_map/cond/branch_1_fun/all_to_all | solution.py:462
  41.8 2.7 %branch_1_fun.15.refs_5_ = f32[16,64,256]{2,1,0:T(8,128)} custom-call(f32[128,2048]{1,0:T(8,128)} %copy-done.5, f32[2,16,8,128]{3,2,1,0:T(8,128)S(1)} %get-tuple-element.86.refs_1_, bf16[2,256,256]{2,1,0:T(8,128)(2,1)S(1)} %get-tuple-element.87.refs_2_), custom_call_target="tpu_custom_call" | custom-call | flops 268435456 | bytes 2752512 | tf_op jit(solution)/shard_map/cond/branch_1_fun/pallas_call | solution.py:399
  44.5 9.5 %all-to-all-done.1.refs_0_ = f32[4,4,128,128]{3,2,1,0:T(8,128)S(1)} async-done(((f32[4,4,128,128]{3,2,1,0:T(8,128)}), f32[4,4,128,128]{3,2,1,0:T(8,128)S(1)}, u32[]{:S(2)}, u32[]{:S(2)}) %all-to-all-start.1) | async-done | bytes 1048608 | tf_op jit(solution)/shard_map/cond/branch_1_fun/all_to_all | solution.py:462
  55.0 6.7 %branch_1_fun.16 = (f32[4,128,128]{2,1,0:T(8,128)}, f32[4,128,128]{2,1,0:T(8,128)}, f32[4,128,128]{2,1,0:T(8,128)}, f32[4,128,128]{2,1,0:T(8,128)}, f32[16,128,256]{2,1,0:T(8,128)}) custom-call(f32[4,4,128,128]{3,2,1,0:T(8,128)} %copy-done.9, f32[2,16,8,128]{3,2,1,0:T(8,128)S(1)} %get-tuple-element.86.refs_1_, ...), custom_call_target="tpu_custom_call" | custom-call | flops 1073741824 | bytes 7471104 | tf_op jit(solution)/shard_map/cond/branch_1_fun/pallas_call | solution.py:399
  62.3 3.5 %collective-permute-start.8 = (f32[4,128,128]{2,1,0:T(8,128)}, f32[4,128,128]{2,1,0:T(8,128)S(1)}, u32[]{:S(2)}, u32[]{:S(2)}) collective-permute-start(f32[4,128,128]{2,1,0:T(8,128)} %get-tuple-element.168), channel_id=1, source_target_pairs={{0,8},{1,9},{2,10},{3,11},{4,12},{5,13},{6,14},{7,15},{8,0},{9,1},... | collective-permute-start | bytes 786440 | tf_op jit(solution)/shard_map/ppermute | solution.py:456
  66.1 26.2 %conditional.6 = (f32[4,4,128,128]{3,2,1,0:T(8,128)}, f32[4,128,128]{2,1,0:T(8,128)}, f32[4,128,128]{2,1,0:T(8,128)}, f32[4,128,128]{2,1,0:T(8,128)}, f32[128,2048]{1,0:T(8,128)S(1)}) conditional(s32[]{:T(128)} %convert_element_type.2, () %tuple.45, (f32[4,4,128,128]{3,2,1,0:T(8,128)}, f32[4,128,128]{2,1,0:T(8,128)}, f32[4,128,128]{2,1,0:T(8,128)}, ...), branch_computations={%region_4.0_spmd, %region_5.0_spmd} | conditional | flops 1610612736 | bytes 20447332 | solution.py:500
  66.8 6.7 %branch_1_fun.17 = (f32[4,4,128,128]{3,2,1,0:T(8,128)}, f32[16,128,256]{2,1,0:T(8,128)}) custom-call(f32[4,4,128,128]{3,2,1,0:T(8,128)} %get-tuple-element.96.refs_0_, f32[4,128,128]{2,1,0:T(8,128)} %get-tuple-element.97.refs_1_, f32[4,128,128]{2,1,0:T(8,128)} %get-tuple-element.98.refs_2_, f32[4,128,128]{2,1,0:T(8,128)} %copy-done.12, ...), custom_call_target="tpu_custom_call" | custom-call | flops 1073741824 | bytes 8519680 | tf_op jit(solution)/shard_map/cond/branch_1_fun/pallas_call | solution.py:399
  73.5 4.3 %all-to-all-start.2 = ((f32[4,4,128,128]{3,2,1,0:T(8,128)}), f32[4,4,128,128]{3,2,1,0:T(8,128)}, u32[]{:S(2)}, u32[]{:S(2)}) async-start(f32[4,4,128,128]{3,2,1,0:T(8,128)} %get-tuple-element.106), calls=%async_computation.2 | async-start | bytes 2097152 | tf_op jit(solution)/shard_map/cond/branch_1_fun/all_to_all | solution.py:462
  77.8 4.4 %branch_1_fun.19 = f32[128,2048]{1,0:T(8,128)S(1)} custom-call(f32[2,16,8,128]{3,2,1,0:T(8,128)S(1)} %get-tuple-element.100.refs_4_.refs_0_, bf16[2,256,256]{2,1,0:T(8,128)(2,1)S(1)} %get-tuple-element.102.refs_6_.refs_1_, f32[16,128,256]{2,1,0:T(8,128)} %get-tuple-element.110.refs_2_, f32[16,128,256]{2,1,0:T(8,128)} %get-tuple-element.111.refs_3_), custom_call_target="tpu_custom_call" | custom-call | flops 536870912 | bytes 5898240 | tf_op jit(solution)/shard_map/cond/branch_1_fun/pallas_call | solution.py:399
  82.2 8.0 %all-to-all-done.2.refs_0_ = f32[4,4,128,128]{3,2,1,0:T(8,128)} async-done(((f32[4,4,128,128]{3,2,1,0:T(8,128)}), f32[4,4,128,128]{3,2,1,0:T(8,128)}, u32[]{:S(2)}, u32[]{:S(2)}) %all-to-all-start.2) | async-done | bytes 1048608 | tf_op jit(solution)/shard_map/cond/branch_1_fun/all_to_all | solution.py:462
  93.8 3.5 %collective-permute-start.11 = (f32[4,128,128]{2,1,0:T(8,128)}, f32[4,128,128]{2,1,0:T(8,128)S(1)}, u32[]{:S(2)}, u32[]{:S(2)}) collective-permute-start(f32[4,128,128]{2,1,0:T(8,128)} %get-tuple-element.173), channel_id=1, source_target_pairs={{0,8},{1,9},{2,10},{3,11},{4,12},{5,13},{6,14},{7,15},{8,0},{9,1},... | collective-permute-start | bytes 786440 | tf_op jit(solution)/shard_map/ppermute | solution.py:456
  98.4 24.9 %conditional.7 = (f32[128,2048]{1,0:T(8,128)S(1)}, f32[1,2048,128]{2,1,0:T(8,128)}, f32[1,2048,128]{2,1,0:T(8,128)}) conditional(s32[]{:T(128)} %convert_element_type.2, () %tuple.44, (f32[128,2048]{1,0:T(8,128)}, f32[4,128,128]{2,1,0:T(8,128)}, f32[4,128,128]{2,1,0:T(8,128)S(1)}, f32[4,128,128]{2,1,0:T(8,128)S(1)}, f32[4,128,128]{2,1,0:T(8,128)}, ...), branch_computations={%region_6.0_spmd, %region_7.0_spmd} | conditional | flops 262144 | bytes 23330964 | solution.py:500
  99.2 2.3 %branch_1_fun.20 = f32[4,4,128,128]{3,2,1,0:T(8,128)} custom-call(f32[4,128,128]{2,1,0:T(8,128)} %get-tuple-element.113.refs_0_, f32[4,128,128]{2,1,0:T(8,128)} %copy-done.13, f32[4,128,128]{2,1,0:T(8,128)} %copy-done.15, f32[4,128,128]{2,1,0:T(8,128)} %get-tuple-element.116.refs_3_, f32[4,128,128]{2,1,0:T(8,128)} %get-tuple-element.117.refs_4_), custom_call_target="tpu_custom_call" | custom-call | bytes 2359296 | tf_op jit(solution)/shard_map/cond/branch_1_fun/pallas_call | solution.py:399
  101.6 18.7 %all_to_all.16.refs_0_ = f32[4,4,128,128]{3,2,1,0:T(8,128)} all-to-all(f32[4,4,128,128]{3,2,1,0:T(8,128)} %branch_1_fun.20), channel_id=1, replica_groups={{0,1,2,3},{4,5,6,7},{8,9,10,11},{12,13,14,15},{16,17,18,19},{20,21,22,2..., dimensions={0} | all-to-all | bytes 2097152 | tf_op jit(solution)/shard_map/cond/branch_1_fun/all_to_all | solution.py:462
  120.2 2.9 %branch_1_fun.21 = (f32[16,128,128]{2,1,0:T(8,128)}, f32[16,128,128]{2,1,0:T(8,128)}) custom-call(f32[4,4,128,128]{3,2,1,0:T(8,128)} %all_to_all.16.refs_0_, f32[16,128,128]{2,1,0:T(8,128)} %get-tuple-element.118.refs_1_, f32[16,128,128]{2,1,0:T(8,128)} %get-tuple-element.119.refs_2_), custom_call_target="tpu_custom_call" | custom-call | bytes 5242880 | tf_op jit(solution)/shard_map/cond/branch_1_fun/pallas_call | solution.py:399
  (65 shorter events, 18.4 us)
Async XLA Ops:
  0.6 7.5 %copy-start.7 = (f32[2,16,8,128]{3,2,1,0:T(8,128)S(1)}, f32[2,16,8,128]{3,2,1,0:T(8,128)}, u32[]{:S(2)}) copy-start(f32[2,16,8,128]{3,2,1,0:T(8,128)} %constant.18.clone) | copy-start | bytes 393220
  0.6 7.5 %copy-start.6 = (bf16[2,256,256]{2,1,0:T(8,128)(2,1)S(1)}, bf16[2,256,256]{2,1,0:T(8,128)(2,1)}, u32[]{:S(2)}) copy-start(bf16[2,256,256]{2,1,0:T(8,128)(2,1)} %constant.5.clone) | copy-start | bytes 786436
  0.7 7.5 %copy-start.4 = (f32[128,2048]{1,0:T(8,128)S(1)}, f32[128,2048]{1,0:T(8,128)}, u32[]{:S(2)}) copy-start(f32[128,2048]{1,0:T(8,128)} %param.19) | copy-start | bytes 3145732
  2.5 32.2 %collective-permute-start.4 = (f32[4,128,128]{2,1,0:T(8,128)S(1)}, f32[4,128,128]{2,1,0:T(8,128)S(1)}, u32[]{:S(2)}, u32[]{:S(2)}) collective-permute-start(f32[4,128,128]{2,1,0:T(8,128)S(1)} %get-tuple-element.158), channel_id=1, source_target_pairs={{0,4},{1,5},{2,6},{3,7},{4,0},{5,1},{6,2},{7,3},{8,12},{9,13},{10,... | collective-permute-start | bytes 786440 | tf_op jit(solution)/shard_map/ppermute | solution.py:456
  5.6 29.4 %collective-permute-start.5 = (f32[4,128,128]{2,1,0:T(8,128)S(1)}, f32[4,128,128]{2,1,0:T(8,128)S(1)}, u32[]{:S(2)}, u32[]{:S(2)}) collective-permute-start(f32[4,128,128]{2,1,0:T(8,128)S(1)} %get-tuple-element.159), channel_id=1, source_target_pairs={{0,8},{1,9},{2,10},{3,11},{4,12},{5,13},{6,14},{7,15},{8,0},{9,1},... | collective-permute-start | bytes 786440 | tf_op jit(solution)/shard_map/ppermute | solution.py:456
  8.1 26.8 %collective-permute-start.6 = (f32[4,128,128]{2,1,0:T(8,128)S(1)}, f32[4,128,128]{2,1,0:T(8,128)S(1)}, u32[]{:S(2)}, u32[]{:S(2)}) collective-permute-start(f32[4,128,128]{2,1,0:T(8,128)S(1)} %get-tuple-element.160), channel_id=1, source_target_pairs={{0,12},{1,13},{2,14},{3,15},{4,8},{5,9},{6,10},{7,11},{8,4},{9,5},... | collective-permute-start | bytes 786440 | tf_op jit(solution)/shard_map/ppermute | solution.py:456
  8.2 26.8 %copy-start.8 = (bf16[2,256,256]{2,1,0:T(8,128)(2,1)S(1)}, bf16[2,256,256]{2,1,0:T(8,128)(2,1)}, u32[]{:S(2)}) copy-start(bf16[2,256,256]{2,1,0:T(8,128)(2,1)} %constant.7.clone) | copy-start | bytes 786436
  10.6 17.7 %all-to-all-start = ((f32[4,4,128,128]{3,2,1,0:T(8,128)}), f32[4,4,128,128]{3,2,1,0:T(8,128)}, u32[]{:S(2)}, u32[]{:S(2)}) async-start(f32[4,4,128,128]{3,2,1,0:T(8,128)} %branch_1_fun.11), calls=%async_computation | async-start | bytes 2097152 | tf_op jit(solution)/shard_map/cond/branch_1_fun/all_to_all | solution.py:462
  30.5 35.3 %collective-permute-start.1 = (f32[4,128,128]{2,1,0:T(8,128)}, f32[4,128,128]{2,1,0:T(8,128)}, u32[]{:S(2)}, u32[]{:S(2)}) collective-permute-start(f32[4,128,128]{2,1,0:T(8,128)} %get-tuple-element.155), channel_id=1, source_target_pairs={{0,4},{1,5},{2,6},{3,7},{4,0},{5,1},{6,2},{7,3},{8,12},{9,13},{10,... | collective-permute-start | bytes 786440 | tf_op jit(solution)/shard_map/ppermute | solution.py:456
  31.2 35.0 %collective-permute-start.2 = (f32[4,128,128]{2,1,0:T(8,128)}, f32[4,128,128]{2,1,0:T(8,128)}, u32[]{:S(2)}, u32[]{:S(2)}) collective-permute-start(f32[4,128,128]{2,1,0:T(8,128)} %get-tuple-element.156), channel_id=1, source_target_pairs={{0,8},{1,9},{2,10},{3,11},{4,12},{5,13},{6,14},{7,15},{8,0},{9,1},... | collective-permute-start | bytes 786440 | tf_op jit(solution)/shard_map/ppermute | solution.py:456
  34.7 31.5 %collective-permute-start.3 = (f32[4,128,128]{2,1,0:T(8,128)}, f32[4,128,128]{2,1,0:T(8,128)S(1)}, u32[]{:S(2)}, u32[]{:S(2)}) collective-permute-start(f32[4,128,128]{2,1,0:T(8,128)} %get-tuple-element.157), channel_id=1, source_target_pairs={{0,12},{1,13},{2,14},{3,15},{4,8},{5,9},{6,10},{7,11},{8,4},{9,5},... | collective-permute-start | bytes 786440 | tf_op jit(solution)/shard_map/ppermute | solution.py:456
  35.0 3.2 %copy-start.5 = (f32[128,2048]{1,0:T(8,128)}, f32[128,2048]{1,0:T(8,128)S(1)}, u32[]{:S(2)}) copy-start(f32[128,2048]{1,0:T(8,128)S(1)} %get-tuple-element.90.refs_0_) | copy-start | bytes 3145732 | tf_op jit(solution)/shard_map/cond
  38.2 15.7 %all-to-all-start.1 = ((f32[4,4,128,128]{3,2,1,0:T(8,128)}), f32[4,4,128,128]{3,2,1,0:T(8,128)S(1)}, u32[]{:S(2)}, u32[]{:S(2)}) async-start(f32[4,4,128,128]{3,2,1,0:T(8,128)} %branch_1_fun.14), calls=%async_computation.1 | async-start | bytes 2097152 | tf_op jit(solution)/shard_map/cond/branch_1_fun/all_to_all | solution.py:462
  61.7 35.7 %collective-permute-start.7 = (f32[4,128,128]{2,1,0:T(8,128)}, f32[4,128,128]{2,1,0:T(8,128)S(1)}, u32[]{:S(2)}, u32[]{:S(2)}) collective-permute-start(f32[4,128,128]{2,1,0:T(8,128)} %get-tuple-element.167), channel_id=1, source_target_pairs={{0,4},{1,5},{2,6},{3,7},{4,0},{5,1},{6,2},{7,3},{8,12},{9,13},{10,... | collective-permute-start | bytes 786440 | tf_op jit(solution)/shard_map/ppermute | solution.py:456
  62.3 35.5 %collective-permute-start.8 = (f32[4,128,128]{2,1,0:T(8,128)}, f32[4,128,128]{2,1,0:T(8,128)S(1)}, u32[]{:S(2)}, u32[]{:S(2)}) collective-permute-start(f32[4,128,128]{2,1,0:T(8,128)} %get-tuple-element.168), channel_id=1, source_target_pairs={{0,8},{1,9},{2,10},{3,11},{4,12},{5,13},{6,14},{7,15},{8,0},{9,1},... | collective-permute-start | bytes 786440 | tf_op jit(solution)/shard_map/ppermute | solution.py:456
  65.8 31.9 %collective-permute-start.9 = (f32[4,128,128]{2,1,0:T(8,128)}, f32[4,128,128]{2,1,0:T(8,128)S(1)}, u32[]{:S(2)}, u32[]{:S(2)}) collective-permute-start(f32[4,128,128]{2,1,0:T(8,128)} %get-tuple-element.169), channel_id=1, source_target_pairs={{0,12},{1,13},{2,14},{3,15},{4,8},{5,9},{6,10},{7,11},{8,4},{9,5},... | collective-permute-start | bytes 786440 | tf_op jit(solution)/shard_map/ppermute | solution.py:456
  73.5 16.7 %all-to-all-start.2 = ((f32[4,4,128,128]{3,2,1,0:T(8,128)}), f32[4,4,128,128]{3,2,1,0:T(8,128)}, u32[]{:S(2)}, u32[]{:S(2)}) async-start(f32[4,4,128,128]{3,2,1,0:T(8,128)} %get-tuple-element.106), calls=%async_computation.2 | async-start | bytes 2097152 | tf_op jit(solution)/shard_map/cond/branch_1_fun/all_to_all | solution.py:462
  93.3 30.0 %collective-permute-start.10 = (f32[4,128,128]{2,1,0:T(8,128)}, f32[4,128,128]{2,1,0:T(8,128)S(1)}, u32[]{:S(2)}, u32[]{:S(2)}) collective-permute-start(f32[4,128,128]{2,1,0:T(8,128)} %get-tuple-element.170), channel_id=1, source_target_pairs={{0,4},{1,5},{2,6},{3,7},{4,0},{5,1},{6,2},{7,3},{8,12},{9,13},{10,... | collective-permute-start | bytes 786440 | tf_op jit(solution)/shard_map/ppermute | solution.py:456
  93.8 29.6 %collective-permute-start.11 = (f32[4,128,128]{2,1,0:T(8,128)}, f32[4,128,128]{2,1,0:T(8,128)S(1)}, u32[]{:S(2)}, u32[]{:S(2)}) collective-permute-start(f32[4,128,128]{2,1,0:T(8,128)} %get-tuple-element.173), channel_id=1, source_target_pairs={{0,8},{1,9},{2,10},{3,11},{4,12},{5,13},{6,14},{7,15},{8,0},{9,1},... | collective-permute-start | bytes 786440 | tf_op jit(solution)/shard_map/ppermute | solution.py:456
  97.3 26.0 %collective-permute-start.12 = (f32[4,128,128]{2,1,0:T(8,128)}, f32[4,128,128]{2,1,0:T(8,128)S(1)}, u32[]{:S(2)}, u32[]{:S(2)}) collective-permute-start(f32[4,128,128]{2,1,0:T(8,128)} %get-tuple-element.174), channel_id=1, source_target_pairs={{0,12},{1,13},{2,14},{3,15},{4,8},{5,9},{6,10},{7,11},{8,4},{9,5},... | collective-permute-start | bytes 786440 | tf_op jit(solution)/shard_map/ppermute | solution.py:456
  98.4 24.9 %copy-start = (f32[1,2048,128]{2,1,0:T(8,128)S(1)}, f32[1,2048,128]{2,1,0:T(8,128)}, u32[]{:S(2)}) copy-start(f32[1,2048,128]{2,1,0:T(8,128)} %param.17) | copy-start | bytes 3145732
  98.4 25.0 %copy-start.1 = (f32[1,2048,128]{2,1,0:T(8,128)S(1)}, f32[1,2048,128]{2,1,0:T(8,128)}, u32[]{:S(2)}) copy-start(f32[1,2048,128]{2,1,0:T(8,128)} %param.18) | copy-start | bytes 3145732
  98.5 24.7 %collective-permute-start = (f32[128,2048]{1,0:T(8,128)}, f32[128,2048]{1,0:T(8,128)S(1)}, u32[]{:S(2)}, u32[]{:S(2)}) collective-permute-start(f32[128,2048]{1,0:T(8,128)} %get-tuple-element.112), channel_id=1, source_target_pairs={{0,16},{16,0},{1,17},{17,1},{2,18},{18,2},{3,19},{19,3},{4,20},{20... | collective-permute-start | bytes 3145736 | tf_op jit(solution)/shard_map/cond/branch_1_fun/ppermute | solution.py:549
  120.2 3.0 %copy-start.3 = (f32[128,2048]{1,0:T(8,128)S(1)}, f32[128,2048]{1,0:T(8,128)}, u32[]{:S(2)}) copy-start(f32[128,2048]{1,0:T(8,128)} %get-tuple-element.112) | copy-start | bytes 3145732 | tf_op jit(solution)/shard_map/cond
  (11 other events, 10.3 us)

commit v6 on v5

--- a/solution.py
+++ b/solution.py
@@ -123,77 +123,85 @@
     return [pltpu.make_async_copy(src, dst, sem.at[i]) for i, (src, dst) in enumerate(pairs)]
 
 
+def load_tables(refs, bufs, sem):
+    loads = copies_of(list(zip(refs, bufs)), sem)
+    start_all(loads)
+    return loads
+
+
 def filter_kernel(
-    first, n, channels, tokens, f_ref, tw_ref, fwd_ref, out_ref, f_buf, y_ref, own_ref, sem
+    first, n, channels, tokens, f_ref, tw_ref, fwd_ref, out_ref,
+    tw_buf, fwd_buf, f_buf, y_ref, own_ref, sem,
 ):
     rows = parts_of(channels, ROWS)
+    load_tw, load_fwd = load_tables((tw_ref, fwd_ref), (tw_buf, fwd_buf), sem.at[0])
     loads = copies_of(
         [(f_ref.at[pl.ds(first + part.start, part.size)], f_buf.at[part]) for part in rows],
-        sem.at[0],
+        sem.at[1],
     )
     start_all(loads)
+    load_tw.wait()
     for part, load in zip(rows, loads):
         load.wait()
         outer_forward(
-            lambda n1, r: f_buf[r, n1 * tokens : (n1 + 1) * tokens], n, part, tokens, tw_ref, y_ref
+            lambda n1, r: f_buf[r, n1 * tokens : (n1 + 1) * tokens], n, part, tokens, tw_buf, y_ref
         )
-    stores = copies_of([(own_ref.at[ms], out_ref.at[ms]) for ms in parts_of(n)], sem.at[1])
+    load_fwd.wait()
+    stores = copies_of([(own_ref.at[ms], out_ref.at[ms]) for ms in parts_of(n)], sem.at[2])
     for ms, store in zip(parts_of(n), stores):
-        own_ref[ms] = times_table(flat(y_ref[ms]), fwd_ref).reshape(ms.size, channels, 2 * tokens)
+        own_ref[ms] = times_table(flat(y_ref[ms]), fwd_buf).reshape(ms.size, channels, 2 * tokens)
         store.start()
     wait_all(stores)
 
 
 def transform(
-    sign, n, channels, tokens, sources, targets, tw_ref, fwd_ref, inv_ref, spec_refs, own_ref,
-    buf_ref, spec_buf, own_buf, y_ref, sem,
+    sign, n, channels, tokens, sources, targets, tables, spec_refs, own_ref,
+    tw_buf, fwd_buf, inv_buf, buf_ref, spec_buf, own_buf, y_ref, sem,
 ):
-    rows = parts_of(channels, ROWS)
-    loads = [copies_of(sources(part), sem.at[0, i]) for i, part in enumerate(rows)]
+    rows = parts_of(channels // 2, ROWS)
+    rows = [(j, part, pl.ds(part.start + j * (channels // 2), part.size)) for j in range(2) for part in rows]
+    load_tw, *load_rest = load_tables(tables, (tw_buf, fwd_buf, inv_buf), sem.at[0, 0])
+    loads = [copies_of(sources(part), sem.at[1, i]) for i, (_, _, part) in enumerate(rows)]
     for load in loads:
         start_all(load)
-    half = channels // 2
-    spec_loads = [
-        copies_of(
-            [
-                (ref.at[ms], spec_buf.at[ms, pl.ds(j * half, half)])
-                for j, ref in enumerate(spec_refs)
-            ],
-            sem.at[1, i],
-        )
-        for i, ms in enumerate(parts_of(n))
-    ]
-    for load in spec_loads:
-        start_all(load)
-    for part, load in zip(rows, loads):
-        wait_all(load)
-        outer_forward(lambda n1, r: buf_ref[n1, r], n, part, tokens, tw_ref, y_ref)
-    own_stores = copies_of([(own_buf.at[ms], own_ref.at[ms]) for ms in parts_of(n)], sem.at[2, 0])
-    for ms, load, store in zip(parts_of(n), spec_loads, own_stores):
-        own = times_table(flat(y_ref[ms]), fwd_ref)
-        own_buf[ms] = own.reshape(ms.size, channels, 2 * tokens)
-        store.start()
-        wait_all(load)
-        spec = flat(spec_buf[ms])
+    spec_loads = copies_of(
+        [(spec_refs[j].at[:, own], spec_buf.at[:, part]) for j, own, part in rows], sem.at[0, 1]
+    )
+    start_all(spec_loads)
+    own_stores = copies_of(
+        [(own_buf.at[:, part], own_ref.at[:, part]) for _, _, part in rows], sem.at[0, 2]
+    )
+    stores = [copies_of(targets(part), sem.at[2, i]) for i, (_, _, part) in enumerate(rows)]
+
+    def write(n1, r, value):
+        buf_ref[n1, r] = value
+
+    load_tw.wait()
+    for i, (_, _, part) in enumerate(rows):
+        wait_all(loads[i])
+        outer_forward(lambda n1, r: buf_ref[n1, r], n, part, tokens, tw_buf, y_ref)
+        if i == 0:
+            wait_all(load_rest)
+        spec_loads[i].wait()
+        shape = (n, part.size, 2 * tokens)
+        own = times_table(flat(y_ref[:, part]), fwd_buf)
+        own_buf[:, part] = own.reshape(shape)
+        own_stores[i].start()
+        spec = flat(spec_buf[:, part])
         re, im = own[:, :tokens], own[:, tokens:]
         s_re, s_im = spec[:, :tokens], spec[:, tokens:] * sign
         both = jnp.concatenate([re * s_re - im * s_im, re * s_im + im * s_re], axis=1)
-        y_ref[ms] = times_table(both, inv_ref).reshape(ms.size, channels, 2 * tokens)
-
-    def write(n1, r, value):
-        buf_ref[n1, r] = value
-
-    stores = [copies_of(targets(part), sem.at[3, i]) for i, part in enumerate(rows)]
-    for part, store in zip(rows, stores):
-        outer_inverse(write, n, part, tokens, tw_ref, y_ref)
-        start_all(store)
+        y_ref[:, part] = times_table(both, inv_buf).reshape(shape)
+        outer_inverse(write, n, part, tokens, tw_buf, y_ref)
+        start_all(stores[i])
     for store in (*stores, own_stores):
         wait_all(store)
 
 
 def conv_kernel(planes, n, channels, tokens, x_ref, *refs):
     tables, spec_refs, refs = refs[:3], refs[3:5], refs[5:]
-    out_refs, (own_ref, buf_ref, *scratch) = refs[:planes], refs[planes:]
+    out_refs, (own_ref, *scratch) = refs[:planes], refs[planes:]
+    buf_ref = scratch[3]
     width = n // planes
     z = plane(width)
 
@@ -207,14 +215,15 @@
         return [(block(d, part), out_refs[d].at[:, part]) for d in range(planes)]
 
     transform(
-        1.0, n, channels, tokens, sources, targets, *tables, spec_refs, own_ref, buf_ref, *scratch
+        1.0, n, channels, tokens, sources, targets, tables, spec_refs, own_ref, *scratch
     )
 
 
 def back_kernel(planes, n, channels, tokens, near_ref, *refs):
     far_refs, refs = refs[: planes - 1], refs[planes - 1 :]
     tables, spec_refs, refs = refs[:3], refs[3:5], refs[5:]
-    after_ref, out_ref, own_ref, buf_ref, *scratch = refs
+    after_ref, out_ref, own_ref, *scratch = refs
+    buf_ref = scratch[3]
     width = n // planes
     z = plane(width)
 
@@ -231,31 +240,38 @@
         return [(block(z, part), out_ref.at[:, z, part]) for z in range(planes)]
 
     transform(
-        -1.0, n, channels, tokens, sources, targets, *tables, spec_refs, own_ref, buf_ref, *scratch
+        -1.0, n, channels, tokens, sources, targets, tables, spec_refs, own_ref, *scratch
     )
 
 
 def filter_grad_kernel(
-    scale, n, channels, tokens, tw_ref, inv_ref, p_ref, g_ref, out_ref, p_buf, g_buf, y_ref, sem
+    scale, n, channels, tokens, tw_ref, inv_ref, p_ref, g_ref, out_ref,
+    tw_buf, inv_buf, p_buf, g_buf, y_ref, sem,
 ):
+    tables = load_tables((tw_ref, inv_ref), (tw_buf, inv_buf), sem.at[PARTS])
     loads = [
         copies_of([(p_ref.at[ms], p_buf.at[ms]), (g_ref.at[ms], g_buf.at[ms])], sem.at[i])
         for i, ms in enumerate(parts_of(n))
     ]
     for load in loads:
         start_all(load)
+    wait_all(tables)
     for ms, load in zip(parts_of(n), loads):
         wait_all(load)
         p, g = flat(p_buf[ms]), flat(g_buf[ms])
         p_re, p_im = p[:, :tokens], p[:, tokens:]
         re, im = g[:, :tokens], g[:, tokens:]
         both = jnp.concatenate([re * p_re + im * p_im, im * p_re - re * p_im], axis=1)
-        y_ref[ms] = times_table(both, inv_ref).reshape(ms.size, channels, 2 * tokens)
+        y_ref[ms] = times_table(both, inv_buf).reshape(ms.size, channels, 2 * tokens)
 
     def write(n1, r, value):
         out_ref[r, n1 * tokens : (n1 + 1) * tokens] = value * scale
 
-    outer_inverse(write, n, pl.ds(0, channels), tokens, tw_ref, y_ref)
+    outer_inverse(write, n, pl.ds(0, channels), tokens, tw_buf, y_ref)
+
+
+def add_kernel(a_ref, b_ref, out_ref):
+    out_ref[...] = a_ref[...] + b_ref[...]
 
 
 def load_pairs(n, a_ref, b_ref, a_buf, b_buf, sem):
@@ -367,7 +383,7 @@
 
 def gate_split_kernel(planes, width, *refs):
     far_refs, refs = refs[: planes - 1], refs[planes - 1 :]
-    a_ref, b_ref, near_ref, oa_ref, ob_ref, x_buf, a_buf, b_buf, sem = refs
+    a_ref, b_ref, near_ref, after_ref, oa_ref, ob_ref, x_buf, a_buf, b_buf, sem = refs
     z = plane(width)
     load = pltpu.make_async_copy(near_ref.at[:, z], x_buf, sem.at[planes, 0])
     load.start()
@@ -468,27 +484,31 @@
     by_plane = pltpu.VMEM((planes, *one), f32)
     outs = [("h", one)] * (planes - 1)
     send = kernel_call(
-        part(send_kernel, planes, width), "h", outs, [by_plane, semaphores(planes, planes + PARTS)]
+        part(send_kernel, planes, width), "a", outs, [by_plane, semaphores(planes, planes + PARTS)]
     )
     merge = kernel_call(
-        part(merge_kernel, planes, width), "h" * planes + "a", [("h", paired)],
+        part(merge_kernel, planes, width), "a" * planes + "a", [("h", paired)],
         [paired_buf, semaphores(PARTS + 1, planes + PARTS)],
     )
     half_sizes = (n, channels // 2, tokens)
     half_spectrum = (n, channels // 2, 2 * tokens)
+    table_bufs = [pltpu.VMEM(table.shape, table.dtype) for table in (tw, fwd, inv)]
 
     def transform_filters(first):
         return kernel_call(
-            part(filter_kernel, first, *half_sizes), "hvv", [("h", half_spectrum)],
+            part(filter_kernel, first, *half_sizes), "hhh", [("h", half_spectrum)],
             [
+                *table_bufs[:2],
                 pltpu.VMEM((channels // 2, length), f32),
                 *[pltpu.VMEM(half_spectrum, f32)] * 2,
-                semaphores(2, PARTS),
+                semaphores(3, PARTS),
             ],
             flops // 2,
         )(filters, tw, fwd)[0]
 
-    transform_scratch = [rows, y, y, y, semaphores(4, PARTS, max(PARTS, planes))]
+    transform_scratch = [
+        *table_bufs, rows, y, y, y, semaphores(3, 2 * PARTS, max(2 * PARTS, planes))
+    ]
     always = lax.axis_index("context") < n
 
     def grouped(body, *args):
@@ -520,7 +540,7 @@
         product_ch = within_plane(*merge(keep_p, *got_p, send_g))
         filt = (filt_a, transform_filters(channels // 2))
         *outs, prod_spec = kernel_call(
-            part(conv_kernel, planes, *sizes), "hvvvhh",
+            part(conv_kernel, planes, *sizes), "ahhhhh",
             [("h", one)] * planes + [("h", spectrum)], transform_scratch, 2 * flops,
         )(product_ch, tw, fwd, inv, *filt)
         return outs, prod_spec, filt
@@ -530,38 +550,39 @@
 
     def third(near_g, far_g, filt, keep_c, prod_spec):
         back_ch, grad_spec = kernel_call(
-            part(back_kernel, planes, *sizes), "h" * planes + "vvvhha",
+            part(back_kernel, planes, *sizes), "a" * planes + "hhhhha",
             [("h", paired), ("h", spectrum)], transform_scratch, 2 * flops,
         )(near_g, *far_g, tw, fwd, inv, *filt, keep_c)
         near_b = within_plane(back_ch)
         (own,) = kernel_call(
-            part(filter_grad_kernel, scale, *sizes), "vvhh", [("u", lags)],
-            [y, y, y, semaphores(PARTS, 2)], flops,
+            part(filter_grad_kernel, scale, *sizes), "hhhh", [("u", lags)],
+            [table_bufs[0], table_bufs[2], y, y, y, semaphores(PARTS + 1, 2)], flops,
         )(tw, inv, prod_spec, grad_spec)
-        return near_b, send(near_b), own
-
-    near_b, send_b, own = grouped(third, near_g, far_g, filt, keep_c, prod_spec)
+        if pair_size == 2:
+            other = lax.ppermute(own, "dp", [(0, 1), (1, 0)])
+        else:
+            other = lax.psum(own, "dp") - own
+        return near_b, send(near_b), own, other
+
+    near_b, send_b, own, other = grouped(third, near_g, far_g, filt, keep_c, prod_spec)
     far_b = along_z(send_b)
 
-    def fourth(keep_c, got_c, send_b, query, cot, own):
+    def fourth(keep_c, got_c, send_b, query, cot, own, other):
         conv_tok = within_plane(*merge(keep_c, *got_c, send_b))
-        if pair_size == 2:
-            grad_filter = own + lax.ppermute(own, "dp", [(0, 1), (1, 0)])
-        else:
-            grad_filter = lax.psum(own, "dp")
+        (grad_filter,) = kernel_call(add_kernel, "vv", [("u", lags)], [])(own, other)
         gated, grad_query = kernel_call(
-            part(gate_kernel, planes, width), "hhh", [("h", blocks)] * 2,
+            part(gate_kernel, planes, width), "ahh", [("h", blocks)] * 2,
             [by_plane, *[rows] * 4, semaphores(2 * planes, 3)],
         )(conv_tok, query, cot)
         return gated, grad_query, grad_filter
 
     gated, grad_query, grad_filter = grouped(
-        fourth, keep_c, got_c, send_b[0], query, cot, own
+        fourth, keep_c, got_c, send_b[0], query, cot, own, other
     )
     grad_key, grad_value = kernel_call(
-        part(gate_split_kernel, planes, width), "v" * (planes + 1) + "h", [("h", blocks)] * 2,
+        part(gate_split_kernel, planes, width), "v" * (planes + 1) + "aa", [("h", blocks)] * 2,
         [pltpu.VMEM(one, f32), rows, rows, semaphores(planes + 1, 2)],
-    )(*far_b, value, key, near_b)
+    )(*far_b, value, key, near_b, gated)
     shape = query_input.shape
     return (
         gated.reshape(shape),

time: 126 us -> 137 us (1.087)
  Pallas kernels: 41.2 us -> 53.8 us
  starting transfers between devices: 31.1 us -> 29.2 us
  waiting for transfers between devices: 28.4 us -> 29.9 us
    pallas_call x13 -> x14, Pallas kernels: 41.2 us -> 53.8 us  [run(): pl.pallas_call(body, in_specs=[pl.BlockSpec(memory_space=SPACES[space]) f...]
    all_to_all x3, waiting for transfers between devices: 28.4 us -> 29.8 us  [within_plane(): lax.all_to_all(x, 'context', 0, 0, axis_index_groups=members, tiled=True)]
    cond x20 -> x13, local copies, waits for them, and re-layouts: 3.3 us -> 3.17 us
  transfers between devices with their start and end apart: 16 -> 16, of which waited for: 3 -> 3; matrix products, arithmetic and copies ran while one was open for 0% -> 2% of each run, Pallas kernels for 30% -> 36%
where the time goes in v6:
time: 137 us; the launch traced here: 136 us
  Pallas kernels  53.8 us (39%)
  waiting for transfers between devices  29.9 us (22%)
  starting transfers between devices  29.2 us (21%)
  blocking collectives  18.2 us (13%)
  local copies, waits for them, and re-layouts  3.99 us (3%)
    pallas_call x14, Pallas kernels, run(): pl.pallas_call(body, in_specs=[pl.BlockSpec(memory_space=SPACES[space]) f...  53.8 us
    all_to_all x3, waiting for transfers between devices, within_plane(): lax.all_to_all(x, 'context', 0, 0, axis_index_groups=members, tiled=True)  29.8 us
    all_to_all x1, blocking collectives, within_plane(): lax.all_to_all(x, 'context', 0, 0, axis_index_groups=members, tiled=True)  18.2 us
    ppermute x12, starting transfers between devices, along_z(): lax.ppermute(x, 'context', [(i, i ^ d * width) for i in range(n)])  17.8 us
    all_to_all x3, starting transfers between devices, within_plane(): lax.all_to_all(x, 'context', 0, 0, axis_index_groups=members, tiled=True)  11.3 us
    cond x13, local copies, waits for them, and re-layouts  3.17 us
  transfers between devices with their start and end apart: 16, of which 3 were waited for; matrix products, arithmetic and copies ran while one was open for 2% of the time, Pallas kernels for 36%

profile of v6, /device:TPU:0, one launch (start us, length us, event | category | flops | bytes accessed | tf_op | source)
XLA Modules:
  0.0 136.1 jit_solution(8013217700392289709)
XLA Ops:
  2.5 3.1 %collective-permute-start.1 = (f32[4,128,128]{2,1,0:T(8,128)S(1)}, f32[4,128,128]{2,1,0:T(8,128)S(1)}, u32[]{:S(2)}, u32[]{:S(2)}) collective-permute-start(f32[4,128,128]{2,1,0:T(8,128)S(1)} %get-tuple-element.159), channel_id=1, source_target_pairs={{0,4},{1,5},{2,6},{3,7},{4,0},{5,1},{6,2},{7,3},{8,12},{9,13},{10,... | collective-permute-start | bytes 786440 | tf_op jit(solution)/shard_map/ppermute | solution.py:472
  5.6 2.6 %collective-permute-start.2 = (f32[4,128,128]{2,1,0:T(8,128)S(1)}, f32[4,128,128]{2,1,0:T(8,128)}, u32[]{:S(2)}, u32[]{:S(2)}) collective-permute-start(f32[4,128,128]{2,1,0:T(8,128)S(1)} %get-tuple-element.160), channel_id=1, source_target_pairs={{0,8},{1,9},{2,10},{3,11},{4,12},{5,13},{6,14},{7,15},{8,0},{9,1},... | collective-permute-start | bytes 786440 | tf_op jit(solution)/shard_map/ppermute | solution.py:472
  8.2 22.3 %conditional.4 = (f32[4,4,128,128]{3,2,1,0:T(8,128)}, f32[4,128,128]{2,1,0:T(8,128)}, f32[4,128,128]{2,1,0:T(8,128)}, f32[4,128,128]{2,1,0:T(8,128)}, f32[16,64,256]{2,1,0:T(8,128)}) conditional(s32[]{:T(128)} %convert_element_type.2, () %tuple.46, (f32[16,128,128]{2,1,0:T(8,128)}, f32[16,128,128]{2,1,0:T(8,128)}, f32[4,128,128]{2,1,0:T(8,128)S(1)}, ...), branch_computations={%region_0.0_spmd, %region_1.0_spmd} | conditional | flops 268435456 | bytes 11141192 | solution.py:520
  8.2 2.4 %branch_1_fun.12 = f32[4,4,128,128]{3,2,1,0:T(8,128)} custom-call(f32[16,128,128]{2,1,0:T(8,128)} %get-tuple-element.74.refs_0_, f32[16,128,128]{2,1,0:T(8,128)} %get-tuple-element.75.refs_1_, f32[4,128,128]{2,1,0:T(8,128)S(1)} %get-tuple-element.76.refs_2_), custom_call_target="tpu_custom_call" | custom-call | bytes 3407872 | tf_op jit(solution)/shard_map/cond/branch_1_fun/pallas_call | solution.py:415
  10.6 4.3 %all-to-all-start = ((f32[4,4,128,128]{3,2,1,0:T(8,128)}), f32[4,4,128,128]{3,2,1,0:T(8,128)}, u32[]{:S(2)}, u32[]{:S(2)}) async-start(f32[4,4,128,128]{3,2,1,0:T(8,128)} %branch_1_fun.12), calls=%async_computation | async-start | bytes 2097152 | tf_op jit(solution)/shard_map/cond/branch_1_fun/all_to_all | solution.py:478
  14.9 2.7 %branch_1_fun.14 = f32[16,64,256]{2,1,0:T(8,128)} custom-call(f32[128,2048]{1,0:T(8,128)S(1)} %get-tuple-element.80.refs_0_, f32[2,16,8,128]{3,2,1,0:T(8,128)S(1)} %get-tuple-element.81.refs_1_, bf16[2,256,256]{2,1,0:T(8,128)(2,1)S(1)} %get-tuple-element.82.refs_2_), custom_call_target="tpu_custom_call" | custom-call | flops 268435456 | bytes 2752512 | tf_op jit(solution)/shard_map/cond/branch_1_fun/pallas_call | solution.py:415
  17.7 10.7 %all-to-all-done.refs_0_ = f32[4,4,128,128]{3,2,1,0:T(8,128)} async-done(((f32[4,4,128,128]{3,2,1,0:T(8,128)}), f32[4,4,128,128]{3,2,1,0:T(8,128)}, u32[]{:S(2)}, u32[]{:S(2)}) %all-to-all-start) | async-done | bytes 1048608 | tf_op jit(solution)/shard_map/cond/branch_1_fun/all_to_all | solution.py:478
  34.6 29.0 %conditional.5 = (f32[4,128,128]{2,1,0:T(8,128)}, f32[4,128,128]{2,1,0:T(8,128)}, f32[4,128,128]{2,1,0:T(8,128)}, f32[4,128,128]{2,1,0:T(8,128)}, f32[16,128,256...) conditional(s32[]{:T(128)} %convert_element_type.2, () %tuple.45, (f32[4,128,128]{2,1,0:T(8,128)S(1)}, ...), branch_computations={%region_2.0_spmd, %region_3.0_spmd} | conditional | flops 1342177280 | bytes 19923060 | solution.py:520
  34.7 2.7 %branch_1_fun.15 = f32[4,4,128,128]{3,2,1,0:T(8,128)} custom-call(f32[4,128,128]{2,1,0:T(8,128)S(1)} %get-tuple-element.83.refs_0_, f32[4,128,128]{2,1,0:T(8,128)S(1)} %get-tuple-element.84.refs_1_, f32[4,128,128]{2,1,0:T(8,128)} %get-tuple-element.85.refs_2_, f32[4,128,128]{2,1,0:T(8,128)} %get-tuple-element.86.refs_3_, ...), custom_call_target="tpu_custom_call" | custom-call | bytes 2359296 | tf_op jit(solution)/shard_map/cond/branch_1_fun/pallas_call | solution.py:415
  37.3 3.5 %all-to-all-start.1 = ((f32[4,4,128,128]{3,2,1,0:T(8,128)}), f32[4,4,128,128]{3,2,1,0:T(8,128)S(1)}, u32[]{:S(2)}, u32[]{:S(2)}) async-start(f32[4,4,128,128]{3,2,1,0:T(8,128)} %branch_1_fun.15), calls=%async_computation.1 | async-start | bytes 2097152 | tf_op jit(solution)/shard_map/cond/branch_1_fun/all_to_all | solution.py:478
  40.9 3.0 %branch_1_fun.16.refs_5_ = f32[16,64,256]{2,1,0:T(8,128)} custom-call(f32[128,2048]{1,0:T(8,128)} %copy-done.4, f32[2,16,8,128]{3,2,1,0:T(8,128)S(1)} %get-tuple-element.88.refs_1_, bf16[2,256,256]{2,1,0:T(8,128)(2,1)S(1)} %get-tuple-element.89.refs_2_), custom_call_target="tpu_custom_call" | custom-call | flops 268435456 | bytes 2752512 | tf_op jit(solution)/shard_map/cond/branch_1_fun/pallas_call | solution.py:415
  43.9 9.5 %all-to-all-done.1.refs_0_ = f32[4,4,128,128]{3,2,1,0:T(8,128)S(1)} async-done(((f32[4,4,128,128]{3,2,1,0:T(8,128)}), f32[4,4,128,128]{3,2,1,0:T(8,128)S(1)}, u32[]{:S(2)}, u32[]{:S(2)}) %all-to-all-start.1) | async-done | bytes 1048608 | tf_op jit(solution)/shard_map/cond/branch_1_fun/all_to_all | solution.py:478
  53.4 10.3 %branch_1_fun.17 = (f32[4,128,128]{2,1,0:T(8,128)}, f32[4,128,128]{2,1,0:T(8,128)}, f32[4,128,128]{2,1,0:T(8,128)}, f32[4,128,128]{2,1,0:T(8,128)}, f32[16,128,256]{2,1,0:T(8,128)}) custom-call(f32[4,4,128,128]{3,2,1,0:T(8,128)S(1)} %all-to-all-done.1.refs_0_, f32[2,16,8,128]{3,2,1,0:T(8,128)S(1)} %get-tuple-element.88.refs_1_, ...), custom_call_target="tpu_custom_call" | custom-call | flops 1073741824 | bytes 7471104 | tf_op jit(solution)/shard_map/cond/branch_1_fun/pallas_call | solution.py:415
  68.1 37.2 %conditional.6 = (f32[4,4,128,128]{3,2,1,0:T(8,128)}, f32[4,128,128]{2,1,0:T(8,128)}, f32[4,128,128]{2,1,0:T(8,128)}, f32[4,128,128]{2,1,0:T(8,128)}, f32[128,2048]{1,0:T(8,128)}, /*index=5*/f32[128,2048]{1,0:T(8,128)}) conditional(s32[]{:T(128)} %convert_element_type.2, () %tuple.49, (f32[4,4,128,128]{3,2,1,0:T(8,128)}, f32[4,128,128]{2,1,0:T(8,128)}, ...), branch_computations={%region_4.0_spmd, %region_5.0_spmd} | conditional | flops 1610612736 | bytes 29360328 | solution.py:520
  68.9 10.3 %branch_1_fun.18 = (f32[4,4,128,128]{3,2,1,0:T(8,128)}, f32[16,128,256]{2,1,0:T(8,128)}) custom-call(f32[4,4,128,128]{3,2,1,0:T(8,128)} %get-tuple-element.98.refs_0_, f32[4,128,128]{2,1,0:T(8,128)} %get-tuple-element.99.refs_1_, f32[4,128,128]{2,1,0:T(8,128)S(1)} %get-tuple-element.100.refs_2_, f32[4,128,128]{2,1,0:T(8,128)} %get-tuple-element.101.refs_3_, ...), custom_call_target="tpu_custom_call" | custom-call | flops 1073741824 | bytes 8519680 | tf_op jit(solution)/shard_map/cond/branch_1_fun/pallas_call | solution.py:415
  79.2 5.6 %branch_1_fun.20 = f32[128,2048]{1,0:T(8,128)} custom-call(f32[2,16,8,128]{3,2,1,0:T(8,128)} %copy-done.8, bf16[2,256,256]{2,1,0:T(8,128)(2,1)} %copy-done.10, f32[16,128,256]{2,1,0:T(8,128)} %get-tuple-element.112.refs_2_, f32[16,128,256]{2,1,0:T(8,128)} %get-tuple-element.113.refs_3_), custom_call_target="tpu_custom_call" | custom-call | flops 536870912 | bytes 5898240 | tf_op jit(solution)/shard_map/cond/branch_1_fun/pallas_call | solution.py:415
  85.0 18.2 %all_to_all.16.refs_0_ = f32[4,4,128,128]{3,2,1,0:T(8,128)} all-to-all(f32[4,4,128,128]{3,2,1,0:T(8,128)S(1)} %copy-done.11), channel_id=1, replica_groups={{0,1,2,3},{4,5,6,7},{8,9,10,11},{12,13,14,15},{16,17,18,19},{20,21,22,2..., dimensions={0} | all-to-all | bytes 2097152 | tf_op jit(solution)/shard_map/cond/branch_1_fun/all_to_all | solution.py:478
  109.7 23.3 %conditional.7 = (f32[16,128,128]{2,1,0:T(8,128)S(1)}, f32[128,2048]{1,0:T(8,128)}, f32[1,2048,128]{2,1,0:T(8,128)}, f32[1,2048,128]{2,1,0:T(8,128)}) conditional(s32[]{:T(128)} %convert_element_type.2, () %tuple.44, (f32[4,128,128]{2,1,0:T(8,128)}, f32[4,128,128]{2,1,0:T(8,128)S(1)}, f32[4,128,128]{2,1,0:T(8,128)}, f32[4,128,128]{2,1,0:T(8,128)}, ...), branch_computations={%region_6.0_spmd, %region_7.0_spmd} | conditional | bytes 20185180 | solution.py:520
  109.7 2.6 %branch_1_fun.21 = f32[4,4,128,128]{3,2,1,0:T(8,128)} custom-call(f32[4,128,128]{2,1,0:T(8,128)} %get-tuple-element.114.refs_0_, f32[4,128,128]{2,1,0:T(8,128)S(1)} %get-tuple-element.115.refs_1_, f32[4,128,128]{2,1,0:T(8,128)} %get-tuple-element.116.refs_2_, f32[4,128,128]{2,1,0:T(8,128)} %get-tuple-element.117.refs_3_, ...), custom_call_target="tpu_custom_call" | custom-call | bytes 2359296 | tf_op jit(solution)/shard_map/cond/branch_1_fun/pallas_call | solution.py:415
  112.3 3.5 %all-to-all-start.3 = ((f32[4,4,128,128]{3,2,1,0:T(8,128)}), f32[4,4,128,128]{3,2,1,0:T(8,128)S(1)}, u32[]{:S(2)}, u32[]{:S(2)}) async-start(f32[4,4,128,128]{3,2,1,0:T(8,128)} %branch_1_fun.21), calls=%async_computation.3 | async-start | bytes 2097152 | tf_op jit(solution)/shard_map/cond/branch_1_fun/all_to_all | solution.py:478
  115.8 2.6 %branch_1_fun.23 = f32[128,2048]{1,0:T(8,128)} custom-call(f32[128,2048]{1,0:T(8,128)} %get-tuple-element.122.a_ref, f32[128,2048]{1,0:T(8,128)} %get-tuple-element.123.b_ref), custom_call_target="tpu_custom_call" | custom-call | bytes 3145728 | tf_op jit(solution)/shard_map/cond/branch_1_fun/pallas_call | solution.py:415
  118.4 9.7 %all-to-all-done.3.refs_0_ = f32[4,4,128,128]{3,2,1,0:T(8,128)S(1)} async-done(((f32[4,4,128,128]{3,2,1,0:T(8,128)}), f32[4,4,128,128]{3,2,1,0:T(8,128)S(1)}, u32[]{:S(2)}, u32[]{:S(2)}) %all-to-all-start.3) | async-done | bytes 1048608 | tf_op jit(solution)/shard_map/cond/branch_1_fun/all_to_all | solution.py:478
  128.1 2.6 %branch_1_fun.22 = (f32[16,128,128]{2,1,0:T(8,128)}, f32[16,128,128]{2,1,0:T(8,128)}) custom-call(f32[4,4,128,128]{3,2,1,0:T(8,128)S(1)} %all-to-all-done.3.refs_0_, f32[16,128,128]{2,1,0:T(8,128)} %get-tuple-element.119.refs_1_, f32[16,128,128]{2,1,0:T(8,128)} %get-tuple-element.120.refs_2_), custom_call_target="tpu_custom_call" | custom-call | bytes 5242880 | tf_op jit(solution)/shard_map/cond/branch_1_fun/pallas_call | solution.py:415
  133.1 3.0 %shard_map.120 = (f32[16,128,128]{2,1,0:T(8,128)}, f32[16,128,128]{2,1,0:T(8,128)}) custom-call(f32[4,128,128]{2,1,0:T(8,128)} %collective-permute-done.10.refs_0_, f32[4,128,128]{2,1,0:T(8,128)S(1)} %collective-permute-done.11.refs_1_, f32[4,128,128]{2,1,0:T(8,128)} %collective-permute-done.12.refs_2_, f32[16,128,128]{2,1,0:T(8,128)S(1)} %bitcast.11, ...), custom_call_target="tpu_custom_call" | custom-call | bytes 7077888 | tf_op jit(solution)/shard_map/pallas_call | solution.py:415
  (56 shorter events, 22.3 us)
Async XLA Ops:
  0.6 7.5 %copy-start.7 = (f32[2,16,8,128]{3,2,1,0:T(8,128)S(1)}, f32[2,16,8,128]{3,2,1,0:T(8,128)}, u32[]{:S(2)}) copy-start(f32[2,16,8,128]{3,2,1,0:T(8,128)} %constant.18.clone) | copy-start | bytes 393220
  0.6 7.5 %copy-start.5 = (bf16[2,256,256]{2,1,0:T(8,128)(2,1)S(1)}, bf16[2,256,256]{2,1,0:T(8,128)(2,1)}, u32[]{:S(2)}) copy-start(bf16[2,256,256]{2,1,0:T(8,128)(2,1)} %constant.5.clone) | copy-start | bytes 786436
  0.7 7.5 %copy-start.3 = (f32[128,2048]{1,0:T(8,128)S(1)}, f32[128,2048]{1,0:T(8,128)}, u32[]{:S(2)}) copy-start(f32[128,2048]{1,0:T(8,128)} %param.19) | copy-start | bytes 3145732
  2.5 31.7 %collective-permute-start.1 = (f32[4,128,128]{2,1,0:T(8,128)S(1)}, f32[4,128,128]{2,1,0:T(8,128)S(1)}, u32[]{:S(2)}, u32[]{:S(2)}) collective-permute-start(f32[4,128,128]{2,1,0:T(8,128)S(1)} %get-tuple-element.159), channel_id=1, source_target_pairs={{0,4},{1,5},{2,6},{3,7},{4,0},{5,1},{6,2},{7,3},{8,12},{9,13},{10,... | collective-permute-start | bytes 786440 | tf_op jit(solution)/shard_map/ppermute | solution.py:472
  5.6 29.1 %collective-permute-start.2 = (f32[4,128,128]{2,1,0:T(8,128)S(1)}, f32[4,128,128]{2,1,0:T(8,128)}, u32[]{:S(2)}, u32[]{:S(2)}) collective-permute-start(f32[4,128,128]{2,1,0:T(8,128)S(1)} %get-tuple-element.160), channel_id=1, source_target_pairs={{0,8},{1,9},{2,10},{3,11},{4,12},{5,13},{6,14},{7,15},{8,0},{9,1},... | collective-permute-start | bytes 786440 | tf_op jit(solution)/shard_map/ppermute | solution.py:472
  8.1 26.5 %collective-permute-start.3 = (f32[4,128,128]{2,1,0:T(8,128)S(1)}, f32[4,128,128]{2,1,0:T(8,128)}, u32[]{:S(2)}, u32[]{:S(2)}) collective-permute-start(f32[4,128,128]{2,1,0:T(8,128)S(1)} %get-tuple-element.161), channel_id=1, source_target_pairs={{0,12},{1,13},{2,14},{3,15},{4,8},{5,9},{6,10},{7,11},{8,4},{9,5},... | collective-permute-start | bytes 786440 | tf_op jit(solution)/shard_map/ppermute | solution.py:472
  8.2 26.5 %copy-start.9 = (bf16[2,256,256]{2,1,0:T(8,128)(2,1)S(1)}, bf16[2,256,256]{2,1,0:T(8,128)(2,1)}, u32[]{:S(2)}) copy-start(bf16[2,256,256]{2,1,0:T(8,128)(2,1)} %constant.7.clone) | copy-start | bytes 786436
  10.6 17.7 %all-to-all-start = ((f32[4,4,128,128]{3,2,1,0:T(8,128)}), f32[4,4,128,128]{3,2,1,0:T(8,128)}, u32[]{:S(2)}, u32[]{:S(2)}) async-start(f32[4,4,128,128]{3,2,1,0:T(8,128)} %branch_1_fun.12), calls=%async_computation | async-start | bytes 2097152 | tf_op jit(solution)/shard_map/cond/branch_1_fun/all_to_all | solution.py:478
  30.5 36.5 %collective-permute-start.8 = (f32[4,128,128]{2,1,0:T(8,128)}, f32[4,128,128]{2,1,0:T(8,128)S(1)}, u32[]{:S(2)}, u32[]{:S(2)}) collective-permute-start(f32[4,128,128]{2,1,0:T(8,128)} %get-tuple-element.169), channel_id=1, source_target_pairs={{0,8},{1,9},{2,10},{3,11},{4,12},{5,13},{6,14},{7,15},{8,0},{9,1},... | collective-permute-start | bytes 786440 | tf_op jit(solution)/shard_map/ppermute | solution.py:472
  32.1 36.0 %collective-permute-start.9 = (f32[4,128,128]{2,1,0:T(8,128)}, f32[4,128,128]{2,1,0:T(8,128)}, u32[]{:S(2)}, u32[]{:S(2)}) collective-permute-start(f32[4,128,128]{2,1,0:T(8,128)} %get-tuple-element.170), channel_id=1, source_target_pairs={{0,12},{1,13},{2,14},{3,15},{4,8},{5,9},{6,10},{7,11},{8,4},{9,5},... | collective-permute-start | bytes 786440 | tf_op jit(solution)/shard_map/ppermute | solution.py:472
  34.1 34.0 %collective-permute-start.7 = (f32[4,128,128]{2,1,0:T(8,128)}, f32[4,128,128]{2,1,0:T(8,128)}, u32[]{:S(2)}, u32[]{:S(2)}) collective-permute-start(f32[4,128,128]{2,1,0:T(8,128)} %get-tuple-element.162), channel_id=1, source_target_pairs={{0,4},{1,5},{2,6},{3,7},{4,0},{5,1},{6,2},{7,3},{8,12},{9,13},{10,... | collective-permute-start | bytes 786440 | tf_op jit(solution)/shard_map/ppermute | solution.py:472
  34.7 2.7 %copy-start.4 = (f32[128,2048]{1,0:T(8,128)}, f32[128,2048]{1,0:T(8,128)S(1)}, u32[]{:S(2)}) copy-start(f32[128,2048]{1,0:T(8,128)S(1)} %get-tuple-element.92.refs_0_) | copy-start | bytes 3145732 | tf_op jit(solution)/shard_map/cond
  37.3 16.0 %all-to-all-start.1 = ((f32[4,4,128,128]{3,2,1,0:T(8,128)}), f32[4,4,128,128]{3,2,1,0:T(8,128)S(1)}, u32[]{:S(2)}, u32[]{:S(2)}) async-start(f32[4,4,128,128]{3,2,1,0:T(8,128)} %branch_1_fun.15), calls=%async_computation.1 | async-start | bytes 2097152 | tf_op jit(solution)/shard_map/cond/branch_1_fun/all_to_all | solution.py:478
  63.7 44.7 %collective-permute-start.4 = (f32[4,128,128]{2,1,0:T(8,128)}, f32[4,128,128]{2,1,0:T(8,128)S(1)}, u32[]{:S(2)}, u32[]{:S(2)}) collective-permute-start(f32[4,128,128]{2,1,0:T(8,128)} %get-tuple-element.165), channel_id=1, source_target_pairs={{0,4},{1,5},{2,6},{3,7},{4,0},{5,1},{6,2},{7,3},{8,12},{9,13},{10,... | collective-permute-start | bytes 786440 | tf_op jit(solution)/shard_map/ppermute | solution.py:472
  65.3 43.6 %collective-permute-start.5 = (f32[4,128,128]{2,1,0:T(8,128)}, f32[4,128,128]{2,1,0:T(8,128)S(1)}, u32[]{:S(2)}, u32[]{:S(2)}) collective-permute-start(f32[4,128,128]{2,1,0:T(8,128)} %get-tuple-element.166), channel_id=1, source_target_pairs={{0,8},{1,9},{2,10},{3,11},{4,12},{5,13},{6,14},{7,15},{8,0},{9,1},... | collective-permute-start | bytes 786440 | tf_op jit(solution)/shard_map/ppermute | solution.py:472
  66.9 42.0 %collective-permute-start.6 = (f32[4,128,128]{2,1,0:T(8,128)}, f32[4,128,128]{2,1,0:T(8,128)S(1)}, u32[]{:S(2)}, u32[]{:S(2)}) collective-permute-start(f32[4,128,128]{2,1,0:T(8,128)} %get-tuple-element.167), channel_id=1, source_target_pairs={{0,12},{1,13},{2,14},{3,15},{4,8},{5,9},{6,10},{7,11},{8,4},{9,5},... | collective-permute-start | bytes 786440 | tf_op jit(solution)/shard_map/ppermute | solution.py:472
  79.2 5.7 %copy-start.11 = (f32[4,4,128,128]{3,2,1,0:T(8,128)S(1)}, f32[4,4,128,128]{3,2,1,0:T(8,128)}, u32[]{:S(2)}) copy-start(f32[4,4,128,128]{3,2,1,0:T(8,128)} %get-tuple-element.108) | copy-start | bytes 3145732 | tf_op jit(solution)/shard_map/cond
  84.9 20.5 %collective-permute-start = (f32[128,2048]{1,0:T(8,128)}, f32[128,2048]{1,0:T(8,128)}, u32[]{:S(2)}, u32[]{:S(2)}) collective-permute-start(f32[128,2048]{1,0:T(8,128)} %branch_1_fun.20), channel_id=1, source_target_pairs={{0,16},{16,0},{1,17},{17,1},{2,18},{18,2},{3,19},{19,3},{4,20},{20... | collective-permute-start | bytes 3145736 | tf_op jit(solution)/shard_map/cond/branch_1_fun/ppermute | solution.py:562
  105.3 27.7 %collective-permute-start.11 = (f32[4,128,128]{2,1,0:T(8,128)}, f32[4,128,128]{2,1,0:T(8,128)S(1)}, u32[]{:S(2)}, u32[]{:S(2)}) collective-permute-start(f32[4,128,128]{2,1,0:T(8,128)} %get-tuple-element.179), channel_id=1, source_target_pairs={{0,8},{1,9},{2,10},{3,11},{4,12},{5,13},{6,14},{7,15},{8,0},{9,1},... | collective-permute-start | bytes 786440 | tf_op jit(solution)/shard_map/ppermute | solution.py:472
  106.1 26.9 %collective-permute-start.12 = (f32[4,128,128]{2,1,0:T(8,128)}, f32[4,128,128]{2,1,0:T(8,128)}, u32[]{:S(2)}, u32[]{:S(2)}) collective-permute-start(f32[4,128,128]{2,1,0:T(8,128)} %get-tuple-element.180), channel_id=1, source_target_pairs={{0,12},{1,13},{2,14},{3,15},{4,8},{5,9},{6,10},{7,11},{8,4},{9,5},... | collective-permute-start | bytes 786440 | tf_op jit(solution)/shard_map/ppermute | solution.py:472
  108.4 24.7 %collective-permute-start.10 = (f32[4,128,128]{2,1,0:T(8,128)}, f32[4,128,128]{2,1,0:T(8,128)}, u32[]{:S(2)}, u32[]{:S(2)}) collective-permute-start(f32[4,128,128]{2,1,0:T(8,128)} %get-tuple-element.174), channel_id=1, source_target_pairs={{0,4},{1,5},{2,6},{3,7},{4,0},{5,1},{6,2},{7,3},{8,12},{9,13},{10,... | collective-permute-start | bytes 786440 | tf_op jit(solution)/shard_map/ppermute | solution.py:472
  109.7 23.4 %copy-start = (f32[1,2048,128]{2,1,0:T(8,128)S(1)}, f32[1,2048,128]{2,1,0:T(8,128)}, u32[]{:S(2)}) copy-start(f32[1,2048,128]{2,1,0:T(8,128)} %param.17) | copy-start | bytes 3145732
  109.7 23.4 %copy-start.1 = (f32[1,2048,128]{2,1,0:T(8,128)S(1)}, f32[1,2048,128]{2,1,0:T(8,128)}, u32[]{:S(2)}) copy-start(f32[1,2048,128]{2,1,0:T(8,128)} %param.18) | copy-start | bytes 3145732
  112.3 15.8 %all-to-all-start.3 = ((f32[4,4,128,128]{3,2,1,0:T(8,128)}), f32[4,4,128,128]{3,2,1,0:T(8,128)S(1)}, u32[]{:S(2)}, u32[]{:S(2)}) async-start(f32[4,4,128,128]{3,2,1,0:T(8,128)} %branch_1_fun.21), calls=%async_computation.3 | async-start | bytes 2097152 | tf_op jit(solution)/shard_map/cond/branch_1_fun/all_to_all | solution.py:478
  (6 other events, 6.1 us)

commit v7 on v5

--- a/solution.py
+++ b/solution.py
@@ -47,18 +47,12 @@
     return out
 
 
-def split(x):
+def times_table(x, table_ref):
     hi = x.astype(jnp.bfloat16)
     lo = (x - hi.astype(jnp.float32)).astype(jnp.bfloat16)
-    return hi, lo
-
-
-def times_table(x, table_ref):
-    hi, lo = split(x)
-    out = jnp.dot(hi, table_ref[0], preferred_element_type=jnp.float32)
-    out += jnp.dot(lo, table_ref[0], preferred_element_type=jnp.float32)
-    out += jnp.dot(hi, table_ref[1], preferred_element_type=jnp.float32)
-    return out
+    return jnp.dot(
+        jnp.concatenate([hi, lo, hi], axis=1), table_ref[...], preferred_element_type=jnp.float32
+    )
 
 
 def outer_forward(read, n, part, tokens, tw_ref, y_ref):
@@ -148,11 +142,11 @@
     sign, n, channels, tokens, sources, targets, tw_ref, fwd_ref, inv_ref, spec_refs, own_ref,
     buf_ref, spec_buf, own_buf, y_ref, sem,
 ):
-    rows = parts_of(channels, ROWS)
+    half = channels // 2
+    rows = [pl.ds(0, half), pl.ds(half, half)]
     loads = [copies_of(sources(part), sem.at[0, i]) for i, part in enumerate(rows)]
     for load in loads:
         start_all(load)
-    half = channels // 2
     spec_loads = [
         copies_of(
             [
@@ -193,7 +187,8 @@
 
 def conv_kernel(planes, n, channels, tokens, x_ref, *refs):
     tables, spec_refs, refs = refs[:3], refs[3:5], refs[5:]
-    out_refs, (own_ref, buf_ref, *scratch) = refs[:planes], refs[planes:]
+    out_refs, (own_ref, *scratch) = refs[:planes], refs[planes:]
+    buf_ref = scratch[0]
     width = n // planes
     z = plane(width)
 
@@ -207,14 +202,15 @@
         return [(block(d, part), out_refs[d].at[:, part]) for d in range(planes)]
 
     transform(
-        1.0, n, channels, tokens, sources, targets, *tables, spec_refs, own_ref, buf_ref, *scratch
+        1.0, n, channels, tokens, sources, targets, *tables, spec_refs, own_ref, *scratch
     )
 
 
 def back_kernel(planes, n, channels, tokens, near_ref, *refs):
     far_refs, refs = refs[: planes - 1], refs[planes - 1 :]
     tables, spec_refs, refs = refs[:3], refs[3:5], refs[5:]
-    after_ref, out_ref, own_ref, buf_ref, *scratch = refs
+    after_ref, out_ref, own_ref, *scratch = refs
+    buf_ref = scratch[0]
     width = n // planes
     z = plane(width)
 
@@ -231,7 +227,7 @@
         return [(block(z, part), out_ref.at[:, z, part]) for z in range(planes)]
 
     transform(
-        -1.0, n, channels, tokens, sources, targets, *tables, spec_refs, own_ref, buf_ref, *scratch
+        -1.0, n, channels, tokens, sources, targets, *tables, spec_refs, own_ref, *scratch
     )
 
 
@@ -258,6 +254,10 @@
     outer_inverse(write, n, pl.ds(0, channels), tokens, tw_ref, y_ref)
 
 
+def add_kernel(a_ref, b_ref, out_ref):
+    out_ref[...] = a_ref[...] + b_ref[...]
+
+
 def load_pairs(n, a_ref, b_ref, a_buf, b_buf, sem):
     loads = [
         copies_of([(a_ref.at[part], a_buf.at[part]), (b_ref.at[part], b_buf.at[part])], sem.at[i])
@@ -365,26 +365,34 @@
     gate_parts(width, blocks, a_in, b_in, (oa_ref, ob_ref), a_buf, b_buf, sem)
 
 
-def gate_split_kernel(planes, width, *refs):
+def gate_near_kernel(
+    planes, width, near_ref, a_ref, b_ref, oa_ref, ob_ref, x_buf, a_buf, b_buf, sem
+):
+    z = plane(width)
+    part = pl.ds(z * width, width)
+    pairs = [(near_ref.at[:, z], x_buf), (a_ref.at[part], a_buf), (b_ref.at[part], b_buf)]
+    loads = copies_of(pairs, sem.at[0])
+    start_all(loads)
+    wait_all(loads)
+    a_buf[...] = x_buf[...] * a_buf[...]
+    b_buf[...] = x_buf[...] * b_buf[...]
+    stores = copies_of([(a_buf, oa_ref.at[part]), (b_buf, ob_ref.at[part])], sem.at[1])
+    start_all(stores)
+    wait_all(stores)
+
+
+def gate_far_kernel(planes, width, *refs):
     far_refs, refs = refs[: planes - 1], refs[planes - 1 :]
-    a_ref, b_ref, near_ref, oa_ref, ob_ref, x_buf, a_buf, b_buf, sem = refs
+    a_ref, b_ref, _, _, _, oa_ref, ob_ref, a_buf, b_buf, sem = refs
     z = plane(width)
-    load = pltpu.make_async_copy(near_ref.at[:, z], x_buf, sem.at[planes, 0])
-    load.start()
-
-    def read():
-        load.wait()
-        return x_buf[...]
-
     blocks = [(lambda d=d: far_refs[d - 1][...], (z ^ d) * width) for d in range(1, planes)]
-    blocks.append((read, z * width))
     gate_parts(width, blocks, a_ref, b_ref, (oa_ref, ob_ref), a_buf, b_buf, sem)
 
 
 SPACES = {"v": pltpu.VMEM, "u": pltpu.VMEM, "h": pltpu.HBM, "a": pl.ANY}
 
 
-def kernel_call(body, ins, outs, scratch, flops=0):
+def kernel_call(body, ins, outs, scratch, flops=0, aliases=None):
     shapes = [
         jax.ShapeDtypeStruct(shape, jnp.float32) if space == "u" else SPACES[space](shape, jnp.float32)
         for space, shape in outs
@@ -402,6 +410,7 @@
             out_specs=[pl.BlockSpec(memory_space=SPACES[space]) for space, _ in outs],
             out_shape=shapes,
             scratch_shapes=scratch,
+            input_output_aliases=aliases or {},
             compiler_params=pltpu.CompilerParams(vmem_limit_bytes=VMEM_BYTES),
             cost_estimate=pl.CostEstimate(flops=flops, bytes_accessed=4 * size, transcendentals=0),
         )(*args)
@@ -422,7 +431,7 @@
     def pair(table):
         hi = table.astype(ml_dtypes.bfloat16)
         lo = (table - hi.astype(np.float64)).astype(ml_dtypes.bfloat16)
-        return jnp.asarray(np.stack([hi, lo]))
+        return jnp.asarray(np.concatenate([hi, hi, lo]))
 
     fwd = pair(np.block([[c, -s], [s, c]]))
     inv = pair(np.block([[c, s], [-s, c]]) / length)
@@ -468,15 +477,14 @@
     by_plane = pltpu.VMEM((planes, *one), f32)
     outs = [("h", one)] * (planes - 1)
     send = kernel_call(
-        part(send_kernel, planes, width), "h", outs, [by_plane, semaphores(planes, planes + PARTS)]
+        part(send_kernel, planes, width), "a", outs, [by_plane, semaphores(planes, planes + PARTS)]
     )
     merge = kernel_call(
-        part(merge_kernel, planes, width), "h" * planes + "a", [("h", paired)],
+        part(merge_kernel, planes, width), "a" * planes + "a", [("h", paired)],
         [paired_buf, semaphores(PARTS + 1, planes + PARTS)],
     )
     half_sizes = (n, channels // 2, tokens)
     half_spectrum = (n, channels // 2, 2 * tokens)
-
     def transform_filters(first):
         return kernel_call(
             part(filter_kernel, first, *half_sizes), "hvv", [("h", half_spectrum)],
@@ -520,7 +528,7 @@
         product_ch = within_plane(*merge(keep_p, *got_p, send_g))
         filt = (filt_a, transform_filters(channels // 2))
         *outs, prod_spec = kernel_call(
-            part(conv_kernel, planes, *sizes), "hvvvhh",
+            part(conv_kernel, planes, *sizes), "avvvhh",
             [("h", one)] * planes + [("h", spectrum)], transform_scratch, 2 * flops,
         )(product_ch, tw, fwd, inv, *filt)
         return outs, prod_spec, filt
@@ -530,7 +538,7 @@
 
     def third(near_g, far_g, filt, keep_c, prod_spec):
         back_ch, grad_spec = kernel_call(
-            part(back_kernel, planes, *sizes), "h" * planes + "vvvhha",
+            part(back_kernel, planes, *sizes), "a" * planes + "vvvhha",
             [("h", paired), ("h", spectrum)], transform_scratch, 2 * flops,
         )(near_g, *far_g, tw, fwd, inv, *filt, keep_c)
         near_b = within_plane(back_ch)
@@ -543,25 +551,30 @@
     near_b, send_b, own = grouped(third, near_g, far_g, filt, keep_c, prod_spec)
     far_b = along_z(send_b)
 
-    def fourth(keep_c, got_c, send_b, query, cot, own):
-        conv_tok = within_plane(*merge(keep_c, *got_c, send_b))
+    def fourth(keep_c, got_c, query, cot, near_b, value, key, own):
         if pair_size == 2:
-            grad_filter = own + lax.ppermute(own, "dp", [(0, 1), (1, 0)])
+            other = lax.ppermute(own, "dp", [(0, 1), (1, 0)])
         else:
-            grad_filter = lax.psum(own, "dp")
+            other = lax.psum(own, "dp") - own
+        conv_tok = within_plane(*merge(keep_c, *got_c, other))
+        (grad_filter,) = kernel_call(add_kernel, "vv", [("u", lags)], [])(own, other)
+        begun = kernel_call(
+            part(gate_near_kernel, planes, width), "ahh", [("h", blocks)] * 2,
+            [pltpu.VMEM(one, f32)] * 3 + [semaphores(2, 3)],
+        )(near_b, value, key)
         gated, grad_query = kernel_call(
-            part(gate_kernel, planes, width), "hhh", [("h", blocks)] * 2,
+            part(gate_kernel, planes, width), "ahh", [("h", blocks)] * 2,
             [by_plane, *[rows] * 4, semaphores(2 * planes, 3)],
         )(conv_tok, query, cot)
-        return gated, grad_query, grad_filter
-
-    gated, grad_query, grad_filter = grouped(
-        fourth, keep_c, got_c, send_b[0], query, cot, own
+        return gated, grad_query, begun, grad_filter
+
+    gated, grad_query, begun, grad_filter = grouped(
+        fourth, keep_c, got_c, query, cot, near_b, value, key, own
     )
     grad_key, grad_value = kernel_call(
-        part(gate_split_kernel, planes, width), "v" * (planes + 1) + "h", [("h", blocks)] * 2,
-        [pltpu.VMEM(one, f32), rows, rows, semaphores(planes + 1, 2)],
-    )(*far_b, value, key, near_b)
+        part(gate_far_kernel, planes, width), "v" * (planes + 1) + "hha", [("h", blocks)] * 2,
+        [rows, rows, semaphores(planes, 2)], aliases={planes + 1: 0, planes + 2: 1},
+    )(*far_b, value, key, *begun, gated)
     shape = query_input.shape
     return (
         gated.reshape(shape),

time: 126 us -> 126 us (level)
  blocking collectives: 18.7 us -> 0 us
  waiting for transfers between devices: 28.4 us -> 42 us
  Pallas kernels: 41.2 us -> 45 us
  starting transfers between devices: 31.1 us -> 34.4 us
  local copies, waits for them, and re-layouts: 5.01 us -> 2.98 us
    all_to_all x1 -> x0, blocking collectives: 18.7 us -> none  [within_plane(): lax.all_to_all(x, 'context', 0, 0, axis_index_groups=members, tiled=True)]
    all_to_all x3 -> x4, waiting for transfers between devices: 28.4 us -> 39.3 us  [within_plane(): lax.all_to_all(x, 'context', 0, 0, axis_index_groups=members, tiled=True)]
    pallas_call x13 -> x15, Pallas kernels: 41.2 us -> 45 us  [run(): pl.pallas_call(body, in_specs=[pl.BlockSpec(memory_space=SPACES[space]) f...]
    all_to_all x3 -> x4, starting transfers between devices: 12.1 us -> 15.6 us  [within_plane(): lax.all_to_all(x, 'context', 0, 0, axis_index_groups=members, tiled=True)]
    ppermute x1, waiting for transfers between devices: 0.01 us -> 2.66 us  [fourth(): other = lax.ppermute(own, 'dp', [(0, 1), (1, 0)])]
    cond x20 -> x7, local copies, waits for them, and re-layouts: 3.3 us -> 2.23 us
  transfers between devices with their start and end apart: 16 -> 17, of which waited for: 3 -> 5; matrix products, arithmetic and copies ran while one was open for 0% -> 1% of each run, Pallas kernels for 30% -> 32%
where the time goes in v7:
time: 126 us; the launch traced here: 125 us
  Pallas kernels  45 us (36%)
  waiting for transfers between devices  42 us (33%)
  starting transfers between devices  34.4 us (27%)
  local copies, waits for them, and re-layouts  2.98 us (2%)
    pallas_call x15, Pallas kernels, run(): pl.pallas_call(body, in_specs=[pl.BlockSpec(memory_space=SPACES[space]) f...  45 us
    all_to_all x4, waiting for transfers between devices, within_plane(): lax.all_to_all(x, 'context', 0, 0, axis_index_groups=members, tiled=True)  39.3 us
    ppermute x12, starting transfers between devices, along_z(): lax.ppermute(x, 'context', [(i, i ^ d * width) for i in range(n)])  18.7 us
    all_to_all x4, starting transfers between devices, within_plane(): lax.all_to_all(x, 'context', 0, 0, axis_index_groups=members, tiled=True)  15.6 us
    ppermute x1, waiting for transfers between devices, fourth(): other = lax.ppermute(own, 'dp', [(0, 1), (1, 0)])  2.66 us
  transfers between devices with their start and end apart: 17, of which 5 were waited for; matrix products, arithmetic and copies ran while one was open for 1% of the time, Pallas kernels for 32%

profile of v7, /device:TPU:0, one launch (start us, length us, event | category | flops | bytes accessed | tf_op | source)
XLA Modules:
  0.0 125.2 jit_solution(336093687625435966)
XLA Ops:
  2.5 3.1 %collective-permute-start.4 = (f32[4,128,128]{2,1,0:T(8,128)S(1)}, f32[4,128,128]{2,1,0:T(8,128)S(1)}, u32[]{:S(2)}, u32[]{:S(2)}) collective-permute-start(f32[4,128,128]{2,1,0:T(8,128)S(1)} %get-tuple-element.169), channel_id=1, source_target_pairs={{0,4},{1,5},{2,6},{3,7},{4,0},{5,1},{6,2},{7,3},{8,12},{9,13},{10,... | collective-permute-start | bytes 786440 | tf_op jit(solution)/shard_map/ppermute | solution.py:465
  5.6 2.6 %collective-permute-start.5 = (f32[4,128,128]{2,1,0:T(8,128)S(1)}, f32[4,128,128]{2,1,0:T(8,128)}, u32[]{:S(2)}, u32[]{:S(2)}) collective-permute-start(f32[4,128,128]{2,1,0:T(8,128)S(1)} %get-tuple-element.170), channel_id=1, source_target_pairs={{0,8},{1,9},{2,10},{3,11},{4,12},{5,13},{6,14},{7,15},{8,0},{9,1},... | collective-permute-start | bytes 786440 | tf_op jit(solution)/shard_map/ppermute | solution.py:465
  8.2 22.0 %conditional.4 = (f32[4,4,128,128]{3,2,1,0:T(8,128)}, f32[4,128,128]{2,1,0:T(8,128)}, f32[4,128,128]{2,1,0:T(8,128)}, f32[4,128,128]{2,1,0:T(8,128)}, f32[16,64,256]{2,1,0:T(8,128)}) conditional(s32[]{:T(128)} %convert_element_type.2, () %tuple.46, (f32[16,128,128]{2,1,0:T(8,128)S(1)}, f32[16,128,128]{2,1,0:T(8,128)}, f32[4,128,128]{2,1,0:T(8,128)S(1)}, ...), branch_computations={%region_0.0_spmd, %region_1.0_spmd} | conditional | flops 268435456 | bytes 11403336 | solution.py:508
  10.4 4.3 %all-to-all-start = ((f32[4,4,128,128]{3,2,1,0:T(8,128)}), f32[4,4,128,128]{3,2,1,0:T(8,128)}, u32[]{:S(2)}, u32[]{:S(2)}) async-start(f32[4,4,128,128]{3,2,1,0:T(8,128)} %branch_1_fun.13), calls=%async_computation | async-start | bytes 2097152 | tf_op jit(solution)/shard_map/cond/branch_1_fun/all_to_all | solution.py:471
  14.7 2.8 %branch_1_fun.15 = f32[16,64,256]{2,1,0:T(8,128)} custom-call(f32[128,2048]{1,0:T(8,128)} %get-tuple-element.82.refs_0_, f32[2,16,8,128]{3,2,1,0:T(8,128)S(1)} %get-tuple-element.83.refs_1_, bf16[768,256]{1,0:T(8,128)(2,1)S(1)} %get-tuple-element.84.refs_2_), custom_call_target="tpu_custom_call" | custom-call | flops 268435456 | bytes 3014656 | tf_op jit(solution)/shard_map/cond/branch_1_fun/pallas_call | solution.py:407
  17.4 10.7 %all-to-all-done.refs_0_ = f32[4,4,128,128]{3,2,1,0:T(8,128)} async-done(((f32[4,4,128,128]{3,2,1,0:T(8,128)}), f32[4,4,128,128]{3,2,1,0:T(8,128)}, u32[]{:S(2)}, u32[]{:S(2)}) %all-to-all-start) | async-done | bytes 1048608 | tf_op jit(solution)/shard_map/cond/branch_1_fun/all_to_all | solution.py:471
  34.4 24.9 %conditional.5 = (f32[4,128,128]{2,1,0:T(8,128)}, f32[4,128,128]{2,1,0:T(8,128)}, f32[4,128,128]{2,1,0:T(8,128)}, f32[4,128,128]{2,1,0:T(8,128)}, f32[16,128,256...) conditional(s32[]{:T(128)} %convert_element_type.2, () %tuple.48, (f32[4,128,128]{2,1,0:T(8,128)S(1)}, ...), branch_computations={%region_2.0_spmd, %region_3.0_spmd} | conditional | flops 1342177280 | bytes 16515160 | solution.py:508
  34.4 2.7 %branch_1_fun.16 = f32[4,4,128,128]{3,2,1,0:T(8,128)} custom-call(f32[4,128,128]{2,1,0:T(8,128)S(1)} %get-tuple-element.85.refs_0_, f32[4,128,128]{2,1,0:T(8,128)S(1)} %get-tuple-element.86.refs_1_, f32[4,128,128]{2,1,0:T(8,128)} %get-tuple-element.87.refs_2_, f32[4,128,128]{2,1,0:T(8,128)} %get-tuple-element.88.refs_3_, ...), custom_call_target="tpu_custom_call" | custom-call | bytes 2359296 | tf_op jit(solution)/shard_map/cond/branch_1_fun/pallas_call | solution.py:407
  37.1 3.5 %all-to-all-start.1 = ((f32[4,4,128,128]{3,2,1,0:T(8,128)}), f32[4,4,128,128]{3,2,1,0:T(8,128)S(1)}, u32[]{:S(2)}, u32[]{:S(2)}) async-start(f32[4,4,128,128]{3,2,1,0:T(8,128)} %branch_1_fun.16), calls=%async_computation.1 | async-start | bytes 2097152 | tf_op jit(solution)/shard_map/cond/branch_1_fun/all_to_all | solution.py:471
  40.6 2.8 %branch_1_fun.17.refs_5_ = f32[16,64,256]{2,1,0:T(8,128)} custom-call(f32[128,2048]{1,0:T(8,128)} %get-tuple-element.94.refs_0_, f32[2,16,8,128]{3,2,1,0:T(8,128)S(1)} %get-tuple-element.90.refs_1_, bf16[768,256]{1,0:T(8,128)(2,1)S(1)} %get-tuple-element.91.refs_2_), custom_call_target="tpu_custom_call" | custom-call | flops 268435456 | bytes 3014656 | tf_op jit(solution)/shard_map/cond/branch_1_fun/pallas_call | solution.py:407
  43.4 9.7 %all-to-all-done.1.refs_0_ = f32[4,4,128,128]{3,2,1,0:T(8,128)S(1)} async-done(((f32[4,4,128,128]{3,2,1,0:T(8,128)}), f32[4,4,128,128]{3,2,1,0:T(8,128)S(1)}, u32[]{:S(2)}, u32[]{:S(2)}) %all-to-all-start.1) | async-done | bytes 1048608 | tf_op jit(solution)/shard_map/cond/branch_1_fun/all_to_all | solution.py:471
  53.1 6.2 %branch_1_fun.18 = (f32[4,128,128]{2,1,0:T(8,128)}, f32[4,128,128]{2,1,0:T(8,128)}, f32[4,128,128]{2,1,0:T(8,128)}, f32[4,128,128]{2,1,0:T(8,128)}, f32[16,128,256]{2,1,0:T(8,128)}) custom-call(f32[4,4,128,128]{3,2,1,0:T(8,128)S(1)} %all-to-all-done.1.refs_0_, f32[2,16,8,128]{3,2,1,0:T(8,128)S(1)} %get-tuple-element.90.refs_1_, ...), custom_call_target="tpu_custom_call" | custom-call | flops 1073741824 | bytes 7995392 | tf_op jit(solution)/shard_map/cond/branch_1_fun/pallas_call | solution.py:407
  63.8 25.6 %conditional.6 = (f32[4,4,128,128]{3,2,1,0:T(8,128)}, f32[4,128,128]{2,1,0:T(8,128)}, f32[4,128,128]{2,1,0:T(8,128)}, f32[4,128,128]{2,1,0:T(8,128)}, f32[128,2048]{1,0:T(8,128)S(1)}) conditional(s32[]{:T(128)} %convert_element_type.2, () %tuple.45, (f32[4,4,128,128]{3,2,1,0:T(8,128)}, f32[4,128,128]{2,1,0:T(8,128)}, f32[4,128,128]{2,1,0:T(8,128)S(1)}, ...), branch_computations={%region_4.0_spmd, %region_5.0_spmd} | conditional | flops 1610612736 | bytes 20185160 | solution.py:508
  63.8 6.9 %branch_1_fun.19 = (f32[4,4,128,128]{3,2,1,0:T(8,128)}, f32[16,128,256]{2,1,0:T(8,128)}) custom-call(f32[4,4,128,128]{3,2,1,0:T(8,128)} %get-tuple-element.100.refs_0_, f32[4,128,128]{2,1,0:T(8,128)} %get-tuple-element.101.refs_1_, f32[4,128,128]{2,1,0:T(8,128)S(1)} %get-tuple-element.102.refs_2_, f32[4,128,128]{2,1,0:T(8,128)} %get-tuple-element.103.refs_3_, ...), custom_call_target="tpu_custom_call" | custom-call | flops 1073741824 | bytes 9043968 | tf_op jit(solution)/shard_map/cond/branch_1_fun/pallas_call | solution.py:407
  70.6 4.3 %all-to-all-start.2 = ((f32[4,4,128,128]{3,2,1,0:T(8,128)}), f32[4,4,128,128]{3,2,1,0:T(8,128)}, u32[]{:S(2)}, u32[]{:S(2)}) async-start(f32[4,4,128,128]{3,2,1,0:T(8,128)} %get-tuple-element.110), calls=%async_computation.2 | async-start | bytes 2097152 | tf_op jit(solution)/shard_map/cond/branch_1_fun/all_to_all | solution.py:471
  74.9 4.4 %branch_1_fun.21 = f32[128,2048]{1,0:T(8,128)S(1)} custom-call(f32[2,16,8,128]{3,2,1,0:T(8,128)S(1)} %get-tuple-element.104.refs_4_.refs_0_, bf16[768,256]{1,0:T(8,128)(2,1)S(1)} %get-tuple-element.106.refs_6_.refs_1_, f32[16,128,256]{2,1,0:T(8,128)} %get-tuple-element.114.refs_2_, f32[16,128,256]{2,1,0:T(8,128)} %get-tuple-element.115.refs_3_), custom_call_target="tpu_custom_call" | custom-call | flops 536870912 | bytes 6160384 | tf_op jit(solution)/shard_map/cond/branch_1_fun/pallas_call | solution.py:407
  79.3 7.9 %all-to-all-done.2.refs_0_ = f32[4,4,128,128]{3,2,1,0:T(8,128)} async-done(((f32[4,4,128,128]{3,2,1,0:T(8,128)}), f32[4,4,128,128]{3,2,1,0:T(8,128)}, u32[]{:S(2)}, u32[]{:S(2)}) %all-to-all-start.2) | async-done | bytes 1048608 | tf_op jit(solution)/shard_map/cond/branch_1_fun/all_to_all | solution.py:471
  90.2 2.5 %collective-permute-start.11 = (f32[4,128,128]{2,1,0:T(8,128)}, f32[4,128,128]{2,1,0:T(8,128)S(1)}, u32[]{:S(2)}, u32[]{:S(2)}) collective-permute-start(f32[4,128,128]{2,1,0:T(8,128)} %get-tuple-element.185), channel_id=1, source_target_pairs={{0,8},{1,9},{2,10},{3,11},{4,12},{5,13},{6,14},{7,15},{8,0},{9,1},... | collective-permute-start | bytes 786440 | tf_op jit(solution)/shard_map/ppermute | solution.py:465
  94.5 27.5 %conditional.7 = (f32[16,128,128]{2,1,0:T(8,128)}, f32[16,128,128]{2,1,0:T(8,128)}, f32[16,128,128]{2,1,0:T(8,128)}, f32[128,2048]{1,0:T(8,128)}, f32[1,2048,128]{2,1,0:T(8,128)S(1)}, /*index=5*/f32[1,2048,128]{2,1,0:T(8,128)}) conditional(s32[]{:T(128)} %convert_element_type.2, () %tuple.44, (f32[128,2048]{1,0:T(8,128)S(1)}, ...), branch_computations={%region_6.0_spmd, %region_7.0_spmd} | conditional | bytes 38797516 | solution.py:508
  95.6 2.7 %collective-permute-done.refs_4_.b_ref = f32[128,2048]{1,0:T(8,128)S(1)} collective-permute-done((f32[128,2048]{1,0:T(8,128)S(1)}, f32[128,2048]{1,0:T(8,128)S(1)}, u32[]{:S(2)}, u32[]{:S(2)}) %collective-permute-start) | collective-permute-done | bytes 1048608 | tf_op jit(solution)/shard_map/cond/branch_1_fun/ppermute | solution.py:556
  100.5 3.5 %all-to-all-start.3 = ((f32[4,4,128,128]{3,2,1,0:T(8,128)}), f32[4,4,128,128]{3,2,1,0:T(8,128)S(1)}, u32[]{:S(2)}, u32[]{:S(2)}) async-start(f32[4,4,128,128]{3,2,1,0:T(8,128)} %branch_1_fun.22), calls=%async_computation.3 | async-start | bytes 2097152 | tf_op jit(solution)/shard_map/cond/branch_1_fun/all_to_all | solution.py:471
  107.2 11.0 %all-to-all-done.3.refs_0_ = f32[4,4,128,128]{3,2,1,0:T(8,128)S(1)} async-done(((f32[4,4,128,128]{3,2,1,0:T(8,128)}), f32[4,4,128,128]{3,2,1,0:T(8,128)S(1)}, u32[]{:S(2)}, u32[]{:S(2)}) %all-to-all-start.3) | async-done | bytes 1048608 | tf_op jit(solution)/shard_map/cond/branch_1_fun/all_to_all | solution.py:471
  118.2 2.6 %branch_1_fun.23 = (f32[16,128,128]{2,1,0:T(8,128)}, f32[16,128,128]{2,1,0:T(8,128)}) custom-call(f32[4,4,128,128]{3,2,1,0:T(8,128)S(1)} %all-to-all-done.3.refs_0_, f32[16,128,128]{2,1,0:T(8,128)} %get-tuple-element.121.refs_1_, f32[16,128,128]{2,1,0:T(8,128)} %copy-done.2), custom_call_target="tpu_custom_call" | custom-call | bytes 5242880 | tf_op jit(solution)/shard_map/cond/branch_1_fun/pallas_call | solution.py:407
  122.1 3.1 %shard_map.120 = (f32[16,128,128]{2,1,0:T(8,128)}, f32[16,128,128]{2,1,0:T(8,128)}) custom-call(f32[4,128,128]{2,1,0:T(8,128)S(1)} %collective-permute-done.10.refs_0_, f32[4,128,128]{2,1,0:T(8,128)S(1)} %collective-permute-done.11.refs_1_, f32[4,128,128]{2,1,0:T(8,128)S(1)} %collective-permute-done.12.refs_2_, ...), custom_call_target="tpu_custom_call", output_to_operand_aliasing={{0}: (5, {}), {1}: (6, {})} | custom-call | bytes 8126464 | tf_op jit(solution)/shard_map/pallas_call | solution.py:407
  (48 shorter events, 27.3 us)
Async XLA Ops:
  0.6 7.5 %copy-start.6 = (f32[2,16,8,128]{3,2,1,0:T(8,128)S(1)}, f32[2,16,8,128]{3,2,1,0:T(8,128)}, u32[]{:S(2)}) copy-start(f32[2,16,8,128]{3,2,1,0:T(8,128)} %constant.18.clone) | copy-start | bytes 393220
  0.6 7.5 %copy-start = (bf16[768,256]{1,0:T(8,128)(2,1)S(1)}, bf16[768,256]{1,0:T(8,128)(2,1)}, u32[]{:S(2)}) copy-start(bf16[768,256]{1,0:T(8,128)(2,1)} %constant.5.clone) | copy-start | bytes 1179652
  0.7 7.5 %copy-start.1 = (f32[1,2048,128]{2,1,0:T(8,128)S(1)}, f32[1,2048,128]{2,1,0:T(8,128)}, u32[]{:S(2)}) copy-start(f32[1,2048,128]{2,1,0:T(8,128)} %param.20) | copy-start | bytes 3145732
  2.5 31.4 %collective-permute-start.4 = (f32[4,128,128]{2,1,0:T(8,128)S(1)}, f32[4,128,128]{2,1,0:T(8,128)S(1)}, u32[]{:S(2)}, u32[]{:S(2)}) collective-permute-start(f32[4,128,128]{2,1,0:T(8,128)S(1)} %get-tuple-element.169), channel_id=1, source_target_pairs={{0,4},{1,5},{2,6},{3,7},{4,0},{5,1},{6,2},{7,3},{8,12},{9,13},{10,... | collective-permute-start | bytes 786440 | tf_op jit(solution)/shard_map/ppermute | solution.py:465
  5.6 28.8 %collective-permute-start.5 = (f32[4,128,128]{2,1,0:T(8,128)S(1)}, f32[4,128,128]{2,1,0:T(8,128)}, u32[]{:S(2)}, u32[]{:S(2)}) collective-permute-start(f32[4,128,128]{2,1,0:T(8,128)S(1)} %get-tuple-element.170), channel_id=1, source_target_pairs={{0,8},{1,9},{2,10},{3,11},{4,12},{5,13},{6,14},{7,15},{8,0},{9,1},... | collective-permute-start | bytes 786440 | tf_op jit(solution)/shard_map/ppermute | solution.py:465
  8.1 26.2 %collective-permute-start.6 = (f32[4,128,128]{2,1,0:T(8,128)S(1)}, f32[4,128,128]{2,1,0:T(8,128)}, u32[]{:S(2)}, u32[]{:S(2)}) collective-permute-start(f32[4,128,128]{2,1,0:T(8,128)S(1)} %get-tuple-element.171), channel_id=1, source_target_pairs={{0,12},{1,13},{2,14},{3,15},{4,8},{5,9},{6,10},{7,11},{8,4},{9,5},... | collective-permute-start | bytes 786440 | tf_op jit(solution)/shard_map/ppermute | solution.py:465
  8.2 26.2 %copy-start.5 = (bf16[768,256]{1,0:T(8,128)(2,1)S(1)}, bf16[768,256]{1,0:T(8,128)(2,1)}, u32[]{:S(2)}) copy-start(bf16[768,256]{1,0:T(8,128)(2,1)} %constant.7.clone) | copy-start | bytes 1179652
  10.4 17.7 %all-to-all-start = ((f32[4,4,128,128]{3,2,1,0:T(8,128)}), f32[4,4,128,128]{3,2,1,0:T(8,128)}, u32[]{:S(2)}, u32[]{:S(2)}) async-start(f32[4,4,128,128]{3,2,1,0:T(8,128)} %branch_1_fun.13), calls=%async_computation | async-start | bytes 2097152 | tf_op jit(solution)/shard_map/cond/branch_1_fun/all_to_all | solution.py:471
  30.2 32.4 %collective-permute-start.2 = (f32[4,128,128]{2,1,0:T(8,128)}, f32[4,128,128]{2,1,0:T(8,128)S(1)}, u32[]{:S(2)}, u32[]{:S(2)}) collective-permute-start(f32[4,128,128]{2,1,0:T(8,128)} %get-tuple-element.167), channel_id=1, source_target_pairs={{0,8},{1,9},{2,10},{3,11},{4,12},{5,13},{6,14},{7,15},{8,0},{9,1},... | collective-permute-start | bytes 786440 | tf_op jit(solution)/shard_map/ppermute | solution.py:465
  31.9 31.9 %collective-permute-start.3 = (f32[4,128,128]{2,1,0:T(8,128)}, f32[4,128,128]{2,1,0:T(8,128)}, u32[]{:S(2)}, u32[]{:S(2)}) collective-permute-start(f32[4,128,128]{2,1,0:T(8,128)} %get-tuple-element.168), channel_id=1, source_target_pairs={{0,12},{1,13},{2,14},{3,15},{4,8},{5,9},{6,10},{7,11},{8,4},{9,5},... | collective-permute-start | bytes 786440 | tf_op jit(solution)/shard_map/ppermute | solution.py:465
  33.9 29.9 %collective-permute-start.1 = (f32[4,128,128]{2,1,0:T(8,128)}, f32[4,128,128]{2,1,0:T(8,128)}, u32[]{:S(2)}, u32[]{:S(2)}) collective-permute-start(f32[4,128,128]{2,1,0:T(8,128)} %get-tuple-element.166), channel_id=1, source_target_pairs={{0,4},{1,5},{2,6},{3,7},{4,0},{5,1},{6,2},{7,3},{8,12},{9,13},{10,... | collective-permute-start | bytes 786440 | tf_op jit(solution)/shard_map/ppermute | solution.py:465
  37.1 16.0 %all-to-all-start.1 = ((f32[4,4,128,128]{3,2,1,0:T(8,128)}), f32[4,4,128,128]{3,2,1,0:T(8,128)S(1)}, u32[]{:S(2)}, u32[]{:S(2)}) async-start(f32[4,4,128,128]{3,2,1,0:T(8,128)} %branch_1_fun.16), calls=%async_computation.1 | async-start | bytes 2097152 | tf_op jit(solution)/shard_map/cond/branch_1_fun/all_to_all | solution.py:471
  59.3 33.3 %collective-permute-start.7 = (f32[4,128,128]{2,1,0:T(8,128)}, f32[4,128,128]{2,1,0:T(8,128)S(1)}, u32[]{:S(2)}, u32[]{:S(2)}) collective-permute-start(f32[4,128,128]{2,1,0:T(8,128)} %get-tuple-element.178), channel_id=1, source_target_pairs={{0,4},{1,5},{2,6},{3,7},{4,0},{5,1},{6,2},{7,3},{8,12},{9,13},{10,... | collective-permute-start | bytes 786440 | tf_op jit(solution)/shard_map/ppermute | solution.py:465
  60.9 33.6 %collective-permute-start.8 = (f32[4,128,128]{2,1,0:T(8,128)}, f32[4,128,128]{2,1,0:T(8,128)}, u32[]{:S(2)}, u32[]{:S(2)}) collective-permute-start(f32[4,128,128]{2,1,0:T(8,128)} %get-tuple-element.179), channel_id=1, source_target_pairs={{0,8},{1,9},{2,10},{3,11},{4,12},{5,13},{6,14},{7,15},{8,0},{9,1},... | collective-permute-start | bytes 786440 | tf_op jit(solution)/shard_map/ppermute | solution.py:465
  62.6 32.0 %collective-permute-start.9 = (f32[4,128,128]{2,1,0:T(8,128)}, f32[4,128,128]{2,1,0:T(8,128)}, u32[]{:S(2)}, u32[]{:S(2)}) collective-permute-start(f32[4,128,128]{2,1,0:T(8,128)} %get-tuple-element.180), channel_id=1, source_target_pairs={{0,12},{1,13},{2,14},{3,15},{4,8},{5,9},{6,10},{7,11},{8,4},{9,5},... | collective-permute-start | bytes 786440 | tf_op jit(solution)/shard_map/ppermute | solution.py:465
  70.6 16.6 %all-to-all-start.2 = ((f32[4,4,128,128]{3,2,1,0:T(8,128)}), f32[4,4,128,128]{3,2,1,0:T(8,128)}, u32[]{:S(2)}, u32[]{:S(2)}) async-start(f32[4,4,128,128]{3,2,1,0:T(8,128)} %get-tuple-element.110), calls=%async_computation.2 | async-start | bytes 2097152 | tf_op jit(solution)/shard_map/cond/branch_1_fun/all_to_all | solution.py:471
  89.4 32.7 %collective-permute-start.10 = (f32[4,128,128]{2,1,0:T(8,128)}, f32[4,128,128]{2,1,0:T(8,128)S(1)}, u32[]{:S(2)}, u32[]{:S(2)}) collective-permute-start(f32[4,128,128]{2,1,0:T(8,128)} %get-tuple-element.184), channel_id=1, source_target_pairs={{0,4},{1,5},{2,6},{3,7},{4,0},{5,1},{6,2},{7,3},{8,12},{9,13},{10,... | collective-permute-start | bytes 786440 | tf_op jit(solution)/shard_map/ppermute | solution.py:465
  90.2 31.9 %collective-permute-start.11 = (f32[4,128,128]{2,1,0:T(8,128)}, f32[4,128,128]{2,1,0:T(8,128)S(1)}, u32[]{:S(2)}, u32[]{:S(2)}) collective-permute-start(f32[4,128,128]{2,1,0:T(8,128)} %get-tuple-element.185), channel_id=1, source_target_pairs={{0,8},{1,9},{2,10},{3,11},{4,12},{5,13},{6,14},{7,15},{8,0},{9,1},... | collective-permute-start | bytes 786440 | tf_op jit(solution)/shard_map/ppermute | solution.py:465
  93.4 28.7 %collective-permute-start.12 = (f32[4,128,128]{2,1,0:T(8,128)}, f32[4,128,128]{2,1,0:T(8,128)S(1)}, u32[]{:S(2)}, u32[]{:S(2)}) collective-permute-start(f32[4,128,128]{2,1,0:T(8,128)} %get-tuple-element.186), channel_id=1, source_target_pairs={{0,12},{1,13},{2,14},{3,15},{4,8},{5,9},{6,10},{7,11},{8,4},{9,5},... | collective-permute-start | bytes 786440 | tf_op jit(solution)/shard_map/ppermute | solution.py:465
  95.5 5.0 %copy-start.3 = (f32[128,2048]{1,0:T(8,128)}, f32[128,2048]{1,0:T(8,128)S(1)}, u32[]{:S(2)}) copy-start(f32[128,2048]{1,0:T(8,128)S(1)} %get-tuple-element.120.a_ref) | copy-start | bytes 3145732 | tf_op jit(solution)/shard_map/cond
  95.5 2.7 %collective-permute-start = (f32[128,2048]{1,0:T(8,128)S(1)}, f32[128,2048]{1,0:T(8,128)S(1)}, u32[]{:S(2)}, u32[]{:S(2)}) collective-permute-start(f32[128,2048]{1,0:T(8,128)S(1)} %get-tuple-element.120.a_ref), channel_id=1, source_target_pairs={{0,16},{16,0},{1,17},{17,1},{2,18},{18,2},{3,19},{19,3},{4,20},{20... | collective-permute-start | bytes 3145736 | tf_op jit(solution)/shard_map/cond/branch_1_fun/ppermute | solution.py:556
  100.5 17.7 %all-to-all-start.3 = ((f32[4,4,128,128]{3,2,1,0:T(8,128)}), f32[4,4,128,128]{3,2,1,0:T(8,128)S(1)}, u32[]{:S(2)}, u32[]{:S(2)}) async-start(f32[4,4,128,128]{3,2,1,0:T(8,128)} %branch_1_fun.22), calls=%async_computation.3 | async-start | bytes 2097152 | tf_op jit(solution)/shard_map/cond/branch_1_fun/all_to_all | solution.py:471
  104.1 2.1 %copy-start.4 = (f32[128,2048]{1,0:T(8,128)S(1)}, f32[128,2048]{1,0:T(8,128)}, u32[]{:S(2)}) copy-start(f32[128,2048]{1,0:T(8,128)} %copy-done.3) | copy-start | bytes 3145732 | tf_op jit(solution)/shard_map/cond
  122.1 3.2 %copy-start.7 = (f32[1,2048,128]{2,1,0:T(8,128)}, f32[1,2048,128]{2,1,0:T(8,128)S(1)}, u32[]{:S(2)}) copy-start(f32[1,2048,128]{2,1,0:T(8,128)S(1)} %get-tuple-element.159) | copy-start | bytes 3145732
  (2 other events, 1.7 us)

commit v8 on v7

--- a/solution.py
+++ b/solution.py
@@ -139,7 +139,7 @@
 
 
 def transform(
-    sign, n, channels, tokens, sources, targets, tw_ref, fwd_ref, inv_ref, spec_refs, own_ref,
+    sign, n, channels, tokens, read, sources, targets, tw_ref, fwd_ref, inv_ref, spec_refs, own_ref,
     buf_ref, spec_buf, own_buf, y_ref, sem,
 ):
     half = channels // 2
@@ -161,7 +161,7 @@
         start_all(load)
     for part, load in zip(rows, loads):
         wait_all(load)
-        outer_forward(lambda n1, r: buf_ref[n1, r], n, part, tokens, tw_ref, y_ref)
+        outer_forward(read, n, part, tokens, tw_ref, y_ref)
     own_stores = copies_of([(own_buf.at[ms], own_ref.at[ms]) for ms in parts_of(n)], sem.at[2, 0])
     for ms, load, store in zip(parts_of(n), spec_loads, own_stores):
         own = times_table(flat(y_ref[ms]), fwd_ref)
@@ -195,14 +195,17 @@
     def block(d, part):
         return buf_ref.at[pl.ds((z ^ d) * width, width), part]
 
+    def read(n1, r):
+        return x_ref[n1 % width, z ^ (n1 // width), r]
+
     def sources(part):
-        return [(x_ref.at[:, d, part], block(d, part)) for d in range(planes)]
+        return []
 
     def targets(part):
         return [(block(d, part), out_refs[d].at[:, part]) for d in range(planes)]
 
     transform(
-        1.0, n, channels, tokens, sources, targets, *tables, spec_refs, own_ref, *scratch
+        1.0, n, channels, tokens, read, sources, targets, *tables, spec_refs, own_ref, *scratch
     )
 
 
@@ -218,16 +221,17 @@
         return buf_ref.at[pl.ds(z * width, width), part]
 
     def sources(part):
-        near = [(near_ref.at[:, z, part], block(z, part))]
-        return near + [
-            (ref.at[:, part], block(z ^ d, part)) for d, ref in enumerate(far_refs, 1)
-        ]
+        blocks = enumerate((near_ref, *far_refs))
+        return [(ref.at[:, part], block(z ^ d, part)) for d, ref in blocks]
+
+    def read(n1, r):
+        return buf_ref[n1, r]
 
     def targets(part):
         return [(block(z, part), out_ref.at[:, z, part]) for z in range(planes)]
 
     transform(
-        -1.0, n, channels, tokens, sources, targets, *tables, spec_refs, own_ref, *scratch
+        -1.0, n, channels, tokens, read, sources, targets, *tables, spec_refs, own_ref, *scratch
     )
 
 
@@ -297,35 +301,17 @@
 
 
 def send_kernel(planes, width, x_ref, *refs):
-    out_refs, (buf_ref, sem) = refs[: planes - 1], refs[planes - 1 :]
+    out_refs, sem = refs[:planes], refs[planes]
     z = plane(width)
-    parts = parts_of(width)
-    loads = [
-        copies_of([(x_ref.at[part, z ^ d], buf_ref.at[d, part]) for part in parts], sem.at[d])
-        for d in range(1, planes)
-    ]
-    for load in loads:
-        start_all(load)
-    stores = copies_of([(buf_ref.at[d + 1], ref) for d, ref in enumerate(out_refs)], sem.at[0])
-    for load, store in zip(loads, stores):
-        wait_all(load)
-        store.start()
+    stores = copies_of([(x_ref.at[:, z ^ d], ref) for d, ref in enumerate(out_refs)], sem)
+    start_all(stores)
     wait_all(stores)
 
 
 def merge_kernel(planes, width, *refs):
-    in_refs, (after_ref, out_ref, buf_ref, sem) = refs[:planes], refs[planes:]
-    parts = parts_of(width)
-    loads = [
-        copies_of([(ref.at[part], buf_ref.at[part, d]) for d, ref in enumerate(in_refs)], sem.at[i])
-        for i, part in enumerate(parts)
-    ]
-    for load in loads:
-        start_all(load)
-    stores = copies_of([(buf_ref.at[part], out_ref.at[part]) for part in parts], sem.at[len(parts)])
-    for load, store in zip(loads, stores):
-        wait_all(load)
-        store.start()
+    in_refs, (after_ref, out_ref, sem) = refs[:planes], refs[planes:]
+    stores = copies_of([(ref, out_ref.at[:, d]) for d, ref in enumerate(in_refs)], sem)
+    start_all(stores)
     wait_all(stores)
 
 
@@ -368,31 +354,47 @@
 def gate_near_kernel(
     planes, width, near_ref, a_ref, b_ref, oa_ref, ob_ref, x_buf, a_buf, b_buf, sem
 ):
-    z = plane(width)
-    part = pl.ds(z * width, width)
-    pairs = [(near_ref.at[:, z], x_buf), (a_ref.at[part], a_buf), (b_ref.at[part], b_buf)]
-    loads = copies_of(pairs, sem.at[0])
+    part = pl.ds(plane(width) * width, width)
+    loads = copies_of(
+        [(near_ref, x_buf), (a_ref.at[part], a_buf), (b_ref.at[part], b_buf)], sem.at[0]
+    )
     start_all(loads)
     wait_all(loads)
     a_buf[...] = x_buf[...] * a_buf[...]
     b_buf[...] = x_buf[...] * b_buf[...]
-    stores = copies_of([(a_buf, oa_ref.at[part]), (b_buf, ob_ref.at[part])], sem.at[1])
+    stores = copies_of([(a_buf, oa_ref), (b_buf, ob_ref)], sem.at[1])
     start_all(stores)
     wait_all(stores)
 
 
 def gate_far_kernel(planes, width, *refs):
     far_refs, refs = refs[: planes - 1], refs[planes - 1 :]
-    a_ref, b_ref, _, _, _, oa_ref, ob_ref, a_buf, b_buf, sem = refs
+    a_ref, b_ref, done_a, done_b, after_ref, oa_ref, ob_ref, a_buf, b_buf, sem = refs
     z = plane(width)
+    part = pl.ds(z * width, width)
+    loads = copies_of([(done_a, a_buf.at[part]), (done_b, b_buf.at[part])], sem.at[0])
+    start_all(loads)
     blocks = [(lambda d=d: far_refs[d - 1][...], (z ^ d) * width) for d in range(1, planes)]
-    gate_parts(width, blocks, a_ref, b_ref, (oa_ref, ob_ref), a_buf, b_buf, sem)
+    stores = []
+    for d, (read, first) in enumerate(blocks, 1):
+        rows = pl.ds(first, width)
+        x = read()
+        a_buf[rows] = x * a_ref[rows]
+        b_buf[rows] = x * b_ref[rows]
+        stores += copies_of([(a_buf.at[rows], oa_ref.at[rows]), (b_buf.at[rows], ob_ref.at[rows])], sem.at[d])
+        start_all(stores[-2:])
+    wait_all(loads)
+    stores += copies_of(
+        [(a_buf.at[part], oa_ref.at[part]), (b_buf.at[part], ob_ref.at[part])], sem.at[planes]
+    )
+    start_all(stores[-2:])
+    wait_all(stores)
 
 
 SPACES = {"v": pltpu.VMEM, "u": pltpu.VMEM, "h": pltpu.HBM, "a": pl.ANY}
 
 
-def kernel_call(body, ins, outs, scratch, flops=0, aliases=None):
+def kernel_call(body, ins, outs, scratch, flops=0):
     shapes = [
         jax.ShapeDtypeStruct(shape, jnp.float32) if space == "u" else SPACES[space](shape, jnp.float32)
         for space, shape in outs
@@ -410,7 +412,6 @@
             out_specs=[pl.BlockSpec(memory_space=SPACES[space]) for space, _ in outs],
             out_shape=shapes,
             scratch_shapes=scratch,
-            input_output_aliases=aliases or {},
             compiler_params=pltpu.CompilerParams(vmem_limit_bytes=VMEM_BYTES),
             cost_estimate=pl.CostEstimate(flops=flops, bytes_accessed=4 * size, transcendentals=0),
         )(*args)
@@ -475,13 +476,11 @@
     )
     rows, paired_buf = pltpu.VMEM(blocks, f32), pltpu.VMEM(paired, f32)
     by_plane = pltpu.VMEM((planes, *one), f32)
-    outs = [("h", one)] * (planes - 1)
     send = kernel_call(
-        part(send_kernel, planes, width), "a", outs, [by_plane, semaphores(planes, planes + PARTS)]
+        part(send_kernel, planes, width), "v", [("h", one)] * planes, [semaphores(planes)]
     )
     merge = kernel_call(
-        part(merge_kernel, planes, width), "a" * planes + "a", [("h", paired)],
-        [paired_buf, semaphores(PARTS + 1, planes + PARTS)],
+        part(merge_kernel, planes, width), "v" * planes + "a", [("h", paired)], [semaphores(planes)]
     )
     half_sizes = (n, channels // 2, tokens)
     half_spectrum = (n, channels // 2, 2 * tokens)
@@ -518,17 +517,16 @@
             part(product_kernel, planes, n), "hha", [("h", paired)],
             [rows, rows, by_plane, semaphores(planes + 1, planes)],
         )(cot, query, keep_p)
-        near_g = within_plane(conv_grad)
-        return near_g, send(near_g), transform_filters(0)
-
-    near_g, send_g, filt_a = grouped(first, cot, query, keep_p)
+        return send(within_plane(conv_grad)), transform_filters(0)
+
+    (near_g, *send_g), filt_a = grouped(first, cot, query, keep_p)
     far_g = along_z(send_g)
 
     def second(keep_p, got_p, send_g, filt_a):
         product_ch = within_plane(*merge(keep_p, *got_p, send_g))
         filt = (filt_a, transform_filters(channels // 2))
         *outs, prod_spec = kernel_call(
-            part(conv_kernel, planes, *sizes), "avvvhh",
+            part(conv_kernel, planes, *sizes), "vvvvhh",
             [("h", one)] * planes + [("h", spectrum)], transform_scratch, 2 * flops,
         )(product_ch, tw, fwd, inv, *filt)
         return outs, prod_spec, filt
@@ -541,14 +539,14 @@
             part(back_kernel, planes, *sizes), "a" * planes + "vvvhha",
             [("h", paired), ("h", spectrum)], transform_scratch, 2 * flops,
         )(near_g, *far_g, tw, fwd, inv, *filt, keep_c)
-        near_b = within_plane(back_ch)
+        sends = send(within_plane(back_ch))
         (own,) = kernel_call(
             part(filter_grad_kernel, scale, *sizes), "vvhh", [("u", lags)],
             [y, y, y, semaphores(PARTS, 2)], flops,
         )(tw, inv, prod_spec, grad_spec)
-        return near_b, send(near_b), own
-
-    near_b, send_b, own = grouped(third, near_g, far_g, filt, keep_c, prod_spec)
+        return sends, own
+
+    (near_b, *send_b), own = grouped(third, near_g, far_g, filt, keep_c, prod_spec)
     far_b = along_z(send_b)
 
     def fourth(keep_c, got_c, query, cot, near_b, value, key, own):
@@ -556,10 +554,10 @@
             other = lax.ppermute(own, "dp", [(0, 1), (1, 0)])
         else:
             other = lax.psum(own, "dp") - own
-        conv_tok = within_plane(*merge(keep_c, *got_c, other))
+        conv_tok = within_plane(*merge(keep_c, *got_c, near_b))
         (grad_filter,) = kernel_call(add_kernel, "vv", [("u", lags)], [])(own, other)
         begun = kernel_call(
-            part(gate_near_kernel, planes, width), "ahh", [("h", blocks)] * 2,
+            part(gate_near_kernel, planes, width), "ahh", [("h", one)] * 2,
             [pltpu.VMEM(one, f32)] * 3 + [semaphores(2, 3)],
         )(near_b, value, key)
         gated, grad_query = kernel_call(
@@ -572,8 +570,8 @@
         fourth, keep_c, got_c, query, cot, near_b, value, key, own
     )
     grad_key, grad_value = kernel_call(
-        part(gate_far_kernel, planes, width), "v" * (planes + 1) + "hha", [("h", blocks)] * 2,
-        [rows, rows, semaphores(planes, 2)], aliases={planes + 1: 0, planes + 2: 1},
+        part(gate_far_kernel, planes, width), "v" * (planes + 1) + "aaa", [("h", blocks)] * 2,
+        [rows, rows, semaphores(planes + 1, 2)],
     )(*far_b, value, key, *begun, gated)
     shape = query_input.shape
     return (

time: 126 us -> 122 us (0.968)
  waiting for transfers between devices: 42 us -> 38.9 us
    ppermute x1, waiting for transfers between devices: 2.66 us -> 0.01 us  [fourth(): other = lax.ppermute(own, 'dp', [(0, 1), (1, 0)])]
    cond x7 -> x17, local copies, waits for them, and re-layouts: 2.23 us -> 3.26 us
  transfers between devices with their start and end apart: 17 -> 17, of which waited for: 5 -> 4; matrix products, arithmetic and copies ran while one was open for 1% -> 2% of each run, Pallas kernels for 32% -> 32%
where the time goes in v8:
time: 122 us
  Pallas kernels  44.7 us (37%)
  waiting for transfers between devices  38.9 us (32%)
  starting transfers between devices  33.8 us (28%)
  local copies, waits for them, and re-layouts  3.28 us (3%)
    pallas_call x15, Pallas kernels, run(): pl.pallas_call(body, in_specs=[pl.BlockSpec(memory_space=SPACES[space]) f...  44.7 us
    all_to_all x4, waiting for transfers between devices, within_plane(): lax.all_to_all(x, 'context', 0, 0, axis_index_groups=members, tiled=True)  38.9 us
    ppermute x12, starting transfers between devices, along_z(): lax.ppermute(x, 'context', [(i, i ^ d * width) for i in range(n)])  19 us
    all_to_all x4, starting transfers between devices, within_plane(): lax.all_to_all(x, 'context', 0, 0, axis_index_groups=members, tiled=True)  14.8 us
    cond x17, local copies, waits for them, and re-layouts  3.26 us
  transfers between devices with their start and end apart: 17, of which 4 were waited for; matrix products, arithmetic and copies ran while one was open for 2% of the time, Pallas kernels for 32%

profile of v8, /device:TPU:0, one launch (start us, length us, event | category | flops | bytes accessed | tf_op | source)
XLA Modules:
  0.0 121.6 jit_solution(9275858556565230305)
XLA Ops:
  3.2 3.1 %collective-permute-start.1 = (f32[4,128,128]{2,1,0:T(8,128)S(1)}, f32[4,128,128]{2,1,0:T(8,128)}, u32[]{:S(2)}, u32[]{:S(2)}) collective-permute-start(f32[4,128,128]{2,1,0:T(8,128)S(1)} %get-tuple-element.167), channel_id=1, source_target_pairs={{0,4},{1,5},{2,6},{3,7},{4,0},{5,1},{6,2},{7,3},{8,12},{9,13},{10,... | collective-permute-start | bytes 786440 | tf_op jit(solution)/shard_map/ppermute | solution.py:466
  6.3 2.6 %collective-permute-start.2 = (f32[4,128,128]{2,1,0:T(8,128)S(1)}, f32[4,128,128]{2,1,0:T(8,128)}, u32[]{:S(2)}, u32[]{:S(2)}) collective-permute-start(f32[4,128,128]{2,1,0:T(8,128)S(1)} %get-tuple-element.168), channel_id=1, source_target_pairs={{0,8},{1,9},{2,10},{3,11},{4,12},{5,13},{6,14},{7,15},{8,0},{9,1},... | collective-permute-start | bytes 786440 | tf_op jit(solution)/shard_map/ppermute | solution.py:466
  8.9 20.0 %conditional.4 = (f32[4,128,128]{2,1,0:T(8,128)}, f32[4,128,128]{2,1,0:T(8,128)}, f32[4,128,128]{2,1,0:T(8,128)}, f32[4,128,128]{2,1,0:T(8,128)}, f32[16,64,256]{2,1,0:T(8,128)}) conditional(s32[]{:T(128)} %convert_element_type.2, () %tuple.46, (f32[16,128,128]{2,1,0:T(8,128)S(1)}, f32[16,128,128]{2,1,0:T(8,128)}, f32[4,128,128]{2,1,0:T(8,128)}, ...), branch_computations={%region_0.0_spmd, %region_1.0_spmd} | conditional | flops 268435456 | bytes 11665480 | solution.py:507
  11.0 3.9 %all-to-all-start = ((f32[4,4,128,128]{3,2,1,0:T(8,128)}), f32[4,4,128,128]{3,2,1,0:T(8,128)S(1)}, u32[]{:S(2)}, u32[]{:S(2)}) async-start(f32[4,4,128,128]{3,2,1,0:T(8,128)} %branch_1_fun.13), calls=%async_computation | async-start | bytes 2097152 | tf_op jit(solution)/shard_map/cond/branch_1_fun/all_to_all | solution.py:472
  15.0 2.7 %branch_1_fun.15 = f32[16,64,256]{2,1,0:T(8,128)} custom-call(f32[128,2048]{1,0:T(8,128)} %get-tuple-element.83.refs_0_, f32[2,16,8,128]{3,2,1,0:T(8,128)S(1)} %get-tuple-element.84.refs_1_, bf16[768,256]{1,0:T(8,128)(2,1)S(1)} %get-tuple-element.85.refs_2_), custom_call_target="tpu_custom_call" | custom-call | flops 268435456 | bytes 3014656 | tf_op jit(solution)/shard_map/cond/branch_1_fun/pallas_call | solution.py:409
  17.7 10.2 %all-to-all-done.refs_0_ = f32[4,4,128,128]{3,2,1,0:T(8,128)S(1)} async-done(((f32[4,4,128,128]{3,2,1,0:T(8,128)}), f32[4,4,128,128]{3,2,1,0:T(8,128)S(1)}, u32[]{:S(2)}, u32[]{:S(2)}) %all-to-all-start) | async-done | bytes 1048608 | tf_op jit(solution)/shard_map/cond/branch_1_fun/all_to_all | solution.py:472
  29.6 3.5 %collective-permute-start.8 = (f32[4,128,128]{2,1,0:T(8,128)}, f32[4,128,128]{2,1,0:T(8,128)}, u32[]{:S(2)}, u32[]{:S(2)}) collective-permute-start(f32[4,128,128]{2,1,0:T(8,128)} %get-tuple-element.177), channel_id=1, source_target_pairs={{0,8},{1,9},{2,10},{3,11},{4,12},{5,13},{6,14},{7,15},{8,0},{9,1},... | collective-permute-start | bytes 786440 | tf_op jit(solution)/shard_map/ppermute | solution.py:466
  33.3 24.0 %conditional.5 = (f32[4,128,128]{2,1,0:T(8,128)}, f32[4,128,128]{2,1,0:T(8,128)}, f32[4,128,128]{2,1,0:T(8,128)}, f32[4,128,128]{2,1,0:T(8,128)}, f32[16,128,256...) conditional(s32[]{:T(128)} %convert_element_type.2, () %tuple.45, (f32[4,128,128]{2,1,0:T(8,128)}, ...), branch_computations={%region_2.0_spmd, %region_3.0_spmd} | conditional | flops 1342177280 | bytes 18088052 | solution.py:507
  35.6 3.7 %all-to-all-start.1 = ((f32[4,4,128,128]{3,2,1,0:T(8,128)}), f32[4,4,128,128]{3,2,1,0:T(8,128)S(1)}, u32[]{:S(2)}, u32[]{:S(2)}) async-start(f32[4,4,128,128]{3,2,1,0:T(8,128)} %branch_1_fun.16), calls=%async_computation.1 | async-start | bytes 2097152 | tf_op jit(solution)/shard_map/cond/branch_1_fun/all_to_all | solution.py:472
  39.2 2.8 %branch_1_fun.17.refs_5_ = f32[16,64,256]{2,1,0:T(8,128)} custom-call(f32[128,2048]{1,0:T(8,128)} %get-tuple-element.95.refs_0_, f32[2,16,8,128]{3,2,1,0:T(8,128)S(1)} %get-tuple-element.91.refs_1_, bf16[768,256]{1,0:T(8,128)(2,1)S(1)} %get-tuple-element.92.refs_2_), custom_call_target="tpu_custom_call" | custom-call | flops 268435456 | bytes 3014656 | tf_op jit(solution)/shard_map/cond/branch_1_fun/pallas_call | solution.py:409
  42.0 9.6 %all-to-all-done.1.refs_0_ = f32[4,4,128,128]{3,2,1,0:T(8,128)S(1)} async-done(((f32[4,4,128,128]{3,2,1,0:T(8,128)}), f32[4,4,128,128]{3,2,1,0:T(8,128)S(1)}, u32[]{:S(2)}, u32[]{:S(2)}) %all-to-all-start.1) | async-done | bytes 1048608 | tf_op jit(solution)/shard_map/cond/branch_1_fun/all_to_all | solution.py:472
  51.5 5.9 %branch_1_fun.18 = (f32[4,128,128]{2,1,0:T(8,128)}, f32[4,128,128]{2,1,0:T(8,128)}, f32[4,128,128]{2,1,0:T(8,128)}, f32[4,128,128]{2,1,0:T(8,128)}, f32[16,128,256]{2,1,0:T(8,128)}) custom-call(f32[4,4,128,128]{3,2,1,0:T(8,128)S(1)} %all-to-all-done.1.refs_0_, f32[2,16,8,128]{3,2,1,0:T(8,128)S(1)} %get-tuple-element.91.refs_1_, ...), custom_call_target="tpu_custom_call" | custom-call | flops 1073741824 | bytes 7995392 | tf_op jit(solution)/shard_map/cond/branch_1_fun/pallas_call | solution.py:409
  57.9 3.5 %collective-permute-start.5 = (f32[4,128,128]{2,1,0:T(8,128)}, f32[4,128,128]{2,1,0:T(8,128)}, u32[]{:S(2)}, u32[]{:S(2)}) collective-permute-start(f32[4,128,128]{2,1,0:T(8,128)} %get-tuple-element.174), channel_id=1, source_target_pairs={{0,8},{1,9},{2,10},{3,11},{4,12},{5,13},{6,14},{7,15},{8,0},{9,1},... | collective-permute-start | bytes 786440 | tf_op jit(solution)/shard_map/ppermute | solution.py:466
  61.9 24.9 %conditional.6 = (f32[4,128,128]{2,1,0:T(8,128)}, f32[4,128,128]{2,1,0:T(8,128)}, f32[4,128,128]{2,1,0:T(8,128)}, f32[4,128,128]{2,1,0:T(8,128)}, f32[128,2048]{1,0:T(8,128)S(1)}) conditional(s32[]{:T(128)} %convert_element_type.2, () %tuple.49, (f32[4,128,128]{2,1,0:T(8,128)}, f32[4,128,128]{2,1,0:T(8,128)S(1)}, f32[4,128,128]{2,1,0:T(8,128)}, ...), branch_computations={%region_4.0_spmd, %region_5.0_spmd} | conditional | flops 1610612736 | bytes 21758080 | solution.py:507
  61.9 7.9 %branch_1_fun.19 = (f32[4,4,128,128]{3,2,1,0:T(8,128)}, f32[16,128,256]{2,1,0:T(8,128)}) custom-call(f32[4,128,128]{2,1,0:T(8,128)} %get-tuple-element.101.refs_0_, f32[4,128,128]{2,1,0:T(8,128)S(1)} %get-tuple-element.102.refs_1_, f32[4,128,128]{2,1,0:T(8,128)} %get-tuple-element.103.refs_2_, f32[4,128,128]{2,1,0:T(8,128)} %get-tuple-element.104.refs_3_, ...), custom_call_target="tpu_custom_call" | custom-call | flops 1073741824 | bytes 8257536 | tf_op jit(solution)/shard_map/cond/branch_1_fun/pallas_call | solution.py:409
  69.8 3.7 %all-to-all-start.2 = ((f32[4,4,128,128]{3,2,1,0:T(8,128)}), f32[4,4,128,128]{3,2,1,0:T(8,128)S(1)}, u32[]{:S(2)}, u32[]{:S(2)}) async-start(f32[4,4,128,128]{3,2,1,0:T(8,128)} %get-tuple-element.111), calls=%async_computation.2 | async-start | bytes 2097152 | tf_op jit(solution)/shard_map/cond/branch_1_fun/all_to_all | solution.py:472
  73.5 5.3 %branch_1_fun.21 = f32[128,2048]{1,0:T(8,128)S(1)} custom-call(f32[2,16,8,128]{3,2,1,0:T(8,128)} %copy-done.8, bf16[768,256]{1,0:T(8,128)(2,1)S(1)} %copy-done.6, f32[16,128,256]{2,1,0:T(8,128)} %get-tuple-element.116.refs_2_, f32[16,128,256]{2,1,0:T(8,128)} %get-tuple-element.117.refs_3_), custom_call_target="tpu_custom_call" | custom-call | flops 536870912 | bytes 6160384 | tf_op jit(solution)/shard_map/cond/branch_1_fun/pallas_call | solution.py:409
  78.8 7.0 %all-to-all-done.2.refs_0_ = f32[4,4,128,128]{3,2,1,0:T(8,128)S(1)} async-done(((f32[4,4,128,128]{3,2,1,0:T(8,128)}), f32[4,4,128,128]{3,2,1,0:T(8,128)S(1)}, u32[]{:S(2)}, u32[]{:S(2)}) %all-to-all-start.2) | async-done | bytes 1048608 | tf_op jit(solution)/shard_map/cond/branch_1_fun/all_to_all | solution.py:472
  87.3 3.5 %collective-permute-start.11 = (f32[4,128,128]{2,1,0:T(8,128)}, f32[4,128,128]{2,1,0:T(8,128)S(1)}, u32[]{:S(2)}, u32[]{:S(2)}) collective-permute-start(f32[4,128,128]{2,1,0:T(8,128)} %get-tuple-element.187), channel_id=1, source_target_pairs={{0,8},{1,9},{2,10},{3,11},{4,12},{5,13},{6,14},{7,15},{8,0},{9,1},... | collective-permute-start | bytes 786440 | tf_op jit(solution)/shard_map/ppermute | solution.py:466
  91.2 27.3 %conditional.7 = (f32[16,128,128]{2,1,0:T(8,128)}, f32[4,128,128]{2,1,0:T(8,128)S(1)}, f32[4,128,128]{2,1,0:T(8,128)S(1)}, f32[128,2048]{1,0:T(8,128)}, f32[1,20...) conditional(s32[]{:T(128)} %convert_element_type.2, () %tuple.44, (f32[4,128,128]{2,1,0:T(8,128)}, ...), branch_computations={%region_6.0_spmd, %region_7.0_spmd} | conditional | bytes 37748996 | solution.py:507
  94.8 3.5 %all-to-all-start.3 = ((f32[4,4,128,128]{3,2,1,0:T(8,128)}), f32[4,4,128,128]{3,2,1,0:T(8,128)S(1)}, u32[]{:S(2)}, u32[]{:S(2)}) async-start(f32[4,4,128,128]{3,2,1,0:T(8,128)} %branch_1_fun.22), calls=%async_computation.3 | async-start | bytes 2097152 | tf_op jit(solution)/shard_map/cond/branch_1_fun/all_to_all | solution.py:472
  100.4 12.2 %all-to-all-done.3.refs_0_ = f32[4,4,128,128]{3,2,1,0:T(8,128)S(1)} async-done(((f32[4,4,128,128]{3,2,1,0:T(8,128)}), f32[4,4,128,128]{3,2,1,0:T(8,128)S(1)}, u32[]{:S(2)}, u32[]{:S(2)}) %all-to-all-start.3) | async-done | bytes 1048608 | tf_op jit(solution)/shard_map/cond/branch_1_fun/all_to_all | solution.py:472
  112.5 2.7 %branch_1_fun.23 = (f32[16,128,128]{2,1,0:T(8,128)}, f32[16,128,128]{2,1,0:T(8,128)}) custom-call(f32[4,4,128,128]{3,2,1,0:T(8,128)S(1)} %all-to-all-done.3.refs_0_, f32[16,128,128]{2,1,0:T(8,128)} %get-tuple-element.123.refs_1_, f32[16,128,128]{2,1,0:T(8,128)} %copy-done.2), custom_call_target="tpu_custom_call" | custom-call | bytes 5242880 | tf_op jit(solution)/shard_map/cond/branch_1_fun/pallas_call | solution.py:409
  118.6 3.0 %shard_map.120 = (f32[16,128,128]{2,1,0:T(8,128)}, f32[16,128,128]{2,1,0:T(8,128)}) custom-call(f32[4,128,128]{2,1,0:T(8,128)S(1)} %collective-permute-done.10.refs_0_, f32[4,128,128]{2,1,0:T(8,128)S(1)} %collective-permute-done.11.refs_1_, f32[4,128,128]{2,1,0:T(8,128)S(1)} %collective-permute-done.12.refs_2_, f32[16,128,128]{2,1,0:T(8,128)} %bitcast.13, ...), custom_call_target="tpu_custom_call" | custom-call | bytes 6553600 | tf_op jit(solution)/shard_map/pallas_call | solution.py:409
  (52 shorter events, 20.6 us)
Async XLA Ops:
  0.6 8.2 %copy-start = (bf16[768,256]{1,0:T(8,128)(2,1)S(1)}, bf16[768,256]{1,0:T(8,128)(2,1)}, u32[]{:S(2)}) copy-start(bf16[768,256]{1,0:T(8,128)(2,1)} %constant.11.clone) | copy-start | bytes 1179652
  0.6 8.2 %copy-start.7 = (f32[2,16,8,128]{3,2,1,0:T(8,128)S(1)}, f32[2,16,8,128]{3,2,1,0:T(8,128)}, u32[]{:S(2)}) copy-start(f32[2,16,8,128]{3,2,1,0:T(8,128)} %constant.17.clone) | copy-start | bytes 393220
  0.7 8.2 %copy-start.1 = (f32[1,2048,128]{2,1,0:T(8,128)S(1)}, f32[1,2048,128]{2,1,0:T(8,128)}, u32[]{:S(2)}) copy-start(f32[1,2048,128]{2,1,0:T(8,128)} %param.20) | copy-start | bytes 3145732
  3.2 29.9 %collective-permute-start.1 = (f32[4,128,128]{2,1,0:T(8,128)S(1)}, f32[4,128,128]{2,1,0:T(8,128)}, u32[]{:S(2)}, u32[]{:S(2)}) collective-permute-start(f32[4,128,128]{2,1,0:T(8,128)S(1)} %get-tuple-element.167), channel_id=1, source_target_pairs={{0,4},{1,5},{2,6},{3,7},{4,0},{5,1},{6,2},{7,3},{8,12},{9,13},{10,... | collective-permute-start | bytes 786440 | tf_op jit(solution)/shard_map/ppermute | solution.py:466
  6.3 27.1 %collective-permute-start.2 = (f32[4,128,128]{2,1,0:T(8,128)S(1)}, f32[4,128,128]{2,1,0:T(8,128)}, u32[]{:S(2)}, u32[]{:S(2)}) collective-permute-start(f32[4,128,128]{2,1,0:T(8,128)S(1)} %get-tuple-element.168), channel_id=1, source_target_pairs={{0,8},{1,9},{2,10},{3,11},{4,12},{5,13},{6,14},{7,15},{8,0},{9,1},... | collective-permute-start | bytes 786440 | tf_op jit(solution)/shard_map/ppermute | solution.py:466
  8.8 24.5 %collective-permute-start.3 = (f32[4,128,128]{2,1,0:T(8,128)S(1)}, f32[4,128,128]{2,1,0:T(8,128)}, u32[]{:S(2)}, u32[]{:S(2)}) collective-permute-start(f32[4,128,128]{2,1,0:T(8,128)S(1)} %get-tuple-element.169), channel_id=1, source_target_pairs={{0,12},{1,13},{2,14},{3,15},{4,8},{5,9},{6,10},{7,11},{8,4},{9,5},... | collective-permute-start | bytes 786440 | tf_op jit(solution)/shard_map/ppermute | solution.py:466
  11.0 16.9 %all-to-all-start = ((f32[4,4,128,128]{3,2,1,0:T(8,128)}), f32[4,4,128,128]{3,2,1,0:T(8,128)S(1)}, u32[]{:S(2)}, u32[]{:S(2)}) async-start(f32[4,4,128,128]{3,2,1,0:T(8,128)} %branch_1_fun.13), calls=%async_computation | async-start | bytes 2097152 | tf_op jit(solution)/shard_map/cond/branch_1_fun/all_to_all | solution.py:472
  28.9 32.6 %collective-permute-start.7 = (f32[4,128,128]{2,1,0:T(8,128)}, f32[4,128,128]{2,1,0:T(8,128)S(1)}, u32[]{:S(2)}, u32[]{:S(2)}) collective-permute-start(f32[4,128,128]{2,1,0:T(8,128)} %get-tuple-element.170), channel_id=1, source_target_pairs={{0,4},{1,5},{2,6},{3,7},{4,0},{5,1},{6,2},{7,3},{8,12},{9,13},{10,... | collective-permute-start | bytes 786440 | tf_op jit(solution)/shard_map/ppermute | solution.py:466
  29.6 32.3 %collective-permute-start.8 = (f32[4,128,128]{2,1,0:T(8,128)}, f32[4,128,128]{2,1,0:T(8,128)}, u32[]{:S(2)}, u32[]{:S(2)}) collective-permute-start(f32[4,128,128]{2,1,0:T(8,128)} %get-tuple-element.177), channel_id=1, source_target_pairs={{0,8},{1,9},{2,10},{3,11},{4,12},{5,13},{6,14},{7,15},{8,0},{9,1},... | collective-permute-start | bytes 786440 | tf_op jit(solution)/shard_map/ppermute | solution.py:466
  33.0 28.8 %collective-permute-start.9 = (f32[4,128,128]{2,1,0:T(8,128)}, f32[4,128,128]{2,1,0:T(8,128)}, u32[]{:S(2)}, u32[]{:S(2)}) collective-permute-start(f32[4,128,128]{2,1,0:T(8,128)} %get-tuple-element.178), channel_id=1, source_target_pairs={{0,12},{1,13},{2,14},{3,15},{4,8},{5,9},{6,10},{7,11},{8,4},{9,5},... | collective-permute-start | bytes 786440 | tf_op jit(solution)/shard_map/ppermute | solution.py:466
  35.5 16.0 %copy-start.5 = (bf16[768,256]{1,0:T(8,128)(2,1)S(1)}, bf16[768,256]{1,0:T(8,128)(2,1)}, u32[]{:S(2)}) copy-start(bf16[768,256]{1,0:T(8,128)(2,1)} %get-tuple-element.93.refs_3_) | copy-start | bytes 1179652 | tf_op jit(solution)/shard_map/cond
  35.6 16.0 %all-to-all-start.1 = ((f32[4,4,128,128]{3,2,1,0:T(8,128)}), f32[4,4,128,128]{3,2,1,0:T(8,128)S(1)}, u32[]{:S(2)}, u32[]{:S(2)}) async-start(f32[4,4,128,128]{3,2,1,0:T(8,128)} %branch_1_fun.16), calls=%async_computation.1 | async-start | bytes 2097152 | tf_op jit(solution)/shard_map/cond/branch_1_fun/all_to_all | solution.py:472
  57.4 33.4 %collective-permute-start.4 = (f32[4,128,128]{2,1,0:T(8,128)}, f32[4,128,128]{2,1,0:T(8,128)}, u32[]{:S(2)}, u32[]{:S(2)}) collective-permute-start(f32[4,128,128]{2,1,0:T(8,128)} %get-tuple-element.173), channel_id=1, source_target_pairs={{0,4},{1,5},{2,6},{3,7},{4,0},{5,1},{6,2},{7,3},{8,12},{9,13},{10,... | collective-permute-start | bytes 786440 | tf_op jit(solution)/shard_map/ppermute | solution.py:466
  57.9 33.3 %collective-permute-start.5 = (f32[4,128,128]{2,1,0:T(8,128)}, f32[4,128,128]{2,1,0:T(8,128)}, u32[]{:S(2)}, u32[]{:S(2)}) collective-permute-start(f32[4,128,128]{2,1,0:T(8,128)} %get-tuple-element.174), channel_id=1, source_target_pairs={{0,8},{1,9},{2,10},{3,11},{4,12},{5,13},{6,14},{7,15},{8,0},{9,1},... | collective-permute-start | bytes 786440 | tf_op jit(solution)/shard_map/ppermute | solution.py:466
  61.4 29.8 %collective-permute-start.6 = (f32[4,128,128]{2,1,0:T(8,128)}, f32[4,128,128]{2,1,0:T(8,128)}, u32[]{:S(2)}, u32[]{:S(2)}) collective-permute-start(f32[4,128,128]{2,1,0:T(8,128)} %get-tuple-element.175), channel_id=1, source_target_pairs={{0,12},{1,13},{2,14},{3,15},{4,8},{5,9},{6,10},{7,11},{8,4},{9,5},... | collective-permute-start | bytes 786440 | tf_op jit(solution)/shard_map/ppermute | solution.py:466
  61.9 7.9 %copy-start.8 = (f32[2,16,8,128]{3,2,1,0:T(8,128)}, f32[2,16,8,128]{3,2,1,0:T(8,128)S(1)}, u32[]{:S(2)}) copy-start(f32[2,16,8,128]{3,2,1,0:T(8,128)S(1)} %get-tuple-element.105.refs_4_.refs_0_) | copy-start | bytes 393220 | tf_op jit(solution)/shard_map/cond
  69.8 3.7 %copy-start.6 = (bf16[768,256]{1,0:T(8,128)(2,1)S(1)}, bf16[768,256]{1,0:T(8,128)(2,1)}, u32[]{:S(2)}) copy-start(bf16[768,256]{1,0:T(8,128)(2,1)} %get-tuple-element.107.refs_6_.refs_1_) | copy-start | bytes 1179652 | tf_op jit(solution)/shard_map/cond
  69.8 16.0 %all-to-all-start.2 = ((f32[4,4,128,128]{3,2,1,0:T(8,128)}), f32[4,4,128,128]{3,2,1,0:T(8,128)S(1)}, u32[]{:S(2)}, u32[]{:S(2)}) async-start(f32[4,4,128,128]{3,2,1,0:T(8,128)} %get-tuple-element.111), calls=%async_computation.2 | async-start | bytes 2097152 | tf_op jit(solution)/shard_map/cond/branch_1_fun/all_to_all | solution.py:472
  86.8 31.8 %collective-permute-start.10 = (f32[4,128,128]{2,1,0:T(8,128)}, f32[4,128,128]{2,1,0:T(8,128)S(1)}, u32[]{:S(2)}, u32[]{:S(2)}) collective-permute-start(f32[4,128,128]{2,1,0:T(8,128)} %get-tuple-element.186), channel_id=1, source_target_pairs={{0,4},{1,5},{2,6},{3,7},{4,0},{5,1},{6,2},{7,3},{8,12},{9,13},{10,... | collective-permute-start | bytes 786440 | tf_op jit(solution)/shard_map/ppermute | solution.py:466
  87.3 31.3 %collective-permute-start.11 = (f32[4,128,128]{2,1,0:T(8,128)}, f32[4,128,128]{2,1,0:T(8,128)S(1)}, u32[]{:S(2)}, u32[]{:S(2)}) collective-permute-start(f32[4,128,128]{2,1,0:T(8,128)} %get-tuple-element.187), channel_id=1, source_target_pairs={{0,8},{1,9},{2,10},{3,11},{4,12},{5,13},{6,14},{7,15},{8,0},{9,1},... | collective-permute-start | bytes 786440 | tf_op jit(solution)/shard_map/ppermute | solution.py:466
  90.8 27.7 %collective-permute-start.12 = (f32[4,128,128]{2,1,0:T(8,128)}, f32[4,128,128]{2,1,0:T(8,128)S(1)}, u32[]{:S(2)}, u32[]{:S(2)}) collective-permute-start(f32[4,128,128]{2,1,0:T(8,128)} %get-tuple-element.188), channel_id=1, source_target_pairs={{0,12},{1,13},{2,14},{3,15},{4,8},{5,9},{6,10},{7,11},{8,4},{9,5},... | collective-permute-start | bytes 786440 | tf_op jit(solution)/shard_map/ppermute | solution.py:466
  92.2 25.2 %collective-permute-start = (f32[128,2048]{1,0:T(8,128)}, f32[128,2048]{1,0:T(8,128)S(1)}, u32[]{:S(2)}, u32[]{:S(2)}) collective-permute-start(f32[128,2048]{1,0:T(8,128)} %copy-done.3), channel_id=1, source_target_pairs={{0,16},{16,0},{1,17},{17,1},{2,18},{18,2},{3,19},{19,3},{4,20},{20... | collective-permute-start | bytes 3145736 | tf_op jit(solution)/shard_map/cond/branch_1_fun/ppermute | solution.py:554
  94.8 17.7 %all-to-all-start.3 = ((f32[4,4,128,128]{3,2,1,0:T(8,128)}), f32[4,4,128,128]{3,2,1,0:T(8,128)S(1)}, u32[]{:S(2)}, u32[]{:S(2)}) async-start(f32[4,4,128,128]{3,2,1,0:T(8,128)} %branch_1_fun.22), calls=%async_computation.3 | async-start | bytes 2097152 | tf_op jit(solution)/shard_map/cond/branch_1_fun/all_to_all | solution.py:472
  112.5 5.0 %copy-start.4 = (f32[128,2048]{1,0:T(8,128)S(1)}, f32[128,2048]{1,0:T(8,128)}, u32[]{:S(2)}) copy-start(f32[128,2048]{1,0:T(8,128)} %copy-done.3) | copy-start | bytes 3145732 | tf_op jit(solution)/shard_map/cond
  (4 other events, 5.7 us)

commit v9 on v8

--- a/solution.py
+++ b/solution.py
@@ -139,14 +139,16 @@
 
 
 def transform(
-    sign, n, channels, tokens, read, sources, targets, tw_ref, fwd_ref, inv_ref, spec_refs, own_ref,
-    buf_ref, spec_buf, own_buf, y_ref, sem,
+    sign, n, channels, tokens, read, sources, targets, tw_ref, fwd_hbm, inv_hbm, spec_refs, own_ref,
+    buf_ref, spec_buf, own_buf, y_ref, fwd_ref, inv_ref, sem,
 ):
     half = channels // 2
     rows = [pl.ds(0, half), pl.ds(half, half)]
     loads = [copies_of(sources(part), sem.at[0, i]) for i, part in enumerate(rows)]
     for load in loads:
         start_all(load)
+    table_loads = copies_of([(fwd_hbm, fwd_ref), (inv_hbm, inv_ref)], sem.at[2, 1])
+    start_all(table_loads)
     spec_loads = [
         copies_of(
             [
@@ -163,6 +165,7 @@
         wait_all(load)
         outer_forward(read, n, part, tokens, tw_ref, y_ref)
     own_stores = copies_of([(own_buf.at[ms], own_ref.at[ms]) for ms in parts_of(n)], sem.at[2, 0])
+    wait_all(table_loads)
     for ms, load, store in zip(parts_of(n), spec_loads, own_stores):
         own = times_table(flat(y_ref[ms]), fwd_ref)
         own_buf[ms] = own.reshape(ms.size, channels, 2 * tokens)
@@ -236,7 +239,8 @@
 
 
 def filter_grad_kernel(
-    scale, n, channels, tokens, tw_ref, inv_ref, p_ref, g_ref, out_ref, p_buf, g_buf, y_ref, sem
+    scale, n, channels, tokens, tw_ref, inv_ref, p_ref, g_ref, out_ref,
+    p_buf, g_buf, y_ref, out_buf, sem,
 ):
     loads = [
         copies_of([(p_ref.at[ms], p_buf.at[ms]), (g_ref.at[ms], g_buf.at[ms])], sem.at[i])
@@ -253,13 +257,14 @@
         y_ref[ms] = times_table(both, inv_ref).reshape(ms.size, channels, 2 * tokens)
 
     def write(n1, r, value):
-        out_ref[r, n1 * tokens : (n1 + 1) * tokens] = value * scale
-
-    outer_inverse(write, n, pl.ds(0, channels), tokens, tw_ref, y_ref)
-
-
-def add_kernel(a_ref, b_ref, out_ref):
-    out_ref[...] = a_ref[...] + b_ref[...]
+        out_buf[r, n1 * tokens : (n1 + 1) * tokens] = value * scale
+
+    rows = parts_of(channels, ROWS)
+    stores = copies_of([(out_buf.at[part], out_ref.at[part]) for part in rows], sem.at[PARTS])
+    for part, store in zip(rows, stores):
+        outer_inverse(write, n, part, tokens, tw_ref, y_ref)
+        store.start()
+    wait_all(stores)
 
 
 def load_pairs(n, a_ref, b_ref, a_buf, b_buf, sem):
@@ -369,25 +374,18 @@
 
 def gate_far_kernel(planes, width, *refs):
     far_refs, refs = refs[: planes - 1], refs[planes - 1 :]
-    a_ref, b_ref, done_a, done_b, after_ref, oa_ref, ob_ref, a_buf, b_buf, sem = refs
+    a_ref, b_ref, done_a, done_b, oa_ref, ob_ref, a_buf, b_buf, sem = refs
     z = plane(width)
-    part = pl.ds(z * width, width)
-    loads = copies_of([(done_a, a_buf.at[part]), (done_b, b_buf.at[part])], sem.at[0])
-    start_all(loads)
-    blocks = [(lambda d=d: far_refs[d - 1][...], (z ^ d) * width) for d in range(1, planes)]
-    stores = []
-    for d, (read, first) in enumerate(blocks, 1):
-        rows = pl.ds(first, width)
-        x = read()
+    rows = pl.ds(z * width, width)
+    stores = copies_of([(done_a, oa_ref.at[rows]), (done_b, ob_ref.at[rows])], sem.at[0])
+    start_all(stores)
+    for d, far_ref in enumerate(far_refs, 1):
+        rows = pl.ds((z ^ d) * width, width)
+        x = far_ref[...]
         a_buf[rows] = x * a_ref[rows]
         b_buf[rows] = x * b_ref[rows]
         stores += copies_of([(a_buf.at[rows], oa_ref.at[rows]), (b_buf.at[rows], ob_ref.at[rows])], sem.at[d])
         start_all(stores[-2:])
-    wait_all(loads)
-    stores += copies_of(
-        [(a_buf.at[part], oa_ref.at[part]), (b_buf.at[part], ob_ref.at[part])], sem.at[planes]
-    )
-    start_all(stores[-2:])
     wait_all(stores)
 
 
@@ -495,7 +493,8 @@
             flops // 2,
         )(filters, tw, fwd)[0]
 
-    transform_scratch = [rows, y, y, y, semaphores(4, PARTS, max(PARTS, planes))]
+    table = pltpu.VMEM(fwd.shape, fwd.dtype)
+    transform_scratch = [rows, y, y, y, table, table, semaphores(4, PARTS, max(PARTS, planes))]
     always = lax.axis_index("context") < n
 
     def grouped(body, *args):
@@ -507,7 +506,7 @@
         return lax.cond(always, body, never, *args)
 
     keep_p, *send_p = kernel_call(
-        part(product_split_kernel, planes, n), "hh", [("u", one)] * planes,
+        part(product_split_kernel, planes, n), "hh", [("u", one)] + [("v", one)] * (planes - 1),
         [rows, rows, semaphores(PARTS, 2)],
     )(key, value)
     got_p = along_z(send_p)
@@ -526,7 +525,7 @@
         product_ch = within_plane(*merge(keep_p, *got_p, send_g))
         filt = (filt_a, transform_filters(channels // 2))
         *outs, prod_spec = kernel_call(
-            part(conv_kernel, planes, *sizes), "vvvvhh",
+            part(conv_kernel, planes, *sizes), "vvhhhh",
             [("h", one)] * planes + [("h", spectrum)], transform_scratch, 2 * flops,
         )(product_ch, tw, fwd, inv, *filt)
         return outs, prod_spec, filt
@@ -536,13 +535,13 @@
 
     def third(near_g, far_g, filt, keep_c, prod_spec):
         back_ch, grad_spec = kernel_call(
-            part(back_kernel, planes, *sizes), "a" * planes + "vvvhha",
+            part(back_kernel, planes, *sizes), "a" * planes + "vhhhha",
             [("h", paired), ("h", spectrum)], transform_scratch, 2 * flops,
         )(near_g, *far_g, tw, fwd, inv, *filt, keep_c)
         sends = send(within_plane(back_ch))
         (own,) = kernel_call(
-            part(filter_grad_kernel, scale, *sizes), "vvhh", [("u", lags)],
-            [y, y, y, semaphores(PARTS, 2)], flops,
+            part(filter_grad_kernel, scale, *sizes), "vvhh", [("h", lags)],
+            [y, y, y, pltpu.VMEM(lags, f32), semaphores(PARTS + 1, PARTS)], flops,
         )(tw, inv, prod_spec, grad_spec)
         return sends, own
 
@@ -551,11 +550,10 @@
 
     def fourth(keep_c, got_c, query, cot, near_b, value, key, own):
         if pair_size == 2:
-            other = lax.ppermute(own, "dp", [(0, 1), (1, 0)])
+            grad_filter = own + lax.ppermute(own, "dp", [(0, 1), (1, 0)])
         else:
-            other = lax.psum(own, "dp") - own
+            grad_filter = lax.psum(own, "dp")
         conv_tok = within_plane(*merge(keep_c, *got_c, near_b))
-        (grad_filter,) = kernel_call(add_kernel, "vv", [("u", lags)], [])(own, other)
         begun = kernel_call(
             part(gate_near_kernel, planes, width), "ahh", [("h", one)] * 2,
             [pltpu.VMEM(one, f32)] * 3 + [semaphores(2, 3)],
@@ -570,9 +568,9 @@
         fourth, keep_c, got_c, query, cot, near_b, value, key, own
     )
     grad_key, grad_value = kernel_call(
-        part(gate_far_kernel, planes, width), "v" * (planes + 1) + "aaa", [("h", blocks)] * 2,
-        [rows, rows, semaphores(planes + 1, 2)],
-    )(*far_b, value, key, *begun, gated)
+        part(gate_far_kernel, planes, width), "v" * (planes + 3), [("h", blocks)] * 2,
+        [rows, rows, semaphores(planes, 2)],
+    )(*far_b, value, key, *begun)
     shape = query_input.shape
     return (
         gated.reshape(shape),

time: 122 us -> 119 us (0.975)
  local copies, waits for them, and re-layouts: 3.28 us -> 0.78 us
  other arithmetic: 0 us -> 1.72 us
  Pallas kernels: 44.7 us -> 43.3 us
    cond x17 -> x12, local copies, waits for them, and re-layouts: 3.26 us -> 0.76 us
    add x0 -> x1, other arithmetic: none -> 1.72 us  [fourth(): grad_filter = own + lax.ppermute(own, 'dp', [(0, 1), (1, 0)])]
    pallas_call x15 -> x14, Pallas kernels: 44.7 us -> 43.3 us  [run(): pl.pallas_call(body, in_specs=[pl.BlockSpec(memory_space=SPACES[space]) f...]
  transfers between devices with their start and end apart: 17 -> 17, of which waited for: 4 -> 4; matrix products, arithmetic and copies ran while one was open for 2% -> 1% of each run, Pallas kernels for 32% -> 32%
where the time goes in v9:
time: 119 us
  Pallas kernels  43.3 us (36%)
  waiting for transfers between devices  38.2 us (32%)
  starting transfers between devices  33.8 us (28%)
  other arithmetic  1.72 us (1%)
    pallas_call x14, Pallas kernels, run(): pl.pallas_call(body, in_specs=[pl.BlockSpec(memory_space=SPACES[space]) f...  43.3 us
    all_to_all x4, waiting for transfers between devices, within_plane(): lax.all_to_all(x, 'context', 0, 0, axis_index_groups=members, tiled=True)  38.1 us
    ppermute x12, starting transfers between devices, along_z(): lax.ppermute(x, 'context', [(i, i ^ d * width) for i in range(n)])  19 us
    all_to_all x4, starting transfers between devices, within_plane(): lax.all_to_all(x, 'context', 0, 0, axis_index_groups=members, tiled=True)  14.7 us
  transfers between devices with their start and end apart: 17, of which 4 were waited for; matrix products, arithmetic and copies ran while one was open for 1% of the time, Pallas kernels for 32%

profile of v9, /device:TPU:0, one launch (start us, length us, event | category | flops | bytes accessed | tf_op | source)
XLA Modules:
  0.0 118.7 jit_solution(17467202726341910238)
XLA Ops:
  3.2 3.1 %collective-permute-start.4 = (f32[4,128,128]{2,1,0:T(8,128)S(1)}, f32[4,128,128]{2,1,0:T(8,128)}, u32[]{:S(2)}, u32[]{:S(2)}) collective-permute-start(f32[4,128,128]{2,1,0:T(8,128)S(1)} %get-tuple-element.170), channel_id=1, source_target_pairs={{0,4},{1,5},{2,6},{3,7},{4,0},{5,1},{6,2},{7,3},{8,12},{9,13},{10,... | collective-permute-start | bytes 786440 | tf_op jit(solution)/shard_map/ppermute | solution.py:464
  6.3 2.6 %collective-permute-start.5 = (f32[4,128,128]{2,1,0:T(8,128)S(1)}, f32[4,128,128]{2,1,0:T(8,128)}, u32[]{:S(2)}, u32[]{:S(2)}) collective-permute-start(f32[4,128,128]{2,1,0:T(8,128)S(1)} %get-tuple-element.171), channel_id=1, source_target_pairs={{0,8},{1,9},{2,10},{3,11},{4,12},{5,13},{6,14},{7,15},{8,0},{9,1},... | collective-permute-start | bytes 786440 | tf_op jit(solution)/shard_map/ppermute | solution.py:464
  8.9 20.0 %conditional.4 = (f32[4,128,128]{2,1,0:T(8,128)}, f32[4,128,128]{2,1,0:T(8,128)}, f32[4,128,128]{2,1,0:T(8,128)}, f32[4,128,128]{2,1,0:T(8,128)}, f32[16,64,256]{2,1,0:T(8,128)}) conditional(s32[]{:T(128)} %convert_element_type.2, () %tuple.46, (f32[16,128,128]{2,1,0:T(8,128)S(1)}, f32[16,128,128]{2,1,0:T(8,128)}, f32[4,128,128]{2,1,0:T(8,128)}, ...), branch_computations={%region_0.0_spmd, %region_1.0_spmd} | conditional | flops 268435456 | bytes 11665480 | solution.py:506
  11.0 3.9 %all-to-all-start = ((f32[4,4,128,128]{3,2,1,0:T(8,128)}), f32[4,4,128,128]{3,2,1,0:T(8,128)S(1)}, u32[]{:S(2)}, u32[]{:S(2)}) async-start(f32[4,4,128,128]{3,2,1,0:T(8,128)} %branch_1_fun.12), calls=%async_computation | async-start | bytes 2097152 | tf_op jit(solution)/shard_map/cond/branch_1_fun/all_to_all | solution.py:470
  15.0 2.7 %branch_1_fun.14 = f32[16,64,256]{2,1,0:T(8,128)} custom-call(f32[128,2048]{1,0:T(8,128)} %get-tuple-element.83.refs_0_, f32[2,16,8,128]{3,2,1,0:T(8,128)S(1)} %get-tuple-element.84.refs_1_, bf16[768,256]{1,0:T(8,128)(2,1)S(1)} %get-tuple-element.85.refs_2_), custom_call_target="tpu_custom_call" | custom-call | flops 268435456 | bytes 3014656 | tf_op jit(solution)/shard_map/cond/branch_1_fun/pallas_call | solution.py:407
  17.7 10.2 %all-to-all-done.refs_0_ = f32[4,4,128,128]{3,2,1,0:T(8,128)S(1)} async-done(((f32[4,4,128,128]{3,2,1,0:T(8,128)}), f32[4,4,128,128]{3,2,1,0:T(8,128)S(1)}, u32[]{:S(2)}, u32[]{:S(2)}) %all-to-all-start) | async-done | bytes 1048608 | tf_op jit(solution)/shard_map/cond/branch_1_fun/all_to_all | solution.py:470
  29.6 3.5 %collective-permute-start.2 = (f32[4,128,128]{2,1,0:T(8,128)}, f32[4,128,128]{2,1,0:T(8,128)S(1)}, u32[]{:S(2)}, u32[]{:S(2)}) collective-permute-start(f32[4,128,128]{2,1,0:T(8,128)} %get-tuple-element.168), channel_id=1, source_target_pairs={{0,8},{1,9},{2,10},{3,11},{4,12},{5,13},{6,14},{7,15},{8,0},{9,1},... | collective-permute-start | bytes 786440 | tf_op jit(solution)/shard_map/ppermute | solution.py:464
  33.3 24.3 %conditional.5 = (f32[4,128,128]{2,1,0:T(8,128)}, f32[4,128,128]{2,1,0:T(8,128)}, f32[4,128,128]{2,1,0:T(8,128)}, f32[4,128,128]{2,1,0:T(8,128)}, f32[16,128,256...) conditional(s32[]{:T(128)} %convert_element_type.2, () %tuple.48, (f32[4,128,128]{2,1,0:T(8,128)}, ...), branch_computations={%region_2.0_spmd, %region_3.0_spmd} | conditional | flops 1342177280 | bytes 16515160 | solution.py:506
  35.5 3.5 %all-to-all-start.1 = ((f32[4,4,128,128]{3,2,1,0:T(8,128)}), f32[4,4,128,128]{3,2,1,0:T(8,128)S(1)}, u32[]{:S(2)}, u32[]{:S(2)}) async-start(f32[4,4,128,128]{3,2,1,0:T(8,128)} %branch_1_fun.15), calls=%async_computation.1 | async-start | bytes 2097152 | tf_op jit(solution)/shard_map/cond/branch_1_fun/all_to_all | solution.py:470
  39.1 2.8 %branch_1_fun.16.refs_5_ = f32[16,64,256]{2,1,0:T(8,128)} custom-call(f32[128,2048]{1,0:T(8,128)} %get-tuple-element.95.refs_0_, f32[2,16,8,128]{3,2,1,0:T(8,128)S(1)} %get-tuple-element.91.refs_1_, bf16[768,256]{1,0:T(8,128)(2,1)S(1)} %get-tuple-element.92.refs_2_), custom_call_target="tpu_custom_call" | custom-call | flops 268435456 | bytes 3014656 | tf_op jit(solution)/shard_map/cond/branch_1_fun/pallas_call | solution.py:407
  41.8 9.6 %all-to-all-done.1.refs_0_ = f32[4,4,128,128]{3,2,1,0:T(8,128)S(1)} async-done(((f32[4,4,128,128]{3,2,1,0:T(8,128)}), f32[4,4,128,128]{3,2,1,0:T(8,128)S(1)}, u32[]{:S(2)}, u32[]{:S(2)}) %all-to-all-start.1) | async-done | bytes 1048608 | tf_op jit(solution)/shard_map/cond/branch_1_fun/all_to_all | solution.py:470
  51.4 6.2 %branch_1_fun.17 = (f32[4,128,128]{2,1,0:T(8,128)}, f32[4,128,128]{2,1,0:T(8,128)}, f32[4,128,128]{2,1,0:T(8,128)}, f32[4,128,128]{2,1,0:T(8,128)}, f32[16,128,256]{2,1,0:T(8,128)}) custom-call(f32[4,4,128,128]{3,2,1,0:T(8,128)S(1)} %all-to-all-done.1.refs_0_, f32[2,16,8,128]{3,2,1,0:T(8,128)S(1)} %get-tuple-element.91.refs_1_, ...), custom_call_target="tpu_custom_call" | custom-call | flops 1073741824 | bytes 7995392 | tf_op jit(solution)/shard_map/cond/branch_1_fun/pallas_call | solution.py:407
  58.1 3.5 %collective-permute-start.8 = (f32[4,128,128]{2,1,0:T(8,128)}, f32[4,128,128]{2,1,0:T(8,128)}, u32[]{:S(2)}, u32[]{:S(2)}) collective-permute-start(f32[4,128,128]{2,1,0:T(8,128)} %get-tuple-element.181), channel_id=1, source_target_pairs={{0,8},{1,9},{2,10},{3,11},{4,12},{5,13},{6,14},{7,15},{8,0},{9,1},... | collective-permute-start | bytes 786440 | tf_op jit(solution)/shard_map/ppermute | solution.py:464
  62.1 24.4 %conditional.6 = (f32[4,128,128]{2,1,0:T(8,128)}, f32[4,128,128]{2,1,0:T(8,128)}, f32[4,128,128]{2,1,0:T(8,128)}, f32[4,128,128]{2,1,0:T(8,128)}, f32[128,2048]{1,0:T(8,128)}) conditional(s32[]{:T(128)} %convert_element_type.2, () %tuple.45, (f32[4,128,128]{2,1,0:T(8,128)}, f32[4,128,128]{2,1,0:T(8,128)S(1)}, f32[4,128,128]{2,1,0:T(8,128)S(1)}, ...), branch_computations={%region_4.0_spmd, %region_5.0_spmd} | conditional | flops 1610612736 | bytes 23330972 | solution.py:506
  62.9 6.7 %branch_1_fun.18 = (f32[4,4,128,128]{3,2,1,0:T(8,128)}, f32[16,128,256]{2,1,0:T(8,128)}) custom-call(f32[4,128,128]{2,1,0:T(8,128)} %get-tuple-element.101.refs_0_, f32[4,128,128]{2,1,0:T(8,128)S(1)} %get-tuple-element.102.refs_1_, f32[4,128,128]{2,1,0:T(8,128)S(1)} %get-tuple-element.103.refs_2_, f32[4,128,128]{2,1,0:T(8,128)S(1)} %get-tuple-element.104.refs_3_, ...), custom_call_target="tpu_custom_call" | custom-call | flops 1073741824 | bytes 8257536 | tf_op jit(solution)/shard_map/cond/branch_1_fun/pallas_call | solution.py:407
  69.6 3.7 %all-to-all-start.2 = ((f32[4,4,128,128]{3,2,1,0:T(8,128)}), f32[4,4,128,128]{3,2,1,0:T(8,128)S(1)}, u32[]{:S(2)}, u32[]{:S(2)}) async-start(f32[4,4,128,128]{3,2,1,0:T(8,128)} %get-tuple-element.111), calls=%async_computation.2 | async-start | bytes 2097152 | tf_op jit(solution)/shard_map/cond/branch_1_fun/all_to_all | solution.py:470
  73.3 6.1 %branch_1_fun.20 = f32[128,2048]{1,0:T(8,128)} custom-call(f32[2,16,8,128]{3,2,1,0:T(8,128)} %copy-done.7, bf16[768,256]{1,0:T(8,128)(2,1)S(1)} %copy-done.5, f32[16,128,256]{2,1,0:T(8,128)} %get-tuple-element.116.refs_2_, f32[16,128,256]{2,1,0:T(8,128)} %get-tuple-element.117.refs_3_), custom_call_target="tpu_custom_call" | custom-call | flops 536870912 | bytes 6160384 | tf_op jit(solution)/shard_map/cond/branch_1_fun/pallas_call | solution.py:407
  79.4 6.1 %all-to-all-done.2.refs_0_ = f32[4,4,128,128]{3,2,1,0:T(8,128)S(1)} async-done(((f32[4,4,128,128]{3,2,1,0:T(8,128)}), f32[4,4,128,128]{3,2,1,0:T(8,128)S(1)}, u32[]{:S(2)}, u32[]{:S(2)}) %all-to-all-start.2) | async-done | bytes 1048608 | tf_op jit(solution)/shard_map/cond/branch_1_fun/all_to_all | solution.py:470
  87.0 3.5 %collective-permute-start.11 = (f32[4,128,128]{2,1,0:T(8,128)}, f32[4,128,128]{2,1,0:T(8,128)S(1)}, u32[]{:S(2)}, u32[]{:S(2)}) collective-permute-start(f32[4,128,128]{2,1,0:T(8,128)} %get-tuple-element.186), channel_id=1, source_target_pairs={{0,8},{1,9},{2,10},{3,11},{4,12},{5,13},{6,14},{7,15},{8,0},{9,1},... | collective-permute-start | bytes 786440 | tf_op jit(solution)/shard_map/ppermute | solution.py:464
  91.0 24.7 %conditional.7 = (f32[4,128,128]{2,1,0:T(8,128)S(1)}, f32[4,128,128]{2,1,0:T(8,128)S(1)}, f32[128,2048]{1,0:T(8,128)S(1)}, f32[1,2048,128]{2,1,0:T(8,128)}, f32[1,2048,128]{2,1,0:T(8,128)}) conditional(s32[]{:T(128)} %convert_element_type.2, () %tuple.44, (f32[4,128,128]{2,1,0:T(8,128)}, f32[16,128,128]{2,1,0:T(8,128)}, ...), branch_computations={%region_6.0_spmd, %region_7.0_spmd} | conditional | flops 262144 | bytes 27263172 | solution.py:506
  93.6 3.5 %all-to-all-start.3 = ((f32[4,4,128,128]{3,2,1,0:T(8,128)}), f32[4,4,128,128]{3,2,1,0:T(8,128)S(1)}, u32[]{:S(2)}, u32[]{:S(2)}) async-start(f32[4,4,128,128]{3,2,1,0:T(8,128)} %branch_1_fun.22), calls=%async_computation.3 | async-start | bytes 2097152 | tf_op jit(solution)/shard_map/cond/branch_1_fun/all_to_all | solution.py:470
  99.1 12.3 %all-to-all-done.3.refs_0_ = f32[4,4,128,128]{3,2,1,0:T(8,128)S(1)} async-done(((f32[4,4,128,128]{3,2,1,0:T(8,128)}), f32[4,4,128,128]{3,2,1,0:T(8,128)S(1)}, u32[]{:S(2)}, u32[]{:S(2)}) %all-to-all-start.3) | async-done | bytes 1048608 | tf_op jit(solution)/shard_map/cond/branch_1_fun/all_to_all | solution.py:470
  111.4 2.6 %branch_1_fun.23 = (f32[16,128,128]{2,1,0:T(8,128)}, f32[16,128,128]{2,1,0:T(8,128)}) custom-call(f32[4,4,128,128]{3,2,1,0:T(8,128)S(1)} %all-to-all-done.3.refs_0_, f32[16,128,128]{2,1,0:T(8,128)} %get-tuple-element.128.refs_1_, f32[16,128,128]{2,1,0:T(8,128)} %copy-done.4), custom_call_target="tpu_custom_call" | custom-call | bytes 5242880 | tf_op jit(solution)/shard_map/cond/branch_1_fun/pallas_call | solution.py:407
  115.8 3.0 %shard_map.120 = (f32[16,128,128]{2,1,0:T(8,128)}, f32[16,128,128]{2,1,0:T(8,128)}) custom-call(f32[4,128,128]{2,1,0:T(8,128)S(1)} %collective-permute-done.10.refs_0_, f32[4,128,128]{2,1,0:T(8,128)S(1)} %collective-permute-done.11.refs_1_, f32[4,128,128]{2,1,0:T(8,128)S(1)} %collective-permute-done.12.refs_2_, f32[16,128,128]{2,1,0:T(8,128)} %bitcast.13, ...), custom_call_target="tpu_custom_call" | custom-call | bytes 5505024 | tf_op jit(solution)/shard_map/pallas_call | solution.py:407
  (51 shorter events, 18.6 us)
Async XLA Ops:
  0.6 8.2 %copy-start.1 = (bf16[768,256]{1,0:T(8,128)(2,1)S(1)}, bf16[768,256]{1,0:T(8,128)(2,1)}, u32[]{:S(2)}) copy-start(bf16[768,256]{1,0:T(8,128)(2,1)} %constant.11.clone) | copy-start | bytes 1179652
  0.6 8.2 %copy-start.6 = (f32[2,16,8,128]{3,2,1,0:T(8,128)S(1)}, f32[2,16,8,128]{3,2,1,0:T(8,128)}, u32[]{:S(2)}) copy-start(f32[2,16,8,128]{3,2,1,0:T(8,128)} %constant.17.clone) | copy-start | bytes 393220
  0.7 8.2 %copy-start.3 = (f32[1,2048,128]{2,1,0:T(8,128)S(1)}, f32[1,2048,128]{2,1,0:T(8,128)}, u32[]{:S(2)}) copy-start(f32[1,2048,128]{2,1,0:T(8,128)} %param.20) | copy-start | bytes 3145732
  3.2 29.9 %collective-permute-start.4 = (f32[4,128,128]{2,1,0:T(8,128)S(1)}, f32[4,128,128]{2,1,0:T(8,128)}, u32[]{:S(2)}, u32[]{:S(2)}) collective-permute-start(f32[4,128,128]{2,1,0:T(8,128)S(1)} %get-tuple-element.170), channel_id=1, source_target_pairs={{0,4},{1,5},{2,6},{3,7},{4,0},{5,1},{6,2},{7,3},{8,12},{9,13},{10,... | collective-permute-start | bytes 786440 | tf_op jit(solution)/shard_map/ppermute | solution.py:464
  6.3 27.1 %collective-permute-start.5 = (f32[4,128,128]{2,1,0:T(8,128)S(1)}, f32[4,128,128]{2,1,0:T(8,128)}, u32[]{:S(2)}, u32[]{:S(2)}) collective-permute-start(f32[4,128,128]{2,1,0:T(8,128)S(1)} %get-tuple-element.171), channel_id=1, source_target_pairs={{0,8},{1,9},{2,10},{3,11},{4,12},{5,13},{6,14},{7,15},{8,0},{9,1},... | collective-permute-start | bytes 786440 | tf_op jit(solution)/shard_map/ppermute | solution.py:464
  8.8 24.5 %collective-permute-start.6 = (f32[4,128,128]{2,1,0:T(8,128)S(1)}, f32[4,128,128]{2,1,0:T(8,128)}, u32[]{:S(2)}, u32[]{:S(2)}) collective-permute-start(f32[4,128,128]{2,1,0:T(8,128)S(1)} %get-tuple-element.172), channel_id=1, source_target_pairs={{0,12},{1,13},{2,14},{3,15},{4,8},{5,9},{6,10},{7,11},{8,4},{9,5},... | collective-permute-start | bytes 786440 | tf_op jit(solution)/shard_map/ppermute | solution.py:464
  11.0 16.9 %all-to-all-start = ((f32[4,4,128,128]{3,2,1,0:T(8,128)}), f32[4,4,128,128]{3,2,1,0:T(8,128)S(1)}, u32[]{:S(2)}, u32[]{:S(2)}) async-start(f32[4,4,128,128]{3,2,1,0:T(8,128)} %branch_1_fun.12), calls=%async_computation | async-start | bytes 2097152 | tf_op jit(solution)/shard_map/cond/branch_1_fun/all_to_all | solution.py:470
  28.9 32.8 %collective-permute-start.1 = (f32[4,128,128]{2,1,0:T(8,128)}, f32[4,128,128]{2,1,0:T(8,128)S(1)}, u32[]{:S(2)}, u32[]{:S(2)}) collective-permute-start(f32[4,128,128]{2,1,0:T(8,128)} %get-tuple-element.167), channel_id=1, source_target_pairs={{0,4},{1,5},{2,6},{3,7},{4,0},{5,1},{6,2},{7,3},{8,12},{9,13},{10,... | collective-permute-start | bytes 786440 | tf_op jit(solution)/shard_map/ppermute | solution.py:464
  29.6 32.5 %collective-permute-start.2 = (f32[4,128,128]{2,1,0:T(8,128)}, f32[4,128,128]{2,1,0:T(8,128)S(1)}, u32[]{:S(2)}, u32[]{:S(2)}) collective-permute-start(f32[4,128,128]{2,1,0:T(8,128)} %get-tuple-element.168), channel_id=1, source_target_pairs={{0,8},{1,9},{2,10},{3,11},{4,12},{5,13},{6,14},{7,15},{8,0},{9,1},... | collective-permute-start | bytes 786440 | tf_op jit(solution)/shard_map/ppermute | solution.py:464
  33.0 29.1 %collective-permute-start.3 = (f32[4,128,128]{2,1,0:T(8,128)}, f32[4,128,128]{2,1,0:T(8,128)S(1)}, u32[]{:S(2)}, u32[]{:S(2)}) collective-permute-start(f32[4,128,128]{2,1,0:T(8,128)} %get-tuple-element.169), channel_id=1, source_target_pairs={{0,12},{1,13},{2,14},{3,15},{4,8},{5,9},{6,10},{7,11},{8,4},{9,5},... | collective-permute-start | bytes 786440 | tf_op jit(solution)/shard_map/ppermute | solution.py:464
  35.5 15.8 %all-to-all-start.1 = ((f32[4,4,128,128]{3,2,1,0:T(8,128)}), f32[4,4,128,128]{3,2,1,0:T(8,128)S(1)}, u32[]{:S(2)}, u32[]{:S(2)}) async-start(f32[4,4,128,128]{3,2,1,0:T(8,128)} %branch_1_fun.15), calls=%async_computation.1 | async-start | bytes 2097152 | tf_op jit(solution)/shard_map/cond/branch_1_fun/all_to_all | solution.py:470
  57.6 32.9 %collective-permute-start.7 = (f32[4,128,128]{2,1,0:T(8,128)}, f32[4,128,128]{2,1,0:T(8,128)}, u32[]{:S(2)}, u32[]{:S(2)}) collective-permute-start(f32[4,128,128]{2,1,0:T(8,128)} %get-tuple-element.180), channel_id=1, source_target_pairs={{0,4},{1,5},{2,6},{3,7},{4,0},{5,1},{6,2},{7,3},{8,12},{9,13},{10,... | collective-permute-start | bytes 786440 | tf_op jit(solution)/shard_map/ppermute | solution.py:464
  58.1 32.8 %collective-permute-start.8 = (f32[4,128,128]{2,1,0:T(8,128)}, f32[4,128,128]{2,1,0:T(8,128)}, u32[]{:S(2)}, u32[]{:S(2)}) collective-permute-start(f32[4,128,128]{2,1,0:T(8,128)} %get-tuple-element.181), channel_id=1, source_target_pairs={{0,8},{1,9},{2,10},{3,11},{4,12},{5,13},{6,14},{7,15},{8,0},{9,1},... | collective-permute-start | bytes 786440 | tf_op jit(solution)/shard_map/ppermute | solution.py:464
  61.7 29.3 %collective-permute-start.9 = (f32[4,128,128]{2,1,0:T(8,128)}, f32[4,128,128]{2,1,0:T(8,128)}, u32[]{:S(2)}, u32[]{:S(2)}) collective-permute-start(f32[4,128,128]{2,1,0:T(8,128)} %get-tuple-element.182), channel_id=1, source_target_pairs={{0,12},{1,13},{2,14},{3,15},{4,8},{5,9},{6,10},{7,11},{8,4},{9,5},... | collective-permute-start | bytes 786440 | tf_op jit(solution)/shard_map/ppermute | solution.py:464
  62.1 28.9 %copy-start = (f32[1,2048,128]{2,1,0:T(8,128)S(1)}, f32[1,2048,128]{2,1,0:T(8,128)}, u32[]{:S(2)}) copy-start(f32[1,2048,128]{2,1,0:T(8,128)} %param.17) | copy-start | bytes 3145732
  62.1 7.5 %copy-start.7 = (f32[2,16,8,128]{3,2,1,0:T(8,128)}, f32[2,16,8,128]{3,2,1,0:T(8,128)S(1)}, u32[]{:S(2)}) copy-start(f32[2,16,8,128]{3,2,1,0:T(8,128)S(1)} %get-tuple-element.105.refs_4_.refs_0_) | copy-start | bytes 393220 | tf_op jit(solution)/shard_map/cond
  69.6 3.7 %copy-start.5 = (bf16[768,256]{1,0:T(8,128)(2,1)S(1)}, bf16[768,256]{1,0:T(8,128)(2,1)}, u32[]{:S(2)}) copy-start(bf16[768,256]{1,0:T(8,128)(2,1)} %get-tuple-element.107.refs_6_.refs_1_) | copy-start | bytes 1179652 | tf_op jit(solution)/shard_map/cond
  69.6 15.9 %all-to-all-start.2 = ((f32[4,4,128,128]{3,2,1,0:T(8,128)}), f32[4,4,128,128]{3,2,1,0:T(8,128)S(1)}, u32[]{:S(2)}, u32[]{:S(2)}) async-start(f32[4,4,128,128]{3,2,1,0:T(8,128)} %get-tuple-element.111), calls=%async_computation.2 | async-start | bytes 2097152 | tf_op jit(solution)/shard_map/cond/branch_1_fun/all_to_all | solution.py:470
  86.5 29.2 %collective-permute-start.10 = (f32[4,128,128]{2,1,0:T(8,128)}, f32[4,128,128]{2,1,0:T(8,128)S(1)}, u32[]{:S(2)}, u32[]{:S(2)}) collective-permute-start(f32[4,128,128]{2,1,0:T(8,128)} %get-tuple-element.185), channel_id=1, source_target_pairs={{0,4},{1,5},{2,6},{3,7},{4,0},{5,1},{6,2},{7,3},{8,12},{9,13},{10,... | collective-permute-start | bytes 786440 | tf_op jit(solution)/shard_map/ppermute | solution.py:464
  87.0 28.7 %collective-permute-start.11 = (f32[4,128,128]{2,1,0:T(8,128)}, f32[4,128,128]{2,1,0:T(8,128)S(1)}, u32[]{:S(2)}, u32[]{:S(2)}) collective-permute-start(f32[4,128,128]{2,1,0:T(8,128)} %get-tuple-element.186), channel_id=1, source_target_pairs={{0,8},{1,9},{2,10},{3,11},{4,12},{5,13},{6,14},{7,15},{8,0},{9,1},... | collective-permute-start | bytes 786440 | tf_op jit(solution)/shard_map/ppermute | solution.py:464
  90.6 25.2 %collective-permute-start.12 = (f32[4,128,128]{2,1,0:T(8,128)}, f32[4,128,128]{2,1,0:T(8,128)S(1)}, u32[]{:S(2)}, u32[]{:S(2)}) collective-permute-start(f32[4,128,128]{2,1,0:T(8,128)} %get-tuple-element.187), channel_id=1, source_target_pairs={{0,12},{1,13},{2,14},{3,15},{4,8},{5,9},{6,10},{7,11},{8,4},{9,5},... | collective-permute-start | bytes 786440 | tf_op jit(solution)/shard_map/ppermute | solution.py:464
  91.0 23.0 %collective-permute-start = (f32[128,2048]{1,0:T(8,128)}, f32[128,2048]{1,0:T(8,128)}, u32[]{:S(2)}, u32[]{:S(2)}) collective-permute-start(f32[128,2048]{1,0:T(8,128)} %get-tuple-element.123), channel_id=1, source_target_pairs={{0,16},{16,0},{1,17},{17,1},{2,18},{18,2},{3,19},{19,3},{4,20},{20... | collective-permute-start | bytes 3145736 | tf_op jit(solution)/shard_map/cond/branch_1_fun/ppermute | solution.py:553
  93.6 17.8 %all-to-all-start.3 = ((f32[4,4,128,128]{3,2,1,0:T(8,128)}), f32[4,4,128,128]{3,2,1,0:T(8,128)S(1)}, u32[]{:S(2)}, u32[]{:S(2)}) async-start(f32[4,4,128,128]{3,2,1,0:T(8,128)} %branch_1_fun.22), calls=%async_computation.3 | async-start | bytes 2097152 | tf_op jit(solution)/shard_map/cond/branch_1_fun/all_to_all | solution.py:470
  115.7 3.0 %copy-start.8 = (f32[128,2048]{1,0:T(8,128)}, f32[128,2048]{1,0:T(8,128)S(1)}, u32[]{:S(2)}) copy-start(f32[128,2048]{1,0:T(8,128)S(1)} %get-tuple-element.164) | copy-start | bytes 3145732
  (4 other events, 6.9 us)

commit v10 on v9

--- a/solution.py
+++ b/solution.py
@@ -12,7 +12,7 @@
 ROWS = 8
 PLANES = 4
 PARTS = 4
-VMEM_BYTES = 24 * 1024 * 1024
+VMEM_BYTES = 16 * 1024 * 1024
 
 
 def twist(value, turn):
@@ -267,25 +267,25 @@
     wait_all(stores)
 
 
-def load_pairs(n, a_ref, b_ref, a_buf, b_buf, sem):
-    loads = [
-        copies_of([(a_ref.at[part], a_buf.at[part]), (b_ref.at[part], b_buf.at[part])], sem.at[i])
-        for i, part in enumerate(parts_of(n))
-    ]
-    for load in loads:
-        start_all(load)
-    return loads
-
-
 def product_split_kernel(planes, n, a_ref, b_ref, *refs):
-    out_refs, (a_buf, b_buf, sem) = refs[:planes], refs[planes:]
+    keep_ref, *send_refs = refs[:planes]
+    a_buf, b_buf, keep_buf, sem, keep_sem = refs[planes:]
     width = n // planes
     z = plane(width)
-    for load in load_pairs(n, a_ref, b_ref, a_buf, b_buf, sem):
-        wait_all(load)
+    loads = []
     for d in range(planes):
-        for q in range(width):
-            out_refs[d][q] = a_buf[(z ^ d) * width + q] * b_buf[(z ^ d) * width + q]
+        part = pl.ds((z ^ d) * width, width)
+        loads.append(
+            copies_of([(a_ref.at[part], a_buf.at[d]), (b_ref.at[part], b_buf.at[d])], sem.at[d])
+        )
+        start_all(loads[d])
+    keep = pltpu.make_async_copy(keep_buf, keep_ref, keep_sem)
+    for d, ref in enumerate((keep_buf, *send_refs)):
+        wait_all(loads[d])
+        ref[...] = a_buf[d] * b_buf[d]
+        if d == 0:
+            keep.start()
+    keep.wait()
 
 
 def product_kernel(planes, n, a_ref, b_ref, after_ref, out_ref, a_buf, b_buf, buf_ref, sem):
@@ -320,40 +320,17 @@
     wait_all(stores)
 
 
-def gate_parts(width, blocks, a_ref, b_ref, outs, a_buf, b_buf, sem):
+def gate_kernel(planes, width, x_ref, a_ref, b_ref, after_ref, oa_ref, ob_ref, a_buf, b_buf, sem):
+    z = plane(width)
     stores = []
-    for d, (read, first) in enumerate(blocks):
-        part = pl.ds(first, width)
-        x = read()
-        a_buf[part] = x * a_ref[part]
-        b_buf[part] = x * b_ref[part]
-        pairs = [(buf.at[part], out.at[part]) for buf, out in zip((a_buf, b_buf), outs)]
-        stores.extend(copies_of(pairs, sem.at[d]))
+    for d in range(planes):
+        rows = pl.ds((z ^ d) * width, width)
+        x = x_ref[:, d]
+        a_buf[rows] = x * a_ref[rows]
+        b_buf[rows] = x * b_ref[rows]
+        stores += copies_of([(a_buf.at[rows], oa_ref.at[rows]), (b_buf.at[rows], ob_ref.at[rows])], sem.at[d])
         start_all(stores[-2:])
     wait_all(stores)
-
-
-def gate_kernel(
-    planes, width, x_ref, a_ref, b_ref, oa_ref, ob_ref, x_buf, a_in, b_in, a_buf, b_buf, sem
-):
-    z = plane(width)
-    loads = []
-    for d in range(planes):
-        part = pl.ds((z ^ d) * width, width)
-        pairs = [
-            (x_ref.at[:, d], x_buf.at[d]),
-            (a_ref.at[part], a_in.at[part]),
-            (b_ref.at[part], b_in.at[part]),
-        ]
-        loads.append(copies_of(pairs, sem.at[planes + d]))
-        start_all(loads[-1])
-
-    def read(d):
-        wait_all(loads[d])
-        return x_buf[d]
-
-    blocks = [(lambda d=d: read(d), (z ^ d) * width) for d in range(planes)]
-    gate_parts(width, blocks, a_in, b_in, (oa_ref, ob_ref), a_buf, b_buf, sem)
 
 
 def gate_near_kernel(
@@ -506,8 +483,8 @@
         return lax.cond(always, body, never, *args)
 
     keep_p, *send_p = kernel_call(
-        part(product_split_kernel, planes, n), "hh", [("u", one)] + [("v", one)] * (planes - 1),
-        [rows, rows, semaphores(PARTS, 2)],
+        part(product_split_kernel, planes, n), "hh", [("h", one)] + [("v", one)] * (planes - 1),
+        [by_plane, by_plane, pltpu.VMEM(one, f32), semaphores(planes, 2), pltpu.SemaphoreType.DMA],
     )(key, value)
     got_p = along_z(send_p)
 
@@ -559,9 +536,9 @@
             [pltpu.VMEM(one, f32)] * 3 + [semaphores(2, 3)],
         )(near_b, value, key)
         gated, grad_query = kernel_call(
-            part(gate_kernel, planes, width), "ahh", [("h", blocks)] * 2,
-            [by_plane, *[rows] * 4, semaphores(2 * planes, 3)],
-        )(conv_tok, query, cot)
+            part(gate_kernel, planes, width), "vvva", [("h", blocks)] * 2,
+            [rows, rows, semaphores(planes, 2)],
+        )(conv_tok, query, cot, grad_filter)
         return gated, grad_query, begun, grad_filter
 
     gated, grad_query, begun, grad_filter = grouped(

time: 119 us -> 118 us (level)
  Pallas kernels: 43.3 us -> 42 us
    pallas_call x14, Pallas kernels: 43.3 us -> 42 us  [run(): pl.pallas_call(body, in_specs=[pl.BlockSpec(memory_space=SPACES[space]) f...]
  transfers between devices with their start and end apart: 17 -> 17, of which waited for: 4 -> 4; matrix products, arithmetic and copies ran while one was open for 1% -> 2% of each run, Pallas kernels for 32% -> 32%
where the time goes in v10:
time: 118 us; the launch traced here: 117 us
  Pallas kernels  42 us (36%)
  waiting for transfers between devices  37.1 us (31%)
  starting transfers between devices  33.8 us (29%)
  other arithmetic  2.64 us (2%)
    pallas_call x14, Pallas kernels, run(): pl.pallas_call(body, in_specs=[pl.BlockSpec(memory_space=SPACES[space]) f...  42 us
    all_to_all x4, waiting for transfers between devices, within_plane(): lax.all_to_all(x, 'context', 0, 0, axis_index_groups=members, tiled=True)  37 us
    ppermute x12, starting transfers between devices, along_z(): lax.ppermute(x, 'context', [(i, i ^ d * width) for i in range(n)])  19 us
    all_to_all x4, starting transfers between devices, within_plane(): lax.all_to_all(x, 'context', 0, 0, axis_index_groups=members, tiled=True)  14.7 us
    add x1, other arithmetic, fourth(): grad_filter = own + lax.ppermute(own, 'dp', [(0, 1), (1, 0)])  2.64 us
  transfers between devices with their start and end apart: 17, of which 4 were waited for; matrix products, arithmetic and copies ran while one was open for 2% of the time, Pallas kernels for 32%

profile of v10, /device:TPU:0, one launch (start us, length us, event | category | flops | bytes accessed | tf_op | source)
XLA Modules:
  0.0 117.2 jit_solution(8307401155519610436)
XLA Ops:
  2.6 3.1 %collective-permute-start.4 = (f32[4,128,128]{2,1,0:T(8,128)S(1)}, f32[4,128,128]{2,1,0:T(8,128)}, u32[]{:S(2)}, u32[]{:S(2)}) collective-permute-start(f32[4,128,128]{2,1,0:T(8,128)S(1)} %get-tuple-element.170), channel_id=1, source_target_pairs={{0,4},{1,5},{2,6},{3,7},{4,0},{5,1},{6,2},{7,3},{8,12},{9,13},{10,... | collective-permute-start | bytes 786440 | tf_op jit(solution)/shard_map/ppermute | solution.py:441
  5.7 2.6 %collective-permute-start.5 = (f32[4,128,128]{2,1,0:T(8,128)S(1)}, f32[4,128,128]{2,1,0:T(8,128)}, u32[]{:S(2)}, u32[]{:S(2)}) collective-permute-start(f32[4,128,128]{2,1,0:T(8,128)S(1)} %get-tuple-element.171), channel_id=1, source_target_pairs={{0,8},{1,9},{2,10},{3,11},{4,12},{5,13},{6,14},{7,15},{8,0},{9,1},... | collective-permute-start | bytes 786440 | tf_op jit(solution)/shard_map/ppermute | solution.py:441
  8.3 20.3 %conditional.4 = (f32[4,128,128]{2,1,0:T(8,128)}, f32[4,128,128]{2,1,0:T(8,128)}, f32[4,128,128]{2,1,0:T(8,128)}, f32[4,128,128]{2,1,0:T(8,128)}, f32[16,64,256]{2,1,0:T(8,128)}) conditional(s32[]{:T(128)} %convert_element_type.2, () %tuple.46, (f32[16,128,128]{2,1,0:T(8,128)}, f32[16,128,128]{2,1,0:T(8,128)}, f32[4,128,128]{2,1,0:T(8,128)}, ...), branch_computations={%region_0.0_spmd, %region_1.0_spmd} | conditional | flops 268435456 | bytes 11665480 | solution.py:483
  10.8 3.9 %all-to-all-start = ((f32[4,4,128,128]{3,2,1,0:T(8,128)}), f32[4,4,128,128]{3,2,1,0:T(8,128)S(1)}, u32[]{:S(2)}, u32[]{:S(2)}) async-start(f32[4,4,128,128]{3,2,1,0:T(8,128)} %branch_1_fun.12), calls=%async_computation | async-start | bytes 2097152 | tf_op jit(solution)/shard_map/cond/branch_1_fun/all_to_all | solution.py:447
  17.2 10.4 %all-to-all-done.refs_0_ = f32[4,4,128,128]{3,2,1,0:T(8,128)S(1)} async-done(((f32[4,4,128,128]{3,2,1,0:T(8,128)}), f32[4,4,128,128]{3,2,1,0:T(8,128)S(1)}, u32[]{:S(2)}, u32[]{:S(2)}) %all-to-all-start) | async-done | bytes 1048608 | tf_op jit(solution)/shard_map/cond/branch_1_fun/all_to_all | solution.py:447
  29.3 3.5 %collective-permute-start.2 = (f32[4,128,128]{2,1,0:T(8,128)}, f32[4,128,128]{2,1,0:T(8,128)}, u32[]{:S(2)}, u32[]{:S(2)}) collective-permute-start(f32[4,128,128]{2,1,0:T(8,128)} %get-tuple-element.168), channel_id=1, source_target_pairs={{0,8},{1,9},{2,10},{3,11},{4,12},{5,13},{6,14},{7,15},{8,0},{9,1},... | collective-permute-start | bytes 786440 | tf_op jit(solution)/shard_map/ppermute | solution.py:441
  33.1 24.7 %conditional.5 = (f32[4,128,128]{2,1,0:T(8,128)}, f32[4,128,128]{2,1,0:T(8,128)}, f32[4,128,128]{2,1,0:T(8,128)}, f32[4,128,128]{2,1,0:T(8,128)}, f32[16,128,256...) conditional(s32[]{:T(128)} %convert_element_type.2, () %tuple.48, (f32[4,128,128]{2,1,0:T(8,128)}, ...), branch_computations={%region_2.0_spmd, %region_3.0_spmd} | conditional | flops 1342177280 | bytes 20709492 | solution.py:483
  35.7 3.5 %all-to-all-start.1 = ((f32[4,4,128,128]{3,2,1,0:T(8,128)}), f32[4,4,128,128]{3,2,1,0:T(8,128)S(1)}, u32[]{:S(2)}, u32[]{:S(2)}) async-start(f32[4,4,128,128]{3,2,1,0:T(8,128)} %branch_1_fun.15), calls=%async_computation.1 | async-start | bytes 2097152 | tf_op jit(solution)/shard_map/cond/branch_1_fun/all_to_all | solution.py:447
  39.2 2.8 %branch_1_fun.16.refs_5_ = f32[16,64,256]{2,1,0:T(8,128)} custom-call(f32[128,2048]{1,0:T(8,128)} %copy-done.4, f32[2,16,8,128]{3,2,1,0:T(8,128)S(1)} %get-tuple-element.91.refs_1_, bf16[768,256]{1,0:T(8,128)(2,1)S(1)} %get-tuple-element.92.refs_2_), custom_call_target="tpu_custom_call" | custom-call | flops 268435456 | bytes 3014656 | tf_op jit(solution)/shard_map/cond/branch_1_fun/pallas_call | solution.py:384
  42.0 9.6 %all-to-all-done.1.refs_0_ = f32[4,4,128,128]{3,2,1,0:T(8,128)S(1)} async-done(((f32[4,4,128,128]{3,2,1,0:T(8,128)}), f32[4,4,128,128]{3,2,1,0:T(8,128)S(1)}, u32[]{:S(2)}, u32[]{:S(2)}) %all-to-all-start.1) | async-done | bytes 1048608 | tf_op jit(solution)/shard_map/cond/branch_1_fun/all_to_all | solution.py:447
  51.5 6.2 %branch_1_fun.17 = (f32[4,128,128]{2,1,0:T(8,128)}, f32[4,128,128]{2,1,0:T(8,128)}, f32[4,128,128]{2,1,0:T(8,128)}, f32[4,128,128]{2,1,0:T(8,128)}, f32[16,128,256]{2,1,0:T(8,128)}) custom-call(f32[4,4,128,128]{3,2,1,0:T(8,128)S(1)} %all-to-all-done.1.refs_0_, f32[2,16,8,128]{3,2,1,0:T(8,128)S(1)} %get-tuple-element.91.refs_1_, ...), custom_call_target="tpu_custom_call" | custom-call | flops 1073741824 | bytes 7995392 | tf_op jit(solution)/shard_map/cond/branch_1_fun/pallas_call | solution.py:384
  58.3 3.5 %collective-permute-start.8 = (f32[4,128,128]{2,1,0:T(8,128)}, f32[4,128,128]{2,1,0:T(8,128)S(1)}, u32[]{:S(2)}, u32[]{:S(2)}) collective-permute-start(f32[4,128,128]{2,1,0:T(8,128)} %get-tuple-element.181), channel_id=1, source_target_pairs={{0,8},{1,9},{2,10},{3,11},{4,12},{5,13},{6,14},{7,15},{8,0},{9,1},... | collective-permute-start | bytes 786440 | tf_op jit(solution)/shard_map/ppermute | solution.py:441
  62.2 24.6 %conditional.6 = (f32[4,128,128]{2,1,0:T(8,128)}, f32[4,128,128]{2,1,0:T(8,128)}, f32[4,128,128]{2,1,0:T(8,128)}, f32[4,128,128]{2,1,0:T(8,128)}, f32[128,2048]{1,0:T(8,128)}) conditional(s32[]{:T(128)} %convert_element_type.2, () %tuple.45, (f32[4,128,128]{2,1,0:T(8,128)}, f32[4,128,128]{2,1,0:T(8,128)S(1)}, f32[4,128,128]{2,1,0:T(8,128)}, ...), branch_computations={%region_4.0_spmd, %region_5.0_spmd} | conditional | flops 1610612736 | bytes 22806656 | solution.py:483
  63.0 6.9 %branch_1_fun.18 = (f32[4,4,128,128]{3,2,1,0:T(8,128)}, f32[16,128,256]{2,1,0:T(8,128)}) custom-call(f32[4,128,128]{2,1,0:T(8,128)} %get-tuple-element.101.refs_0_, f32[4,128,128]{2,1,0:T(8,128)S(1)} %get-tuple-element.102.refs_1_, f32[4,128,128]{2,1,0:T(8,128)} %get-tuple-element.103.refs_2_, f32[4,128,128]{2,1,0:T(8,128)} %get-tuple-element.104.refs_3_, ...), custom_call_target="tpu_custom_call" | custom-call | flops 1073741824 | bytes 8257536 | tf_op jit(solution)/shard_map/cond/branch_1_fun/pallas_call | solution.py:384
  69.9 3.7 %all-to-all-start.2 = ((f32[4,4,128,128]{3,2,1,0:T(8,128)}), f32[4,4,128,128]{3,2,1,0:T(8,128)S(1)}, u32[]{:S(2)}, u32[]{:S(2)}) async-start(f32[4,4,128,128]{3,2,1,0:T(8,128)} %get-tuple-element.111), calls=%async_computation.2 | async-start | bytes 2097152 | tf_op jit(solution)/shard_map/cond/branch_1_fun/all_to_all | solution.py:447
  73.6 5.2 %branch_1_fun.20 = f32[128,2048]{1,0:T(8,128)} custom-call(f32[2,16,8,128]{3,2,1,0:T(8,128)S(1)} %get-tuple-element.105.refs_4_.refs_0_, bf16[768,256]{1,0:T(8,128)(2,1)S(1)} %copy-done.5, f32[16,128,256]{2,1,0:T(8,128)} %get-tuple-element.116.refs_2_, f32[16,128,256]{2,1,0:T(8,128)} %get-tuple-element.117.refs_3_), custom_call_target="tpu_custom_call" | custom-call | flops 536870912 | bytes 6160384 | tf_op jit(solution)/shard_map/cond/branch_1_fun/pallas_call | solution.py:384
  78.7 7.1 %all-to-all-done.2.refs_0_ = f32[4,4,128,128]{3,2,1,0:T(8,128)S(1)} async-done(((f32[4,4,128,128]{3,2,1,0:T(8,128)}), f32[4,4,128,128]{3,2,1,0:T(8,128)S(1)}, u32[]{:S(2)}, u32[]{:S(2)}) %all-to-all-start.2) | async-done | bytes 1048608 | tf_op jit(solution)/shard_map/cond/branch_1_fun/all_to_all | solution.py:447
  87.3 3.5 %collective-permute-start.11 = (f32[4,128,128]{2,1,0:T(8,128)}, f32[4,128,128]{2,1,0:T(8,128)S(1)}, u32[]{:S(2)}, u32[]{:S(2)}) collective-permute-start(f32[4,128,128]{2,1,0:T(8,128)} %get-tuple-element.186), channel_id=1, source_target_pairs={{0,8},{1,9},{2,10},{3,11},{4,12},{5,13},{6,14},{7,15},{8,0},{9,1},... | collective-permute-start | bytes 786440 | tf_op jit(solution)/shard_map/ppermute | solution.py:441
  91.3 23.2 %conditional.7 = (f32[4,128,128]{2,1,0:T(8,128)S(1)}, f32[4,128,128]{2,1,0:T(8,128)S(1)}, f32[128,2048]{1,0:T(8,128)}, f32[1,2048,128]{2,1,0:T(8,128)}, f32[1,2048,128]{2,1,0:T(8,128)}) conditional(s32[]{:T(128)} %convert_element_type.2, () %tuple.44, (f32[4,128,128]{2,1,0:T(8,128)}, f32[16,128,128]{2,1,0:T(8,128)}, f32[16,128,128]{2,1,0:T(8,128)S(1)}, ...), branch_computations={%region_6.0_spmd, %region_7.0_spmd} | conditional | flops 262144 | bytes 24117416 | solution.py:483
  93.5 3.5 %all-to-all-start.3 = ((f32[4,4,128,128]{3,2,1,0:T(8,128)}), f32[4,4,128,128]{3,2,1,0:T(8,128)S(1)}, u32[]{:S(2)}, u32[]{:S(2)}) async-start(f32[4,4,128,128]{3,2,1,0:T(8,128)} %branch_1_fun.22), calls=%async_computation.3 | async-start | bytes 2097152 | tf_op jit(solution)/shard_map/cond/branch_1_fun/all_to_all | solution.py:447
  98.9 2.6 %add.2.refs_3_ = f32[128,2048]{1,0:T(8,128)} add(f32[128,2048]{1,0:T(8,128)} %get-tuple-element.123, f32[128,2048]{1,0:T(8,128)} %collective-permute-done) | non-fusion elementwise | flops 262144 | bytes 3145728 | tf_op jit(solution)/shard_map/cond/branch_1_fun/add | solution.py:530
  101.6 10.0 %all-to-all-done.3.refs_0_ = f32[4,4,128,128]{3,2,1,0:T(8,128)S(1)} async-done(((f32[4,4,128,128]{3,2,1,0:T(8,128)}), f32[4,4,128,128]{3,2,1,0:T(8,128)S(1)}, u32[]{:S(2)}, u32[]{:S(2)}) %all-to-all-start.3) | async-done | bytes 1048608 | tf_op jit(solution)/shard_map/cond/branch_1_fun/all_to_all | solution.py:447
  111.5 3.0 %branch_1_fun.23 = (f32[16,128,128]{2,1,0:T(8,128)}, f32[16,128,128]{2,1,0:T(8,128)}) custom-call(f32[4,4,128,128]{3,2,1,0:T(8,128)S(1)} %all-to-all-done.3.refs_0_, f32[16,128,128]{2,1,0:T(8,128)} %get-tuple-element.128.refs_1_, f32[16,128,128]{2,1,0:T(8,128)} %get-tuple-element.129.refs_2_, f32[128,2048]{1,0:T(8,128)} %add.2.refs_3_), custom_call_target="tpu_custom_call" | custom-call | bytes 6291456 | tf_op jit(solution)/shard_map/cond/branch_1_fun/pallas_call | solution.py:384
  114.6 2.6 %shard_map.120 = (f32[16,128,128]{2,1,0:T(8,128)}, f32[16,128,128]{2,1,0:T(8,128)}) custom-call(f32[4,128,128]{2,1,0:T(8,128)S(1)} %collective-permute-done.10.refs_0_, f32[4,128,128]{2,1,0:T(8,128)S(1)} %collective-permute-done.11.refs_1_, f32[4,128,128]{2,1,0:T(8,128)S(1)} %collective-permute-done.12.refs_2_, f32[16,128,128]{2,1,0:T(8,128)} %bitcast.13, ...), custom_call_target="tpu_custom_call" | custom-call | bytes 5505024 | tf_op jit(solution)/shard_map/pallas_call | solution.py:384
  (47 shorter events, 19.1 us)
Async XLA Ops:
  0.6 7.7 %copy-start.1 = (bf16[768,256]{1,0:T(8,128)(2,1)S(1)}, bf16[768,256]{1,0:T(8,128)(2,1)}, u32[]{:S(2)}) copy-start(bf16[768,256]{1,0:T(8,128)(2,1)} %constant.11.clone) | copy-start | bytes 1179652
  0.6 7.7 %copy-start.6 = (f32[2,16,8,128]{3,2,1,0:T(8,128)S(1)}, f32[2,16,8,128]{3,2,1,0:T(8,128)}, u32[]{:S(2)}) copy-start(f32[2,16,8,128]{3,2,1,0:T(8,128)} %constant.17.clone) | copy-start | bytes 393220
  0.7 7.7 %copy-start.3 = (f32[128,2048]{1,0:T(8,128)S(1)}, f32[128,2048]{1,0:T(8,128)}, u32[]{:S(2)}) copy-start(f32[128,2048]{1,0:T(8,128)} %param.19) | copy-start | bytes 3145732
  2.6 30.1 %collective-permute-start.4 = (f32[4,128,128]{2,1,0:T(8,128)S(1)}, f32[4,128,128]{2,1,0:T(8,128)}, u32[]{:S(2)}, u32[]{:S(2)}) collective-permute-start(f32[4,128,128]{2,1,0:T(8,128)S(1)} %get-tuple-element.170), channel_id=1, source_target_pairs={{0,4},{1,5},{2,6},{3,7},{4,0},{5,1},{6,2},{7,3},{8,12},{9,13},{10,... | collective-permute-start | bytes 786440 | tf_op jit(solution)/shard_map/ppermute | solution.py:441
  5.7 27.4 %collective-permute-start.5 = (f32[4,128,128]{2,1,0:T(8,128)S(1)}, f32[4,128,128]{2,1,0:T(8,128)}, u32[]{:S(2)}, u32[]{:S(2)}) collective-permute-start(f32[4,128,128]{2,1,0:T(8,128)S(1)} %get-tuple-element.171), channel_id=1, source_target_pairs={{0,8},{1,9},{2,10},{3,11},{4,12},{5,13},{6,14},{7,15},{8,0},{9,1},... | collective-permute-start | bytes 786440 | tf_op jit(solution)/shard_map/ppermute | solution.py:441
  8.3 24.8 %collective-permute-start.6 = (f32[4,128,128]{2,1,0:T(8,128)S(1)}, f32[4,128,128]{2,1,0:T(8,128)}, u32[]{:S(2)}, u32[]{:S(2)}) collective-permute-start(f32[4,128,128]{2,1,0:T(8,128)S(1)} %get-tuple-element.172), channel_id=1, source_target_pairs={{0,12},{1,13},{2,14},{3,15},{4,8},{5,9},{6,10},{7,11},{8,4},{9,5},... | collective-permute-start | bytes 786440 | tf_op jit(solution)/shard_map/ppermute | solution.py:441
  10.8 16.9 %all-to-all-start = ((f32[4,4,128,128]{3,2,1,0:T(8,128)}), f32[4,4,128,128]{3,2,1,0:T(8,128)S(1)}, u32[]{:S(2)}, u32[]{:S(2)}) async-start(f32[4,4,128,128]{3,2,1,0:T(8,128)} %branch_1_fun.12), calls=%async_computation | async-start | bytes 2097152 | tf_op jit(solution)/shard_map/cond/branch_1_fun/all_to_all | solution.py:447
  28.6 33.2 %collective-permute-start.1 = (f32[4,128,128]{2,1,0:T(8,128)}, f32[4,128,128]{2,1,0:T(8,128)S(1)}, u32[]{:S(2)}, u32[]{:S(2)}) collective-permute-start(f32[4,128,128]{2,1,0:T(8,128)} %get-tuple-element.167), channel_id=1, source_target_pairs={{0,4},{1,5},{2,6},{3,7},{4,0},{5,1},{6,2},{7,3},{8,12},{9,13},{10,... | collective-permute-start | bytes 786440 | tf_op jit(solution)/shard_map/ppermute | solution.py:441
  29.3 32.9 %collective-permute-start.2 = (f32[4,128,128]{2,1,0:T(8,128)}, f32[4,128,128]{2,1,0:T(8,128)}, u32[]{:S(2)}, u32[]{:S(2)}) collective-permute-start(f32[4,128,128]{2,1,0:T(8,128)} %get-tuple-element.168), channel_id=1, source_target_pairs={{0,8},{1,9},{2,10},{3,11},{4,12},{5,13},{6,14},{7,15},{8,0},{9,1},... | collective-permute-start | bytes 786440 | tf_op jit(solution)/shard_map/ppermute | solution.py:441
  32.8 29.4 %collective-permute-start.3 = (f32[4,128,128]{2,1,0:T(8,128)}, f32[4,128,128]{2,1,0:T(8,128)}, u32[]{:S(2)}, u32[]{:S(2)}) collective-permute-start(f32[4,128,128]{2,1,0:T(8,128)} %get-tuple-element.169), channel_id=1, source_target_pairs={{0,12},{1,13},{2,14},{3,15},{4,8},{5,9},{6,10},{7,11},{8,4},{9,5},... | collective-permute-start | bytes 786440 | tf_op jit(solution)/shard_map/ppermute | solution.py:441
  35.7 15.8 %all-to-all-start.1 = ((f32[4,4,128,128]{3,2,1,0:T(8,128)}), f32[4,4,128,128]{3,2,1,0:T(8,128)S(1)}, u32[]{:S(2)}, u32[]{:S(2)}) async-start(f32[4,4,128,128]{3,2,1,0:T(8,128)} %branch_1_fun.15), calls=%async_computation.1 | async-start | bytes 2097152 | tf_op jit(solution)/shard_map/cond/branch_1_fun/all_to_all | solution.py:447
  57.8 33.1 %collective-permute-start.7 = (f32[4,128,128]{2,1,0:T(8,128)}, f32[4,128,128]{2,1,0:T(8,128)S(1)}, u32[]{:S(2)}, u32[]{:S(2)}) collective-permute-start(f32[4,128,128]{2,1,0:T(8,128)} %get-tuple-element.180), channel_id=1, source_target_pairs={{0,4},{1,5},{2,6},{3,7},{4,0},{5,1},{6,2},{7,3},{8,12},{9,13},{10,... | collective-permute-start | bytes 786440 | tf_op jit(solution)/shard_map/ppermute | solution.py:441
  58.3 33.1 %collective-permute-start.8 = (f32[4,128,128]{2,1,0:T(8,128)}, f32[4,128,128]{2,1,0:T(8,128)S(1)}, u32[]{:S(2)}, u32[]{:S(2)}) collective-permute-start(f32[4,128,128]{2,1,0:T(8,128)} %get-tuple-element.181), channel_id=1, source_target_pairs={{0,8},{1,9},{2,10},{3,11},{4,12},{5,13},{6,14},{7,15},{8,0},{9,1},... | collective-permute-start | bytes 786440 | tf_op jit(solution)/shard_map/ppermute | solution.py:441
  61.8 29.5 %collective-permute-start.9 = (f32[4,128,128]{2,1,0:T(8,128)}, f32[4,128,128]{2,1,0:T(8,128)}, u32[]{:S(2)}, u32[]{:S(2)}) collective-permute-start(f32[4,128,128]{2,1,0:T(8,128)} %get-tuple-element.182), channel_id=1, source_target_pairs={{0,12},{1,13},{2,14},{3,15},{4,8},{5,9},{6,10},{7,11},{8,4},{9,5},... | collective-permute-start | bytes 786440 | tf_op jit(solution)/shard_map/ppermute | solution.py:441
  62.2 29.1 %copy-start = (f32[1,2048,128]{2,1,0:T(8,128)S(1)}, f32[1,2048,128]{2,1,0:T(8,128)}, u32[]{:S(2)}) copy-start(f32[1,2048,128]{2,1,0:T(8,128)} %param.17) | copy-start | bytes 3145732
  69.9 3.7 %copy-start.5 = (bf16[768,256]{1,0:T(8,128)(2,1)S(1)}, bf16[768,256]{1,0:T(8,128)(2,1)}, u32[]{:S(2)}) copy-start(bf16[768,256]{1,0:T(8,128)(2,1)} %get-tuple-element.107.refs_6_.refs_1_) | copy-start | bytes 1179652 | tf_op jit(solution)/shard_map/cond
  69.9 16.0 %all-to-all-start.2 = ((f32[4,4,128,128]{3,2,1,0:T(8,128)}), f32[4,4,128,128]{3,2,1,0:T(8,128)S(1)}, u32[]{:S(2)}, u32[]{:S(2)}) async-start(f32[4,4,128,128]{3,2,1,0:T(8,128)} %get-tuple-element.111), calls=%async_computation.2 | async-start | bytes 2097152 | tf_op jit(solution)/shard_map/cond/branch_1_fun/all_to_all | solution.py:447
  86.9 27.7 %collective-permute-start.10 = (f32[4,128,128]{2,1,0:T(8,128)}, f32[4,128,128]{2,1,0:T(8,128)S(1)}, u32[]{:S(2)}, u32[]{:S(2)}) collective-permute-start(f32[4,128,128]{2,1,0:T(8,128)} %get-tuple-element.185), channel_id=1, source_target_pairs={{0,4},{1,5},{2,6},{3,7},{4,0},{5,1},{6,2},{7,3},{8,12},{9,13},{10,... | collective-permute-start | bytes 786440 | tf_op jit(solution)/shard_map/ppermute | solution.py:441
  87.3 27.3 %collective-permute-start.11 = (f32[4,128,128]{2,1,0:T(8,128)}, f32[4,128,128]{2,1,0:T(8,128)S(1)}, u32[]{:S(2)}, u32[]{:S(2)}) collective-permute-start(f32[4,128,128]{2,1,0:T(8,128)} %get-tuple-element.186), channel_id=1, source_target_pairs={{0,8},{1,9},{2,10},{3,11},{4,12},{5,13},{6,14},{7,15},{8,0},{9,1},... | collective-permute-start | bytes 786440 | tf_op jit(solution)/shard_map/ppermute | solution.py:441
  90.8 23.8 %collective-permute-start.12 = (f32[4,128,128]{2,1,0:T(8,128)}, f32[4,128,128]{2,1,0:T(8,128)S(1)}, u32[]{:S(2)}, u32[]{:S(2)}) collective-permute-start(f32[4,128,128]{2,1,0:T(8,128)} %get-tuple-element.187), channel_id=1, source_target_pairs={{0,12},{1,13},{2,14},{3,15},{4,8},{5,9},{6,10},{7,11},{8,4},{9,5},... | collective-permute-start | bytes 786440 | tf_op jit(solution)/shard_map/ppermute | solution.py:441
  91.4 7.6 %collective-permute-start = (f32[128,2048]{1,0:T(8,128)}, f32[128,2048]{1,0:T(8,128)}, u32[]{:S(2)}, u32[]{:S(2)}) collective-permute-start(f32[128,2048]{1,0:T(8,128)} %get-tuple-element.123), channel_id=1, source_target_pairs={{0,16},{16,0},{1,17},{17,1},{2,18},{18,2},{3,19},{19,3},{4,20},{20... | collective-permute-start | bytes 3145736 | tf_op jit(solution)/shard_map/cond/branch_1_fun/ppermute | solution.py:530
  93.5 18.1 %all-to-all-start.3 = ((f32[4,4,128,128]{3,2,1,0:T(8,128)}), f32[4,4,128,128]{3,2,1,0:T(8,128)S(1)}, u32[]{:S(2)}, u32[]{:S(2)}) async-start(f32[4,4,128,128]{3,2,1,0:T(8,128)} %branch_1_fun.22), calls=%async_computation.3 | async-start | bytes 2097152 | tf_op jit(solution)/shard_map/cond/branch_1_fun/all_to_all | solution.py:447
  111.5 3.0 %copy-start.7 = (f32[4,128,128]{2,1,0:T(8,128)S(1)}, f32[4,128,128]{2,1,0:T(8,128)}, u32[]{:S(2)}) copy-start(f32[4,128,128]{2,1,0:T(8,128)} %get-tuple-element.232) | copy-start | bytes 786436 | tf_op jit(solution)/shard_map/cond
  111.5 3.0 %copy-start.8 = (f32[4,128,128]{2,1,0:T(8,128)S(1)}, f32[4,128,128]{2,1,0:T(8,128)}, u32[]{:S(2)}) copy-start(f32[4,128,128]{2,1,0:T(8,128)} %get-tuple-element.233) | copy-start | bytes 786436 | tf_op jit(solution)/shard_map/cond
  (2 other events, 3.3 us)

commit v11 on v10

--- a/solution.py
+++ b/solution.py
@@ -118,12 +118,12 @@
 
 
 def filter_kernel(
-    first, n, channels, tokens, f_ref, tw_ref, fwd_ref, out_ref, f_buf, y_ref, own_ref, sem
+    first, n, channels, tokens, f_ref, tw_ref, fwd_ref, out_ref, f_buf, y_ref, sem
 ):
     rows = parts_of(channels, ROWS)
     loads = copies_of(
         [(f_ref.at[pl.ds(first + part.start, part.size)], f_buf.at[part]) for part in rows],
-        sem.at[0],
+        sem,
     )
     start_all(loads)
     for part, load in zip(rows, loads):
@@ -131,16 +131,13 @@
         outer_forward(
             lambda n1, r: f_buf[r, n1 * tokens : (n1 + 1) * tokens], n, part, tokens, tw_ref, y_ref
         )
-    stores = copies_of([(own_ref.at[ms], out_ref.at[ms]) for ms in parts_of(n)], sem.at[1])
-    for ms, store in zip(parts_of(n), stores):
-        own_ref[ms] = times_table(flat(y_ref[ms]), fwd_ref).reshape(ms.size, channels, 2 * tokens)
-        store.start()
-    wait_all(stores)
+    for ms in parts_of(n):
+        out_ref[ms] = times_table(flat(y_ref[ms]), fwd_ref).reshape(ms.size, channels, 2 * tokens)
 
 
 def transform(
     sign, n, channels, tokens, read, sources, targets, tw_ref, fwd_hbm, inv_hbm, spec_refs, own_ref,
-    buf_ref, spec_buf, own_buf, y_ref, fwd_ref, inv_ref, sem,
+    buf_ref, y_ref, fwd_ref, inv_ref, sem,
 ):
     half = channels // 2
     rows = [pl.ds(0, half), pl.ds(half, half)]
@@ -149,42 +146,28 @@
         start_all(load)
     table_loads = copies_of([(fwd_hbm, fwd_ref), (inv_hbm, inv_ref)], sem.at[2, 1])
     start_all(table_loads)
-    spec_loads = [
-        copies_of(
-            [
-                (ref.at[ms], spec_buf.at[ms, pl.ds(j * half, half)])
-                for j, ref in enumerate(spec_refs)
-            ],
-            sem.at[1, i],
-        )
-        for i, ms in enumerate(parts_of(n))
-    ]
-    for load in spec_loads:
-        start_all(load)
     for part, load in zip(rows, loads):
         wait_all(load)
         outer_forward(read, n, part, tokens, tw_ref, y_ref)
-    own_stores = copies_of([(own_buf.at[ms], own_ref.at[ms]) for ms in parts_of(n)], sem.at[2, 0])
     wait_all(table_loads)
-    for ms, load, store in zip(parts_of(n), spec_loads, own_stores):
-        own = times_table(flat(y_ref[ms]), fwd_ref)
-        own_buf[ms] = own.reshape(ms.size, channels, 2 * tokens)
-        store.start()
-        wait_all(load)
-        spec = flat(spec_buf[ms])
-        re, im = own[:, :tokens], own[:, tokens:]
-        s_re, s_im = spec[:, :tokens], spec[:, tokens:] * sign
-        both = jnp.concatenate([re * s_re - im * s_im, re * s_im + im * s_re], axis=1)
-        y_ref[ms] = times_table(both, inv_ref).reshape(ms.size, channels, 2 * tokens)
+    stores = [copies_of(targets(part), sem.at[3, i]) for i, part in enumerate(rows)]
 
     def write(n1, r, value):
         buf_ref[n1, r] = value
 
-    stores = [copies_of(targets(part), sem.at[3, i]) for i, part in enumerate(rows)]
-    for part, store in zip(rows, stores):
+    for j, part in enumerate(rows):
+        for ms in (pl.ds(0, n // 2), pl.ds(n // 2, n // 2)):
+            shape = (n // 2, half, 2 * tokens)
+            own = times_table(flat(y_ref[ms, part]), fwd_ref)
+            own_ref[ms, part] = own.reshape(shape)
+            spec = flat(spec_refs[j][ms])
+            re, im = own[:, :tokens], own[:, tokens:]
+            s_re, s_im = spec[:, :tokens], spec[:, tokens:] * sign
+            both = jnp.concatenate([re * s_re - im * s_im, re * s_im + im * s_re], axis=1)
+            y_ref[ms, part] = times_table(both, inv_ref).reshape(shape)
         outer_inverse(write, n, part, tokens, tw_ref, y_ref)
-        start_all(store)
-    for store in (*stores, own_stores):
+        start_all(stores[j])
+    for store in stores:
         wait_all(store)
 
 
@@ -240,17 +223,10 @@
 
 def filter_grad_kernel(
     scale, n, channels, tokens, tw_ref, inv_ref, p_ref, g_ref, out_ref,
-    p_buf, g_buf, y_ref, out_buf, sem,
+    y_ref, out_buf, sem,
 ):
-    loads = [
-        copies_of([(p_ref.at[ms], p_buf.at[ms]), (g_ref.at[ms], g_buf.at[ms])], sem.at[i])
-        for i, ms in enumerate(parts_of(n))
-    ]
-    for load in loads:
-        start_all(load)
-    for ms, load in zip(parts_of(n), loads):
-        wait_all(load)
-        p, g = flat(p_buf[ms]), flat(g_buf[ms])
+    for ms in parts_of(n):
+        p, g = flat(p_ref[ms]), flat(g_ref[ms])
         p_re, p_im = p[:, :tokens], p[:, tokens:]
         re, im = g[:, :tokens], g[:, tokens:]
         both = jnp.concatenate([re * p_re + im * p_im, im * p_re - re * p_im], axis=1)
@@ -260,48 +236,41 @@
         out_buf[r, n1 * tokens : (n1 + 1) * tokens] = value * scale
 
     rows = parts_of(channels, ROWS)
-    stores = copies_of([(out_buf.at[part], out_ref.at[part]) for part in rows], sem.at[PARTS])
+    stores = copies_of([(out_buf.at[part], out_ref.at[part]) for part in rows], sem)
     for part, store in zip(rows, stores):
         outer_inverse(write, n, part, tokens, tw_ref, y_ref)
         store.start()
     wait_all(stores)
 
 
-def product_split_kernel(planes, n, a_ref, b_ref, *refs):
-    keep_ref, *send_refs = refs[:planes]
-    a_buf, b_buf, keep_buf, sem, keep_sem = refs[planes:]
+def product_kernel(planes, n, a_ref, b_ref, c_ref, d_ref, *refs):
+    keep_ref, *send_refs, last_ref = refs[: planes + 1]
+    a_buf, b_buf, c_buf, d_buf, keep_buf, sem, last_sem, keep_sem = refs[planes + 1 :]
     width = n // planes
     z = plane(width)
-    loads = []
+    loads, last_loads = [], []
     for d in range(planes):
         part = pl.ds((z ^ d) * width, width)
         loads.append(
             copies_of([(a_ref.at[part], a_buf.at[d]), (b_ref.at[part], b_buf.at[d])], sem.at[d])
         )
         start_all(loads[d])
-    keep = pltpu.make_async_copy(keep_buf, keep_ref, keep_sem)
+    for p in range(planes):
+        part = pl.ds(p * width, width)
+        pairs = [(c_ref.at[part], c_buf.at[p]), (d_ref.at[part], d_buf.at[p])]
+        last_loads.append(copies_of(pairs, last_sem.at[p]))
+        start_all(last_loads[p])
+    stores = [pltpu.make_async_copy(keep_buf, keep_ref, keep_sem.at[planes])]
     for d, ref in enumerate((keep_buf, *send_refs)):
         wait_all(loads[d])
         ref[...] = a_buf[d] * b_buf[d]
         if d == 0:
-            keep.start()
-    keep.wait()
-
-
-def product_kernel(planes, n, a_ref, b_ref, after_ref, out_ref, a_buf, b_buf, buf_ref, sem):
-    width = n // planes
-    parts = [pl.ds(z * width, width) for z in range(planes)]
-    loads = [
-        copies_of([(a_ref.at[part], a_buf.at[part]), (b_ref.at[part], b_buf.at[part])], sem.at[z])
-        for z, part in enumerate(parts)
-    ]
-    for load in loads:
-        start_all(load)
-    stores = copies_of([(buf_ref.at[z], out_ref.at[:, z]) for z in range(planes)], sem.at[planes])
-    for z, part in enumerate(parts):
-        wait_all(loads[z])
-        buf_ref[z] = a_buf[part] * b_buf[part]
-        stores[z].start()
+            stores[0].start()
+    for p in range(planes):
+        wait_all(last_loads[p])
+        c_buf[p] = c_buf[p] * d_buf[p]
+        stores.append(pltpu.make_async_copy(c_buf.at[p], last_ref.at[:, p], keep_sem.at[p]))
+        stores[-1].start()
     wait_all(stores)
 
 
@@ -333,20 +302,14 @@
     wait_all(stores)
 
 
-def gate_near_kernel(
-    planes, width, near_ref, a_ref, b_ref, oa_ref, ob_ref, x_buf, a_buf, b_buf, sem
-):
+def gate_near_kernel(planes, width, near_ref, *refs):
+    in_refs, (oa_ref, ob_ref, *out_refs, x_buf, sem) = refs[:4], refs[4:]
     part = pl.ds(plane(width) * width, width)
-    loads = copies_of(
-        [(near_ref, x_buf), (a_ref.at[part], a_buf), (b_ref.at[part], b_buf)], sem.at[0]
-    )
+    loads = copies_of([(near_ref, x_buf), *zip(in_refs, out_refs)], sem)
     start_all(loads)
     wait_all(loads)
-    a_buf[...] = x_buf[...] * a_buf[...]
-    b_buf[...] = x_buf[...] * b_buf[...]
-    stores = copies_of([(a_buf, oa_ref), (b_buf, ob_ref)], sem.at[1])
-    start_all(stores)
-    wait_all(stores)
+    oa_ref[...] = x_buf[...] * out_refs[0][part]
+    ob_ref[...] = x_buf[...] * out_refs[1][part]
 
 
 def gate_far_kernel(planes, width, *refs):
@@ -452,7 +415,7 @@
     rows, paired_buf = pltpu.VMEM(blocks, f32), pltpu.VMEM(paired, f32)
     by_plane = pltpu.VMEM((planes, *one), f32)
     send = kernel_call(
-        part(send_kernel, planes, width), "v", [("h", one)] * planes, [semaphores(planes)]
+        part(send_kernel, planes, width), "v", [("v", one)] * planes, [semaphores(planes)]
     )
     merge = kernel_call(
         part(merge_kernel, planes, width), "v" * planes + "a", [("h", paired)], [semaphores(planes)]
@@ -461,17 +424,17 @@
     half_spectrum = (n, channels // 2, 2 * tokens)
     def transform_filters(first):
         return kernel_call(
-            part(filter_kernel, first, *half_sizes), "hvv", [("h", half_spectrum)],
+            part(filter_kernel, first, *half_sizes), "hvv", [("v", half_spectrum)],
             [
                 pltpu.VMEM((channels // 2, length), f32),
-                *[pltpu.VMEM(half_spectrum, f32)] * 2,
-                semaphores(2, PARTS),
+                pltpu.VMEM(half_spectrum, f32),
+                semaphores(PARTS),
             ],
             flops // 2,
         )(filters, tw, fwd)[0]
 
     table = pltpu.VMEM(fwd.shape, fwd.dtype)
-    transform_scratch = [rows, y, y, y, table, table, semaphores(4, PARTS, max(PARTS, planes))]
+    transform_scratch = [rows, y, table, table, semaphores(4, PARTS, max(PARTS, planes))]
     always = lax.axis_index("context") < n
 
     def grouped(body, *args):
@@ -482,28 +445,28 @@
 
         return lax.cond(always, body, never, *args)
 
-    keep_p, *send_p = kernel_call(
-        part(product_split_kernel, planes, n), "hh", [("h", one)] + [("v", one)] * (planes - 1),
-        [by_plane, by_plane, pltpu.VMEM(one, f32), semaphores(planes, 2), pltpu.SemaphoreType.DMA],
-    )(key, value)
+    keep_p, *send_p, conv_grad = kernel_call(
+        part(product_kernel, planes, n), "hhhh",
+        [("v", one)] * planes + [("h", paired)],
+        [
+            *[by_plane] * 4, pltpu.VMEM(one, f32),
+            semaphores(planes, 2), semaphores(planes, 2), semaphores(planes + 1),
+        ],
+    )(key, value, cot, query)
     got_p = along_z(send_p)
 
-    def first(cot, query, keep_p):
-        (conv_grad,) = kernel_call(
-            part(product_kernel, planes, n), "hha", [("h", paired)],
-            [rows, rows, by_plane, semaphores(planes + 1, planes)],
-        )(cot, query, keep_p)
+    def first(conv_grad):
         return send(within_plane(conv_grad)), transform_filters(0)
 
-    (near_g, *send_g), filt_a = grouped(first, cot, query, keep_p)
+    (near_g, *send_g), filt_a = grouped(first, conv_grad)
     far_g = along_z(send_g)
 
     def second(keep_p, got_p, send_g, filt_a):
         product_ch = within_plane(*merge(keep_p, *got_p, send_g))
         filt = (filt_a, transform_filters(channels // 2))
         *outs, prod_spec = kernel_call(
-            part(conv_kernel, planes, *sizes), "vvhhhh",
-            [("h", one)] * planes + [("h", spectrum)], transform_scratch, 2 * flops,
+            part(conv_kernel, planes, *sizes), "vvhhvv",
+            [("v", one)] * planes + [("v", spectrum)], transform_scratch, 2 * flops,
         )(product_ch, tw, fwd, inv, *filt)
         return outs, prod_spec, filt
 
@@ -512,13 +475,13 @@
 
     def third(near_g, far_g, filt, keep_c, prod_spec):
         back_ch, grad_spec = kernel_call(
-            part(back_kernel, planes, *sizes), "a" * planes + "vhhhha",
-            [("h", paired), ("h", spectrum)], transform_scratch, 2 * flops,
+            part(back_kernel, planes, *sizes), "a" * planes + "vhhvva",
+            [("h", paired), ("v", spectrum)], transform_scratch, 2 * flops,
         )(near_g, *far_g, tw, fwd, inv, *filt, keep_c)
         sends = send(within_plane(back_ch))
         (own,) = kernel_call(
-            part(filter_grad_kernel, scale, *sizes), "vvhh", [("h", lags)],
-            [y, y, y, pltpu.VMEM(lags, f32), semaphores(PARTS + 1, PARTS)], flops,
+            part(filter_grad_kernel, scale, *sizes), "vvvv", [("h", lags)],
+            [y, pltpu.VMEM(lags, f32), semaphores(PARTS)], flops,
         )(tw, inv, prod_spec, grad_spec)
         return sends, own
 
@@ -531,15 +494,15 @@
         else:
             grad_filter = lax.psum(own, "dp")
         conv_tok = within_plane(*merge(keep_c, *got_c, near_b))
-        begun = kernel_call(
-            part(gate_near_kernel, planes, width), "ahh", [("h", one)] * 2,
-            [pltpu.VMEM(one, f32)] * 3 + [semaphores(2, 3)],
-        )(near_b, value, key)
+        *begun, value, key, query, cot = kernel_call(
+            part(gate_near_kernel, planes, width), "ahhhh", [("v", one)] * 2 + [("v", blocks)] * 4,
+            [pltpu.VMEM(one, f32), semaphores(5)],
+        )(near_b, value, key, query, cot)
         gated, grad_query = kernel_call(
             part(gate_kernel, planes, width), "vvva", [("h", blocks)] * 2,
             [rows, rows, semaphores(planes, 2)],
         )(conv_tok, query, cot, grad_filter)
-        return gated, grad_query, begun, grad_filter
+        return gated, grad_query, (value, key, *begun), grad_filter
 
     gated, grad_query, begun, grad_filter = grouped(
         fourth, keep_c, got_c, query, cot, near_b, value, key, own
@@ -547,7 +510,7 @@
     grad_key, grad_value = kernel_call(
         part(gate_far_kernel, planes, width), "v" * (planes + 3), [("h", blocks)] * 2,
         [rows, rows, semaphores(planes, 2)],
-    )(*far_b, value, key, *begun)
+    )(*far_b, *begun)
     shape = query_input.shape
     return (
         gated.reshape(shape),

time: 118 us -> 132 us (1.12)
  local copies, waits for them, and re-layouts: 0.78 us -> 10.2 us
  starting transfers between devices: 33.8 us -> 43.2 us
  waiting for transfers between devices: 37.1 us -> 31.3 us
    ppermute x12, starting transfers between devices: 19 us -> 28.7 us  [along_z(): lax.ppermute(x, 'context', [(i, i ^ d * width) for i in range(n)])]
    cond x10 -> x18, local copies, waits for them, and re-layouts: 0.76 us -> 10.2 us
    all_to_all x4, waiting for transfers between devices: 37 us -> 31.3 us  [within_plane(): lax.all_to_all(x, 'context', 0, 0, axis_index_groups=members, tiled=True)]
    pallas_call x14 -> x13, Pallas kernels: 42 us -> 42.7 us  [run(): pl.pallas_call(body, in_specs=[pl.BlockSpec(memory_space=SPACES[space]) f...]
  transfers between devices with their start and end apart: 17 -> 17, of which waited for: 4 -> 4; matrix products, arithmetic and copies ran while one was open for 2% -> 2% of each run, Pallas kernels for 32% -> 27%
where the time goes in v11:
time: 132 us; the launch traced here: 131 us
  starting transfers between devices  43.2 us (33%)
  Pallas kernels  42.7 us (32%)
  waiting for transfers between devices  31.3 us (24%)
  local copies, waits for them, and re-layouts  10.2 us (8%)
  other arithmetic  2.64 us (2%)
    pallas_call x13, Pallas kernels, run(): pl.pallas_call(body, in_specs=[pl.BlockSpec(memory_space=SPACES[space]) f...  42.7 us
    all_to_all x4, waiting for transfers between devices, within_plane(): lax.all_to_all(x, 'context', 0, 0, axis_index_groups=members, tiled=True)  31.3 us
    ppermute x12, starting transfers between devices, along_z(): lax.ppermute(x, 'context', [(i, i ^ d * width) for i in range(n)])  28.7 us
    all_to_all x4, starting transfers between devices, within_plane(): lax.all_to_all(x, 'context', 0, 0, axis_index_groups=members, tiled=True)  14.5 us
    cond x18, local copies, waits for them, and re-layouts  10.2 us
    add x1, other arithmetic, fourth(): grad_filter = own + lax.ppermute(own, 'dp', [(0, 1), (1, 0)])  2.64 us
  transfers between devices with their start and end apart: 17, of which 4 were waited for; matrix products, arithmetic and copies ran while one was open for 2% of the time, Pallas kernels for 27%

profile of v11, /device:TPU:0, one launch (start us, length us, event | category | flops | bytes accessed | tf_op | source)
XLA Modules:
  0.0 131.0 jit_solution(9149120733386276254)
XLA Ops:
  0.7 4.1 %shard_map.119 = (f32[4,128,128]{2,1,0:T(8,128)S(1)}, f32[4,128,128]{2,1,0:T(8,128)}, f32[4,128,128]{2,1,0:T(8,128)}, f32[4,128,128]{2,1,0:T(8,128)S(1)}, f32[4,4,128,128]{3,2,1,0:T(8,128)}) custom-call(f32[16,128,128]{2,1,0:T(8,128)} %bitcast.8, f32[16,128,128]{2,1,0:T(8,128)} %bitcast.10, f32[16,128,128]{2,1,0:T(8,128)} %bitcast.12, f32[16,128,128]{2,1,0:T(8,128)} %bitcast.14), custom_call_target="tpu_custom_call" | custom-call | bytes 6291456 | tf_op jit(solution)/shard_map/pallas_call | solution.py:347
  4.8 3.1 %collective-permute-start.4 = (f32[4,128,128]{2,1,0:T(8,128)}, f32[4,128,128]{2,1,0:T(8,128)}, u32[]{:S(2)}, u32[]{:S(2)}) collective-permute-start(f32[4,128,128]{2,1,0:T(8,128)} %get-tuple-element.172), channel_id=1, source_target_pairs={{0,4},{1,5},{2,6},{3,7},{4,0},{5,1},{6,2},{7,3},{8,12},{9,13},{10,... | collective-permute-start | bytes 786440 | tf_op jit(solution)/shard_map/ppermute | solution.py:404
  7.9 2.6 %collective-permute-start.5 = (f32[4,128,128]{2,1,0:T(8,128)}, f32[4,128,128]{2,1,0:T(8,128)}, u32[]{:S(2)}, u32[]{:S(2)}) collective-permute-start(f32[4,128,128]{2,1,0:T(8,128)} %get-tuple-element.173), channel_id=1, source_target_pairs={{0,8},{1,9},{2,10},{3,11},{4,12},{5,13},{6,14},{7,15},{8,0},{9,1},... | collective-permute-start | bytes 786440 | tf_op jit(solution)/shard_map/ppermute | solution.py:404
  10.5 18.6 %conditional.4 = (f32[4,128,128]{2,1,0:T(8,128)}, f32[4,128,128]{2,1,0:T(8,128)}, f32[4,128,128]{2,1,0:T(8,128)}, f32[4,128,128]{2,1,0:T(8,128)}, f32[16,64,256]{2,1,0:T(8,128)S(1)}) conditional(s32[]{:T(128)} %convert_element_type.2, () %tuple.46, (f32[4,4,128,128]{3,2,1,0:T(8,128)}, f32[128,2048]{1,0:T(8,128)}, f32[2,16,8,128]{3,2,1,0:T(8,128)S(1)}, ...), branch_computations={%region_0.0_spmd, %region_1.0_spmd} | conditional | flops 268435456 | bytes 9306212 | solution.py:446
  10.5 3.9 %all-to-all-start = ((f32[4,4,128,128]{3,2,1,0:T(8,128)}), f32[4,4,128,128]{3,2,1,0:T(8,128)S(1)}, u32[]{:S(2)}, u32[]{:S(2)}) async-start(f32[4,4,128,128]{3,2,1,0:T(8,128)} %get-tuple-element.72), calls=%async_computation | async-start | bytes 2097152 | tf_op jit(solution)/shard_map/cond/branch_1_fun/all_to_all | solution.py:410
  16.3 11.0 %all-to-all-done.refs_0_ = f32[4,4,128,128]{3,2,1,0:T(8,128)S(1)} async-done(((f32[4,4,128,128]{3,2,1,0:T(8,128)}), f32[4,4,128,128]{3,2,1,0:T(8,128)S(1)}, u32[]{:S(2)}, u32[]{:S(2)}) %all-to-all-start) | async-done | bytes 1048608 | tf_op jit(solution)/shard_map/cond/branch_1_fun/all_to_all | solution.py:410
  33.1 28.2 %conditional.5 = (f32[4,128,128]{2,1,0:T(8,128)S(1)}, f32[4,128,128]{2,1,0:T(8,128)}, f32[4,128,128]{2,1,0:T(8,128)}, f32[4,128,128]{2,1,0:T(8,128)}, f32[16,128...) conditional(s32[]{:T(128)} %convert_element_type.2, () %tuple.48, ...), branch_computations={%region_2.0_spmd, %region_3.0_spmd} | conditional | flops 1342177280 | bytes 24903824 | solution.py:446
  35.3 3.5 %all-to-all-start.1 = ((f32[4,4,128,128]{3,2,1,0:T(8,128)}), f32[4,4,128,128]{3,2,1,0:T(8,128)S(1)}, u32[]{:S(2)}, u32[]{:S(2)}) async-start(f32[4,4,128,128]{3,2,1,0:T(8,128)} %branch_1_fun.13), calls=%async_computation.1 | async-start | bytes 2097152 | tf_op jit(solution)/shard_map/cond/branch_1_fun/all_to_all | solution.py:410
  38.9 3.9 %branch_1_fun.14.refs_5_ = f32[16,64,256]{2,1,0:T(8,128)} custom-call(f32[128,2048]{1,0:T(8,128)} %get-tuple-element.89.refs_0_, f32[2,16,8,128]{3,2,1,0:T(8,128)S(1)} %get-tuple-element.85.refs_1_, bf16[768,256]{1,0:T(8,128)(2,1)} %get-tuple-element.86.refs_2_), custom_call_target="tpu_custom_call" | custom-call | flops 268435456 | bytes 3014656 | tf_op jit(solution)/shard_map/cond/branch_1_fun/pallas_call | solution.py:347
  42.8 8.7 %all-to-all-done.1.refs_0_ = f32[4,4,128,128]{3,2,1,0:T(8,128)S(1)} async-done(((f32[4,4,128,128]{3,2,1,0:T(8,128)}), f32[4,4,128,128]{3,2,1,0:T(8,128)S(1)}, u32[]{:S(2)}, u32[]{:S(2)}) %all-to-all-start.1) | async-done | bytes 1048608 | tf_op jit(solution)/shard_map/cond/branch_1_fun/all_to_all | solution.py:410
  53.7 7.7 %branch_1_fun.15 = (f32[4,128,128]{2,1,0:T(8,128)S(1)}, f32[4,128,128]{2,1,0:T(8,128)}, f32[4,128,128]{2,1,0:T(8,128)}, f32[4,128,128]{2,1,0:T(8,128)}, f32[16,128,256]{2,1,0:T(8,128)S(1)}) custom-call(f32[4,4,128,128]{3,2,1,0:T(8,128)S(1)} %copy-done.1, f32[2,16,8,128]{3,2,1,0:T(8,128)S(1)} %get-tuple-element.85.refs_1_, ...), custom_call_target="tpu_custom_call" | custom-call | flops 1073741824 | bytes 7995392 | tf_op jit(solution)/shard_map/cond/branch_1_fun/pallas_call | solution.py:347
  61.4 11.5 %collective-permute-start.7 = (f32[4,128,128]{2,1,0:T(8,128)}, f32[4,128,128]{2,1,0:T(8,128)}, u32[]{:S(2)}, u32[]{:S(2)}) collective-permute-start(f32[4,128,128]{2,1,0:T(8,128)} %get-tuple-element.182), channel_id=1, source_target_pairs={{0,4},{1,5},{2,6},{3,7},{4,0},{5,1},{6,2},{7,3},{8,12},{9,13},{10,... | collective-permute-start | bytes 786440 | tf_op jit(solution)/shard_map/ppermute | solution.py:404
  75.9 23.9 %conditional.6 = (f32[4,128,128]{2,1,0:T(8,128)}, f32[4,128,128]{2,1,0:T(8,128)}, f32[4,128,128]{2,1,0:T(8,128)}, f32[4,128,128]{2,1,0:T(8,128)}, f32[128,2048]{1,0:T(8,128)}) conditional(s32[]{:T(128)} %convert_element_type.2, () %tuple.45, (f32[4,128,128]{2,1,0:T(8,128)}, f32[4,128,128]{2,1,0:T(8,128)}, f32[4,128,128]{2,1,0:T(8,128)}, ...), branch_computations={%region_4.0_spmd, %region_5.0_spmd} | conditional | flops 1610612736 | bytes 36438144 | solution.py:446
  75.9 8.0 %branch_1_fun.16 = (f32[4,4,128,128]{3,2,1,0:T(8,128)}, f32[16,128,256]{2,1,0:T(8,128)S(1)}) custom-call(f32[4,128,128]{2,1,0:T(8,128)} %get-tuple-element.95.refs_0_, f32[4,128,128]{2,1,0:T(8,128)} %get-tuple-element.96.refs_1_, f32[4,128,128]{2,1,0:T(8,128)} %get-tuple-element.97.refs_2_, f32[4,128,128]{2,1,0:T(8,128)} %get-tuple-element.98.refs_3_, ...), custom_call_target="tpu_custom_call" | custom-call | flops 1073741824 | bytes 8257536 | tf_op jit(solution)/shard_map/cond/branch_1_fun/pallas_call | solution.py:347
  85.2 3.5 %all-to-all-start.2 = ((f32[4,4,128,128]{3,2,1,0:T(8,128)}), f32[4,4,128,128]{3,2,1,0:T(8,128)S(1)}, u32[]{:S(2)}, u32[]{:S(2)}) async-start(f32[4,4,128,128]{3,2,1,0:T(8,128)} %get-tuple-element.105), calls=%async_computation.2 | async-start | bytes 2097152 | tf_op jit(solution)/shard_map/cond/branch_1_fun/all_to_all | solution.py:410
  90.3 3.6 %branch_1_fun.18 = f32[128,2048]{1,0:T(8,128)} custom-call(f32[2,16,8,128]{3,2,1,0:T(8,128)S(1)} %get-tuple-element.99.refs_4_.refs_0_, bf16[768,256]{1,0:T(8,128)(2,1)} %get-tuple-element.101.refs_6_.refs_1_, f32[16,128,256]{2,1,0:T(8,128)S(1)} %get-tuple-element.110.refs_2_, f32[16,128,256]{2,1,0:T(8,128)S(1)} %copy-done.3), custom_call_target="tpu_custom_call" | custom-call | flops 536870912 | bytes 6160384 | tf_op jit(solution)/shard_map/cond/branch_1_fun/pallas_call | solution.py:347
  93.9 4.8 %all-to-all-done.2.refs_0_ = f32[4,4,128,128]{3,2,1,0:T(8,128)S(1)} async-done(((f32[4,4,128,128]{3,2,1,0:T(8,128)}), f32[4,4,128,128]{3,2,1,0:T(8,128)S(1)}, u32[]{:S(2)}, u32[]{:S(2)}) %all-to-all-start.2) | async-done | bytes 1048608 | tf_op jit(solution)/shard_map/cond/branch_1_fun/all_to_all | solution.py:410
  100.4 2.4 %collective-permute-start.11 = (f32[4,128,128]{2,1,0:T(8,128)}, f32[4,128,128]{2,1,0:T(8,128)}, u32[]{:S(2)}, u32[]{:S(2)}) collective-permute-start(f32[4,128,128]{2,1,0:T(8,128)} %get-tuple-element.188), channel_id=1, source_target_pairs={{0,8},{1,9},{2,10},{3,11},{4,12},{5,13},{6,14},{7,15},{8,0},{9,1},... | collective-permute-start | bytes 786440 | tf_op jit(solution)/shard_map/ppermute | solution.py:404
  104.2 24.1 %conditional.7 = (f32[16,128,128]{2,1,0:T(8,128)S(1)}, f32[16,128,128]{2,1,0:T(8,128)S(1)}, f32[4,128,128]{2,1,0:T(8,128)}, f32[4,128,128]{2,1,0:T(8,128)}, f32[...) conditional(s32[]{:T(128)} %convert_element_type.2, () %tuple.44, ...), branch_computations={%region_6.0_spmd, %region_7.0_spmd} | conditional | flops 262144 | bytes 45089008 | solution.py:446
  106.4 3.5 %all-to-all-start.3 = ((f32[4,4,128,128]{3,2,1,0:T(8,128)}), f32[4,4,128,128]{3,2,1,0:T(8,128)S(1)}, u32[]{:S(2)}, u32[]{:S(2)}) async-start(f32[4,4,128,128]{3,2,1,0:T(8,128)} %branch_1_fun.20), calls=%async_computation.3 | async-start | bytes 2097152 | tf_op jit(solution)/shard_map/cond/branch_1_fun/all_to_all | solution.py:410
  109.9 3.2 %branch_1_fun.19 = (f32[4,128,128]{2,1,0:T(8,128)}, f32[4,128,128]{2,1,0:T(8,128)}, f32[16,128,128]{2,1,0:T(8,128)S(1)}, f32[16,128,128]{2,1,0:T(8,128)S(1)}, f3...) custom-call(f32[4,128,128]{2,1,0:T(8,128)} %get-tuple-element.112.refs_0_.refs_4_, ...), custom_call_target="tpu_custom_call" | custom-call | bytes 9175040 | tf_op jit(solution)/shard_map/cond/branch_1_fun/pallas_call | solution.py:347
  115.0 2.6 %add.2.refs_3_ = f32[128,2048]{1,0:T(8,128)} add(f32[128,2048]{1,0:T(8,128)} %get-tuple-element.121, f32[128,2048]{1,0:T(8,128)} %collective-permute-done) | non-fusion elementwise | flops 262144 | bytes 3145728 | tf_op jit(solution)/shard_map/cond/branch_1_fun/add | solution.py:493
  117.7 6.8 %all-to-all-done.3.refs_0_ = f32[4,4,128,128]{3,2,1,0:T(8,128)S(1)} async-done(((f32[4,4,128,128]{3,2,1,0:T(8,128)}), f32[4,4,128,128]{3,2,1,0:T(8,128)S(1)}, u32[]{:S(2)}, u32[]{:S(2)}) %all-to-all-start.3) | async-done | bytes 1048608 | tf_op jit(solution)/shard_map/cond/branch_1_fun/all_to_all | solution.py:410
  128.3 2.6 %shard_map.120 = (f32[16,128,128]{2,1,0:T(8,128)}, f32[16,128,128]{2,1,0:T(8,128)}) custom-call(f32[4,128,128]{2,1,0:T(8,128)} %collective-permute-done.10.refs_0_, f32[4,128,128]{2,1,0:T(8,128)} %collective-permute-done.11.refs_1_, f32[4,128,128]{2,1,0:T(8,128)} %collective-permute-done.12.refs_2_, f32[16,128,128]{2,1,0:T(8,128)S(1)} %get-tuple-element.190.refs_3_, ...), custom_call_target="tpu_custom_call" | custom-call | bytes 5505024 | tf_op jit(solution)/shard_map/pallas_call | solution.py:347
  (52 shorter events, 29.1 us)
Async XLA Ops:
  0.6 9.8 %copy-start.10 = (bf16[768,256]{1,0:T(8,128)(2,1)S(1)}, bf16[768,256]{1,0:T(8,128)(2,1)}, u32[]{:S(2)}) copy-start(bf16[768,256]{1,0:T(8,128)(2,1)} %constant.11.clone) | copy-start | bytes 1179652
  0.6 9.8 %copy-start.11 = (f32[2,16,8,128]{3,2,1,0:T(8,128)S(1)}, f32[2,16,8,128]{3,2,1,0:T(8,128)}, u32[]{:S(2)}) copy-start(f32[2,16,8,128]{3,2,1,0:T(8,128)} %constant.17.clone) | copy-start | bytes 393220
  4.8 5.7 %copy-start.9 = (f32[4,128,128]{2,1,0:T(8,128)}, f32[4,128,128]{2,1,0:T(8,128)S(1)}, u32[]{:S(2)}) copy-start(f32[4,128,128]{2,1,0:T(8,128)S(1)} %get-tuple-element.171) | copy-start | bytes 786436
  4.8 27.8 %collective-permute-start.4 = (f32[4,128,128]{2,1,0:T(8,128)}, f32[4,128,128]{2,1,0:T(8,128)}, u32[]{:S(2)}, u32[]{:S(2)}) collective-permute-start(f32[4,128,128]{2,1,0:T(8,128)} %get-tuple-element.172), channel_id=1, source_target_pairs={{0,4},{1,5},{2,6},{3,7},{4,0},{5,1},{6,2},{7,3},{8,12},{9,13},{10,... | collective-permute-start | bytes 786440 | tf_op jit(solution)/shard_map/ppermute | solution.py:404
  7.9 25.3 %collective-permute-start.5 = (f32[4,128,128]{2,1,0:T(8,128)}, f32[4,128,128]{2,1,0:T(8,128)}, u32[]{:S(2)}, u32[]{:S(2)}) collective-permute-start(f32[4,128,128]{2,1,0:T(8,128)} %get-tuple-element.173), channel_id=1, source_target_pairs={{0,8},{1,9},{2,10},{3,11},{4,12},{5,13},{6,14},{7,15},{8,0},{9,1},... | collective-permute-start | bytes 786440 | tf_op jit(solution)/shard_map/ppermute | solution.py:404
  10.5 22.7 %collective-permute-start.6 = (f32[4,128,128]{2,1,0:T(8,128)S(1)}, f32[4,128,128]{2,1,0:T(8,128)}, u32[]{:S(2)}, u32[]{:S(2)}) collective-permute-start(f32[4,128,128]{2,1,0:T(8,128)S(1)} %get-tuple-element.174), channel_id=1, source_target_pairs={{0,12},{1,13},{2,14},{3,15},{4,8},{5,9},{6,10},{7,11},{8,4},{9,5},... | collective-permute-start | bytes 786440 | tf_op jit(solution)/shard_map/ppermute | solution.py:404
  10.5 16.9 %all-to-all-start = ((f32[4,4,128,128]{3,2,1,0:T(8,128)}), f32[4,4,128,128]{3,2,1,0:T(8,128)S(1)}, u32[]{:S(2)}, u32[]{:S(2)}) async-start(f32[4,4,128,128]{3,2,1,0:T(8,128)} %get-tuple-element.72), calls=%async_computation | async-start | bytes 2097152 | tf_op jit(solution)/shard_map/cond/branch_1_fun/all_to_all | solution.py:410
  29.0 45.4 %collective-permute-start.2 = (f32[4,128,128]{2,1,0:T(8,128)}, f32[4,128,128]{2,1,0:T(8,128)}, u32[]{:S(2)}, u32[]{:S(2)}) collective-permute-start(f32[4,128,128]{2,1,0:T(8,128)} %get-tuple-element.169), channel_id=1, source_target_pairs={{0,8},{1,9},{2,10},{3,11},{4,12},{5,13},{6,14},{7,15},{8,0},{9,1},... | collective-permute-start | bytes 786440 | tf_op jit(solution)/shard_map/ppermute | solution.py:404
  30.7 45.2 %collective-permute-start.3 = (f32[4,128,128]{2,1,0:T(8,128)}, f32[4,128,128]{2,1,0:T(8,128)}, u32[]{:S(2)}, u32[]{:S(2)}) collective-permute-start(f32[4,128,128]{2,1,0:T(8,128)} %get-tuple-element.170), channel_id=1, source_target_pairs={{0,12},{1,13},{2,14},{3,15},{4,8},{5,9},{6,10},{7,11},{8,4},{9,5},... | collective-permute-start | bytes 786440 | tf_op jit(solution)/shard_map/ppermute | solution.py:404
  32.6 43.3 %collective-permute-start.1 = (f32[4,128,128]{2,1,0:T(8,128)}, f32[4,128,128]{2,1,0:T(8,128)}, u32[]{:S(2)}, u32[]{:S(2)}) collective-permute-start(f32[4,128,128]{2,1,0:T(8,128)} %get-tuple-element.168), channel_id=1, source_target_pairs={{0,4},{1,5},{2,6},{3,7},{4,0},{5,1},{6,2},{7,3},{8,12},{9,13},{10,... | collective-permute-start | bytes 786440 | tf_op jit(solution)/shard_map/ppermute | solution.py:404
  35.3 16.1 %all-to-all-start.1 = ((f32[4,4,128,128]{3,2,1,0:T(8,128)}), f32[4,4,128,128]{3,2,1,0:T(8,128)S(1)}, u32[]{:S(2)}, u32[]{:S(2)}) async-start(f32[4,4,128,128]{3,2,1,0:T(8,128)} %branch_1_fun.13), calls=%async_computation.1 | async-start | bytes 2097152 | tf_op jit(solution)/shard_map/cond/branch_1_fun/all_to_all | solution.py:410
  52.4 1.2 copy-start.1
  61.4 41.5 %collective-permute-start.7 = (f32[4,128,128]{2,1,0:T(8,128)}, f32[4,128,128]{2,1,0:T(8,128)}, u32[]{:S(2)}, u32[]{:S(2)}) collective-permute-start(f32[4,128,128]{2,1,0:T(8,128)} %get-tuple-element.182), channel_id=1, source_target_pairs={{0,4},{1,5},{2,6},{3,7},{4,0},{5,1},{6,2},{7,3},{8,12},{9,13},{10,... | collective-permute-start | bytes 786440 | tf_op jit(solution)/shard_map/ppermute | solution.py:404
  72.8 31.4 %collective-permute-start.8 = (f32[4,128,128]{2,1,0:T(8,128)}, f32[4,128,128]{2,1,0:T(8,128)}, u32[]{:S(2)}, u32[]{:S(2)}) collective-permute-start(f32[4,128,128]{2,1,0:T(8,128)} %get-tuple-element.183), channel_id=1, source_target_pairs={{0,8},{1,9},{2,10},{3,11},{4,12},{5,13},{6,14},{7,15},{8,0},{9,1},... | collective-permute-start | bytes 786440 | tf_op jit(solution)/shard_map/ppermute | solution.py:404
  74.5 29.8 %collective-permute-start.9 = (f32[4,128,128]{2,1,0:T(8,128)}, f32[4,128,128]{2,1,0:T(8,128)}, u32[]{:S(2)}, u32[]{:S(2)}) collective-permute-start(f32[4,128,128]{2,1,0:T(8,128)} %get-tuple-element.184), channel_id=1, source_target_pairs={{0,12},{1,13},{2,14},{3,15},{4,8},{5,9},{6,10},{7,11},{8,4},{9,5},... | collective-permute-start | bytes 786440 | tf_op jit(solution)/shard_map/ppermute | solution.py:404
  83.9 1.3 %copy-start.2 = (f32[16,128,256]{2,1,0:T(8,128)}, f32[16,128,256]{2,1,0:T(8,128)S(1)}, u32[]{:S(2)}) copy-start(f32[16,128,256]{2,1,0:T(8,128)S(1)} %get-tuple-element.111.refs_3_) | copy-start | bytes 6291460 | tf_op jit(solution)/shard_map/cond
  85.2 13.5 %all-to-all-start.2 = ((f32[4,4,128,128]{3,2,1,0:T(8,128)}), f32[4,4,128,128]{3,2,1,0:T(8,128)S(1)}, u32[]{:S(2)}, u32[]{:S(2)}) async-start(f32[4,4,128,128]{3,2,1,0:T(8,128)} %get-tuple-element.105), calls=%async_computation.2 | async-start | bytes 2097152 | tf_op jit(solution)/shard_map/cond/branch_1_fun/all_to_all | solution.py:410
  88.7 1.6 %copy-start.3 = (f32[16,128,256]{2,1,0:T(8,128)S(1)}, f32[16,128,256]{2,1,0:T(8,128)}, u32[]{:S(2)}) copy-start(f32[16,128,256]{2,1,0:T(8,128)} %copy-done.2) | copy-start | bytes 6291460 | tf_op jit(solution)/shard_map/cond
  99.8 28.5 %collective-permute-start.10 = (f32[4,128,128]{2,1,0:T(8,128)}, f32[4,128,128]{2,1,0:T(8,128)}, u32[]{:S(2)}, u32[]{:S(2)}) collective-permute-start(f32[4,128,128]{2,1,0:T(8,128)} %get-tuple-element.187), channel_id=1, source_target_pairs={{0,4},{1,5},{2,6},{3,7},{4,0},{5,1},{6,2},{7,3},{8,12},{9,13},{10,... | collective-permute-start | bytes 786440 | tf_op jit(solution)/shard_map/ppermute | solution.py:404
  100.4 27.9 %collective-permute-start.11 = (f32[4,128,128]{2,1,0:T(8,128)}, f32[4,128,128]{2,1,0:T(8,128)}, u32[]{:S(2)}, u32[]{:S(2)}) collective-permute-start(f32[4,128,128]{2,1,0:T(8,128)} %get-tuple-element.188), channel_id=1, source_target_pairs={{0,8},{1,9},{2,10},{3,11},{4,12},{5,13},{6,14},{7,15},{8,0},{9,1},... | collective-permute-start | bytes 786440 | tf_op jit(solution)/shard_map/ppermute | solution.py:404
  102.9 25.5 %collective-permute-start.12 = (f32[4,128,128]{2,1,0:T(8,128)}, f32[4,128,128]{2,1,0:T(8,128)}, u32[]{:S(2)}, u32[]{:S(2)}) collective-permute-start(f32[4,128,128]{2,1,0:T(8,128)} %get-tuple-element.189), channel_id=1, source_target_pairs={{0,12},{1,13},{2,14},{3,15},{4,8},{5,9},{6,10},{7,11},{8,4},{9,5},... | collective-permute-start | bytes 786440 | tf_op jit(solution)/shard_map/ppermute | solution.py:404
  104.2 10.8 %collective-permute-start = (f32[128,2048]{1,0:T(8,128)}, f32[128,2048]{1,0:T(8,128)}, u32[]{:S(2)}, u32[]{:S(2)}) collective-permute-start(f32[128,2048]{1,0:T(8,128)} %get-tuple-element.121), channel_id=1, source_target_pairs={{0,16},{16,0},{1,17},{17,1},{2,18},{18,2},{3,19},{19,3},{4,20},{20... | collective-permute-start | bytes 3145736 | tf_op jit(solution)/shard_map/cond/branch_1_fun/ppermute | solution.py:493
  106.4 18.1 %all-to-all-start.3 = ((f32[4,4,128,128]{3,2,1,0:T(8,128)}), f32[4,4,128,128]{3,2,1,0:T(8,128)S(1)}, u32[]{:S(2)}, u32[]{:S(2)}) async-start(f32[4,4,128,128]{3,2,1,0:T(8,128)} %branch_1_fun.20), calls=%async_computation.3 | async-start | bytes 2097152 | tf_op jit(solution)/shard_map/cond/branch_1_fun/all_to_all | solution.py:410
  124.5 1.2 copy-start.6
  (5 other events, 4.8 us)

commit v12 on v10

--- a/solution.py
+++ b/solution.py
@@ -56,7 +56,7 @@
 
 
 def outer_forward(read, n, part, tokens, tw_ref, y_ref):
-    @pl.loop(part.start // ROWS, (part.start + part.size) // ROWS)
+    @pl.loop(part.start // ROWS, (part.start + part.size) // ROWS, unroll=min(2, part.size // ROWS))
     def _(r):
         rows = pl.ds(pl.multiple_of(r * ROWS, ROWS), ROWS)
         values = []
@@ -74,7 +74,7 @@
 
 
 def outer_inverse(write, n, part, tokens, tw_ref, y_ref):
-    @pl.loop(part.start // ROWS, (part.start + part.size) // ROWS)
+    @pl.loop(part.start // ROWS, (part.start + part.size) // ROWS, unroll=min(2, part.size // ROWS))
     def _(r):
         rows = pl.ds(pl.multiple_of(r * ROWS, ROWS), ROWS)
         values = []
@@ -320,15 +320,29 @@
     wait_all(stores)
 
 
-def gate_kernel(planes, width, x_ref, a_ref, b_ref, after_ref, oa_ref, ob_ref, a_buf, b_buf, sem):
-    z = plane(width)
+def load_rows(planes, width, refs, bufs, sem):
+    z = plane(width)
+    loads = []
+    for d in range(planes):
+        rows = pl.ds((z ^ d) * width, width)
+        loads.append(copies_of([(ref.at[rows], buf.at[d]) for ref, buf in zip(refs, bufs)], sem.at[d]))
+        start_all(loads[d])
+    return loads
+
+
+def gate_kernel(
+    planes, width, x_ref, a_ref, b_ref, after_ref, oa_ref, ob_ref, a_buf, b_buf, load_sem, sem
+):
+    z = plane(width)
+    loads = load_rows(planes, width, (a_ref, b_ref), (a_buf, b_buf), load_sem)
     stores = []
     for d in range(planes):
         rows = pl.ds((z ^ d) * width, width)
         x = x_ref[:, d]
-        a_buf[rows] = x * a_ref[rows]
-        b_buf[rows] = x * b_ref[rows]
-        stores += copies_of([(a_buf.at[rows], oa_ref.at[rows]), (b_buf.at[rows], ob_ref.at[rows])], sem.at[d])
+        wait_all(loads[d])
+        a_buf[d] = x * a_buf[d]
+        b_buf[d] = x * b_buf[d]
+        stores += copies_of([(a_buf.at[d], oa_ref.at[rows]), (b_buf.at[d], ob_ref.at[rows])], sem.at[d])
         start_all(stores[-2:])
     wait_all(stores)
 
@@ -351,18 +365,21 @@
 
 def gate_far_kernel(planes, width, *refs):
     far_refs, refs = refs[: planes - 1], refs[planes - 1 :]
-    a_ref, b_ref, done_a, done_b, oa_ref, ob_ref, a_buf, b_buf, sem = refs
-    z = plane(width)
+    a_ref, b_ref, done_a, done_b, oa_ref, ob_ref, a_buf, b_buf, load_sem, sem = refs
+    z = plane(width)
+    loads = load_rows(planes, width, (a_ref, b_ref), (a_buf, b_buf), load_sem)
     rows = pl.ds(z * width, width)
     stores = copies_of([(done_a, oa_ref.at[rows]), (done_b, ob_ref.at[rows])], sem.at[0])
     start_all(stores)
     for d, far_ref in enumerate(far_refs, 1):
         rows = pl.ds((z ^ d) * width, width)
         x = far_ref[...]
-        a_buf[rows] = x * a_ref[rows]
-        b_buf[rows] = x * b_ref[rows]
-        stores += copies_of([(a_buf.at[rows], oa_ref.at[rows]), (b_buf.at[rows], ob_ref.at[rows])], sem.at[d])
+        wait_all(loads[d])
+        a_buf[d] = x * a_buf[d]
+        b_buf[d] = x * b_buf[d]
+        stores += copies_of([(a_buf.at[d], oa_ref.at[rows]), (b_buf.at[d], ob_ref.at[rows])], sem.at[d])
         start_all(stores[-2:])
+    wait_all(loads[0])
     wait_all(stores)
 
 
@@ -461,7 +478,7 @@
     half_spectrum = (n, channels // 2, 2 * tokens)
     def transform_filters(first):
         return kernel_call(
-            part(filter_kernel, first, *half_sizes), "hvv", [("h", half_spectrum)],
+            part(filter_kernel, first, *half_sizes), "avv", [("h", half_spectrum)],
             [
                 pltpu.VMEM((channels // 2, length), f32),
                 *[pltpu.VMEM(half_spectrum, f32)] * 2,
@@ -502,7 +519,7 @@
         product_ch = within_plane(*merge(keep_p, *got_p, send_g))
         filt = (filt_a, transform_filters(channels // 2))
         *outs, prod_spec = kernel_call(
-            part(conv_kernel, planes, *sizes), "vvhhhh",
+            part(conv_kernel, planes, *sizes), "vvaahh",
             [("h", one)] * planes + [("h", spectrum)], transform_scratch, 2 * flops,
         )(product_ch, tw, fwd, inv, *filt)
         return outs, prod_spec, filt
@@ -512,7 +529,7 @@
 
     def third(near_g, far_g, filt, keep_c, prod_spec):
         back_ch, grad_spec = kernel_call(
-            part(back_kernel, planes, *sizes), "a" * planes + "vhhhha",
+            part(back_kernel, planes, *sizes), "a" * planes + "vaahha",
             [("h", paired), ("h", spectrum)], transform_scratch, 2 * flops,
         )(near_g, *far_g, tw, fwd, inv, *filt, keep_c)
         sends = send(within_plane(back_ch))
@@ -536,8 +553,8 @@
             [pltpu.VMEM(one, f32)] * 3 + [semaphores(2, 3)],
         )(near_b, value, key)
         gated, grad_query = kernel_call(
-            part(gate_kernel, planes, width), "vvva", [("h", blocks)] * 2,
-            [rows, rows, semaphores(planes, 2)],
+            part(gate_kernel, planes, width), "vaaa", [("h", blocks)] * 2,
+            [by_plane, by_plane, semaphores(planes, 2), semaphores(planes, 2)],
         )(conv_tok, query, cot, grad_filter)
         return gated, grad_query, begun, grad_filter
 
@@ -545,8 +562,8 @@
         fourth, keep_c, got_c, query, cot, near_b, value, key, own
     )
     grad_key, grad_value = kernel_call(
-        part(gate_far_kernel, planes, width), "v" * (planes + 3), [("h", blocks)] * 2,
-        [rows, rows, semaphores(planes, 2)],
+        part(gate_far_kernel, planes, width), "v" * (planes - 1) + "aavv", [("h", blocks)] * 2,
+        [by_plane, by_plane, semaphores(planes, 2), semaphores(planes, 2)],
     )(*far_b, value, key, *begun)
     shape = query_input.shape
     return (

time: 118 us -> 116 us (0.983)
  Pallas kernels: 42 us -> 40.8 us
    pallas_call x14, Pallas kernels: 42 us -> 40.8 us  [run(): pl.pallas_call(body, in_specs=[pl.BlockSpec(memory_space=SPACES[space]) f...]
  transfers between devices with their start and end apart: 17 -> 17, of which waited for: 4 -> 4; matrix products, arithmetic and copies ran while one was open for 2% -> 2% of each run, Pallas kernels for 32% -> 31%
where the time goes in v12:
time: 116 us
  Pallas kernels  40.8 us (35%)
  waiting for transfers between devices  37.5 us (32%)
  starting transfers between devices  33.9 us (29%)
  other arithmetic  2.64 us (2%)
    pallas_call x14, Pallas kernels, run(): pl.pallas_call(body, in_specs=[pl.BlockSpec(memory_space=SPACES[space]) f...  40.8 us
    all_to_all x4, waiting for transfers between devices, within_plane(): lax.all_to_all(x, 'context', 0, 0, axis_index_groups=members, tiled=True)  37.5 us
    ppermute x12, starting transfers between devices, along_z(): lax.ppermute(x, 'context', [(i, i ^ d * width) for i in range(n)])  19 us
    all_to_all x4, starting transfers between devices, within_plane(): lax.all_to_all(x, 'context', 0, 0, axis_index_groups=members, tiled=True)  14.8 us
    add x1, other arithmetic, fourth(): grad_filter = own + lax.ppermute(own, 'dp', [(0, 1), (1, 0)])  2.64 us
  transfers between devices with their start and end apart: 17, of which 4 were waited for; matrix products, arithmetic and copies ran while one was open for 2% of the time, Pallas kernels for 31%

profile of v12, /device:TPU:0, one launch (start us, length us, event | category | flops | bytes accessed | tf_op | source)
XLA Modules:
  0.0 115.9 jit_solution(12462645227155423207)
XLA Ops:
  2.6 3.1 %collective-permute-start.4 = (f32[4,128,128]{2,1,0:T(8,128)S(1)}, f32[4,128,128]{2,1,0:T(8,128)}, u32[]{:S(2)}, u32[]{:S(2)}) collective-permute-start(f32[4,128,128]{2,1,0:T(8,128)S(1)} %get-tuple-element.170), channel_id=1, source_target_pairs={{0,4},{1,5},{2,6},{3,7},{4,0},{5,1},{6,2},{7,3},{8,12},{9,13},{10,... | collective-permute-start | bytes 786440 | tf_op jit(solution)/shard_map/ppermute | solution.py:458
  5.7 2.6 %collective-permute-start.5 = (f32[4,128,128]{2,1,0:T(8,128)S(1)}, f32[4,128,128]{2,1,0:T(8,128)}, u32[]{:S(2)}, u32[]{:S(2)}) collective-permute-start(f32[4,128,128]{2,1,0:T(8,128)S(1)} %get-tuple-element.171), channel_id=1, source_target_pairs={{0,8},{1,9},{2,10},{3,11},{4,12},{5,13},{6,14},{7,15},{8,0},{9,1},... | collective-permute-start | bytes 786440 | tf_op jit(solution)/shard_map/ppermute | solution.py:458
  8.3 20.3 %conditional.4 = (f32[4,128,128]{2,1,0:T(8,128)}, f32[4,128,128]{2,1,0:T(8,128)}, f32[4,128,128]{2,1,0:T(8,128)}, f32[4,128,128]{2,1,0:T(8,128)}, f32[16,64,256]{2,1,0:T(8,128)}) conditional(s32[]{:T(128)} %convert_element_type.2, () %tuple.46, (f32[16,128,128]{2,1,0:T(8,128)}, f32[16,128,128]{2,1,0:T(8,128)}, f32[4,128,128]{2,1,0:T(8,128)}, ...), branch_computations={%region_0.0_spmd, %region_1.0_spmd} | conditional | flops 268435456 | bytes 11665480 | solution.py:500
  10.8 3.9 %all-to-all-start = ((f32[4,4,128,128]{3,2,1,0:T(8,128)}), f32[4,4,128,128]{3,2,1,0:T(8,128)S(1)}, u32[]{:S(2)}, u32[]{:S(2)}) async-start(f32[4,4,128,128]{3,2,1,0:T(8,128)} %branch_1_fun.12), calls=%async_computation | async-start | bytes 2097152 | tf_op jit(solution)/shard_map/cond/branch_1_fun/all_to_all | solution.py:464
  17.1 10.5 %all-to-all-done.refs_0_ = f32[4,4,128,128]{3,2,1,0:T(8,128)S(1)} async-done(((f32[4,4,128,128]{3,2,1,0:T(8,128)}), f32[4,4,128,128]{3,2,1,0:T(8,128)S(1)}, u32[]{:S(2)}, u32[]{:S(2)}) %all-to-all-start) | async-done | bytes 1048608 | tf_op jit(solution)/shard_map/cond/branch_1_fun/all_to_all | solution.py:464
  29.3 3.5 %collective-permute-start.2 = (f32[4,128,128]{2,1,0:T(8,128)}, f32[4,128,128]{2,1,0:T(8,128)}, u32[]{:S(2)}, u32[]{:S(2)}) collective-permute-start(f32[4,128,128]{2,1,0:T(8,128)} %get-tuple-element.168), channel_id=1, source_target_pairs={{0,8},{1,9},{2,10},{3,11},{4,12},{5,13},{6,14},{7,15},{8,0},{9,1},... | collective-permute-start | bytes 786440 | tf_op jit(solution)/shard_map/ppermute | solution.py:458
  33.1 24.5 %conditional.5 = (f32[4,128,128]{2,1,0:T(8,128)}, f32[4,128,128]{2,1,0:T(8,128)}, f32[4,128,128]{2,1,0:T(8,128)}, f32[4,128,128]{2,1,0:T(8,128)}, f32[16,128,256...) conditional(s32[]{:T(128)} %convert_element_type.2, () %tuple.48, (f32[4,128,128]{2,1,0:T(8,128)}, ...), branch_computations={%region_2.0_spmd, %region_3.0_spmd} | conditional | flops 1342177280 | bytes 18088052 | solution.py:500
  35.3 3.7 %all-to-all-start.1 = ((f32[4,4,128,128]{3,2,1,0:T(8,128)}), f32[4,4,128,128]{3,2,1,0:T(8,128)S(1)}, u32[]{:S(2)}, u32[]{:S(2)}) async-start(f32[4,4,128,128]{3,2,1,0:T(8,128)} %branch_1_fun.15), calls=%async_computation.1 | async-start | bytes 2097152 | tf_op jit(solution)/shard_map/cond/branch_1_fun/all_to_all | solution.py:464
  39.0 2.4 %branch_1_fun.16.refs_5_ = f32[16,64,256]{2,1,0:T(8,128)} custom-call(f32[128,2048]{1,0:T(8,128)S(1)} %get-tuple-element.95.refs_0_, f32[2,16,8,128]{3,2,1,0:T(8,128)S(1)} %get-tuple-element.91.refs_1_, bf16[768,256]{1,0:T(8,128)(2,1)S(1)} %get-tuple-element.92.refs_2_), custom_call_target="tpu_custom_call" | custom-call | flops 268435456 | bytes 3014656 | tf_op jit(solution)/shard_map/cond/branch_1_fun/pallas_call | solution.py:401
  41.4 9.9 %all-to-all-done.1.refs_0_ = f32[4,4,128,128]{3,2,1,0:T(8,128)S(1)} async-done(((f32[4,4,128,128]{3,2,1,0:T(8,128)}), f32[4,4,128,128]{3,2,1,0:T(8,128)S(1)}, u32[]{:S(2)}, u32[]{:S(2)}) %all-to-all-start.1) | async-done | bytes 1048608 | tf_op jit(solution)/shard_map/cond/branch_1_fun/all_to_all | solution.py:464
  51.3 6.4 %branch_1_fun.17 = (f32[4,128,128]{2,1,0:T(8,128)}, f32[4,128,128]{2,1,0:T(8,128)}, f32[4,128,128]{2,1,0:T(8,128)}, f32[4,128,128]{2,1,0:T(8,128)}, f32[16,128,256]{2,1,0:T(8,128)}) custom-call(f32[4,4,128,128]{3,2,1,0:T(8,128)S(1)} %all-to-all-done.1.refs_0_, f32[2,16,8,128]{3,2,1,0:T(8,128)S(1)} %get-tuple-element.91.refs_1_, ...), custom_call_target="tpu_custom_call" | custom-call | flops 1073741824 | bytes 7995392 | tf_op jit(solution)/shard_map/cond/branch_1_fun/pallas_call | solution.py:401
  58.2 3.5 %collective-permute-start.8 = (f32[4,128,128]{2,1,0:T(8,128)}, f32[4,128,128]{2,1,0:T(8,128)S(1)}, u32[]{:S(2)}, u32[]{:S(2)}) collective-permute-start(f32[4,128,128]{2,1,0:T(8,128)} %get-tuple-element.181), channel_id=1, source_target_pairs={{0,8},{1,9},{2,10},{3,11},{4,12},{5,13},{6,14},{7,15},{8,0},{9,1},... | collective-permute-start | bytes 786440 | tf_op jit(solution)/shard_map/ppermute | solution.py:458
  62.1 23.9 %conditional.6 = (f32[4,128,128]{2,1,0:T(8,128)}, f32[4,128,128]{2,1,0:T(8,128)}, f32[4,128,128]{2,1,0:T(8,128)}, f32[4,128,128]{2,1,0:T(8,128)}, f32[128,2048]{1,0:T(8,128)}) conditional(s32[]{:T(128)} %convert_element_type.2, () %tuple.45, (f32[4,128,128]{2,1,0:T(8,128)}, f32[4,128,128]{2,1,0:T(8,128)S(1)}, f32[4,128,128]{2,1,0:T(8,128)}, ...), branch_computations={%region_4.0_spmd, %region_5.0_spmd} | conditional | flops 1610612736 | bytes 21233764 | solution.py:500
  62.1 6.9 %branch_1_fun.18 = (f32[4,4,128,128]{3,2,1,0:T(8,128)}, f32[16,128,256]{2,1,0:T(8,128)}) custom-call(f32[4,128,128]{2,1,0:T(8,128)} %get-tuple-element.101.refs_0_, f32[4,128,128]{2,1,0:T(8,128)S(1)} %get-tuple-element.102.refs_1_, f32[4,128,128]{2,1,0:T(8,128)} %get-tuple-element.103.refs_2_, f32[4,128,128]{2,1,0:T(8,128)} %get-tuple-element.104.refs_3_, ...), custom_call_target="tpu_custom_call" | custom-call | flops 1073741824 | bytes 8257536 | tf_op jit(solution)/shard_map/cond/branch_1_fun/pallas_call | solution.py:401
  69.1 3.7 %all-to-all-start.2 = ((f32[4,4,128,128]{3,2,1,0:T(8,128)}), f32[4,4,128,128]{3,2,1,0:T(8,128)S(1)}, u32[]{:S(2)}, u32[]{:S(2)}) async-start(f32[4,4,128,128]{3,2,1,0:T(8,128)} %get-tuple-element.111), calls=%async_computation.2 | async-start | bytes 2097152 | tf_op jit(solution)/shard_map/cond/branch_1_fun/all_to_all | solution.py:464
  72.7 5.2 %branch_1_fun.20 = f32[128,2048]{1,0:T(8,128)} custom-call(f32[2,16,8,128]{3,2,1,0:T(8,128)S(1)} %get-tuple-element.105.refs_4_.refs_0_, bf16[768,256]{1,0:T(8,128)(2,1)S(1)} %copy-done.4, f32[16,128,256]{2,1,0:T(8,128)} %get-tuple-element.116.refs_2_, f32[16,128,256]{2,1,0:T(8,128)} %get-tuple-element.117.refs_3_), custom_call_target="tpu_custom_call" | custom-call | flops 536870912 | bytes 6160384 | tf_op jit(solution)/shard_map/cond/branch_1_fun/pallas_call | solution.py:401
  77.9 7.1 %all-to-all-done.2.refs_0_ = f32[4,4,128,128]{3,2,1,0:T(8,128)S(1)} async-done(((f32[4,4,128,128]{3,2,1,0:T(8,128)}), f32[4,4,128,128]{3,2,1,0:T(8,128)S(1)}, u32[]{:S(2)}, u32[]{:S(2)}) %all-to-all-start.2) | async-done | bytes 1048608 | tf_op jit(solution)/shard_map/cond/branch_1_fun/all_to_all | solution.py:464
  86.6 3.5 %collective-permute-start.11 = (f32[4,128,128]{2,1,0:T(8,128)}, f32[4,128,128]{2,1,0:T(8,128)S(1)}, u32[]{:S(2)}, u32[]{:S(2)}) collective-permute-start(f32[4,128,128]{2,1,0:T(8,128)} %get-tuple-element.186), channel_id=1, source_target_pairs={{0,8},{1,9},{2,10},{3,11},{4,12},{5,13},{6,14},{7,15},{8,0},{9,1},... | collective-permute-start | bytes 786440 | tf_op jit(solution)/shard_map/ppermute | solution.py:458
  90.5 22.8 %conditional.7 = (f32[4,128,128]{2,1,0:T(8,128)S(1)}, f32[4,128,128]{2,1,0:T(8,128)S(1)}, f32[128,2048]{1,0:T(8,128)}, f32[1,2048,128]{2,1,0:T(8,128)}, f32[1,2048,128]{2,1,0:T(8,128)}) conditional(s32[]{:T(128)} %convert_element_type.2, () %tuple.44, (f32[4,128,128]{2,1,0:T(8,128)}, f32[16,128,128]{2,1,0:T(8,128)}, f32[16,128,128]{2,1,0:T(8,128)S(1)}, ...), branch_computations={%region_6.0_spmd, %region_7.0_spmd} | conditional | flops 262144 | bytes 24117416 | solution.py:500
  92.6 3.5 %all-to-all-start.3 = ((f32[4,4,128,128]{3,2,1,0:T(8,128)}), f32[4,4,128,128]{3,2,1,0:T(8,128)S(1)}, u32[]{:S(2)}, u32[]{:S(2)}) async-start(f32[4,4,128,128]{3,2,1,0:T(8,128)} %branch_1_fun.22), calls=%async_computation.3 | async-start | bytes 2097152 | tf_op jit(solution)/shard_map/cond/branch_1_fun/all_to_all | solution.py:464
  98.1 2.6 %add.2.refs_3_ = f32[128,2048]{1,0:T(8,128)} add(f32[128,2048]{1,0:T(8,128)} %get-tuple-element.123, f32[128,2048]{1,0:T(8,128)} %collective-permute-done) | non-fusion elementwise | flops 262144 | bytes 3145728 | tf_op jit(solution)/shard_map/cond/branch_1_fun/add | solution.py:547
  100.8 10.0 %all-to-all-done.3.refs_0_ = f32[4,4,128,128]{3,2,1,0:T(8,128)S(1)} async-done(((f32[4,4,128,128]{3,2,1,0:T(8,128)}), f32[4,4,128,128]{3,2,1,0:T(8,128)S(1)}, u32[]{:S(2)}, u32[]{:S(2)}) %all-to-all-start.3) | async-done | bytes 1048608 | tf_op jit(solution)/shard_map/cond/branch_1_fun/all_to_all | solution.py:464
  110.7 2.6 %branch_1_fun.23 = (f32[16,128,128]{2,1,0:T(8,128)}, f32[16,128,128]{2,1,0:T(8,128)}) custom-call(f32[4,4,128,128]{3,2,1,0:T(8,128)S(1)} %all-to-all-done.3.refs_0_, f32[16,128,128]{2,1,0:T(8,128)} %get-tuple-element.128.refs_1_, f32[16,128,128]{2,1,0:T(8,128)} %get-tuple-element.129.refs_2_, f32[128,2048]{1,0:T(8,128)} %add.2.refs_3_), custom_call_target="tpu_custom_call" | custom-call | bytes 6291456 | tf_op jit(solution)/shard_map/cond/branch_1_fun/pallas_call | solution.py:401
  113.4 2.5 %shard_map.120 = (f32[16,128,128]{2,1,0:T(8,128)}, f32[16,128,128]{2,1,0:T(8,128)}) custom-call(f32[4,128,128]{2,1,0:T(8,128)S(1)} %collective-permute-done.10.refs_0_, f32[4,128,128]{2,1,0:T(8,128)S(1)} %collective-permute-done.11.refs_1_, f32[4,128,128]{2,1,0:T(8,128)S(1)} %collective-permute-done.12.refs_2_, f32[16,128,128]{2,1,0:T(8,128)} %bitcast.13, ...), custom_call_target="tpu_custom_call" | custom-call | bytes 5505024 | tf_op jit(solution)/shard_map/pallas_call | solution.py:401
  (45 shorter events, 17.9 us)
Async XLA Ops:
  0.6 7.7 %copy-start.1 = (bf16[768,256]{1,0:T(8,128)(2,1)S(1)}, bf16[768,256]{1,0:T(8,128)(2,1)}, u32[]{:S(2)}) copy-start(bf16[768,256]{1,0:T(8,128)(2,1)} %constant.11.clone) | copy-start | bytes 1179652
  0.6 7.7 %copy-start.5 = (f32[2,16,8,128]{3,2,1,0:T(8,128)S(1)}, f32[2,16,8,128]{3,2,1,0:T(8,128)}, u32[]{:S(2)}) copy-start(f32[2,16,8,128]{3,2,1,0:T(8,128)} %constant.17.clone) | copy-start | bytes 393220
  0.7 7.7 %copy-start.2 = (f32[128,2048]{1,0:T(8,128)S(1)}, f32[128,2048]{1,0:T(8,128)}, u32[]{:S(2)}) copy-start(f32[128,2048]{1,0:T(8,128)} %param.19) | copy-start | bytes 3145732
  2.6 30.2 %collective-permute-start.4 = (f32[4,128,128]{2,1,0:T(8,128)S(1)}, f32[4,128,128]{2,1,0:T(8,128)}, u32[]{:S(2)}, u32[]{:S(2)}) collective-permute-start(f32[4,128,128]{2,1,0:T(8,128)S(1)} %get-tuple-element.170), channel_id=1, source_target_pairs={{0,4},{1,5},{2,6},{3,7},{4,0},{5,1},{6,2},{7,3},{8,12},{9,13},{10,... | collective-permute-start | bytes 786440 | tf_op jit(solution)/shard_map/ppermute | solution.py:458
  5.7 27.4 %collective-permute-start.5 = (f32[4,128,128]{2,1,0:T(8,128)S(1)}, f32[4,128,128]{2,1,0:T(8,128)}, u32[]{:S(2)}, u32[]{:S(2)}) collective-permute-start(f32[4,128,128]{2,1,0:T(8,128)S(1)} %get-tuple-element.171), channel_id=1, source_target_pairs={{0,8},{1,9},{2,10},{3,11},{4,12},{5,13},{6,14},{7,15},{8,0},{9,1},... | collective-permute-start | bytes 786440 | tf_op jit(solution)/shard_map/ppermute | solution.py:458
  8.3 24.8 %collective-permute-start.6 = (f32[4,128,128]{2,1,0:T(8,128)S(1)}, f32[4,128,128]{2,1,0:T(8,128)}, u32[]{:S(2)}, u32[]{:S(2)}) collective-permute-start(f32[4,128,128]{2,1,0:T(8,128)S(1)} %get-tuple-element.172), channel_id=1, source_target_pairs={{0,12},{1,13},{2,14},{3,15},{4,8},{5,9},{6,10},{7,11},{8,4},{9,5},... | collective-permute-start | bytes 786440 | tf_op jit(solution)/shard_map/ppermute | solution.py:458
  10.8 16.9 %all-to-all-start = ((f32[4,4,128,128]{3,2,1,0:T(8,128)}), f32[4,4,128,128]{3,2,1,0:T(8,128)S(1)}, u32[]{:S(2)}, u32[]{:S(2)}) async-start(f32[4,4,128,128]{3,2,1,0:T(8,128)} %branch_1_fun.12), calls=%async_computation | async-start | bytes 2097152 | tf_op jit(solution)/shard_map/cond/branch_1_fun/all_to_all | solution.py:464
  28.6 33.1 %collective-permute-start.1 = (f32[4,128,128]{2,1,0:T(8,128)}, f32[4,128,128]{2,1,0:T(8,128)S(1)}, u32[]{:S(2)}, u32[]{:S(2)}) collective-permute-start(f32[4,128,128]{2,1,0:T(8,128)} %get-tuple-element.167), channel_id=1, source_target_pairs={{0,4},{1,5},{2,6},{3,7},{4,0},{5,1},{6,2},{7,3},{8,12},{9,13},{10,... | collective-permute-start | bytes 786440 | tf_op jit(solution)/shard_map/ppermute | solution.py:458
  29.3 32.8 %collective-permute-start.2 = (f32[4,128,128]{2,1,0:T(8,128)}, f32[4,128,128]{2,1,0:T(8,128)}, u32[]{:S(2)}, u32[]{:S(2)}) collective-permute-start(f32[4,128,128]{2,1,0:T(8,128)} %get-tuple-element.168), channel_id=1, source_target_pairs={{0,8},{1,9},{2,10},{3,11},{4,12},{5,13},{6,14},{7,15},{8,0},{9,1},... | collective-permute-start | bytes 786440 | tf_op jit(solution)/shard_map/ppermute | solution.py:458
  32.8 29.3 %collective-permute-start.3 = (f32[4,128,128]{2,1,0:T(8,128)}, f32[4,128,128]{2,1,0:T(8,128)}, u32[]{:S(2)}, u32[]{:S(2)}) collective-permute-start(f32[4,128,128]{2,1,0:T(8,128)} %get-tuple-element.169), channel_id=1, source_target_pairs={{0,12},{1,13},{2,14},{3,15},{4,8},{5,9},{6,10},{7,11},{8,4},{9,5},... | collective-permute-start | bytes 786440 | tf_op jit(solution)/shard_map/ppermute | solution.py:458
  35.3 16.0 %copy-start.3 = (bf16[768,256]{1,0:T(8,128)(2,1)S(1)}, bf16[768,256]{1,0:T(8,128)(2,1)}, u32[]{:S(2)}) copy-start(bf16[768,256]{1,0:T(8,128)(2,1)} %get-tuple-element.93.refs_3_) | copy-start | bytes 1179652 | tf_op jit(solution)/shard_map/cond
  35.3 16.0 %all-to-all-start.1 = ((f32[4,4,128,128]{3,2,1,0:T(8,128)}), f32[4,4,128,128]{3,2,1,0:T(8,128)S(1)}, u32[]{:S(2)}, u32[]{:S(2)}) async-start(f32[4,4,128,128]{3,2,1,0:T(8,128)} %branch_1_fun.15), calls=%async_computation.1 | async-start | bytes 2097152 | tf_op jit(solution)/shard_map/cond/branch_1_fun/all_to_all | solution.py:464
  57.7 32.4 %collective-permute-start.7 = (f32[4,128,128]{2,1,0:T(8,128)}, f32[4,128,128]{2,1,0:T(8,128)S(1)}, u32[]{:S(2)}, u32[]{:S(2)}) collective-permute-start(f32[4,128,128]{2,1,0:T(8,128)} %get-tuple-element.180), channel_id=1, source_target_pairs={{0,4},{1,5},{2,6},{3,7},{4,0},{5,1},{6,2},{7,3},{8,12},{9,13},{10,... | collective-permute-start | bytes 786440 | tf_op jit(solution)/shard_map/ppermute | solution.py:458
  58.2 32.4 %collective-permute-start.8 = (f32[4,128,128]{2,1,0:T(8,128)}, f32[4,128,128]{2,1,0:T(8,128)S(1)}, u32[]{:S(2)}, u32[]{:S(2)}) collective-permute-start(f32[4,128,128]{2,1,0:T(8,128)} %get-tuple-element.181), channel_id=1, source_target_pairs={{0,8},{1,9},{2,10},{3,11},{4,12},{5,13},{6,14},{7,15},{8,0},{9,1},... | collective-permute-start | bytes 786440 | tf_op jit(solution)/shard_map/ppermute | solution.py:458
  61.7 28.8 %collective-permute-start.9 = (f32[4,128,128]{2,1,0:T(8,128)}, f32[4,128,128]{2,1,0:T(8,128)}, u32[]{:S(2)}, u32[]{:S(2)}) collective-permute-start(f32[4,128,128]{2,1,0:T(8,128)} %get-tuple-element.182), channel_id=1, source_target_pairs={{0,12},{1,13},{2,14},{3,15},{4,8},{5,9},{6,10},{7,11},{8,4},{9,5},... | collective-permute-start | bytes 786440 | tf_op jit(solution)/shard_map/ppermute | solution.py:458
  62.1 28.4 %copy-start = (f32[1,2048,128]{2,1,0:T(8,128)S(1)}, f32[1,2048,128]{2,1,0:T(8,128)}, u32[]{:S(2)}) copy-start(f32[1,2048,128]{2,1,0:T(8,128)} %param.17) | copy-start | bytes 3145732
  69.0 3.7 %copy-start.4 = (bf16[768,256]{1,0:T(8,128)(2,1)S(1)}, bf16[768,256]{1,0:T(8,128)(2,1)}, u32[]{:S(2)}) copy-start(bf16[768,256]{1,0:T(8,128)(2,1)} %get-tuple-element.107.refs_6_.refs_1_) | copy-start | bytes 1179652 | tf_op jit(solution)/shard_map/cond
  69.1 16.0 %all-to-all-start.2 = ((f32[4,4,128,128]{3,2,1,0:T(8,128)}), f32[4,4,128,128]{3,2,1,0:T(8,128)S(1)}, u32[]{:S(2)}, u32[]{:S(2)}) async-start(f32[4,4,128,128]{3,2,1,0:T(8,128)} %get-tuple-element.111), calls=%async_computation.2 | async-start | bytes 2097152 | tf_op jit(solution)/shard_map/cond/branch_1_fun/all_to_all | solution.py:464
  86.1 27.3 %collective-permute-start.10 = (f32[4,128,128]{2,1,0:T(8,128)}, f32[4,128,128]{2,1,0:T(8,128)S(1)}, u32[]{:S(2)}, u32[]{:S(2)}) collective-permute-start(f32[4,128,128]{2,1,0:T(8,128)} %get-tuple-element.185), channel_id=1, source_target_pairs={{0,4},{1,5},{2,6},{3,7},{4,0},{5,1},{6,2},{7,3},{8,12},{9,13},{10,... | collective-permute-start | bytes 786440 | tf_op jit(solution)/shard_map/ppermute | solution.py:458
  86.6 26.8 %collective-permute-start.11 = (f32[4,128,128]{2,1,0:T(8,128)}, f32[4,128,128]{2,1,0:T(8,128)S(1)}, u32[]{:S(2)}, u32[]{:S(2)}) collective-permute-start(f32[4,128,128]{2,1,0:T(8,128)} %get-tuple-element.186), channel_id=1, source_target_pairs={{0,8},{1,9},{2,10},{3,11},{4,12},{5,13},{6,14},{7,15},{8,0},{9,1},... | collective-permute-start | bytes 786440 | tf_op jit(solution)/shard_map/ppermute | solution.py:458
  90.1 23.3 %collective-permute-start.12 = (f32[4,128,128]{2,1,0:T(8,128)}, f32[4,128,128]{2,1,0:T(8,128)S(1)}, u32[]{:S(2)}, u32[]{:S(2)}) collective-permute-start(f32[4,128,128]{2,1,0:T(8,128)} %get-tuple-element.187), channel_id=1, source_target_pairs={{0,12},{1,13},{2,14},{3,15},{4,8},{5,9},{6,10},{7,11},{8,4},{9,5},... | collective-permute-start | bytes 786440 | tf_op jit(solution)/shard_map/ppermute | solution.py:458
  90.5 7.6 %collective-permute-start = (f32[128,2048]{1,0:T(8,128)}, f32[128,2048]{1,0:T(8,128)}, u32[]{:S(2)}, u32[]{:S(2)}) collective-permute-start(f32[128,2048]{1,0:T(8,128)} %get-tuple-element.123), channel_id=1, source_target_pairs={{0,16},{16,0},{1,17},{17,1},{2,18},{18,2},{3,19},{19,3},{4,20},{20... | collective-permute-start | bytes 3145736 | tf_op jit(solution)/shard_map/cond/branch_1_fun/ppermute | solution.py:547
  92.6 18.1 %all-to-all-start.3 = ((f32[4,4,128,128]{3,2,1,0:T(8,128)}), f32[4,4,128,128]{3,2,1,0:T(8,128)S(1)}, u32[]{:S(2)}, u32[]{:S(2)}) async-start(f32[4,4,128,128]{3,2,1,0:T(8,128)} %branch_1_fun.22), calls=%async_computation.3 | async-start | bytes 2097152 | tf_op jit(solution)/shard_map/cond/branch_1_fun/all_to_all | solution.py:464
  110.7 2.6 %copy-start.7 = (f32[4,128,128]{2,1,0:T(8,128)S(1)}, f32[4,128,128]{2,1,0:T(8,128)}, u32[]{:S(2)}) copy-start(f32[4,128,128]{2,1,0:T(8,128)} %get-tuple-element.233) | copy-start | bytes 786436 | tf_op jit(solution)/shard_map/cond
  (1 other events, 2.6 us)

commit v13 on v12

--- a/solution.py
+++ b/solution.py
@@ -143,6 +143,7 @@
     buf_ref, spec_buf, own_buf, y_ref, fwd_ref, inv_ref, sem,
 ):
     half = channels // 2
+    groups = [pl.ds(0, n // 2), pl.ds(n // 2, n // 2)]
     rows = [pl.ds(0, half), pl.ds(half, half)]
     loads = [copies_of(sources(part), sem.at[0, i]) for i, part in enumerate(rows)]
     for load in loads:
@@ -157,16 +158,16 @@
             ],
             sem.at[1, i],
         )
-        for i, ms in enumerate(parts_of(n))
+        for i, ms in enumerate(groups)
     ]
     for load in spec_loads:
         start_all(load)
     for part, load in zip(rows, loads):
         wait_all(load)
         outer_forward(read, n, part, tokens, tw_ref, y_ref)
-    own_stores = copies_of([(own_buf.at[ms], own_ref.at[ms]) for ms in parts_of(n)], sem.at[2, 0])
+    own_stores = copies_of([(own_buf.at[ms], own_ref.at[ms]) for ms in groups], sem.at[2, 0])
     wait_all(table_loads)
-    for ms, load, store in zip(parts_of(n), spec_loads, own_stores):
+    for ms, load, store in zip(groups, spec_loads, own_stores):
         own = times_table(flat(y_ref[ms]), fwd_ref)
         own_buf[ms] = own.reshape(ms.size, channels, 2 * tokens)
         store.start()
@@ -320,12 +321,12 @@
     wait_all(stores)
 
 
-def load_rows(planes, width, refs, bufs, sem):
-    z = plane(width)
-    loads = []
-    for d in range(planes):
+def load_rows(distances, width, refs, bufs, sem):
+    z = plane(width)
+    loads = {}
+    for d in distances:
         rows = pl.ds((z ^ d) * width, width)
-        loads.append(copies_of([(ref.at[rows], buf.at[d]) for ref, buf in zip(refs, bufs)], sem.at[d]))
+        loads[d] = copies_of([(ref.at[rows], buf.at[d]) for ref, buf in zip(refs, bufs)], sem.at[d])
         start_all(loads[d])
     return loads
 
@@ -334,7 +335,7 @@
     planes, width, x_ref, a_ref, b_ref, after_ref, oa_ref, ob_ref, a_buf, b_buf, load_sem, sem
 ):
     z = plane(width)
-    loads = load_rows(planes, width, (a_ref, b_ref), (a_buf, b_buf), load_sem)
+    loads = load_rows(range(planes), width, (a_ref, b_ref), (a_buf, b_buf), load_sem)
     stores = []
     for d in range(planes):
         rows = pl.ds((z ^ d) * width, width)
@@ -367,7 +368,7 @@
     far_refs, refs = refs[: planes - 1], refs[planes - 1 :]
     a_ref, b_ref, done_a, done_b, oa_ref, ob_ref, a_buf, b_buf, load_sem, sem = refs
     z = plane(width)
-    loads = load_rows(planes, width, (a_ref, b_ref), (a_buf, b_buf), load_sem)
+    loads = load_rows(range(1, planes), width, (a_ref, b_ref), (a_buf, b_buf), load_sem)
     rows = pl.ds(z * width, width)
     stores = copies_of([(done_a, oa_ref.at[rows]), (done_b, ob_ref.at[rows])], sem.at[0])
     start_all(stores)
@@ -379,7 +380,6 @@
         b_buf[d] = x * b_buf[d]
         stores += copies_of([(a_buf.at[d], oa_ref.at[rows]), (b_buf.at[d], ob_ref.at[rows])], sem.at[d])
         start_all(stores[-2:])
-    wait_all(loads[0])
     wait_all(stores)
 
 

time: 116 us -> 116 us (level)
  no operation moved by 1% of the time
where the time goes in v13:
time: 116 us
  Pallas kernels  40.8 us (35%)
  waiting for transfers between devices  37.5 us (32%)
  starting transfers between devices  33.9 us (29%)
  other arithmetic  2.64 us (2%)
    pallas_call x14, Pallas kernels, run(): pl.pallas_call(body, in_specs=[pl.BlockSpec(memory_space=SPACES[space]) f...  40.8 us
    all_to_all x4, waiting for transfers between devices, within_plane(): lax.all_to_all(x, 'context', 0, 0, axis_index_groups=members, tiled=True)  37.5 us
    ppermute x12, starting transfers between devices, along_z(): lax.ppermute(x, 'context', [(i, i ^ d * width) for i in range(n)])  19 us
    all_to_all x4, starting transfers between devices, within_plane(): lax.all_to_all(x, 'context', 0, 0, axis_index_groups=members, tiled=True)  14.8 us
    add x1, other arithmetic, fourth(): grad_filter = own + lax.ppermute(own, 'dp', [(0, 1), (1, 0)])  2.64 us
  transfers between devices with their start and end apart: 17, of which 4 were waited for; matrix products, arithmetic and copies ran while one was open for 2% of the time, Pallas kernels for 31%

profile of v13, /device:TPU:0, one launch (start us, length us, event | category | flops | bytes accessed | tf_op | source)
XLA Modules:
  0.0 115.8 jit_solution(17603401006271559713)
XLA Ops:
  2.6 3.1 %collective-permute-start.4 = (f32[4,128,128]{2,1,0:T(8,128)S(1)}, f32[4,128,128]{2,1,0:T(8,128)}, u32[]{:S(2)}, u32[]{:S(2)}) collective-permute-start(f32[4,128,128]{2,1,0:T(8,128)S(1)} %get-tuple-element.170), channel_id=1, source_target_pairs={{0,4},{1,5},{2,6},{3,7},{4,0},{5,1},{6,2},{7,3},{8,12},{9,13},{10,... | collective-permute-start | bytes 786440 | tf_op jit(solution)/shard_map/ppermute | solution.py:458
  5.7 2.6 %collective-permute-start.5 = (f32[4,128,128]{2,1,0:T(8,128)S(1)}, f32[4,128,128]{2,1,0:T(8,128)}, u32[]{:S(2)}, u32[]{:S(2)}) collective-permute-start(f32[4,128,128]{2,1,0:T(8,128)S(1)} %get-tuple-element.171), channel_id=1, source_target_pairs={{0,8},{1,9},{2,10},{3,11},{4,12},{5,13},{6,14},{7,15},{8,0},{9,1},... | collective-permute-start | bytes 786440 | tf_op jit(solution)/shard_map/ppermute | solution.py:458
  8.3 20.3 %conditional.4 = (f32[4,128,128]{2,1,0:T(8,128)}, f32[4,128,128]{2,1,0:T(8,128)}, f32[4,128,128]{2,1,0:T(8,128)}, f32[4,128,128]{2,1,0:T(8,128)}, f32[16,64,256]{2,1,0:T(8,128)}) conditional(s32[]{:T(128)} %convert_element_type.2, () %tuple.46, (f32[16,128,128]{2,1,0:T(8,128)}, f32[16,128,128]{2,1,0:T(8,128)}, f32[4,128,128]{2,1,0:T(8,128)}, ...), branch_computations={%region_0.0_spmd, %region_1.0_spmd} | conditional | flops 268435456 | bytes 11665480 | solution.py:500
  8.3 2.4 %branch_1_fun.12 = f32[4,4,128,128]{3,2,1,0:T(8,128)} custom-call(f32[16,128,128]{2,1,0:T(8,128)} %get-tuple-element.76.refs_0_, f32[16,128,128]{2,1,0:T(8,128)} %get-tuple-element.77.refs_1_, f32[4,128,128]{2,1,0:T(8,128)} %get-tuple-element.78.refs_2_), custom_call_target="tpu_custom_call" | custom-call | bytes 3407872 | tf_op jit(solution)/shard_map/cond/branch_1_fun/pallas_call | solution.py:401
  10.8 3.9 %all-to-all-start = ((f32[4,4,128,128]{3,2,1,0:T(8,128)}), f32[4,4,128,128]{3,2,1,0:T(8,128)S(1)}, u32[]{:S(2)}, u32[]{:S(2)}) async-start(f32[4,4,128,128]{3,2,1,0:T(8,128)} %branch_1_fun.12), calls=%async_computation | async-start | bytes 2097152 | tf_op jit(solution)/shard_map/cond/branch_1_fun/all_to_all | solution.py:464
  17.1 10.5 %all-to-all-done.refs_0_ = f32[4,4,128,128]{3,2,1,0:T(8,128)S(1)} async-done(((f32[4,4,128,128]{3,2,1,0:T(8,128)}), f32[4,4,128,128]{3,2,1,0:T(8,128)S(1)}, u32[]{:S(2)}, u32[]{:S(2)}) %all-to-all-start) | async-done | bytes 1048608 | tf_op jit(solution)/shard_map/cond/branch_1_fun/all_to_all | solution.py:464
  29.3 3.5 %collective-permute-start.2 = (f32[4,128,128]{2,1,0:T(8,128)}, f32[4,128,128]{2,1,0:T(8,128)}, u32[]{:S(2)}, u32[]{:S(2)}) collective-permute-start(f32[4,128,128]{2,1,0:T(8,128)} %get-tuple-element.168), channel_id=1, source_target_pairs={{0,8},{1,9},{2,10},{3,11},{4,12},{5,13},{6,14},{7,15},{8,0},{9,1},... | collective-permute-start | bytes 786440 | tf_op jit(solution)/shard_map/ppermute | solution.py:458
  33.1 24.6 %conditional.5 = (f32[4,128,128]{2,1,0:T(8,128)}, f32[4,128,128]{2,1,0:T(8,128)}, f32[4,128,128]{2,1,0:T(8,128)}, f32[4,128,128]{2,1,0:T(8,128)}, f32[16,128,256...) conditional(s32[]{:T(128)} %convert_element_type.2, () %tuple.48, (f32[4,128,128]{2,1,0:T(8,128)}, ...), branch_computations={%region_2.0_spmd, %region_3.0_spmd} | conditional | flops 1342177280 | bytes 18088052 | solution.py:500
  35.3 3.7 %all-to-all-start.1 = ((f32[4,4,128,128]{3,2,1,0:T(8,128)}), f32[4,4,128,128]{3,2,1,0:T(8,128)S(1)}, u32[]{:S(2)}, u32[]{:S(2)}) async-start(f32[4,4,128,128]{3,2,1,0:T(8,128)} %branch_1_fun.15), calls=%async_computation.1 | async-start | bytes 2097152 | tf_op jit(solution)/shard_map/cond/branch_1_fun/all_to_all | solution.py:464
  39.0 2.4 %branch_1_fun.16.refs_5_ = f32[16,64,256]{2,1,0:T(8,128)} custom-call(f32[128,2048]{1,0:T(8,128)S(1)} %get-tuple-element.95.refs_0_, f32[2,16,8,128]{3,2,1,0:T(8,128)S(1)} %get-tuple-element.91.refs_1_, bf16[768,256]{1,0:T(8,128)(2,1)S(1)} %get-tuple-element.92.refs_2_), custom_call_target="tpu_custom_call" | custom-call | flops 268435456 | bytes 3014656 | tf_op jit(solution)/shard_map/cond/branch_1_fun/pallas_call | solution.py:401
  41.4 9.9 %all-to-all-done.1.refs_0_ = f32[4,4,128,128]{3,2,1,0:T(8,128)S(1)} async-done(((f32[4,4,128,128]{3,2,1,0:T(8,128)}), f32[4,4,128,128]{3,2,1,0:T(8,128)S(1)}, u32[]{:S(2)}, u32[]{:S(2)}) %all-to-all-start.1) | async-done | bytes 1048608 | tf_op jit(solution)/shard_map/cond/branch_1_fun/all_to_all | solution.py:464
  51.3 6.4 %branch_1_fun.17 = (f32[4,128,128]{2,1,0:T(8,128)}, f32[4,128,128]{2,1,0:T(8,128)}, f32[4,128,128]{2,1,0:T(8,128)}, f32[4,128,128]{2,1,0:T(8,128)}, f32[16,128,256]{2,1,0:T(8,128)}) custom-call(f32[4,4,128,128]{3,2,1,0:T(8,128)S(1)} %all-to-all-done.1.refs_0_, f32[2,16,8,128]{3,2,1,0:T(8,128)S(1)} %get-tuple-element.91.refs_1_, ...), custom_call_target="tpu_custom_call" | custom-call | flops 1073741824 | bytes 7995392 | tf_op jit(solution)/shard_map/cond/branch_1_fun/pallas_call | solution.py:401
  58.2 3.5 %collective-permute-start.8 = (f32[4,128,128]{2,1,0:T(8,128)}, f32[4,128,128]{2,1,0:T(8,128)S(1)}, u32[]{:S(2)}, u32[]{:S(2)}) collective-permute-start(f32[4,128,128]{2,1,0:T(8,128)} %get-tuple-element.181), channel_id=1, source_target_pairs={{0,8},{1,9},{2,10},{3,11},{4,12},{5,13},{6,14},{7,15},{8,0},{9,1},... | collective-permute-start | bytes 786440 | tf_op jit(solution)/shard_map/ppermute | solution.py:458
  62.2 24.0 %conditional.6 = (f32[4,128,128]{2,1,0:T(8,128)}, f32[4,128,128]{2,1,0:T(8,128)}, f32[4,128,128]{2,1,0:T(8,128)}, f32[4,128,128]{2,1,0:T(8,128)}, f32[128,2048]{1,0:T(8,128)}) conditional(s32[]{:T(128)} %convert_element_type.2, () %tuple.45, (f32[4,128,128]{2,1,0:T(8,128)}, f32[4,128,128]{2,1,0:T(8,128)S(1)}, f32[4,128,128]{2,1,0:T(8,128)}, ...), branch_computations={%region_4.0_spmd, %region_5.0_spmd} | conditional | flops 1610612736 | bytes 21233764 | solution.py:500
  62.2 6.9 %branch_1_fun.18 = (f32[4,4,128,128]{3,2,1,0:T(8,128)}, f32[16,128,256]{2,1,0:T(8,128)}) custom-call(f32[4,128,128]{2,1,0:T(8,128)} %get-tuple-element.101.refs_0_, f32[4,128,128]{2,1,0:T(8,128)S(1)} %get-tuple-element.102.refs_1_, f32[4,128,128]{2,1,0:T(8,128)} %get-tuple-element.103.refs_2_, f32[4,128,128]{2,1,0:T(8,128)} %get-tuple-element.104.refs_3_, ...), custom_call_target="tpu_custom_call" | custom-call | flops 1073741824 | bytes 8257536 | tf_op jit(solution)/shard_map/cond/branch_1_fun/pallas_call | solution.py:401
  69.1 3.7 %all-to-all-start.2 = ((f32[4,4,128,128]{3,2,1,0:T(8,128)}), f32[4,4,128,128]{3,2,1,0:T(8,128)S(1)}, u32[]{:S(2)}, u32[]{:S(2)}) async-start(f32[4,4,128,128]{3,2,1,0:T(8,128)} %get-tuple-element.111), calls=%async_computation.2 | async-start | bytes 2097152 | tf_op jit(solution)/shard_map/cond/branch_1_fun/all_to_all | solution.py:464
  72.8 5.2 %branch_1_fun.20 = f32[128,2048]{1,0:T(8,128)} custom-call(f32[2,16,8,128]{3,2,1,0:T(8,128)S(1)} %get-tuple-element.105.refs_4_.refs_0_, bf16[768,256]{1,0:T(8,128)(2,1)S(1)} %copy-done.4, f32[16,128,256]{2,1,0:T(8,128)} %get-tuple-element.116.refs_2_, f32[16,128,256]{2,1,0:T(8,128)} %get-tuple-element.117.refs_3_), custom_call_target="tpu_custom_call" | custom-call | flops 536870912 | bytes 6160384 | tf_op jit(solution)/shard_map/cond/branch_1_fun/pallas_call | solution.py:401
  78.0 7.1 %all-to-all-done.2.refs_0_ = f32[4,4,128,128]{3,2,1,0:T(8,128)S(1)} async-done(((f32[4,4,128,128]{3,2,1,0:T(8,128)}), f32[4,4,128,128]{3,2,1,0:T(8,128)S(1)}, u32[]{:S(2)}, u32[]{:S(2)}) %all-to-all-start.2) | async-done | bytes 1048608 | tf_op jit(solution)/shard_map/cond/branch_1_fun/all_to_all | solution.py:464
  86.6 3.5 %collective-permute-start.11 = (f32[4,128,128]{2,1,0:T(8,128)}, f32[4,128,128]{2,1,0:T(8,128)S(1)}, u32[]{:S(2)}, u32[]{:S(2)}) collective-permute-start(f32[4,128,128]{2,1,0:T(8,128)} %get-tuple-element.186), channel_id=1, source_target_pairs={{0,8},{1,9},{2,10},{3,11},{4,12},{5,13},{6,14},{7,15},{8,0},{9,1},... | collective-permute-start | bytes 786440 | tf_op jit(solution)/shard_map/ppermute | solution.py:458
  90.6 22.8 %conditional.7 = (f32[4,128,128]{2,1,0:T(8,128)S(1)}, f32[4,128,128]{2,1,0:T(8,128)S(1)}, f32[128,2048]{1,0:T(8,128)}, f32[1,2048,128]{2,1,0:T(8,128)}, f32[1,2048,128]{2,1,0:T(8,128)}) conditional(s32[]{:T(128)} %convert_element_type.2, () %tuple.44, (f32[4,128,128]{2,1,0:T(8,128)}, f32[16,128,128]{2,1,0:T(8,128)}, f32[16,128,128]{2,1,0:T(8,128)S(1)}, ...), branch_computations={%region_6.0_spmd, %region_7.0_spmd} | conditional | flops 262144 | bytes 24117416 | solution.py:500
  92.7 3.5 %all-to-all-start.3 = ((f32[4,4,128,128]{3,2,1,0:T(8,128)}), f32[4,4,128,128]{3,2,1,0:T(8,128)S(1)}, u32[]{:S(2)}, u32[]{:S(2)}) async-start(f32[4,4,128,128]{3,2,1,0:T(8,128)} %branch_1_fun.22), calls=%async_computation.3 | async-start | bytes 2097152 | tf_op jit(solution)/shard_map/cond/branch_1_fun/all_to_all | solution.py:464
  98.2 2.6 %add.2.refs_3_ = f32[128,2048]{1,0:T(8,128)} add(f32[128,2048]{1,0:T(8,128)} %get-tuple-element.123, f32[128,2048]{1,0:T(8,128)} %collective-permute-done) | non-fusion elementwise | flops 262144 | bytes 3145728 | tf_op jit(solution)/shard_map/cond/branch_1_fun/add | solution.py:547
  100.8 10.0 %all-to-all-done.3.refs_0_ = f32[4,4,128,128]{3,2,1,0:T(8,128)S(1)} async-done(((f32[4,4,128,128]{3,2,1,0:T(8,128)}), f32[4,4,128,128]{3,2,1,0:T(8,128)S(1)}, u32[]{:S(2)}, u32[]{:S(2)}) %all-to-all-start.3) | async-done | bytes 1048608 | tf_op jit(solution)/shard_map/cond/branch_1_fun/all_to_all | solution.py:464
  110.8 2.6 %branch_1_fun.23 = (f32[16,128,128]{2,1,0:T(8,128)}, f32[16,128,128]{2,1,0:T(8,128)}) custom-call(f32[4,4,128,128]{3,2,1,0:T(8,128)S(1)} %all-to-all-done.3.refs_0_, f32[16,128,128]{2,1,0:T(8,128)} %get-tuple-element.128.refs_1_, f32[16,128,128]{2,1,0:T(8,128)} %get-tuple-element.129.refs_2_, f32[128,2048]{1,0:T(8,128)} %add.2.refs_3_), custom_call_target="tpu_custom_call" | custom-call | bytes 6291456 | tf_op jit(solution)/shard_map/cond/branch_1_fun/pallas_call | solution.py:401
  (45 shorter events, 17.8 us)
Async XLA Ops:
  0.6 7.7 %copy-start.1 = (bf16[768,256]{1,0:T(8,128)(2,1)S(1)}, bf16[768,256]{1,0:T(8,128)(2,1)}, u32[]{:S(2)}) copy-start(bf16[768,256]{1,0:T(8,128)(2,1)} %constant.11.clone) | copy-start | bytes 1179652
  0.6 7.7 %copy-start.5 = (f32[2,16,8,128]{3,2,1,0:T(8,128)S(1)}, f32[2,16,8,128]{3,2,1,0:T(8,128)}, u32[]{:S(2)}) copy-start(f32[2,16,8,128]{3,2,1,0:T(8,128)} %constant.17.clone) | copy-start | bytes 393220
  0.7 7.7 %copy-start.2 = (f32[128,2048]{1,0:T(8,128)S(1)}, f32[128,2048]{1,0:T(8,128)}, u32[]{:S(2)}) copy-start(f32[128,2048]{1,0:T(8,128)} %param.19) | copy-start | bytes 3145732
  2.6 30.2 %collective-permute-start.4 = (f32[4,128,128]{2,1,0:T(8,128)S(1)}, f32[4,128,128]{2,1,0:T(8,128)}, u32[]{:S(2)}, u32[]{:S(2)}) collective-permute-start(f32[4,128,128]{2,1,0:T(8,128)S(1)} %get-tuple-element.170), channel_id=1, source_target_pairs={{0,4},{1,5},{2,6},{3,7},{4,0},{5,1},{6,2},{7,3},{8,12},{9,13},{10,... | collective-permute-start | bytes 786440 | tf_op jit(solution)/shard_map/ppermute | solution.py:458
  5.7 27.4 %collective-permute-start.5 = (f32[4,128,128]{2,1,0:T(8,128)S(1)}, f32[4,128,128]{2,1,0:T(8,128)}, u32[]{:S(2)}, u32[]{:S(2)}) collective-permute-start(f32[4,128,128]{2,1,0:T(8,128)S(1)} %get-tuple-element.171), channel_id=1, source_target_pairs={{0,8},{1,9},{2,10},{3,11},{4,12},{5,13},{6,14},{7,15},{8,0},{9,1},... | collective-permute-start | bytes 786440 | tf_op jit(solution)/shard_map/ppermute | solution.py:458
  8.3 24.8 %collective-permute-start.6 = (f32[4,128,128]{2,1,0:T(8,128)S(1)}, f32[4,128,128]{2,1,0:T(8,128)}, u32[]{:S(2)}, u32[]{:S(2)}) collective-permute-start(f32[4,128,128]{2,1,0:T(8,128)S(1)} %get-tuple-element.172), channel_id=1, source_target_pairs={{0,12},{1,13},{2,14},{3,15},{4,8},{5,9},{6,10},{7,11},{8,4},{9,5},... | collective-permute-start | bytes 786440 | tf_op jit(solution)/shard_map/ppermute | solution.py:458
  10.8 16.9 %all-to-all-start = ((f32[4,4,128,128]{3,2,1,0:T(8,128)}), f32[4,4,128,128]{3,2,1,0:T(8,128)S(1)}, u32[]{:S(2)}, u32[]{:S(2)}) async-start(f32[4,4,128,128]{3,2,1,0:T(8,128)} %branch_1_fun.12), calls=%async_computation | async-start | bytes 2097152 | tf_op jit(solution)/shard_map/cond/branch_1_fun/all_to_all | solution.py:464
  28.6 33.1 %collective-permute-start.1 = (f32[4,128,128]{2,1,0:T(8,128)}, f32[4,128,128]{2,1,0:T(8,128)S(1)}, u32[]{:S(2)}, u32[]{:S(2)}) collective-permute-start(f32[4,128,128]{2,1,0:T(8,128)} %get-tuple-element.167), channel_id=1, source_target_pairs={{0,4},{1,5},{2,6},{3,7},{4,0},{5,1},{6,2},{7,3},{8,12},{9,13},{10,... | collective-permute-start | bytes 786440 | tf_op jit(solution)/shard_map/ppermute | solution.py:458
  29.3 32.8 %collective-permute-start.2 = (f32[4,128,128]{2,1,0:T(8,128)}, f32[4,128,128]{2,1,0:T(8,128)}, u32[]{:S(2)}, u32[]{:S(2)}) collective-permute-start(f32[4,128,128]{2,1,0:T(8,128)} %get-tuple-element.168), channel_id=1, source_target_pairs={{0,8},{1,9},{2,10},{3,11},{4,12},{5,13},{6,14},{7,15},{8,0},{9,1},... | collective-permute-start | bytes 786440 | tf_op jit(solution)/shard_map/ppermute | solution.py:458
  32.8 29.3 %collective-permute-start.3 = (f32[4,128,128]{2,1,0:T(8,128)}, f32[4,128,128]{2,1,0:T(8,128)}, u32[]{:S(2)}, u32[]{:S(2)}) collective-permute-start(f32[4,128,128]{2,1,0:T(8,128)} %get-tuple-element.169), channel_id=1, source_target_pairs={{0,12},{1,13},{2,14},{3,15},{4,8},{5,9},{6,10},{7,11},{8,4},{9,5},... | collective-permute-start | bytes 786440 | tf_op jit(solution)/shard_map/ppermute | solution.py:458
  35.3 16.0 %copy-start.3 = (bf16[768,256]{1,0:T(8,128)(2,1)S(1)}, bf16[768,256]{1,0:T(8,128)(2,1)}, u32[]{:S(2)}) copy-start(bf16[768,256]{1,0:T(8,128)(2,1)} %get-tuple-element.93.refs_3_) | copy-start | bytes 1179652 | tf_op jit(solution)/shard_map/cond
  35.3 16.0 %all-to-all-start.1 = ((f32[4,4,128,128]{3,2,1,0:T(8,128)}), f32[4,4,128,128]{3,2,1,0:T(8,128)S(1)}, u32[]{:S(2)}, u32[]{:S(2)}) async-start(f32[4,4,128,128]{3,2,1,0:T(8,128)} %branch_1_fun.15), calls=%async_computation.1 | async-start | bytes 2097152 | tf_op jit(solution)/shard_map/cond/branch_1_fun/all_to_all | solution.py:464
  57.7 32.5 %collective-permute-start.7 = (f32[4,128,128]{2,1,0:T(8,128)}, f32[4,128,128]{2,1,0:T(8,128)S(1)}, u32[]{:S(2)}, u32[]{:S(2)}) collective-permute-start(f32[4,128,128]{2,1,0:T(8,128)} %get-tuple-element.180), channel_id=1, source_target_pairs={{0,4},{1,5},{2,6},{3,7},{4,0},{5,1},{6,2},{7,3},{8,12},{9,13},{10,... | collective-permute-start | bytes 786440 | tf_op jit(solution)/shard_map/ppermute | solution.py:458
  58.2 32.4 %collective-permute-start.8 = (f32[4,128,128]{2,1,0:T(8,128)}, f32[4,128,128]{2,1,0:T(8,128)S(1)}, u32[]{:S(2)}, u32[]{:S(2)}) collective-permute-start(f32[4,128,128]{2,1,0:T(8,128)} %get-tuple-element.181), channel_id=1, source_target_pairs={{0,8},{1,9},{2,10},{3,11},{4,12},{5,13},{6,14},{7,15},{8,0},{9,1},... | collective-permute-start | bytes 786440 | tf_op jit(solution)/shard_map/ppermute | solution.py:458
  61.7 28.9 %collective-permute-start.9 = (f32[4,128,128]{2,1,0:T(8,128)}, f32[4,128,128]{2,1,0:T(8,128)}, u32[]{:S(2)}, u32[]{:S(2)}) collective-permute-start(f32[4,128,128]{2,1,0:T(8,128)} %get-tuple-element.182), channel_id=1, source_target_pairs={{0,12},{1,13},{2,14},{3,15},{4,8},{5,9},{6,10},{7,11},{8,4},{9,5},... | collective-permute-start | bytes 786440 | tf_op jit(solution)/shard_map/ppermute | solution.py:458
  62.2 28.4 %copy-start = (f32[1,2048,128]{2,1,0:T(8,128)S(1)}, f32[1,2048,128]{2,1,0:T(8,128)}, u32[]{:S(2)}) copy-start(f32[1,2048,128]{2,1,0:T(8,128)} %param.17) | copy-start | bytes 3145732
  69.1 3.7 %copy-start.4 = (bf16[768,256]{1,0:T(8,128)(2,1)S(1)}, bf16[768,256]{1,0:T(8,128)(2,1)}, u32[]{:S(2)}) copy-start(bf16[768,256]{1,0:T(8,128)(2,1)} %get-tuple-element.107.refs_6_.refs_1_) | copy-start | bytes 1179652 | tf_op jit(solution)/shard_map/cond
  69.1 16.0 %all-to-all-start.2 = ((f32[4,4,128,128]{3,2,1,0:T(8,128)}), f32[4,4,128,128]{3,2,1,0:T(8,128)S(1)}, u32[]{:S(2)}, u32[]{:S(2)}) async-start(f32[4,4,128,128]{3,2,1,0:T(8,128)} %get-tuple-element.111), calls=%async_computation.2 | async-start | bytes 2097152 | tf_op jit(solution)/shard_map/cond/branch_1_fun/all_to_all | solution.py:464
  86.1 27.3 %collective-permute-start.10 = (f32[4,128,128]{2,1,0:T(8,128)}, f32[4,128,128]{2,1,0:T(8,128)S(1)}, u32[]{:S(2)}, u32[]{:S(2)}) collective-permute-start(f32[4,128,128]{2,1,0:T(8,128)} %get-tuple-element.185), channel_id=1, source_target_pairs={{0,4},{1,5},{2,6},{3,7},{4,0},{5,1},{6,2},{7,3},{8,12},{9,13},{10,... | collective-permute-start | bytes 786440 | tf_op jit(solution)/shard_map/ppermute | solution.py:458
  86.6 26.8 %collective-permute-start.11 = (f32[4,128,128]{2,1,0:T(8,128)}, f32[4,128,128]{2,1,0:T(8,128)S(1)}, u32[]{:S(2)}, u32[]{:S(2)}) collective-permute-start(f32[4,128,128]{2,1,0:T(8,128)} %get-tuple-element.186), channel_id=1, source_target_pairs={{0,8},{1,9},{2,10},{3,11},{4,12},{5,13},{6,14},{7,15},{8,0},{9,1},... | collective-permute-start | bytes 786440 | tf_op jit(solution)/shard_map/ppermute | solution.py:458
  90.2 23.2 %collective-permute-start.12 = (f32[4,128,128]{2,1,0:T(8,128)}, f32[4,128,128]{2,1,0:T(8,128)S(1)}, u32[]{:S(2)}, u32[]{:S(2)}) collective-permute-start(f32[4,128,128]{2,1,0:T(8,128)} %get-tuple-element.187), channel_id=1, source_target_pairs={{0,12},{1,13},{2,14},{3,15},{4,8},{5,9},{6,10},{7,11},{8,4},{9,5},... | collective-permute-start | bytes 786440 | tf_op jit(solution)/shard_map/ppermute | solution.py:458
  90.6 7.6 %collective-permute-start = (f32[128,2048]{1,0:T(8,128)}, f32[128,2048]{1,0:T(8,128)}, u32[]{:S(2)}, u32[]{:S(2)}) collective-permute-start(f32[128,2048]{1,0:T(8,128)} %get-tuple-element.123), channel_id=1, source_target_pairs={{0,16},{16,0},{1,17},{17,1},{2,18},{18,2},{3,19},{19,3},{4,20},{20... | collective-permute-start | bytes 3145736 | tf_op jit(solution)/shard_map/cond/branch_1_fun/ppermute | solution.py:547
  92.7 18.1 %all-to-all-start.3 = ((f32[4,4,128,128]{3,2,1,0:T(8,128)}), f32[4,4,128,128]{3,2,1,0:T(8,128)S(1)}, u32[]{:S(2)}, u32[]{:S(2)}) async-start(f32[4,4,128,128]{3,2,1,0:T(8,128)} %branch_1_fun.22), calls=%async_computation.3 | async-start | bytes 2097152 | tf_op jit(solution)/shard_map/cond/branch_1_fun/all_to_all | solution.py:464
  110.8 2.6 %copy-start.7 = (f32[4,128,128]{2,1,0:T(8,128)S(1)}, f32[4,128,128]{2,1,0:T(8,128)}, u32[]{:S(2)}) copy-start(f32[4,128,128]{2,1,0:T(8,128)} %get-tuple-element.233) | copy-start | bytes 786436 | tf_op jit(solution)/shard_map/cond
  (1 other events, 2.6 us)
